TPU v7x, 32 devices: a whole 2x2x4 slice. The times are simulated.
32 devices in a mesh: dp: 16 (over z, y, x), tensor: 2 (over core).
Axes of the slice: x: 2, y: 2, z: 4, core: 2. Of those that a mesh axis runs over, the one named last changes fastest.
Arguments:
- queries: bfloat16 [4096, 4096], P('dp', 'tensor'), may hold values from -8 to 8
- neighbour_keys: bfloat16 [128, 128, 4096], P('dp', None, 'tensor'), may hold values from -8 to 8
- neighbour_values: bfloat16 [128, 128, 4096], P('dp', None, 'tensor'), may hold values from -6 to 6
- residual: bfloat16 [4096, 4096], P(('dp', 'tensor')), may hold values from -1.5 to 1.5
- out_weight: bfloat16 [4096, 4096], P('tensor', 'dp'), may hold values from -0.09375 to 0.09375
- drop_mask: int32 [4096, 4096], P(('dp', 'tensor')), may hold values 0 or 1
- norm_gain: float32 [4096], replicated, may hold values from 0.5 to 1.5
- norm_bias: float32 [4096], replicated, may hold values from -0.5 to 0.5
- neighbour_owner: int32 [64, 2], P('dp'), may hold values from 0 to 15, as said below
- neighbour_slot: int32 [64, 2], P('dp'), may hold values from 0 to 7, as said below
Outputs:
- residual_next: bfloat16 [4096, 4096], P(('dp', 'tensor'))
- layer_normed: bfloat16 [4096, 4096], P(('dp', 'tensor'))
Inputs may be any that keep to these rules, and one draw needn't show every extreme that they name: `neighbour_owner`: the 8 neighbours of the blocks of one dp index are stored on 8 different devices. A device receives at most 12 of all blocks' neighbour requests, and some device exactly that many. `neighbour_slot`: several blocks may use the same stored row.
All inputs are finite; a program needn't handle non-finite values. No bound on the sum of `drop_mask` on one device may be relied on, other than what follows from the above.
Results may differ from a plain program's by a relative error of at most 0.017.
Values may be sent and summed in bfloat16 or wider, within the bound.
No kernel may reach another device: no remote copies, remote signals or barrier semaphores. Data moves between devices by JAX's collectives and lax.ppermute only.
A program may use at most 128 MiB of HBM per device.

v0:
```python
import math

import jax
import jax.numpy as jnp
from jax import lax
from jax.sharding import PartitionSpec as P

HEAD = 128


keep_rate = 0.9
norm_eps = 1e-05


def shifted(x, axis, by):
    count = lax.axis_size(axis)
    pairs = [(i, i + by) for i in range(count) if 0 <= i + by < count]
    return lax.ppermute(x, axis, pairs)


def attend_block(query_rows, key_rows, value_rows):
    count_b, count_r, row_width = query_rows.shape
    length = key_rows.shape[1]
    heads_here = row_width // HEAD
    query_heads = query_rows.reshape(count_b, count_r, heads_here, HEAD)
    key_heads = key_rows.reshape(count_b, length, heads_here, HEAD)
    value_heads = value_rows.reshape(count_b, length, heads_here, HEAD)
    scores = jnp.einsum(
        "brhe,blhe->bhrl", query_heads, key_heads, preferred_element_type=jnp.float32
    ) * HEAD ** (-0.5)
    peak_rows = jnp.max(scores, axis=-1)
    raised = jnp.exp(scores - peak_rows[..., None])
    totals = jnp.sum(raised, axis=-1)
    weights = (raised / totals[..., None]).astype(jnp.bfloat16)
    partial_value = jnp.einsum(
        "bhrl,blhe->brhe", weights, value_heads, preferred_element_type=jnp.float32
    )
    partial_value = partial_value.astype(jnp.bfloat16).reshape(count_b, count_r, row_width)
    return (partial_value, jnp.transpose(peak_rows, (0, 2, 1)), jnp.transpose(totals, (0, 2, 1)))


def merge_pair(partials, peak_rows, totals):
    highest = jnp.max(peak_rows, axis=1, keepdims=True)
    merge_weight = totals * jnp.exp(peak_rows - highest)
    weight_sum = jnp.sum(merge_weight, axis=1)
    part_shape = partials.shape
    part_heads = partials.reshape(part_shape[0], part_shape[1], part_shape[2], -1, HEAD).astype(
        jnp.float32
    )
    combined = jnp.sum(part_heads * merge_weight[..., None], axis=1) / weight_sum[..., None]
    return combined.reshape(part_shape[0], part_shape[2], part_shape[3]).astype(jnp.bfloat16)


def local(
    queries,
    neighbour_keys,
    neighbour_values,
    residual,
    out_weight,
    drop_mask,
    norm_gain,
    norm_bias,
    neighbour_owner,
    neighbour_slot,
):
    peer_count = lax.axis_size("dp")
    row_width = queries.shape[1]
    capacity = neighbour_keys.shape[0]
    blocks = neighbour_owner.shape[0]
    span_len = queries.shape[0] // blocks
    carried = shifted(queries[-1:], "dp", 1)
    block_queries = jnp.concatenate([carried, queries[:-1]], axis=0).reshape(
        blocks, span_len, row_width
    )
    owners = neighbour_owner.reshape(-1)
    slot_rows = neighbour_slot.reshape(-1)
    pair_count = owners.shape[0]
    per_block = pair_count // blocks
    peer_ids = jnp.arange(peer_count, dtype=jnp.int32)
    selector = owners[None, :] == peer_ids[:, None]
    repeated = jnp.repeat(block_queries, per_block, axis=0)
    outgoing = jnp.einsum(
        "pn,ncw->pcw", selector.astype(jnp.bfloat16), repeated, preferred_element_type=jnp.float32
    ).astype(jnp.bfloat16)
    wanted = jnp.sum(jnp.where(selector, slot_rows[None, :] + 1, 0), axis=1) - 1
    wanted_rows = jnp.broadcast_to(wanted[:, None], (peer_count, span_len))
    asked_rows = lax.all_to_all(outgoing, "dp", split_axis=0, concat_axis=0, tiled=True)
    asked_slot = lax.all_to_all(wanted_rows, "dp", split_axis=0, concat_axis=0, tiled=True)
    peer_slot = jnp.max(asked_slot, axis=1, initial=-1)
    chosen = jnp.clip(peer_slot, 0, capacity - 1)
    group_size = math.gcd(peer_count, 16)
    rounds = peer_count // group_size

    def one_group(group_items):
        group_rows, group_slots = group_items
        return attend_block(
            group_rows,
            jnp.take(neighbour_keys, group_slots, axis=0),
            jnp.take(neighbour_values, group_slots, axis=0),
        )

    results = lax.map(
        one_group,
        (
            asked_rows.reshape((rounds, group_size) + asked_rows.shape[1:]),
            chosen.reshape(rounds, group_size),
        ),
    )
    part_answer = results[0].reshape((peer_count,) + results[0].shape[2:])
    peak_answer = results[1].reshape((peer_count,) + results[1].shape[2:])
    total_answer = results[2].reshape((peer_count,) + results[2].shape[2:])
    part_back = lax.all_to_all(part_answer, "dp", split_axis=0, concat_axis=0, tiled=True)
    own_partial = jnp.take(part_back, owners, axis=0).reshape(
        blocks, per_block, span_len, row_width
    )
    own_peak = jnp.take(
        lax.all_to_all(peak_answer, "dp", split_axis=0, concat_axis=0, tiled=True), owners, axis=0
    ).reshape(blocks, per_block, span_len, -1)
    own_total = jnp.take(
        lax.all_to_all(total_answer, "dp", split_axis=0, concat_axis=0, tiled=True), owners, axis=0
    ).reshape(blocks, per_block, span_len, -1)
    merged = merge_pair(own_partial, own_peak, own_total)
    flat_rows = merged.reshape(-1, row_width)
    following = shifted(flat_rows[:1], "dp", -1)
    cross_rows = jnp.concatenate([flat_rows[1:], following], axis=0)
    whole_weight = lax.all_gather(out_weight, "dp", axis=1, tiled=True)
    branch = lax.psum_scatter(
        jnp.dot(cross_rows, whole_weight, preferred_element_type=jnp.float32).astype(jnp.bfloat16),
        "tensor",
        scatter_dimension=0,
        tiled=True,
    ).astype(jnp.float32)
    keep_scale = drop_mask.astype(jnp.float32) * (1.0 / keep_rate)
    stream = residual.astype(jnp.float32) + keep_scale * branch
    centre = jnp.mean(stream, axis=1, keepdims=True)
    spread = jnp.mean(jnp.square(stream - centre), axis=1, keepdims=True)
    normed = (stream - centre) * lax.rsqrt(spread + norm_eps) * norm_gain + norm_bias
    return (stream.astype(jnp.bfloat16), normed.astype(jnp.bfloat16))


def solution(mesh):
    placed = (
        P("dp", "tensor"),
        P("dp", None, "tensor"),
        P("dp", None, "tensor"),
        P(("dp", "tensor"), None),
        P("tensor", "dp"),
        P(("dp", "tensor"), None),
        P(),
        P(),
        P("dp", None),
        P("dp", None),
    )
    return jax.shard_map(
        local,
        mesh=mesh,
        in_specs=placed,
        out_specs=(P(("dp", "tensor"), None), P(("dp", "tensor"), None)),
        check_vma=False,
    )
```

profile of v0, /device:TPU:0, one launch (start us, length us, event | category | flops | bytes accessed | tf_op | source)
XLA Modules:
  0.0 449.6 jit_solution(1741660373379523364)
XLA Ops:
  7.2 0.0 all-gather.2.cloned.1.call-start
  7.2 0.7 all-gather.2.cloned.1.call-update
  7.9 0.8 slice.12
  8.7 4.8 %collective-permute-start = (bf16[1,2048]{1,0:T(2,128)(2,1)S(1)}, bf16[1,2048]{1,0:T(2,128)(2,1)S(1)}, u32[]{:S(2)}, u32[]{:S(2)}) collective-permute-start(bf16[1,2048]{1,0:T(2,128)(2,1)S(1)} %slice.12), channel_id=1, source_target_pairs={{0,2},{2,4},{4,6},{6,8},{8,10},{10,12},{12,14},{14,16},{16,18},{18... | collective-permute-start | bytes 12296 | tf_op jit(solution)/shard_map/ppermute | solution.py:18
  13.5 0.8 copy.67
  14.3 0.1 reshape.153
  14.4 0.7 broadcast_add_fusion
  15.1 0.1 copy.68
  15.2 0.1 add.66
  15.2 0.1 select_reduce_fusion
  15.3 0.7 broadcast_in_dim.73
  16.0 5.9 %all-to-all-start = ((s32[16,1,64]{2,1,0:T(1,128)}), s32[16,1,64]{2,1,0:T(1,128)S(1)}, u32[]{:S(2)}, u32[]{:S(2)}) async-start(s32[16,1,64]{2,1,0:T(1,128)} %broadcast_in_dim.73), calls=%async_computation | async-start | bytes 16384 | tf_op jit(solution)/shard_map/all_to_all | solution.py:88
  22.0 1.6 pad_maximum_fusion
  23.6 0.8 copy.70
  24.4 3.5 broadcast_in_dim.74
  27.8 2.7 reshape.156
  30.6 1.7 convolution_convert_fusion.1
  32.3 4.2 copy.71
  36.5 7.0 %all-to-all-start.1 = ((bf16[16,64,2048]{2,1,0:T(8,128)(2,1)}), bf16[16,64,2048]{2,1,0:T(8,128)(2,1)}, u32[]{:S(2)}, u32[]{:S(2)}) async-start(bf16[16,64,2048]{2,1,0:T(8,128)(2,1)} %copy.71), calls=%async_computation.1 | async-start | bytes 8388608 | tf_op jit(solution)/shard_map/all_to_all | solution.py:87
  43.5 0.1 reduce_max.28
  43.6 6.8 %gather_fusion.1 = bf16[16,128,2048]{2,1,0:T(8,128)(2,1)} fusion(bf16[8,128,2048]{2,1,0:T(8,128)(2,1)} %param.16, s32[1024]{0:T(1024)S(1)} %pad_clamp_fusion.2), kind=kCustom, calls=%fused_computation.clone | custom fusion | bytes 16777280 | tf_op jit(solution)/shard_map/while/body/eval_jaxpr/jit(_take)/gather | solution.py:99
  50.5 6.8 %gather_fusion.2 = bf16[16,128,2048]{2,1,0:T(8,128)(2,1)} fusion(bf16[8,128,2048]{2,1,0:T(8,128)(2,1)} %param.15, s32[1024]{0:T(1024)S(1)} %pad_clamp_fusion.2), kind=kCustom, calls=%fused_computation.2.clone | custom fusion | bytes 16777280 | tf_op jit(solution)/shard_map/while/body/eval_jaxpr/jit(_take)/gather | solution.py:98
  57.2 11.6 %select_bitcast_fusion.1 = (bf16[16,16,16,8,128]{4,3,2,1,0:T(8,128)(2,1)}, bf16[16,16,16,8,128]{4,3,2,1,0:T(8,128)(2,1)}) fusion(bf16[16,128,2048]{2,1,0:T(8,128)(2,1)} %gather_fusion.1, pred[16]{0:T(512)(128)(4,1)S(1)} %get-tuple-element.32, bf16[16,128,2048]{2,1,0:T(8,128)(2,1)} %gather_fusion.2), kind=kLoop, calls=%fused_computation.12 | loop fusion | flops 8388608 | bytes 33554448
  68.8 91.0 %all-to-all-done.1 = bf16[16,64,2048]{2,1,0:T(8,128)(2,1)} async-done(((bf16[16,64,2048]{2,1,0:T(8,128)(2,1)}), bf16[16,64,2048]{2,1,0:T(8,128)(2,1)}, u32[]{:S(2)}, u32[]{:S(2)}) %all-to-all-start.1) | async-done | bytes 4194336 | tf_op jit(solution)/shard_map/all_to_all | solution.py:87
  159.9 14.0 %multiply_reduce_fusion = (f32[16,16,64]{2,1,0:T(8,128)S(1)}, f32[16,16,64,128]{3,2,1,0:T(8,128)}) fusion(bf16[16,16,16,8,128]{4,3,2,1,0:T(8,128)(2,1)} %get-tuple-element.37, bf16[16,64,2048]{2,1,0:T(8,128)(2,1)} %all-to-all-done.1), kind=kOutput, calls=%fused_computation.15 | convolution fusion | flops 541048832 | bytes 21037056 | tf_op jit(solution)/shard_map/while/body/eval_jaxpr/brhe,blhe->bhrl/dot_general | solution.py:28
  173.9 7.0 %fusion.6 = f32[16,16,64]{2,1,0:T(8,128)S(1)} fusion(f32[16,16,64,128]{3,2,1,0:T(8,128)} %get-tuple-element.39, f32[16,16,64]{2,1,0:T(8,128)S(1)} %get-tuple-element.38), kind=kLoop, calls=%fused_computation.16 | loop fusion | flops 6275072 | bytes 8519680 | tf_op jit(solution)/shard_map/while/body/eval_jaxpr/reduce_sum | solution.py:33
  180.9 0.8 reshape.216
  181.7 47.2 %all-to-all-start.3 = ((f32[16,1,1024]{2,1,0:T(1,128)}), f32[16,1,1024]{2,1,0:T(1,128)S(1)}, u32[]{:S(2)}, u32[]{:S(2)}) async-start(f32[16,1,1024]{2,1,0:T(1,128)} %reshape.216), calls=%async_computation.3 | async-start | bytes 131072 | tf_op jit(solution)/shard_map/all_to_all | solution.py:120
  228.9 0.8 reshape.218
  229.7 13.0 %all-to-all-done.3 = f32[16,1,1024]{2,1,0:T(1,128)S(1)} async-done(((f32[16,1,1024]{2,1,0:T(1,128)}), f32[16,1,1024]{2,1,0:T(1,128)S(1)}, u32[]{:S(2)}, u32[]{:S(2)}) %all-to-all-start.3) | async-done | bytes 65568 | tf_op jit(solution)/shard_map/all_to_all | solution.py:120
  242.7 3.5 all-to-all-start.4
  246.2 8.7 %convert_bitcast_fusion = bf16[16,16,8,8,128]{4,3,2,1,0:T(8,128)(2,1)S(1)} fusion(bf16[16,16,16,8,128]{4,3,2,1,0:T(8,128)(2,1)} %get-tuple-element.36, f32[16,16,64,128]{3,2,1,0:T(8,128)} %get-tuple-element.39, f32[16,16,64]{2,1,0:T(8,128)S(1)} %fusion.6, f32[16,16,64]{2,1,0:T(8,128)S(1)} %get-tuple-element.38), kind=kOutput, calls=%fused_computation.22 | convolution fusion | flops 547356672 | bytes 21102592 | tf_op jit(solution)/shard_map/while/body/eval_jaxpr/bhrl,blhe->brhe/dot_general | solution.py:35
  254.9 3.1 copy.105
  258.1 14.8 %all-to-all-start.2 = ((bf16[16,64,2048]{2,1,0:T(8,128)(2,1)}), bf16[16,64,2048]{2,1,0:T(8,128)(2,1)}, u32[]{:S(2)}, u32[]{:S(2)}) async-start(bf16[16,64,2048]{2,1,0:T(8,128)(2,1)} %bitcast.70), calls=%async_computation.2 | async-start | bytes 8388608 | tf_op jit(solution)/shard_map/all_to_all | solution.py:112
  272.9 0.3 reduce-scatter.2.cloned.1.call-start
  273.1 0.1 reshape.160
  273.2 0.1 copy.66
  273.4 0.5 broadcast.185
  273.9 0.8 reduce.2
  274.7 0.1 reshape.217
  274.8 0.8 reduce.1
  275.6 0.1 reshape.219
  275.7 0.6 gather_fusion.3
  276.3 0.6 gather_fusion.4
  276.8 0.1 bitcast_reduce_fusion
  276.9 0.1 fusion.26
  277.0 0.1 copy.77
  277.1 0.1 copy.78
  277.2 112.2 %all-to-all-done.2 = bf16[16,64,2048]{2,1,0:T(8,128)(2,1)} async-done(((bf16[16,64,2048]{2,1,0:T(8,128)(2,1)}), bf16[16,64,2048]{2,1,0:T(8,128)(2,1)}, u32[]{:S(2)}, u32[]{:S(2)}) %all-to-all-start.2) | async-done | bytes 4194336 | tf_op jit(solution)/shard_map/all_to_all | solution.py:112
  389.4 2.9 gather_fusion
  392.3 0.6 copy.83
  392.9 1.4 multiply_reduce_fusion.1
  394.3 0.7 divide_convert_fusion.4
  395.1 0.3 copy.106
  395.4 1.3 collective-permute-start.1
  396.7 1.2 slice.26
  397.9 3.0 collective-permute-done.1
  400.9 12.0 %convolution_convert_fusion = bf16[256,4096]{1,0:T(8,128)(2,1)} fusion(bf16[2048,4096]{1,0:T(8,128)(2,1)} %all-gather.2.cloned.1.call-done, bf16[1,2048]{1,0:T(2,128)(2,1)S(1)} %collective-permute-done.1, bf16[255,2048]{1,0:T(8,128)(2,1)} %slice.26), kind=kOutput, calls=%fused_computation.17 | convolution fusion | flops 4298113024 | bytes 19922944 | tf_op jit(solution)/shard_map/dot_general | solution.py:128
  412.9 0.0 reduce-scatter.2.cloned.1.call-update
  412.9 0.0 copy-start.2
  412.9 25.9 %reduce-scatter.2.cloned.1.call-done = bf16[128,4096]{1,0:T(8,128)(2,1)} async-done(((bf16[256,4096]{1,0:T(8,128)(2,1)}), bf16[128,4096]{1,0:T(8,128)(2,1)}) %reduce-scatter.2.cloned.1.call-update) | async-done | bytes 1048592 | tf_op jit(solution)/shard_map/reduce_scatter | solution.py:127
  438.8 1.8 fusion.25
  440.6 0.4 multiply_reduce_fusion.2
  441.0 1.8 add_convert_fusion
  (27 shorter events, 0.1 us)
Async XLA Ops:
  7.2 393.7 %all-gather.2.cloned.1.call-start = ((), (), s32[]{:S(2)}) async-start(), calls=%async_computation.6 | async-start | bytes 17825792 | tf_op jit(solution)/shard_map/all_gather | solution.py:126
  8.7 13.3 %collective-permute-start = (bf16[1,2048]{1,0:T(2,128)(2,1)S(1)}, bf16[1,2048]{1,0:T(2,128)(2,1)S(1)}, u32[]{:S(2)}, u32[]{:S(2)}) collective-permute-start(bf16[1,2048]{1,0:T(2,128)(2,1)S(1)} %slice.12), channel_id=1, source_target_pairs={{0,2},{2,4},{4,6},{6,8},{8,10},{10,12},{12,14},{14,16},{16,18},{18... | collective-permute-start | bytes 12296 | tf_op jit(solution)/shard_map/ppermute | solution.py:18
  16.0 20.5 %all-to-all-start = ((s32[16,1,64]{2,1,0:T(1,128)}), s32[16,1,64]{2,1,0:T(1,128)S(1)}, u32[]{:S(2)}, u32[]{:S(2)}) async-start(s32[16,1,64]{2,1,0:T(1,128)} %broadcast_in_dim.73), calls=%async_computation | async-start | bytes 16384 | tf_op jit(solution)/shard_map/all_to_all | solution.py:88
  36.5 123.3 %all-to-all-start.1 = ((bf16[16,64,2048]{2,1,0:T(8,128)(2,1)}), bf16[16,64,2048]{2,1,0:T(8,128)(2,1)}, u32[]{:S(2)}, u32[]{:S(2)}) async-start(bf16[16,64,2048]{2,1,0:T(8,128)(2,1)} %copy.71), calls=%async_computation.1 | async-start | bytes 8388608 | tf_op jit(solution)/shard_map/all_to_all | solution.py:87
  181.7 61.0 %all-to-all-start.3 = ((f32[16,1,1024]{2,1,0:T(1,128)}), f32[16,1,1024]{2,1,0:T(1,128)S(1)}, u32[]{:S(2)}, u32[]{:S(2)}) async-start(f32[16,1,1024]{2,1,0:T(1,128)} %reshape.216), calls=%async_computation.3 | async-start | bytes 131072 | tf_op jit(solution)/shard_map/all_to_all | solution.py:120
  242.7 15.4 %all-to-all-start.4 = ((f32[16,1,1024]{2,1,0:T(1,128)}), f32[16,1,1024]{2,1,0:T(1,128)S(1)}, u32[]{:S(2)}, u32[]{:S(2)}) async-start(f32[16,1,1024]{2,1,0:T(1,128)} %reshape.218), calls=%async_computation.4 | async-start | bytes 131072 | tf_op jit(solution)/shard_map/all_to_all | solution.py:117
  258.1 15.2 %copy-start.4 = (s32[4,2]{0,1:T(2,128)S(1)}, s32[4,2]{0,1:T(2,128)}, u32[]{:S(2)}) copy-start(s32[4,2]{0,1:T(2,128)} %param.22) | copy-start | bytes 100
  258.1 131.3 %all-to-all-start.2 = ((bf16[16,64,2048]{2,1,0:T(8,128)(2,1)}), bf16[16,64,2048]{2,1,0:T(8,128)(2,1)}, u32[]{:S(2)}, u32[]{:S(2)}) async-start(bf16[16,64,2048]{2,1,0:T(8,128)(2,1)} %bitcast.70), calls=%async_computation.2 | async-start | bytes 8388608 | tf_op jit(solution)/shard_map/all_to_all | solution.py:112
  272.9 165.9 %reduce-scatter.2.cloned.1.call-start = ((), (), s32[]{:S(2)}) async-start(), calls=%async_computation.7 | async-start | bytes 3145728 | tf_op jit(solution)/shard_map/reduce_scatter | solution.py:127
  395.4 5.5 %collective-permute-start.1 = (bf16[1,2048]{1,0:T(2,128)(2,1)S(1)}, bf16[1,2048]{1,0:T(2,128)(2,1)S(1)}, u32[]{:S(2)}, u32[]{:S(2)}) collective-permute-start(bf16[1,2048]{1,0:T(2,128)(2,1)S(1)} %slice.27), channel_id=1, source_target_pairs={{2,0},{4,2},{6,4},{8,6},{10,8},{12,10},{14,12},{16,14},{18,16},{20... | collective-permute-start | bytes 12296 | tf_op jit(solution)/shard_map/ppermute | solution.py:18
  397.9 40.9 %copy-start = (s32[128,4096]{1,0:T(8,128)S(1)}, s32[128,4096]{1,0:T(8,128)}, u32[]{:S(2)}) copy-start(s32[128,4096]{1,0:T(8,128)} %param.19) | copy-start | bytes 6291460
  397.9 40.9 %copy-start.1 = (bf16[128,4096]{1,0:T(8,128)(2,1)S(1)}, bf16[128,4096]{1,0:T(8,128)(2,1)}, u32[]{:S(2)}) copy-start(bf16[128,4096]{1,0:T(8,128)(2,1)} %param.17) | copy-start | bytes 3145732
  412.9 28.1 %copy-start.2 = (f32[4096]{0:T(1024)S(1)}, f32[4096]{0:T(1024)}, u32[]{:S(2)}) copy-start(f32[4096]{0:T(1024)} %param.21) | copy-start | bytes 49156
  412.9 28.1 %copy-start.3 = (f32[4096]{0:T(1024)S(1)}, f32[4096]{0:T(1024)}, u32[]{:S(2)}) copy-start(f32[4096]{0:T(1024)} %param.20) | copy-start | bytes 49156
Sparse Core Ops, SparseCore 0:
  10.7 372.2 all-gather.1
  413.0 25.7 reduce-scatter.1
where the time goes:
time: 451 us; the launch traced here: 450 us
  waiting for transfers between devices  246 us (55%)
  starting transfers between devices  84.9 us (19%)
  local copies, waits for them, and re-layouts  39.2 us (9%)
  matrix products  36.4 us (8%)
  other arithmetic  29 us (6%)
  between operations  14.4 us (3%)
    all_to_all x1, waiting for transfers between devices, local(): lax.all_to_all(part_answer, 'dp', split_axis=0, concat_axis=0, tiled=True)  112 us
    all_to_all x1, waiting for transfers between devices, local(): lax.all_to_all(outgoing, 'dp', split_axis=0, concat_axis=0, tiled=True)  91 us
    all_to_all x1, starting transfers between devices, local(): lax.all_to_all(total_answer, 'dp', split_axis=0, concat_axis=0, tiled=True)  47.2 us
    reduce_scatter x1, waiting for transfers between devices, local(): lax.psum_scatter(jnp.dot(cross_rows, whole_weight, preferred_element_type...  25.9 us
    all_to_all x1, starting transfers between devices, local(): lax.all_to_all(part_answer, 'dp', split_axis=0, concat_axis=0, tiled=True)  14.8 us
    dot_general x1, matrix products, attend_block(): jnp.einsum('brhe,blhe->bhrl', query_heads, key_heads, preferred_element_t...  14 us
    all_to_all x1, waiting for transfers between devices, local(): lax.all_to_all(total_answer, 'dp', split_axis=0, concat_axis=0, tiled=True)  13 us
    dot_general x1, matrix products, local(): jnp.dot(cross_rows, whole_weight, preferred_element_type=jnp.float32)  12 us
  transfers between devices with their start and end apart: 9, of which 5 were waited for; matrix products, arithmetic and copies ran while one was open for 20% of the time, Pallas kernels for 0%

commit v1 on v0

v1 whole, which is shorter than its diff:
```python
import functools

import jax
import jax.numpy as jnp
from jax import lax
from jax.experimental import pallas as pl
from jax.experimental.pallas import tpu as pltpu
from jax.sharding import PartitionSpec as P

HEAD = 128
LANES = 128
MIB = 1024 * 1024
ROW_TILE = 16
PLANE = 4

keep_rate = 0.9
norm_eps = 1e-05


def shifted(x, axis, by):
    count = lax.axis_size(axis)
    pairs = [(i, i + by) for i in range(count) if 0 <= i + by < count]
    return lax.ppermute(x, axis, pairs)


def spread_kernel(tagged, block_ref, slot_ref, carried_ref, *refs):
    *pieces, out_ref, moved, tags, sems = refs
    peers, span_len, _ = out_ref.shape
    rows, piece_width = pieces[0].shape
    row_width = moved.shape[1]
    at = 0
    for piece in pieces:
        for start in range(0, piece_width, 512):
            size = min(512, piece_width - start)
            held = piece[:, start : start + size].astype(jnp.float32)
            rolled = pltpu.roll(held, 1, 0)
            first = lax.broadcasted_iota(jnp.int32, (rows, size), 0) == 0
            above = carried_ref[0:1, at : at + size].astype(jnp.float32)
            moved[:, at : at + size] = jnp.where(first, above, rolled).astype(moved.dtype)
            at += size

    def copies(peer):
        start = pl.multiple_of(block_ref[peer] * span_len, span_len)
        yield pltpu.make_async_copy(
            moved.at[pl.ds(start, span_len)],
            out_ref.at[peer, :, pl.ds(0, row_width)],
            sems.at[0, peer],
        )
        if tagged:
            yield pltpu.make_async_copy(
                tags.at[peer], out_ref.at[peer, :, pl.ds(row_width, LANES)], sems.at[1, peer]
            )

    for peer in range(peers):
        if tagged:
            slot = slot_ref[peer].astype(jnp.float32)
            tags[peer] = jnp.full((span_len, LANES), slot, jnp.float32).astype(tags.dtype)
        for copy in copies(peer):
            copy.start()
    for peer in range(peers):
        for copy in copies(peer):
            copy.wait()


def spread(pieces, carried, block_of_peer, slot_of_peer, span_len, chunk, tagged):
    peers = block_of_peer.shape[0]
    rows, piece_width = pieces[0].shape
    row_width = piece_width * len(pieces)
    wide = row_width + (LANES if tagged else 0)
    return pl.pallas_call(
        functools.partial(spread_kernel, tagged),
        grid_spec=pltpu.PrefetchScalarGridSpec(
            num_scalar_prefetch=2,
            grid=(1,),
            in_specs=[pl.BlockSpec((1, row_width), lambda i, *_: (0, chunk))]
            + [pl.BlockSpec((rows, piece_width), lambda i, *_: (0, 0))] * len(pieces),
            out_specs=pl.BlockSpec(memory_space=pl.ANY),
            scratch_shapes=[
                pltpu.VMEM((rows, row_width), carried.dtype),
                pltpu.VMEM((peers, span_len, LANES), carried.dtype),
                pltpu.SemaphoreType.DMA((2, peers)),
            ],
        ),
        out_shape=jax.ShapeDtypeStruct((peers, span_len, wide), carried.dtype),
        compiler_params=pltpu.CompilerParams(vmem_limit_bytes=32 * MIB),
        name="spread_queries",
    )(block_of_peer, slot_of_peer, carried, *pieces)


def pack_levels(stats, heads):
    part = lax.broadcasted_iota(jnp.int32, stats.shape, 1) // heads
    high = stats.astype(jnp.bfloat16).astype(jnp.float32)
    rest = stats - high
    middle = rest.astype(jnp.bfloat16).astype(jnp.float32)
    low = rest - middle
    return jnp.where(part == 0, high, jnp.where(part == 1, middle, jnp.where(part == 2, low, 0.0)))


def unpack_levels(packed, heads):
    packed = packed.astype(jnp.float32)
    return (
        packed
        + pltpu.roll(packed, LANES - heads, 1)
        + pltpu.roll(packed, LANES - 2 * heads, 1)
    )


def attend_kernel(valid_ref, slot_ref, query_ref, key_ref, value_ref, out_ref):
    row_width = query_ref.shape[2]
    span_len = query_ref.shape[1]
    length = key_ref.shape[1]
    heads = row_width // HEAD
    group = min(heads, 4)
    peer = pl.program_id(0)

    @pl.when(valid_ref[peer] > 0)
    def _():
        lane = lax.broadcasted_iota(jnp.int32, (span_len, LANES), 1)
        stats = jnp.zeros((span_len, LANES), jnp.float32)
        ones = jnp.ones((length, HEAD), jnp.bfloat16)
        for first in range(0, heads, group):
            chosen = range(first, first + group)
            cuts = [slice(head * HEAD, (head + 1) * HEAD) for head in chosen]
            scores = [
                lax.dot_general(
                    query_ref[0, :, cut],
                    key_ref[0, :, cut],
                    (((1,), (1,)), ((), ())),
                    preferred_element_type=jnp.float32,
                )
                * HEAD ** (-0.5)
                for cut in cuts
            ]
            peaks = [jnp.max(score, axis=1, keepdims=True) for score in scores]
            raised = [
                jnp.exp(score - peak).astype(jnp.bfloat16) for score, peak in zip(scores, peaks)
            ]
            sums = [
                jnp.dot(
                    weight,
                    jnp.concatenate([value_ref[0, :, cut], ones], axis=1),
                    preferred_element_type=jnp.float32,
                )
                for weight, cut in zip(raised, cuts)
            ]
            for head, cut, peak, both in zip(chosen, cuts, peaks, sums):
                total = both[:, HEAD:]
                out_ref[0, :, cut] = (both[:, :HEAD] / total).astype(out_ref.dtype)
                stats = jnp.where(lane % heads == head, peak + jnp.log(total), stats)
        out_ref[0, :, row_width:] = pack_levels(stats, heads).astype(out_ref.dtype)


def attend(asked, keys, values, valid, slots, width, chunk, part):
    peers, span_len, _ = asked.shape
    length = keys.shape[1]
    heads = width // HEAD
    wide = width + LANES
    return pl.pallas_call(
        attend_kernel,
        grid_spec=pltpu.PrefetchScalarGridSpec(
            num_scalar_prefetch=2,
            grid=(peers,),
            in_specs=[
                pl.BlockSpec((1, span_len, width), lambda i, v, s: (i, 0, part)),
                pl.BlockSpec((1, length, width), lambda i, v, s: (s[i], 0, chunk)),
                pl.BlockSpec((1, length, width), lambda i, v, s: (s[i], 0, chunk)),
            ],
            out_specs=pl.BlockSpec((1, span_len, wide), lambda i, v, s: (i, 0, 0)),
        ),
        out_shape=jax.ShapeDtypeStruct((peers, span_len, wide), asked.dtype),
        compiler_params=pltpu.CompilerParams(vmem_limit_bytes=56 * MIB),
        cost_estimate=pl.CostEstimate(
            flops=4 * peers * heads * span_len * length * HEAD,
            bytes_accessed=2 * peers * width * (2 * span_len + 2 * length),
            transcendentals=peers * heads * span_len * length,
        ),
        name="attend_blocks",
    )(valid, slots, asked, keys, values)


def merge_block(uses, parts):
    row_width = parts[0].shape[2] - LANES
    heads = row_width // HEAD

    def masked(use, held, other):
        return held if use is None else jnp.where(use, held, other)

    levels = [
        masked(use, unpack_levels(ref[0, :, row_width:], heads), -1e30)
        for use, ref in zip(uses, parts)
    ]
    highest = functools.reduce(jnp.maximum, levels)
    weights = [jnp.exp(level - highest) for level in levels]
    total = functools.reduce(jnp.add, weights)
    weights = [weight / total for weight in weights]
    for head in range(heads):
        cut = slice(head * HEAD, (head + 1) * HEAD)
        merged = functools.reduce(
            jnp.add,
            [
                weight[:, head : head + 1]
                * masked(use, ref[0, :, cut].astype(jnp.float32), 0.0)
                for use, weight, ref in zip(uses, weights, parts)
            ],
        )
        yield cut, merged
    lane = lax.broadcasted_iota(jnp.int32, highest.shape, 1)
    level = jnp.where(lane < heads, highest + jnp.log(total), 0.0)
    level = level + pltpu.roll(level, heads, 1) + pltpu.roll(level, 2 * heads, 1)
    yield slice(row_width, row_width + LANES), pack_levels(level, heads)


def merge_far_kernel(picked, index_ref, use_ref, *refs):
    block = pl.program_id(0)
    uses = [use_ref[block * picked + r] > 0 for r in range(picked)]
    out_ref = refs[-1]
    for cut, merged in merge_block(uses, refs[:-1]):
        out_ref[0, :, cut] = merged.astype(out_ref.dtype)


def merge_all_kernel(picked, index_ref, use_ref, *refs):
    out_ref, kept = refs[-2:]
    parts = refs[:-2]
    span_len = parts[0].shape[1]
    rows, row_width = out_ref.shape
    rows -= ROW_TILE
    step = pl.program_id(0)
    block = rows // span_len - 1 - step
    uses = [use_ref[block * picked + r] > 0 for r in range(picked)] + [None]
    start = pl.multiple_of(block * span_len, span_len)
    last = lax.broadcasted_iota(jnp.int32, (span_len, HEAD), 0) == span_len - 1

    @pl.when(step == 0)
    def _():
        kept[...] = jnp.zeros_like(kept)

    for cut, merged in merge_block(uses, parts):
        if cut.start < row_width:
            moved = pltpu.roll(merged, span_len - 1, 0)
            moved = jnp.where(last, kept[0:1, cut], moved)
            out_ref[pl.ds(start, span_len), cut] = moved.astype(out_ref.dtype)
            kept[:, cut] = merged[:8]
            out_ref[rows:, cut] = merged[:ROW_TILE].astype(out_ref.dtype)


def merge_far(parts, index, use, blocks):
    _, span_len, wide = parts.shape
    picked = index.shape[0] // blocks
    specs = [
        pl.BlockSpec(
            (1, span_len, wide),
            functools.partial(lambda r, i, index, use: (index[i * picked + r], 0, 0), r),
        )
        for r in range(picked)
    ]
    return pl.pallas_call(
        functools.partial(merge_far_kernel, picked),
        grid_spec=pltpu.PrefetchScalarGridSpec(
            num_scalar_prefetch=2,
            grid=(blocks,),
            in_specs=specs,
            out_specs=pl.BlockSpec((1, span_len, wide), lambda i, *_: (i, 0, 0)),
        ),
        out_shape=jax.ShapeDtypeStruct((blocks, span_len, wide), parts.dtype),
        compiler_params=pltpu.CompilerParams(vmem_limit_bytes=32 * MIB),
        name="merge_far",
    )(index, use, *([parts] * picked))


def merge_all(parts, index, use, blocks, far):
    _, span_len, wide = parts.shape
    row_width = wide - LANES
    picked = index.shape[0] // blocks
    rows = blocks * span_len
    specs = [
        pl.BlockSpec(
            (1, span_len, wide),
            functools.partial(
                lambda r, i, index, use: (index[(blocks - 1 - i) * picked + r], 0, 0), r
            ),
        )
        for r in range(picked)
    ]
    specs.append(pl.BlockSpec((1, span_len, wide), lambda i, *_: (blocks - 1 - i, 0, 0)))
    return pl.pallas_call(
        functools.partial(merge_all_kernel, picked),
        grid_spec=pltpu.PrefetchScalarGridSpec(
            num_scalar_prefetch=2,
            grid=(blocks,),
            in_specs=specs,
            out_specs=pl.BlockSpec((rows + ROW_TILE, row_width), lambda i, *_: (0, 0)),
            scratch_shapes=[pltpu.VMEM((8, row_width), jnp.float32)],
        ),
        out_shape=jax.ShapeDtypeStruct((rows + ROW_TILE, row_width), parts.dtype),
        compiler_params=pltpu.CompilerParams(vmem_limit_bytes=32 * MIB),
        name="merge_all",
    )(index, use, *([parts] * picked), far)


def project_kernel(place_ref, stay_ref, *refs):
    *rest, keep_ref, send_ref, rows_ref, first_ref = refs
    sources, below_ref, weights = rest[: -PLANE - 1], rest[-PLANE - 1], rest[-PLANE:]
    half = keep_ref.shape[0]
    part = half // PLANE
    step = pl.program_id(0)

    @pl.when(step == 0)
    def _():
        for at, ref in enumerate(sources):
            member = place_ref[0] ^ (at % PLANE)
            width = ref.shape[1]
            cut = slice(at // PLANE * width, (at // PLANE + 1) * width)
            for side in range(2):
                to = pl.multiple_of(side * half + member * part, part)
                rows_ref[pl.ds(to, part), cut] = ref[side * part : (side + 1) * part]
            to = pl.multiple_of(member * ROW_TILE, ROW_TILE)
            first_ref[pl.ds(to, ROW_TILE), cut] = ref[2 * part :]
        shape = (ROW_TILE, rows_ref.shape[1])
        last = lax.broadcasted_iota(jnp.int32, shape, 0) == ROW_TILE - 1
        for member in range(PLANE):
            if member < PLANE - 1:
                at = (member + 1) * ROW_TILE
                below = first_ref[at : at + ROW_TILE].astype(jnp.float32)[0:1]
            else:
                below = below_ref[...].astype(jnp.float32)[0:1]
            end = half + (member + 1) * part
            held = rows_ref[end - ROW_TILE : end].astype(jnp.float32)
            rows_ref[end - ROW_TILE : end] = jnp.where(last, below, held).astype(rows_ref.dtype)

    stay = pl.multiple_of(stay_ref[0] * half, half)
    go = pl.multiple_of((1 - stay_ref[0]) * half, half)
    for at, weight_ref in enumerate(weights):

        @pl.when(step == at)
        def _():
            for start, ref in ((go, send_ref), (stay, keep_ref)):
                ref[...] = jnp.dot(
                    rows_ref[pl.ds(start, half)],
                    weight_ref[...],
                    preferred_element_type=jnp.float32,
                ).astype(ref.dtype)


def project(sources, below, weights, place, stay):
    height, width = sources[0].shape
    row_width = below.shape[1]
    rows = PLANE * (height - ROW_TILE)
    shards = len(weights)
    tile = weights[0].shape[1]
    columns = shards * tile
    half = rows // 2
    return pl.pallas_call(
        project_kernel,
        grid_spec=pltpu.PrefetchScalarGridSpec(
            num_scalar_prefetch=2,
            grid=(shards,),
            in_specs=[pl.BlockSpec((height, width), lambda i, *_: (0, 0))] * len(sources)
            + [pl.BlockSpec((1, row_width), lambda i, *_: (0, 0))]
            + [pl.BlockSpec((row_width, tile), lambda i, *_: (0, 0))] * shards,
            out_specs=[
                pl.BlockSpec((half, tile), lambda i, *_: (0, i)),
                pl.BlockSpec((half, tile), lambda i, *_: (0, i)),
            ],
            scratch_shapes=[
                pltpu.VMEM((rows, row_width), sources[0].dtype),
                pltpu.VMEM((PLANE * ROW_TILE, row_width), sources[0].dtype),
            ],
        ),
        out_shape=[jax.ShapeDtypeStruct((half, columns), sources[0].dtype)] * 2,
        compiler_params=pltpu.CompilerParams(vmem_limit_bytes=30 * MIB),
        name="project_rows",
    )(place, stay, *sources, below, *weights)


def add_kernel(place_ref, keep_ref, other_ref, *outs):
    for at, ref in enumerate(outs):
        member = place_ref[0] ^ at
        ref[...] = (
            keep_ref[member].astype(jnp.float32) + other_ref[member].astype(jnp.float32)
        ).astype(ref.dtype)


def add_cores(keep, other, place):
    half, columns = keep.shape
    part = half // PLANE
    tile = min(columns, 512)
    folded = (PLANE, part, columns)
    return pl.pallas_call(
        add_kernel,
        grid_spec=pltpu.PrefetchScalarGridSpec(
            num_scalar_prefetch=1,
            grid=(columns // tile,),
            in_specs=[pl.BlockSpec((PLANE, part, tile), lambda i, *_: (0, 0, i))] * 2,
            out_specs=[pl.BlockSpec((part, tile), lambda i, *_: (0, i))] * PLANE,
        ),
        out_shape=[jax.ShapeDtypeStruct((part, columns), keep.dtype)] * PLANE,
        compiler_params=pltpu.CompilerParams(vmem_limit_bytes=32 * MIB),
        name="add_cores",
    )(place, keep.reshape(folded), other.reshape(folded))


def norm_kernel(strip, place_ref, line_ref, *refs):
    branches = refs[:-7]
    residual_ref, mask_ref, gain_ref, bias_ref, next_ref, normed_ref, branch_ref = refs[-7:]
    if len(branches) == 1:
        branch_ref[...] = branches[0][...].astype(jnp.float32)
    else:
        for at, ref in enumerate(branches):
            member = place_ref[0] ^ at
            for shard in range(ref.shape[1] // strip):
                to = pl.multiple_of((line_ref[shard] * PLANE + member) * strip, strip)
                branch_ref[:, pl.ds(to, strip)] = ref[
                    :, shard * strip : (shard + 1) * strip
                ].astype(jnp.float32)
    keep_scale = mask_ref[...].astype(jnp.float32) * (1.0 / keep_rate)
    stream = residual_ref[...].astype(jnp.float32) + keep_scale * branch_ref[...]
    centre = jnp.mean(stream, axis=1, keepdims=True)
    moved = stream - centre
    spread_of = jnp.mean(jnp.square(moved), axis=1, keepdims=True)
    normed = moved * lax.rsqrt(spread_of + norm_eps) * gain_ref[...] + bias_ref[...]
    next_ref[...] = stream.astype(next_ref.dtype)
    normed_ref[...] = normed.astype(normed_ref.dtype)


def add_norm(place, line, branches, strip, residual, drop_mask, gain, bias):
    rows, columns = residual.shape
    tile = min(32, rows)
    row_spec = pl.BlockSpec((tile, columns), lambda i, *_: (i, 0))
    branch_spec = pl.BlockSpec((tile, branches[0].shape[1]), lambda i, *_: (i, 0))
    flat_spec = pl.BlockSpec((1, columns), lambda i, *_: (0, 0))
    return pl.pallas_call(
        functools.partial(norm_kernel, strip),
        grid_spec=pltpu.PrefetchScalarGridSpec(
            num_scalar_prefetch=2,
            grid=(rows // tile,),
            in_specs=[branch_spec] * len(branches) + [row_spec, row_spec, flat_spec, flat_spec],
            out_specs=[row_spec, row_spec],
            scratch_shapes=[pltpu.VMEM((tile, columns), jnp.float32)],
        ),
        out_shape=[jax.ShapeDtypeStruct((rows, columns), residual.dtype)] * 2,
        compiler_params=pltpu.CompilerParams(vmem_limit_bytes=32 * MIB),
        name="add_norm",
    )(place, line, *branches, residual, drop_mask, gain[None], bias[None])


def pick_requests(owners, slots, peers, per_block):
    selector = owners[None, :] == peers[:, None]
    pair_block = jnp.arange(owners.shape[0], dtype=jnp.int32) // per_block
    return (
        jnp.sum(jnp.where(selector, pair_block[None, :], 0), axis=1),
        jnp.sum(jnp.where(selector, slots[None, :] + 1, 0), axis=1),
    )


def within(owners, base, half):
    index = owners - base
    use = (index >= 0) & (index < half)
    return jnp.where(use, index, 0), use.astype(jnp.int32)


def local(
    queries,
    neighbour_keys,
    neighbour_values,
    residual,
    out_weight,
    drop_mask,
    norm_gain,
    norm_bias,
    neighbour_owner,
    neighbour_slot,
):
    peer_count = lax.axis_size("dp")
    side_count = lax.axis_size("tensor")
    half = peer_count // 2
    halves = [list(range(half)), list(range(half, peer_count))]
    across = [(i, (i + half) % peer_count) for i in range(peer_count)]
    by_plane = side_count == 2 and peer_count == 4 * PLANE
    blocks, per_block = neighbour_owner.shape
    rows, row_width = queries.shape
    span_len = rows // blocks
    here = lax.axis_index("dp").astype(jnp.int32)
    upper = here // half
    base = upper * half
    partner = lax.rem(here + half, peer_count)

    def exchange(x):
        return lax.all_to_all(
            x, "dp", split_axis=0, concat_axis=0, tiled=True, axis_index_groups=halves
        )

    def pinned(*values):
        return lax.optimization_barrier(values)

    def to_partner(x):
        return lax.ppermute(x, "dp", across)

    chunks = 2
    width = row_width // chunks
    far_first = to_partner(queries[:, :width])
    carried = shifted(queries[-1:], "dp", 1)
    owners = neighbour_owner.reshape(-1)
    slot_rows = neighbour_slot.reshape(-1)
    near_peers = base + jnp.arange(half, dtype=jnp.int32)
    near_out = spread(
        [queries], carried, *pick_requests(owners, slot_rows, near_peers, per_block),
        span_len, 0, True,
    )
    near_asked = exchange(near_out)
    far_carried = lax.ppermute(
        queries[-1:], "dp", [(i - 1, (i + half) % peer_count) for i in range(1, peer_count)]
    )
    requests = owners.shape[0]
    far_table = to_partner(
        jnp.pad(jnp.concatenate([owners, slot_rows]), (0, LANES - 2 * requests))[None, :]
    )
    far_first, far_carried, far_table, held_queries, _ = pinned(
        far_first, far_carried, far_table, queries, near_out
    )
    far_owners = far_table[0, :requests]
    far_picked = pick_requests(
        far_owners, far_table[0, requests : 2 * requests], near_peers, per_block
    )

    def slots_of(asked):
        return asked[:, 0, -LANES].astype(jnp.int32)

    def answer(asked, tags, chunk, part):
        valid = (tags > 0).astype(jnp.int32)
        slots = jnp.maximum(tags - 1, 0)
        return attend(
            asked, neighbour_keys, neighbour_values, valid, slots, width, chunk, part
        )

    far_second = to_partner(held_queries[:, width:])
    near_index, near_use = within(owners, base, half)
    far_index, far_use = within(far_owners, base, half)
    far_out = spread([far_first], far_carried, *far_picked, span_len, 0, True)
    far_asked = exchange(far_out)
    near_asked, _ = pinned(near_asked, far_out)
    near_tags = slots_of(near_asked)
    near_parts = [answer(near_asked, near_tags, chunk, chunk) for chunk in range(chunks)]
    far_asked, far_second, weight, *near_parts = pinned(
        far_asked, far_second, out_weight, *near_parts
    )

    middle = row_width // 2
    far_out = spread([far_second], far_carried, *far_picked, span_len, 1, False)
    next_asked = exchange(far_out)
    near_part, far_asked, _ = pinned(near_parts[0], far_asked, far_out)
    near_back = exchange(near_part)
    far_weight = [to_partner(weight[:middle])] if by_plane else []
    far_tags = slots_of(far_asked)
    far_parts = answer(far_asked, far_tags, 0, 0)
    far_parts, next_asked, near_back, near_part, weight, *far_weight = pinned(
        far_parts, next_asked, near_back, near_parts[1], weight, *far_weight
    )

    far_back = exchange(far_parts)
    next_back = exchange(near_part)
    if by_plane:
        far_weight.append(to_partner(weight[middle:]))
    far_parts = answer(next_asked, far_tags, 1, 0)
    far_back, far_parts, next_back, weight, *far_weight = pinned(
        far_back, far_parts, next_back, weight, *far_weight
    )

    far_merged = merge_far(far_back, far_index, far_use, blocks)
    far_home = to_partner(far_merged)
    far_back = exchange(far_parts)
    far_home, far_back, weight = pinned(far_home, far_back, weight)

    def swap(x, by):
        return lax.ppermute(x, "dp", [(i, i ^ by) for i in range(peer_count)])

    def plane_rows(moved):
        return [moved] + [swap(moved, by) for by in range(1, PLANE)] if by_plane else [moved]

    far_merged = merge_far(far_back, far_index, far_use, blocks)
    far_home, near_back, weight, _ = pinned(far_home, near_back, weight, far_merged)
    next_home = to_partner(far_merged)
    sources = plane_rows(merge_all(near_back, near_index, near_use, blocks, far_home))
    near_swap = [swap(weight, PLANE)] if by_plane else []
    count = len(sources)
    next_home, next_back = pinned(next_home, next_back)
    next_home, next_back, *held = pinned(next_home, next_back, *sources, *near_swap)
    sources, near_swap = held[:count], held[count:]
    moved = merge_all(next_back, near_index, near_use, blocks, next_home)
    if by_plane:
        place = lax.rem(here, PLANE).reshape(1)
        stay = lax.axis_index("tensor").astype(jnp.int32).reshape(1)
        far_weight = jnp.concatenate(far_weight, axis=0)
        far_weight, moved = pinned(far_weight, moved)
        shards = [weight, *near_swap, far_weight, swap(far_weight, PLANE)]
        line = jnp.stack(
            [here // PLANE, (here ^ PLANE) // PLANE, partner // PLANE, (partner ^ PLANE) // PLANE]
        )
        first_rows = [moved_part[rows : rows + 1] for moved_part in (sources[0], moved)]
        sources += plane_rows(moved)
        first_row = jnp.concatenate(first_rows, axis=1)
        below = functools.reduce(
            jnp.add,
            [
                lax.ppermute(
                    first_row,
                    "dp",
                    [(i + PLANE, i + at) for i in range(0, peer_count - PLANE, PLANE)],
                )
                for at in range(PLANE)
            ],
        )
        keep, send = project(sources, below, shards, place, stay)
        summed = add_cores(keep, lax.ppermute(send, "tensor", [(0, 1), (1, 0)]), place)
        branches = [summed[0]] + [swap(summed[by], by) for by in range(1, PLANE)]
    else:
        whole_weight = lax.all_gather(out_weight, "dp", axis=1, tiled=True)
        moved = jnp.concatenate([sources[0], moved], axis=1)
        below = shifted(moved[rows : rows + 1], "dp", -1)
        cross_rows = jnp.concatenate([moved[: rows - 1], below], axis=0)
        branch = jnp.dot(cross_rows, whole_weight, preferred_element_type=jnp.float32)
        branches = [
            lax.psum_scatter(
                branch.astype(jnp.bfloat16), "tensor", scatter_dimension=0, tiled=True
            )
        ]
        place = line = jnp.zeros((1,), jnp.int32)
    return tuple(
        add_norm(
            place, line, branches, out_weight.shape[1], residual, drop_mask, norm_gain, norm_bias
        )
    )


def solution(mesh):
    placed = (
        P("dp", "tensor"),
        P("dp", None, "tensor"),
        P("dp", None, "tensor"),
        P(("dp", "tensor"), None),
        P("tensor", "dp"),
        P(("dp", "tensor"), None),
        P(),
        P(),
        P("dp", None),
        P("dp", None),
    )
    return jax.shard_map(
        local,
        mesh=mesh,
        in_specs=placed,
        out_specs=(P(("dp", "tensor"), None), P(("dp", "tensor"), None)),
        check_vma=False,
    )
```

time: 451 us -> 324 us (0.72)
  waiting for transfers between devices: 246 us -> 162 us
  Pallas kernels: 0 us -> 57 us
  matrix products: 36.4 us -> 0 us
  other arithmetic: 29 us -> 4.51 us
  local copies, waits for them, and re-layouts: 39.2 us -> 15.8 us
  starting transfers between devices: 84.9 us -> 62.1 us
  blocking collectives: 0 us -> 19.7 us
  between operations: 14.4 us -> 1.09 us
    all_to_all x5 -> x6, waiting for transfers between devices: 216 us -> 17.4 us  [exchange(): lax.all_to_all(x, 'dp', split_axis=0, concat_axis=0, tiled=True, axis_ind...]
    ppermute x0 -> x24, waiting for transfers between devices: none -> 145 us  [the longest x7 106 us: to_partner(): return lax.ppermute(x, 'dp', across)]
    pallas_call x0 -> x14, Pallas kernels: none -> 57 us  [the longest x4 28.5 us: attend(): pl.pallas_call(attend_kernel, grid_spec=pltpu.PrefetchScalarGridSpec(num_...]
    all_to_all x5 -> x6, starting transfers between devices: 78.4 us -> 26.2 us  [exchange(): lax.all_to_all(x, 'dp', split_axis=0, concat_axis=0, tiled=True, axis_ind...]
    dot_general x4 -> x0, matrix products: 36.4 us -> none  [the longest x1 14 us: attend_block(): jnp.einsum('brhe,blhe->bhrl', query_heads, key_heads, preferred_element_t...]
    ppermute x0 -> x24, starting transfers between devices: none -> 31 us  [the longest x11 12.2 us: swap(): return lax.ppermute(x, 'dp', [(i, i ^ by) for i in range(peer_count)])]
    reduce_scatter x1 -> x0, waiting for transfers between devices: 25.9 us -> none  [local(): lax.psum_scatter(jnp.dot(cross_rows, whole_weight, preferred_element_type...]
    all_to_all x0 -> x1, blocking collectives: none -> 19.7 us  [exchange(): lax.all_to_all(x, 'dp', split_axis=0, concat_axis=0, tiled=True, axis_ind...]
  transfers between devices with their start and end apart: 9 -> 31, of which waited for: 5 -> 14; matrix products, arithmetic and copies ran while one was open for 20% -> 3% of each run, Pallas kernels for 0% -> 11%
where the time goes in v1:
time: 324 us; the launch traced here: 322 us
  waiting for transfers between devices  162 us (50%)
  starting transfers between devices  62.1 us (19%)
  Pallas kernels  57 us (18%)
  blocking collectives  19.7 us (6%)
  local copies, waits for them, and re-layouts  15.8 us (5%)
  other arithmetic  4.51 us (1%)
    ppermute x7, waiting for transfers between devices, to_partner(): return lax.ppermute(x, 'dp', across)  106 us
    pallas_call x4, Pallas kernels, attend(): pl.pallas_call(attend_kernel, grid_spec=pltpu.PrefetchScalarGridSpec(num_...  28.5 us
    all_to_all x6, starting transfers between devices, exchange(): lax.all_to_all(x, 'dp', split_axis=0, concat_axis=0, tiled=True, axis_ind...  26.2 us
    ppermute x4, waiting for transfers between devices, local(): lax.ppermute(first_row, 'dp', [(i + PLANE, i + at) for i in range(0, peer...  21.4 us
    all_to_all x1, blocking collectives, exchange(): lax.all_to_all(x, 'dp', split_axis=0, concat_axis=0, tiled=True, axis_ind...  19.7 us
    all_to_all x6, waiting for transfers between devices, exchange(): lax.all_to_all(x, 'dp', split_axis=0, concat_axis=0, tiled=True, axis_ind...  17.4 us
    unnamed x46, local copies, waits for them, and re-layouts  12.9 us
    ppermute x11, starting transfers between devices, swap(): return lax.ppermute(x, 'dp', [(i, i ^ by) for i in range(peer_count)])  12.2 us
  transfers between devices with their start and end apart: 31, of which 14 were waited for; matrix products, arithmetic and copies ran while one was open for 3% of the time, Pallas kernels for 11%

profile of v1, /device:TPU:0, one launch (start us, length us, event | category | flops | bytes accessed | tf_op | source)
XLA Modules:
  0.0 322.1 jit_solution(7598353400261864146)
XLA Ops:
  0.6 0.8 slice.35
  1.4 4.8 %collective-permute-start.3 = (bf16[1,2048]{1,0:T(2,128)(2,1)S(1)}, bf16[1,2048]{1,0:T(2,128)(2,1)S(1)}, u32[]{:S(2)}, u32[]{:S(2)}) collective-permute-start(bf16[1,2048]{1,0:T(2,128)(2,1)S(1)} %slice.35), channel_id=1, source_target_pairs={{0,2},{2,4},{4,6},{6,8},{8,10},{10,12},{12,14},{14,16},{16,18},{18... | collective-permute-start | bytes 12296 | tf_op jit(solution)/shard_map/ppermute | solution.py:23
  6.3 0.8 copy.16
  7.1 0.8 copy.17
  8.2 1.2 copy-done
  9.4 2.3 spread_queries.3
  11.7 5.1 %all-to-all-start.1 = ((bf16[8,64,2176]{2,1,0:T(8,128)(2,1)}), bf16[8,64,2176]{2,1,0:T(8,128)(2,1)S(1)}, u32[]{:S(2)}, u32[]{:S(2)}) async-start(bf16[8,64,2176]{2,1,0:T(8,128)(2,1)} %spread_queries.3), calls=%async_computation.1 | async-start | bytes 4456448 | tf_op jit(solution)/shard_map/all_to_all | solution.py:488
  16.9 3.3 %collective-permute-start = (bf16[256,1024]{1,0:T(8,128)(2,1)S(1)}, bf16[256,1024]{1,0:T(8,128)(2,1)S(1)}, u32[]{:S(2)}, u32[]{:S(2)}) collective-permute-start(bf16[256,1024]{1,0:T(8,128)(2,1)S(1)} %slice.34), channel_id=1, source_target_pairs={{0,16},{2,18},{4,20},{6,22},{8,24},{10,26},{12,28},{14,30},{16,0},... | collective-permute-start | bytes 1572872 | tf_op jit(solution)/shard_map/ppermute | solution.py:496
  20.2 3.3 %collective-permute-start.1 = (bf16[1,2048]{1,0:T(2,128)(2,1)S(1)}, bf16[1,2048]{1,0:T(2,128)(2,1)S(1)}, u32[]{:S(2)}, u32[]{:S(2)}) collective-permute-start(bf16[1,2048]{1,0:T(2,128)(2,1)S(1)} %slice.35), channel_id=1, source_target_pairs={{0,18},{2,20},{4,22},{6,24},{8,26},{10,28},{12,30},{14,0},{16,2},{... | collective-permute-start | bytes 12296 | tf_op jit(solution)/shard_map/ppermute | solution.py:510
  23.6 2.9 collective-permute-start.2
  26.5 25.5 %collective-permute-done.2 = s32[1,128]{1,0:T(1,128)S(1)} collective-permute-done((s32[1,128]{1,0:T(1,128)S(1)}, s32[1,128]{1,0:T(1,128)S(1)}, u32[]{:S(2)}, u32[]{:S(2)}) %collective-permute-start.2) | collective-permute-done | bytes 544 | tf_op jit(solution)/shard_map/ppermute | solution.py:496
  52.0 4.0 %collective-permute-done.1.carried_ref = bf16[1,2048]{1,0:T(2,128)(2,1)S(1)} collective-permute-done((bf16[1,2048]{1,0:T(2,128)(2,1)S(1)}, bf16[1,2048]{1,0:T(2,128)(2,1)S(1)}, u32[]{:S(2)}, u32[]{:S(2)}) %collective-permute-start.1) | collective-permute-done | bytes 4128 | tf_op jit(solution)/shard_map/ppermute | solution.py:510
  56.2 1.8 spread_queries.4
  58.1 5.2 %all-to-all-start = ((bf16[8,64,1152]{2,1,0:T(8,128)(2,1)}), bf16[8,64,1152]{2,1,0:T(8,128)(2,1)}, u32[]{:S(2)}, u32[]{:S(2)}) async-start(bf16[8,64,1152]{2,1,0:T(8,128)(2,1)} %spread_queries.4), calls=%async_computation | async-start | bytes 2359296 | tf_op jit(solution)/shard_map/all_to_all | solution.py:488
  63.4 0.9 collective-permute-start.4
  64.2 0.9 maximum_reduce_fusion.1
  65.1 8.2 %attend_blocks.5 = bf16[8,64,1152]{2,1,0:T(8,128)(2,1)} custom-call(s32[8]{0:T(128)} %get-tuple-element.97.valid_ref, s32[8]{0:T(128)} %get-tuple-element.96.slot_ref, bf16[8,64,2176]{2,1,0:T(8,128)(2,1)} %copy-done.20, bf16[8,128,2048]{2,1,0:T(8,128)(2,1)} %key_ref.7, bf16[8,128,2048]{2,1,0:T(8,128)(2,1)} %value_ref.7), custom_call_target="tpu_custom_call" | custom-call | flops 268435456 | bytes 6291456 | tf_op jit(solution)/shard_map/attend_blocks/pallas_call | solution.py:158
  73.3 8.2 %attend_blocks.4 = bf16[8,64,1152]{2,1,0:T(8,128)(2,1)} custom-call(s32[8]{0:T(128)} %get-tuple-element.97.valid_ref, s32[8]{0:T(128)} %get-tuple-element.96.slot_ref, bf16[8,64,2176]{2,1,0:T(8,128)(2,1)} %copy-done.20, bf16[8,128,2048]{2,1,0:T(8,128)(2,1)} %key_ref.7, bf16[8,128,2048]{2,1,0:T(8,128)(2,1)} %value_ref.7), custom_call_target="tpu_custom_call" | custom-call | flops 268435456 | bytes 6291456 | tf_op jit(solution)/shard_map/attend_blocks/pallas_call | solution.py:158
  81.6 3.8 %collective-permute-done.4.refs_0_ = bf16[256,1024]{1,0:T(8,128)(2,1)S(1)} collective-permute-done((bf16[256,1024]{1,0:T(8,128)(2,1)S(1)}, bf16[256,1024]{1,0:T(8,128)(2,1)S(1)}, u32[]{:S(2)}, u32[]{:S(2)}) %collective-permute-start.4) | collective-permute-done | bytes 524320 | tf_op jit(solution)/shard_map/ppermute | solution.py:496
  85.4 2.1 all-to-all-done.query_ref
  87.5 1.8 spread_queries.5
  89.3 4.5 %all-to-all-start.2 = ((bf16[8,64,1024]{2,1,0:T(8,128)(2,1)}), bf16[8,64,1024]{2,1,0:T(8,128)(2,1)S(1)}, u32[]{:S(2)}, u32[]{:S(2)}) async-start(bf16[8,64,1024]{2,1,0:T(8,128)(2,1)} %spread_queries.5), calls=%async_computation.2 | async-start | bytes 2097152 | tf_op jit(solution)/shard_map/all_to_all | solution.py:488
  93.8 13.1 %all-to-all-done.2.query_ref = bf16[8,64,1024]{2,1,0:T(8,128)(2,1)S(1)} async-done(((bf16[8,64,1024]{2,1,0:T(8,128)(2,1)}), bf16[8,64,1024]{2,1,0:T(8,128)(2,1)S(1)}, u32[]{:S(2)}, u32[]{:S(2)}) %all-to-all-start.2) | async-done | bytes 1048608 | tf_op jit(solution)/shard_map/all_to_all | solution.py:488
  106.9 1.0 copy-done.21
  107.8 3.6 %all-to-all-start.3 = ((bf16[8,64,1152]{2,1,0:T(8,128)(2,1)}), bf16[8,64,1152]{2,1,0:T(8,128)(2,1)S(1)}, u32[]{:S(2)}, u32[]{:S(2)}) async-start(bf16[8,64,1152]{2,1,0:T(8,128)(2,1)} %attend_blocks.4), calls=%async_computation.3 | async-start | bytes 2359296 | tf_op jit(solution)/shard_map/all_to_all | solution.py:488
  111.5 1.7 maximum_reduce_fusion
  113.2 6.0 %attend_blocks.6 = bf16[8,64,1152]{2,1,0:T(8,128)(2,1)} custom-call(s32[8]{0:T(128)} %get-tuple-element.99.valid_ref, s32[8]{0:T(128)} %get-tuple-element.98.slot_ref, bf16[8,64,1152]{2,1,0:T(8,128)(2,1)} %all-to-all-done.query_ref, bf16[8,128,2048]{2,1,0:T(8,128)(2,1)} %key_ref.7, bf16[8,128,2048]{2,1,0:T(8,128)(2,1)} %value_ref.7), custom_call_target="tpu_custom_call" | custom-call | flops 268435456 | bytes 6291456 | tf_op jit(solution)/shard_map/attend_blocks/pallas_call | solution.py:158
  119.2 15.4 %collective-permute-done.5 = bf16[1024,256]{1,0:T(8,128)(2,1)} collective-permute-done((bf16[1024,256]{1,0:T(8,128)(2,1)S(1)}, bf16[1024,256]{1,0:T(8,128)(2,1)}, u32[]{:S(2)}, u32[]{:S(2)}) %collective-permute-start.5) | collective-permute-done | bytes 524320 | tf_op jit(solution)/shard_map/ppermute | solution.py:496
  134.7 2.2 all-to-all-done.3.refs_0_.refs_1_
  136.9 19.7 %all_to_all.35.refs_0_.refs_1_ = bf16[8,64,1152]{2,1,0:T(8,128)(2,1)S(1)} all-to-all(bf16[8,64,1152]{2,1,0:T(8,128)(2,1)} %attend_blocks.6), channel_id=1, replica_groups={{0,2,4,6,8,10,12,14},{16,18,20,22,24,26,28,30},{1,3,5,7,9,11,13,15},{17..., dimensions={0} | all-to-all | bytes 2359296 | tf_op jit(solution)/shard_map/all_to_all | solution.py:488
  156.5 3.6 %all-to-all-start.5 = ((bf16[8,64,1152]{2,1,0:T(8,128)(2,1)}), bf16[8,64,1152]{2,1,0:T(8,128)(2,1)S(1)}, u32[]{:S(2)}, u32[]{:S(2)}) async-start(bf16[8,64,1152]{2,1,0:T(8,128)(2,1)} %attend_blocks.5), calls=%async_computation.5 | async-start | bytes 2359296 | tf_op jit(solution)/shard_map/all_to_all | solution.py:488
  160.1 1.1 slice.42
  161.6 6.0 %attend_blocks.7 = bf16[8,64,1152]{2,1,0:T(8,128)(2,1)} custom-call(s32[8]{0:T(128)} %get-tuple-element.99.valid_ref, s32[8]{0:T(128)} %get-tuple-element.98.slot_ref, bf16[8,64,1024]{2,1,0:T(8,128)(2,1)} %copy-done.21, bf16[8,128,2048]{2,1,0:T(8,128)(2,1)} %key_ref.7, bf16[8,128,2048]{2,1,0:T(8,128)(2,1)} %value_ref.7), custom_call_target="tpu_custom_call" | custom-call | flops 268435456 | bytes 6291456 | tf_op jit(solution)/shard_map/attend_blocks/pallas_call | solution.py:158
  167.6 17.5 %collective-permute-done.6 = bf16[1024,256]{1,0:T(8,128)(2,1)} collective-permute-done((bf16[1024,256]{1,0:T(8,128)(2,1)S(1)}, bf16[1024,256]{1,0:T(8,128)(2,1)}, u32[]{:S(2)}, u32[]{:S(2)}) %collective-permute-start.6) | collective-permute-done | bytes 524320 | tf_op jit(solution)/shard_map/ppermute | solution.py:496
  185.1 4.3 %all-to-all-start.6 = ((bf16[8,64,1152]{2,1,0:T(8,128)(2,1)}), bf16[8,64,1152]{2,1,0:T(8,128)(2,1)}, u32[]{:S(2)}, u32[]{:S(2)}) async-start(bf16[8,64,1152]{2,1,0:T(8,128)(2,1)} %attend_blocks.7), calls=%async_computation.6 | async-start | bytes 2359296 | tf_op jit(solution)/shard_map/all_to_all | solution.py:488
  189.4 2.0 merge_far.2
  191.4 0.9 collective-permute-start.7
  192.3 23.8 %collective-permute-done.7.refs_2_ = bf16[4,64,1152]{2,1,0:T(8,128)(2,1)S(1)} collective-permute-done((bf16[4,64,1152]{2,1,0:T(8,128)(2,1)S(1)}, bf16[4,64,1152]{2,1,0:T(8,128)(2,1)S(1)}, u32[]{:S(2)}, u32[]{:S(2)}) %collective-permute-start.7) | collective-permute-done | bytes 589856 | tf_op jit(solution)/shard_map/ppermute | solution.py:496
  216.1 0.8 copy-done.10
  216.9 3.6 %merge_far.3 = bf16[4,64,1152]{2,1,0:T(8,128)(2,1)S(1)} custom-call(s32[8]{0:T(128)S(1)} %subtract_select_fusion.1.index_ref, s32[8]{0:T(128)S(1)} %fusion.7.use_ref, bf16[8,64,1152]{2,1,0:T(8,128)(2,1)} %all-to-all-done.6.refs_0_.refs_1_, bf16[8,64,1152]{2,1,0:T(8,128)(2,1)} %all-to-all-done.6.refs_0_.refs_1_), custom_call_target="tpu_custom_call" | custom-call | tf_op jit(solution)/shard_map/merge_far/pallas_call | solution.py:256
  221.0 3.5 %collective-permute-start.8 = (bf16[4,64,1152]{2,1,0:T(8,128)(2,1)S(1)}, bf16[4,64,1152]{2,1,0:T(8,128)(2,1)S(1)}, u32[]{:S(2)}, u32[]{:S(2)}) collective-permute-start(bf16[4,64,1152]{2,1,0:T(8,128)(2,1)S(1)} %merge_far.3), channel_id=1, source_target_pairs={{0,16},{2,18},{4,20},{6,22},{8,24},{10,26},{12,28},{14,30},{16,0},... | collective-permute-start | bytes 1769480 | tf_op jit(solution)/shard_map/ppermute | solution.py:496
  224.5 2.2 merge_all.2.refs_0_
  226.7 2.4 collective-permute-start.11
  230.3 1.3 pad_maximum_fusion.refs_11_
  231.6 19.9 %collective-permute-done.8.refs_2_ = bf16[4,64,1152]{2,1,0:T(8,128)(2,1)S(1)} collective-permute-done((bf16[4,64,1152]{2,1,0:T(8,128)(2,1)S(1)}, bf16[4,64,1152]{2,1,0:T(8,128)(2,1)S(1)}, u32[]{:S(2)}, u32[]{:S(2)}) %collective-permute-start.8) | collective-permute-done | bytes 589856 | tf_op jit(solution)/shard_map/ppermute | solution.py:496
  251.5 0.9 copy-done.14
  252.3 0.8 copy-done.16
  253.1 3.0 merge_all.3.refs_4_
  257.5 3.6 %collective-permute-start.15 = (bf16[272,1024]{1,0:T(8,128)(2,1)}, bf16[272,1024]{1,0:T(8,128)(2,1)}, u32[]{:S(2)}, u32[]{:S(2)}) collective-permute-start(bf16[272,1024]{1,0:T(8,128)(2,1)} %merge_all.3.refs_4_), channel_id=1, source_target_pairs={{0,6},{2,4},{4,2},{6,0},{8,14},{10,12},{12,10},{14,8},{16,22},{18,... | collective-permute-start | bytes 1671176 | tf_op jit(solution)/shard_map/ppermute | solution.py:574
  263.7 1.5 collective-permute-start.16
  265.2 21.4 %collective-permute-done.16 = bf16[1,2048]{1,0:T(2,128)(2,1)S(1)} collective-permute-done((bf16[1,2048]{1,0:T(2,128)(2,1)S(1)}, bf16[1,2048]{1,0:T(2,128)(2,1)S(1)}, u32[]{:S(2)}, u32[]{:S(2)}) %collective-permute-start.16) | collective-permute-done | bytes 4128 | tf_op jit(solution)/shard_map/ppermute | solution.py:604
  286.7 1.0 copy-done.5
  287.7 1.2 copy-done.9
  288.9 1.1 copy-done.13
  290.0 1.1 copy-done.15
  291.0 1.1 copy-done.17
  292.1 7.3 %project_rows.1 = (bf16[512,1024]{1,0:T(8,128)(2,1)S(1)}, bf16[512,1024]{1,0:T(8,128)(2,1)S(1)}) custom-call(s32[1]{0:T(128)} %bitcast.place_ref, s32[1]{0:T(128)} %bitcast.5.stay_ref, bf16[272,1024]{1,0:T(8,128)(2,1)S(1)} %copy-done.5, bf16[272,1024]{1,0:T(8,128)(2,1)S(1)} %copy-done.17, bf16[272,1024]{1,0:T(8,128)(2,1)S(1)} %copy-done.15, ...), custom_call_target="tpu_custom_call" | custom-call | tf_op jit(solution)/shard_map/project_rows/pallas_call | solution.py:352
  299.5 2.6 collective-permute-done.21
  302.1 1.2 add_cores.1
  303.3 3.5 %collective-permute-start.24 = (bf16[128,1024]{1,0:T(8,128)(2,1)S(1)}, bf16[128,1024]{1,0:T(8,128)(2,1)S(1)}, u32[]{:S(2)}, u32[]{:S(2)}) collective-permute-start(bf16[128,1024]{1,0:T(8,128)(2,1)S(1)} %get-tuple-element.95), channel_id=1, source_target_pairs={{0,6},{2,4},{4,2},{6,0},{8,14},{10,12},{12,10},{14,8},{16,22},{18,... | collective-permute-start | bytes 786440 | tf_op jit(solution)/shard_map/ppermute | solution.py:574
  306.9 5.8 %collective-permute-done.22.refs_1_ = bf16[128,1024]{1,0:T(8,128)(2,1)S(1)} collective-permute-done((bf16[128,1024]{1,0:T(8,128)(2,1)}, bf16[128,1024]{1,0:T(8,128)(2,1)S(1)}, u32[]{:S(2)}, u32[]{:S(2)}) %collective-permute-start.22) | collective-permute-done | bytes 262176 | tf_op jit(solution)/shard_map/ppermute | solution.py:574
  312.7 4.8 %collective-permute-done.23.refs_2_ = bf16[128,1024]{1,0:T(8,128)(2,1)S(1)} collective-permute-done((bf16[128,1024]{1,0:T(8,128)(2,1)}, bf16[128,1024]{1,0:T(8,128)(2,1)S(1)}, u32[]{:S(2)}, u32[]{:S(2)}) %collective-permute-start.23) | collective-permute-done | bytes 262176 | tf_op jit(solution)/shard_map/ppermute | solution.py:574
  317.5 1.2 copy-done.7
  318.7 3.3 %add_norm.1 = (bf16[128,4096]{1,0:T(8,128)(2,1)}, bf16[128,4096]{1,0:T(8,128)(2,1)}) custom-call(s32[1]{0:T(128)} %bitcast.place_ref, s32[4]{0:T(128)S(1)} %pad_add_fusion.line_ref, bf16[128,1024]{1,0:T(8,128)(2,1)S(1)} %get-tuple-element.92.refs_0_, bf16[128,1024]{1,0:T(8,128)(2,1)S(1)} %collective-permute-done.22.refs_1_, ...), custom_call_target="tpu_custom_call" | custom-call | tf_op jit(solution)/shard_map/add_norm/pallas_call | solution.py:431
  (85 shorter events, 7.1 us)
Async XLA Ops:
  1.4 6.8 %collective-permute-start.3 = (bf16[1,2048]{1,0:T(2,128)(2,1)S(1)}, bf16[1,2048]{1,0:T(2,128)(2,1)S(1)}, u32[]{:S(2)}, u32[]{:S(2)}) collective-permute-start(bf16[1,2048]{1,0:T(2,128)(2,1)S(1)} %slice.35), channel_id=1, source_target_pairs={{0,2},{2,4},{4,6},{6,8},{8,10},{10,12},{12,14},{14,16},{16,18},{18... | collective-permute-start | bytes 12296 | tf_op jit(solution)/shard_map/ppermute | solution.py:23
  8.2 1.2 copy-start
  11.7 5.1 %copy-start.1 = (bf16[256,2048]{1,0:T(8,128)(2,1)S(1)}, bf16[256,2048]{1,0:T(8,128)(2,1)}, u32[]{:S(2)}) copy-start(bf16[256,2048]{1,0:T(8,128)(2,1)} %refs_0_.1) | copy-start | bytes 3145732
  11.7 46.3 %all-to-all-start.1 = ((bf16[8,64,2176]{2,1,0:T(8,128)(2,1)}), bf16[8,64,2176]{2,1,0:T(8,128)(2,1)S(1)}, u32[]{:S(2)}, u32[]{:S(2)}) async-start(bf16[8,64,2176]{2,1,0:T(8,128)(2,1)} %spread_queries.3), calls=%async_computation.1 | async-start | bytes 4456448 | tf_op jit(solution)/shard_map/all_to_all | solution.py:488
  16.9 39.1 %collective-permute-start = (bf16[256,1024]{1,0:T(8,128)(2,1)S(1)}, bf16[256,1024]{1,0:T(8,128)(2,1)S(1)}, u32[]{:S(2)}, u32[]{:S(2)}) collective-permute-start(bf16[256,1024]{1,0:T(8,128)(2,1)S(1)} %slice.34), channel_id=1, source_target_pairs={{0,16},{2,18},{4,20},{6,22},{8,24},{10,26},{12,28},{14,30},{16,0},... | collective-permute-start | bytes 1572872 | tf_op jit(solution)/shard_map/ppermute | solution.py:496
  20.2 35.7 %collective-permute-start.1 = (bf16[1,2048]{1,0:T(2,128)(2,1)S(1)}, bf16[1,2048]{1,0:T(2,128)(2,1)S(1)}, u32[]{:S(2)}, u32[]{:S(2)}) collective-permute-start(bf16[1,2048]{1,0:T(2,128)(2,1)S(1)} %slice.35), channel_id=1, source_target_pairs={{0,18},{2,20},{4,22},{6,24},{8,26},{10,28},{12,30},{14,0},{16,2},{... | collective-permute-start | bytes 12296 | tf_op jit(solution)/shard_map/ppermute | solution.py:510
  23.6 28.4 %collective-permute-start.2 = (s32[1,128]{1,0:T(1,128)S(1)}, s32[1,128]{1,0:T(1,128)S(1)}, u32[]{:S(2)}, u32[]{:S(2)}) collective-permute-start(s32[1,128]{1,0:T(1,128)S(1)} %pad_bitcast_fusion), channel_id=1, source_target_pairs={{0,16},{2,18},{4,20},{6,22},{8,24},{10,26},{12,28},{14,30},{16,0},... | collective-permute-start | bytes 1544 | tf_op jit(solution)/shard_map/ppermute | solution.py:496
  58.1 6.1 %copy-start.20 = (bf16[8,64,2176]{2,1,0:T(8,128)(2,1)}, bf16[8,64,2176]{2,1,0:T(8,128)(2,1)S(1)}, u32[]{:S(2)}) copy-start(bf16[8,64,2176]{2,1,0:T(8,128)(2,1)S(1)} %all-to-all-done.1.query_ref) | copy-start | bytes 6684676
  58.1 29.4 %all-to-all-start = ((bf16[8,64,1152]{2,1,0:T(8,128)(2,1)}), bf16[8,64,1152]{2,1,0:T(8,128)(2,1)}, u32[]{:S(2)}, u32[]{:S(2)}) async-start(bf16[8,64,1152]{2,1,0:T(8,128)(2,1)} %spread_queries.4), calls=%async_computation | async-start | bytes 2359296 | tf_op jit(solution)/shard_map/all_to_all | solution.py:488
  63.4 22.0 %collective-permute-start.4 = (bf16[256,1024]{1,0:T(8,128)(2,1)S(1)}, bf16[256,1024]{1,0:T(8,128)(2,1)S(1)}, u32[]{:S(2)}, u32[]{:S(2)}) collective-permute-start(bf16[256,1024]{1,0:T(8,128)(2,1)S(1)} %slice.38), channel_id=1, source_target_pairs={{0,16},{2,18},{4,20},{6,22},{8,24},{10,26},{12,28},{14,30},{16,0},... | collective-permute-start | bytes 1572872 | tf_op jit(solution)/shard_map/ppermute | solution.py:496
  89.3 17.6 %all-to-all-start.2 = ((bf16[8,64,1024]{2,1,0:T(8,128)(2,1)}), bf16[8,64,1024]{2,1,0:T(8,128)(2,1)S(1)}, u32[]{:S(2)}, u32[]{:S(2)}) async-start(bf16[8,64,1024]{2,1,0:T(8,128)(2,1)} %spread_queries.5), calls=%async_computation.2 | async-start | bytes 2097152 | tf_op jit(solution)/shard_map/all_to_all | solution.py:488
  93.8 17.6 %copy-start.2 = (bf16[2048,256]{1,0:T(8,128)(2,1)S(1)}, bf16[2048,256]{1,0:T(8,128)(2,1)}, u32[]{:S(2)}) copy-start(bf16[2048,256]{1,0:T(8,128)(2,1)} %refs_9_) | copy-start | bytes 3145732
  106.9 1.0 copy-start.21
  107.8 29.0 %all-to-all-start.3 = ((bf16[8,64,1152]{2,1,0:T(8,128)(2,1)}), bf16[8,64,1152]{2,1,0:T(8,128)(2,1)S(1)}, u32[]{:S(2)}, u32[]{:S(2)}) async-start(bf16[8,64,1152]{2,1,0:T(8,128)(2,1)} %attend_blocks.4), calls=%async_computation.3 | async-start | bytes 2359296 | tf_op jit(solution)/shard_map/all_to_all | solution.py:488
  111.4 23.2 %collective-permute-start.5 = (bf16[1024,256]{1,0:T(8,128)(2,1)S(1)}, bf16[1024,256]{1,0:T(8,128)(2,1)}, u32[]{:S(2)}, u32[]{:S(2)}) collective-permute-start(bf16[1024,256]{1,0:T(8,128)(2,1)S(1)} %slice.41), channel_id=1, source_target_pairs={{0,16},{2,18},{4,20},{6,22},{8,24},{10,26},{12,28},{14,30},{16,0},... | collective-permute-start | bytes 1572872 | tf_op jit(solution)/shard_map/ppermute | solution.py:496
  156.5 28.6 %all-to-all-start.5 = ((bf16[8,64,1152]{2,1,0:T(8,128)(2,1)}), bf16[8,64,1152]{2,1,0:T(8,128)(2,1)S(1)}, u32[]{:S(2)}, u32[]{:S(2)}) async-start(bf16[8,64,1152]{2,1,0:T(8,128)(2,1)} %attend_blocks.5), calls=%async_computation.5 | async-start | bytes 2359296 | tf_op jit(solution)/shard_map/all_to_all | solution.py:488
  161.2 23.9 %collective-permute-start.6 = (bf16[1024,256]{1,0:T(8,128)(2,1)S(1)}, bf16[1024,256]{1,0:T(8,128)(2,1)}, u32[]{:S(2)}, u32[]{:S(2)}) collective-permute-start(bf16[1024,256]{1,0:T(8,128)(2,1)S(1)} %slice.42), channel_id=1, source_target_pairs={{0,16},{2,18},{4,20},{6,22},{8,24},{10,26},{12,28},{14,30},{16,0},... | collective-permute-start | bytes 1572872 | tf_op jit(solution)/shard_map/ppermute | solution.py:496
  185.1 31.9 %all-to-all-start.6 = ((bf16[8,64,1152]{2,1,0:T(8,128)(2,1)}), bf16[8,64,1152]{2,1,0:T(8,128)(2,1)}, u32[]{:S(2)}, u32[]{:S(2)}) async-start(bf16[8,64,1152]{2,1,0:T(8,128)(2,1)} %attend_blocks.7), calls=%async_computation.6 | async-start | bytes 2359296 | tf_op jit(solution)/shard_map/all_to_all | solution.py:488
  191.4 29.2 %copy-start.3 = (bf16[2048,256]{1,0:T(8,128)(2,1)S(1)}, bf16[2048,256]{1,0:T(8,128)(2,1)}, u32[]{:S(2)}) copy-start(bf16[2048,256]{1,0:T(8,128)(2,1)} %refs_9_) | copy-start | bytes 3145732
  191.4 24.8 %collective-permute-start.7 = (bf16[4,64,1152]{2,1,0:T(8,128)(2,1)S(1)}, bf16[4,64,1152]{2,1,0:T(8,128)(2,1)S(1)}, u32[]{:S(2)}, u32[]{:S(2)}) collective-permute-start(bf16[4,64,1152]{2,1,0:T(8,128)(2,1)S(1)} %merge_far.2), channel_id=1, source_target_pairs={{0,16},{2,18},{4,20},{6,22},{8,24},{10,26},{12,28},{14,30},{16,0},... | collective-permute-start | bytes 1769480 | tf_op jit(solution)/shard_map/ppermute | solution.py:496
  216.1 0.8 copy-start.10
  216.9 7.6 %copy-start.11 = (bf16[4,64,1152]{2,1,0:T(8,128)(2,1)S(1)}, bf16[4,64,1152]{2,1,0:T(8,128)(2,1)}, u32[]{:S(2)}) copy-start(bf16[4,64,1152]{2,1,0:T(8,128)(2,1)} %copy-done.10) | copy-start | bytes 1769476
  220.6 32.6 %collective-permute-start.12 = (bf16[2048,256]{1,0:T(8,128)(2,1)S(1)}, bf16[2048,256]{1,0:T(8,128)(2,1)S(1)}, u32[]{:S(2)}, u32[]{:S(2)}) collective-permute-start(bf16[2048,256]{1,0:T(8,128)(2,1)S(1)} %copy-done.3), channel_id=1, source_target_pairs={{0,8},{2,10},{4,12},{6,14},{8,0},{10,2},{12,4},{14,6},{16,24},{18,... | collective-permute-start | bytes 3145736 | tf_op jit(solution)/shard_map/ppermute | solution.py:574
  221.0 30.5 %collective-permute-start.8 = (bf16[4,64,1152]{2,1,0:T(8,128)(2,1)S(1)}, bf16[4,64,1152]{2,1,0:T(8,128)(2,1)S(1)}, u32[]{:S(2)}, u32[]{:S(2)}) collective-permute-start(bf16[4,64,1152]{2,1,0:T(8,128)(2,1)S(1)} %merge_far.3), channel_id=1, source_target_pairs={{0,16},{2,18},{4,20},{6,22},{8,24},{10,26},{12,28},{14,30},{16,0},... | collective-permute-start | bytes 1769480 | tf_op jit(solution)/shard_map/ppermute | solution.py:496
  226.7 34.9 %copy-start.4 = (bf16[272,1024]{1,0:T(8,128)(2,1)}, bf16[272,1024]{1,0:T(8,128)(2,1)S(1)}, u32[]{:S(2)}) copy-start(bf16[272,1024]{1,0:T(8,128)(2,1)S(1)} %merge_all.2.refs_0_) | copy-start | bytes 1671172
  226.7 24.7 %collective-permute-start.11 = (bf16[272,1024]{1,0:T(8,128)(2,1)S(1)}, bf16[272,1024]{1,0:T(8,128)(2,1)S(1)}, u32[]{:S(2)}, u32[]{:S(2)}) collective-permute-start(bf16[272,1024]{1,0:T(8,128)(2,1)S(1)} %merge_all.2.refs_0_), channel_id=1, source_target_pairs={{0,6},{2,4},{4,2},{6,0},{8,14},{10,12},{12,10},{14,8},{16,22},{18,... | collective-permute-start | bytes 1671176 | tf_op jit(solution)/shard_map/ppermute | solution.py:574
  229.1 22.3 %collective-permute-start.10 = (bf16[272,1024]{1,0:T(8,128)(2,1)S(1)}, bf16[272,1024]{1,0:T(8,128)(2,1)S(1)}, u32[]{:S(2)}, u32[]{:S(2)}) collective-permute-start(bf16[272,1024]{1,0:T(8,128)(2,1)S(1)} %merge_all.2.refs_0_), channel_id=1, source_target_pairs={{0,4},{2,6},{4,0},{6,2},{8,12},{10,14},{12,8},{14,10},{16,20},{18,... | collective-permute-start | bytes 1671176 | tf_op jit(solution)/shard_map/ppermute | solution.py:574
  229.7 22.6 %collective-permute-start.9 = (bf16[272,1024]{1,0:T(8,128)(2,1)S(1)}, bf16[272,1024]{1,0:T(8,128)(2,1)S(1)}, u32[]{:S(2)}, u32[]{:S(2)}) collective-permute-start(bf16[272,1024]{1,0:T(8,128)(2,1)S(1)} %merge_all.2.refs_0_), channel_id=1, source_target_pairs={{0,2},{2,0},{4,6},{6,4},{8,10},{10,8},{12,14},{14,12},{16,18},{18,... | collective-permute-start | bytes 1671176 | tf_op jit(solution)/shard_map/ppermute | solution.py:574
  251.4 4.7 %copy-start.12 = (bf16[272,1024]{1,0:T(8,128)(2,1)}, bf16[272,1024]{1,0:T(8,128)(2,1)S(1)}, u32[]{:S(2)}) copy-start(bf16[272,1024]{1,0:T(8,128)(2,1)S(1)} %collective-permute-done.11.refs_3_) | copy-start | bytes 1671172
  251.5 0.9 copy-start.14
  252.3 0.8 copy-start.16
  253.1 3.0 copy-start.8
  256.2 30.5 %collective-permute-start.20 = (bf16[2048,256]{1,0:T(8,128)(2,1)S(1)}, bf16[2048,256]{1,0:T(8,128)(2,1)S(1)}, u32[]{:S(2)}, u32[]{:S(2)}) collective-permute-start(bf16[2048,256]{1,0:T(8,128)(2,1)S(1)} %pad_maximum_fusion.refs_11_), channel_id=1, source_target_pairs={{0,8},{2,10},{4,12},{6,14},{8,0},{10,2},{12,4},{14,6},{16,24},{18,... | collective-permute-start | bytes 3145736 | tf_op jit(solution)/shard_map/ppermute | solution.py:574
  257.5 29.1 %collective-permute-start.15 = (bf16[272,1024]{1,0:T(8,128)(2,1)}, bf16[272,1024]{1,0:T(8,128)(2,1)}, u32[]{:S(2)}, u32[]{:S(2)}) collective-permute-start(bf16[272,1024]{1,0:T(8,128)(2,1)} %merge_all.3.refs_4_), channel_id=1, source_target_pairs={{0,6},{2,4},{4,2},{6,0},{8,14},{10,12},{12,10},{14,8},{16,22},{18,... | collective-permute-start | bytes 1671176 | tf_op jit(solution)/shard_map/ppermute | solution.py:574
  261.1 25.5 %collective-permute-start.14 = (bf16[272,1024]{1,0:T(8,128)(2,1)}, bf16[272,1024]{1,0:T(8,128)(2,1)}, u32[]{:S(2)}, u32[]{:S(2)}) collective-permute-start(bf16[272,1024]{1,0:T(8,128)(2,1)} %merge_all.3.refs_4_), channel_id=1, source_target_pairs={{0,4},{2,6},{4,0},{6,2},{8,12},{10,14},{12,8},{14,10},{16,20},{18,... | collective-permute-start | bytes 1671176 | tf_op jit(solution)/shard_map/ppermute | solution.py:574
  261.6 25.1 %collective-permute-start.13 = (bf16[272,1024]{1,0:T(8,128)(2,1)}, bf16[272,1024]{1,0:T(8,128)(2,1)}, u32[]{:S(2)}, u32[]{:S(2)}) collective-permute-start(bf16[272,1024]{1,0:T(8,128)(2,1)} %merge_all.3.refs_4_), channel_id=1, source_target_pairs={{0,2},{2,0},{4,6},{6,4},{8,10},{10,8},{12,14},{14,12},{16,18},{18,... | collective-permute-start | bytes 1671176 | tf_op jit(solution)/shard_map/ppermute | solution.py:574
  261.7 0.7 collective-permute-start.19
  262.3 0.7 collective-permute-start.18
  263.0 0.7 collective-permute-start.17
  263.7 22.9 %collective-permute-start.16 = (bf16[1,2048]{1,0:T(2,128)(2,1)S(1)}, bf16[1,2048]{1,0:T(2,128)(2,1)S(1)}, u32[]{:S(2)}, u32[]{:S(2)}) collective-permute-start(bf16[1,2048]{1,0:T(2,128)(2,1)S(1)} %pad_maximum_fusion.1), channel_id=1, source_target_pairs={{8,0},{16,8},{24,16},{9,1},{17,9},{25,17}} | collective-permute-start | bytes 12296 | tf_op jit(solution)/shard_map/ppermute | solution.py:604
  286.6 1.1 copy-start.5
  287.7 1.2 copy-start.9
  288.9 1.1 copy-start.13
  290.0 1.1 copy-start.15
  291.0 1.1 copy-start.17
  299.4 18.1 %copy-start.6 = (s32[128,4096]{1,0:T(8,128)S(1)}, s32[128,4096]{1,0:T(8,128)}, u32[]{:S(2)}) copy-start(s32[128,4096]{1,0:T(8,128)} %refs_5_.1) | copy-start | bytes 6291460
  299.4 18.1 %copy-start.18 = (f32[4096]{0:T(1024)S(1)}, f32[4096]{0:T(1024)}, u32[]{:S(2)}) copy-start(f32[4096]{0:T(1024)} %param.16) | copy-start | bytes 49156
  299.4 18.1 %copy-start.19 = (f32[4096]{0:T(1024)S(1)}, f32[4096]{0:T(1024)}, u32[]{:S(2)}) copy-start(f32[4096]{0:T(1024)} %param.17) | copy-start | bytes 49156
  299.4 2.7 collective-permute-start.21
  303.3 9.4 %collective-permute-start.22 = (bf16[128,1024]{1,0:T(8,128)(2,1)}, bf16[128,1024]{1,0:T(8,128)(2,1)S(1)}, u32[]{:S(2)}, u32[]{:S(2)}) collective-permute-start(bf16[128,1024]{1,0:T(8,128)(2,1)} %get-tuple-element.93), channel_id=1, source_target_pairs={{0,2},{2,0},{4,6},{6,4},{8,10},{10,8},{12,14},{14,12},{16,18},{18,... | collective-permute-start | bytes 786440 | tf_op jit(solution)/shard_map/ppermute | solution.py:574
  303.3 14.2 %collective-permute-start.23 = (bf16[128,1024]{1,0:T(8,128)(2,1)}, bf16[128,1024]{1,0:T(8,128)(2,1)S(1)}, u32[]{:S(2)}, u32[]{:S(2)}) collective-permute-start(bf16[128,1024]{1,0:T(8,128)(2,1)} %get-tuple-element.94), channel_id=1, source_target_pairs={{0,4},{2,6},{4,0},{6,2},{8,12},{10,14},{12,8},{14,10},{16,20},{18,... | collective-permute-start | bytes 786440 | tf_op jit(solution)/shard_map/ppermute | solution.py:574
  303.3 14.2 %collective-permute-start.24 = (bf16[128,1024]{1,0:T(8,128)(2,1)S(1)}, bf16[128,1024]{1,0:T(8,128)(2,1)S(1)}, u32[]{:S(2)}, u32[]{:S(2)}) collective-permute-start(bf16[128,1024]{1,0:T(8,128)(2,1)S(1)} %get-tuple-element.95), channel_id=1, source_target_pairs={{0,6},{2,4},{4,2},{6,0},{8,14},{10,12},{12,10},{14,8},{16,22},{18,... | collective-permute-start | bytes 786440 | tf_op jit(solution)/shard_map/ppermute | solution.py:574
  317.5 1.2 copy-start.7

commit v2 on v1

--- a/solution.py
+++ b/solution.py
@@ -23,8 +23,9 @@
     return lax.ppermute(x, axis, pairs)
 
 
-def spread_kernel(tagged, block_ref, slot_ref, carried_ref, *refs):
-    *pieces, out_ref, moved, tags, sems = refs
+def spread_kernel(count, column, block_ref, slot_ref, carried_ref, *refs):
+    pieces = refs[:count]
+    out_ref, moved, tags, sems = refs[-4:]
     peers, span_len, _ = out_ref.shape
     rows, piece_width = pieces[0].shape
     row_width = moved.shape[1]
@@ -43,18 +44,18 @@
         start = pl.multiple_of(block_ref[peer] * span_len, span_len)
         yield pltpu.make_async_copy(
             moved.at[pl.ds(start, span_len)],
-            out_ref.at[peer, :, pl.ds(0, row_width)],
+            out_ref.at[peer, :, pl.ds(column, row_width)],
             sems.at[0, peer],
         )
-        if tagged:
-            yield pltpu.make_async_copy(
-                tags.at[peer], out_ref.at[peer, :, pl.ds(row_width, LANES)], sems.at[1, peer]
-            )
+        yield pltpu.make_async_copy(
+            tags.at[peer],
+            out_ref.at[peer, :, pl.ds(column + row_width, LANES)],
+            sems.at[1, peer],
+        )
 
     for peer in range(peers):
-        if tagged:
-            slot = slot_ref[peer].astype(jnp.float32)
-            tags[peer] = jnp.full((span_len, LANES), slot, jnp.float32).astype(tags.dtype)
+        slot = slot_ref[peer].astype(jnp.float32)
+        tags[peer] = jnp.full((span_len, LANES), slot, jnp.float32).astype(tags.dtype)
         for copy in copies(peer):
             copy.start()
     for peer in range(peers):
@@ -62,18 +63,21 @@
             copy.wait()
 
 
-def spread(pieces, carried, block_of_peer, slot_of_peer, span_len, chunk, tagged):
+def spread(pieces, carried, block_of_peer, slot_of_peer, span_len, chunk, shared=None):
     peers = block_of_peer.shape[0]
     rows, piece_width = pieces[0].shape
     row_width = piece_width * len(pieces)
-    wide = row_width + (LANES if tagged else 0)
+    wide = row_width + LANES
+    whole = wide if shared is None else shared.shape[2]
+    extra = [] if shared is None else [shared]
     return pl.pallas_call(
-        functools.partial(spread_kernel, tagged),
+        functools.partial(spread_kernel, len(pieces), whole - wide),
         grid_spec=pltpu.PrefetchScalarGridSpec(
             num_scalar_prefetch=2,
             grid=(1,),
             in_specs=[pl.BlockSpec((1, row_width), lambda i, *_: (0, chunk))]
-            + [pl.BlockSpec((rows, piece_width), lambda i, *_: (0, 0))] * len(pieces),
+            + [pl.BlockSpec((rows, piece_width), lambda i, *_: (0, 0))] * len(pieces)
+            + [pl.BlockSpec(memory_space=pl.ANY)] * len(extra),
             out_specs=pl.BlockSpec(memory_space=pl.ANY),
             scratch_shapes=[
                 pltpu.VMEM((rows, row_width), carried.dtype),
@@ -81,10 +85,11 @@
                 pltpu.SemaphoreType.DMA((2, peers)),
             ],
         ),
-        out_shape=jax.ShapeDtypeStruct((peers, span_len, wide), carried.dtype),
+        out_shape=jax.ShapeDtypeStruct((peers, span_len, whole), carried.dtype),
+        input_output_aliases={3 + len(pieces): 0} if extra else {},
         compiler_params=pltpu.CompilerParams(vmem_limit_bytes=32 * MIB),
         name="spread_queries",
-    )(block_of_peer, slot_of_peer, carried, *pieces)
+    )(block_of_peer, slot_of_peer, carried, *pieces, *extra)
 
 
 def pack_levels(stats, heads):
@@ -105,8 +110,9 @@
     )
 
 
-def attend_kernel(valid_ref, slot_ref, query_ref, key_ref, value_ref, out_ref):
-    row_width = query_ref.shape[2]
+def attend_kernel(valid_ref, slot_ref, query_ref, key_ref, value_ref, *refs):
+    out_ref = refs[-1]
+    row_width = key_ref.shape[2]
     span_len = query_ref.shape[1]
     length = key_ref.shape[1]
     heads = row_width // HEAD
@@ -150,24 +156,27 @@
         out_ref[0, :, row_width:] = pack_levels(stats, heads).astype(out_ref.dtype)
 
 
-def attend(asked, keys, values, valid, slots, width, chunk, part):
+def attend(asked, keys, values, valid, slots, width, chunk, part, size, place, places, shared):
     peers, span_len, _ = asked.shape
     length = keys.shape[1]
     heads = width // HEAD
     wide = width + LANES
+    extra = [] if shared is None else [shared]
     return pl.pallas_call(
         attend_kernel,
         grid_spec=pltpu.PrefetchScalarGridSpec(
             num_scalar_prefetch=2,
             grid=(peers,),
             in_specs=[
-                pl.BlockSpec((1, span_len, width), lambda i, v, s: (i, 0, part)),
+                pl.BlockSpec((1, span_len, size), lambda i, v, s: (i, 0, part)),
                 pl.BlockSpec((1, length, width), lambda i, v, s: (s[i], 0, chunk)),
                 pl.BlockSpec((1, length, width), lambda i, v, s: (s[i], 0, chunk)),
-            ],
-            out_specs=pl.BlockSpec((1, span_len, wide), lambda i, v, s: (i, 0, 0)),
-        ),
-        out_shape=jax.ShapeDtypeStruct((peers, span_len, wide), asked.dtype),
+            ]
+            + [pl.BlockSpec(memory_space=pl.ANY)] * len(extra),
+            out_specs=pl.BlockSpec((1, span_len, wide), lambda i, v, s: (i, 0, place)),
+        ),
+        out_shape=jax.ShapeDtypeStruct((peers, span_len, places * wide), asked.dtype),
+        input_output_aliases={5: 0} if extra else {},
         compiler_params=pltpu.CompilerParams(vmem_limit_bytes=56 * MIB),
         cost_estimate=pl.CostEstimate(
             flops=4 * peers * heads * span_len * length * HEAD,
@@ -175,7 +184,7 @@
             transcendentals=peers * heads * span_len * length,
         ),
         name="attend_blocks",
-    )(valid, slots, asked, keys, values)
+    )(valid, slots, asked, keys, values, *extra)
 
 
 def merge_block(uses, parts):
@@ -243,13 +252,13 @@
             out_ref[rows:, cut] = merged[:ROW_TILE].astype(out_ref.dtype)
 
 
-def merge_far(parts, index, use, blocks):
-    _, span_len, wide = parts.shape
+def merge_far(parts, column, wide, index, use, blocks):
+    span_len = parts.shape[1]
     picked = index.shape[0] // blocks
     specs = [
         pl.BlockSpec(
             (1, span_len, wide),
-            functools.partial(lambda r, i, index, use: (index[i * picked + r], 0, 0), r),
+            functools.partial(lambda r, i, index, use: (index[i * picked + r], 0, column), r),
         )
         for r in range(picked)
     ]
@@ -267,8 +276,8 @@
     )(index, use, *([parts] * picked))
 
 
-def merge_all(parts, index, use, blocks, far):
-    _, span_len, wide = parts.shape
+def merge_all(parts, column, wide, index, use, blocks, far):
+    span_len = parts.shape[1]
     row_width = wide - LANES
     picked = index.shape[0] // blocks
     rows = blocks * span_len
@@ -276,7 +285,7 @@
         pl.BlockSpec(
             (1, span_len, wide),
             functools.partial(
-                lambda r, i, index, use: (index[(blocks - 1 - i) * picked + r], 0, 0), r
+                lambda r, i, index, use: (index[(blocks - 1 - i) * picked + r], 0, column), r
             ),
         )
         for r in range(picked)
@@ -297,76 +306,91 @@
     )(index, use, *([parts] * picked), far)
 
 
-def project_kernel(place_ref, stay_ref, *refs):
-    *rest, keep_ref, send_ref, rows_ref, first_ref = refs
-    sources, below_ref, weights = rest[: -PLANE - 1], rest[-PLANE - 1], rest[-PLANE:]
+def project_kernel(count, place_ref, stay_ref, *refs):
+    sources, below_ref, weights = refs[:count], refs[count], refs[count + 1 : -7]
+    keep_ref, send_ref, rows_ref, first_ref, held_ref, row_sems, weight_sems = refs[-7:]
     half = keep_ref.shape[0]
     part = half // PLANE
-    step = pl.program_id(0)
-
-    @pl.when(step == 0)
-    def _():
+    tile = held_ref.shape[2]
+
+    def source_copies():
         for at, ref in enumerate(sources):
             member = place_ref[0] ^ (at % PLANE)
             width = ref.shape[1]
-            cut = slice(at // PLANE * width, (at // PLANE + 1) * width)
+            cut = pl.ds(at // PLANE * width, width)
             for side in range(2):
                 to = pl.multiple_of(side * half + member * part, part)
-                rows_ref[pl.ds(to, part), cut] = ref[side * part : (side + 1) * part]
+                yield pltpu.make_async_copy(
+                    ref.at[pl.ds(side * part, part)],
+                    rows_ref.at[pl.ds(to, part), cut],
+                    row_sems.at[at, side],
+                )
             to = pl.multiple_of(member * ROW_TILE, ROW_TILE)
-            first_ref[pl.ds(to, ROW_TILE), cut] = ref[2 * part :]
-        shape = (ROW_TILE, rows_ref.shape[1])
-        last = lax.broadcasted_iota(jnp.int32, shape, 0) == ROW_TILE - 1
-        for member in range(PLANE):
-            if member < PLANE - 1:
-                at = (member + 1) * ROW_TILE
-                below = first_ref[at : at + ROW_TILE].astype(jnp.float32)[0:1]
-            else:
-                below = below_ref[...].astype(jnp.float32)[0:1]
-            end = half + (member + 1) * part
-            held = rows_ref[end - ROW_TILE : end].astype(jnp.float32)
-            rows_ref[end - ROW_TILE : end] = jnp.where(last, below, held).astype(rows_ref.dtype)
-
+            yield pltpu.make_async_copy(
+                ref.at[pl.ds(2 * part, ROW_TILE)],
+                first_ref.at[pl.ds(to, ROW_TILE), cut],
+                row_sems.at[at, 2],
+            )
+
+    def weight_copy(shard):
+        return pltpu.make_async_copy(weights[shard], held_ref.at[shard], weight_sems.at[shard])
+
+    for copy in source_copies():
+        copy.start()
+    for shard in range(len(weights)):
+        weight_copy(shard).start()
+    for copy in source_copies():
+        copy.wait()
+    shape = (ROW_TILE, rows_ref.shape[1])
+    last = lax.broadcasted_iota(jnp.int32, shape, 0) == ROW_TILE - 1
+    for member in range(PLANE):
+        if member < PLANE - 1:
+            at = (member + 1) * ROW_TILE
+            below = first_ref[at : at + ROW_TILE].astype(jnp.float32)[0:1]
+        else:
+            below = below_ref[...].astype(jnp.float32)[0:1]
+        end = half + (member + 1) * part
+        held = rows_ref[end - ROW_TILE : end].astype(jnp.float32)
+        rows_ref[end - ROW_TILE : end] = jnp.where(last, below, held).astype(rows_ref.dtype)
     stay = pl.multiple_of(stay_ref[0] * half, half)
     go = pl.multiple_of((1 - stay_ref[0]) * half, half)
-    for at, weight_ref in enumerate(weights):
-
-        @pl.when(step == at)
-        def _():
-            for start, ref in ((go, send_ref), (stay, keep_ref)):
-                ref[...] = jnp.dot(
-                    rows_ref[pl.ds(start, half)],
-                    weight_ref[...],
-                    preferred_element_type=jnp.float32,
-                ).astype(ref.dtype)
+    for shard in range(len(weights)):
+        weight_copy(shard).wait()
+        for start, ref in ((go, send_ref), (stay, keep_ref)):
+            ref[:, shard * tile : (shard + 1) * tile] = jnp.dot(
+                rows_ref[pl.ds(start, half)],
+                held_ref[shard],
+                preferred_element_type=jnp.float32,
+            ).astype(ref.dtype)
 
 
 def project(sources, below, weights, place, stay):
-    height, width = sources[0].shape
+    height = sources[0].shape[0]
     row_width = below.shape[1]
     rows = PLANE * (height - ROW_TILE)
     shards = len(weights)
     tile = weights[0].shape[1]
     columns = shards * tile
     half = rows // 2
+    kind = sources[0].dtype
     return pl.pallas_call(
-        project_kernel,
+        functools.partial(project_kernel, len(sources)),
         grid_spec=pltpu.PrefetchScalarGridSpec(
             num_scalar_prefetch=2,
-            grid=(shards,),
-            in_specs=[pl.BlockSpec((height, width), lambda i, *_: (0, 0))] * len(sources)
+            grid=(1,),
+            in_specs=[pl.BlockSpec(memory_space=pl.ANY)] * len(sources)
             + [pl.BlockSpec((1, row_width), lambda i, *_: (0, 0))]
-            + [pl.BlockSpec((row_width, tile), lambda i, *_: (0, 0))] * shards,
-            out_specs=[
-                pl.BlockSpec((half, tile), lambda i, *_: (0, i)),
-                pl.BlockSpec((half, tile), lambda i, *_: (0, i)),
+            + [pl.BlockSpec(memory_space=pl.ANY)] * shards,
+            out_specs=[pl.BlockSpec((half, columns), lambda i, *_: (0, 0))] * 2,
+            scratch_shapes=[
+                pltpu.VMEM((rows, row_width), kind),
+                pltpu.VMEM((PLANE * ROW_TILE, row_width), kind),
+                pltpu.VMEM((shards, row_width, tile), kind),
+                pltpu.SemaphoreType.DMA((len(sources), 3)),
+                pltpu.SemaphoreType.DMA((shards,)),
             ],
-            scratch_shapes=[
-                pltpu.VMEM((rows, row_width), sources[0].dtype),
-                pltpu.VMEM((PLANE * ROW_TILE, row_width), sources[0].dtype),
-            ],
-        ),
-        out_shape=[jax.ShapeDtypeStruct((half, columns), sources[0].dtype)] * 2,
+        ),
+        out_shape=[jax.ShapeDtypeStruct((half, columns), kind)] * 2,
         compiler_params=pltpu.CompilerParams(vmem_limit_bytes=30 * MIB),
         name="project_rows",
     )(place, stay, *sources, below, *weights)
@@ -504,7 +528,7 @@
     near_peers = base + jnp.arange(half, dtype=jnp.int32)
     near_out = spread(
         [queries], carried, *pick_requests(owners, slot_rows, near_peers, per_block),
-        span_len, 0, True,
+        span_len, 0,
     )
     near_asked = exchange(near_out)
     far_carried = lax.ppermute(
@@ -525,47 +549,45 @@
     def slots_of(asked):
         return asked[:, 0, -LANES].astype(jnp.int32)
 
-    def answer(asked, tags, chunk, part):
+    def answer(asked, tags, chunk, part, size, place, places, shared=None):
         valid = (tags > 0).astype(jnp.int32)
         slots = jnp.maximum(tags - 1, 0)
         return attend(
-            asked, neighbour_keys, neighbour_values, valid, slots, width, chunk, part
-        )
-
+            asked, neighbour_keys, neighbour_values, valid, slots, width, chunk, part, size,
+            place, places, shared,
+        )
+
+    wide = width + LANES
     far_second = to_partner(held_queries[:, width:])
     near_index, near_use = within(owners, base, half)
     far_index, far_use = within(far_owners, base, half)
-    far_out = spread([far_first], far_carried, *far_picked, span_len, 0, True)
+    far_out = spread([far_first], far_carried, *far_picked, span_len, 0)
     far_asked = exchange(far_out)
     near_asked, _ = pinned(near_asked, far_out)
     near_tags = slots_of(near_asked)
-    near_parts = [answer(near_asked, near_tags, chunk, chunk) for chunk in range(chunks)]
-    far_asked, far_second, weight, *near_parts = pinned(
-        far_asked, far_second, out_weight, *near_parts
+    near_first = answer(near_asked, near_tags, 0, 0, width, 0, 2)
+    near_second = answer(near_asked, near_tags, 1, 1, width, 1, 2)
+    far_asked, far_second, weight, near_first, near_second = pinned(
+        far_asked, far_second, out_weight, near_first, near_second
     )
 
     middle = row_width // 2
-    far_out = spread([far_second], far_carried, *far_picked, span_len, 1, False)
-    next_asked = exchange(far_out)
-    near_part, far_asked, _ = pinned(near_parts[0], far_asked, far_out)
-    near_back = exchange(near_part)
+    mixed = spread([far_second], far_carried, *far_picked, span_len, 1, near_first)
+    next_asked = exchange(mixed)
+    far_asked, near_second, _ = pinned(far_asked, near_second, mixed)
     far_weight = [to_partner(weight[:middle])] if by_plane else []
     far_tags = slots_of(far_asked)
-    far_parts = answer(far_asked, far_tags, 0, 0)
-    far_parts, next_asked, near_back, near_part, weight, *far_weight = pinned(
-        far_parts, next_asked, near_back, near_parts[1], weight, *far_weight
-    )
-
-    far_back = exchange(far_parts)
-    next_back = exchange(near_part)
+    mixed = answer(far_asked, far_tags, 0, 0, wide, 0, 2, near_second)
+    mixed, next_asked, weight, *far_weight = pinned(mixed, next_asked, weight, *far_weight)
+
+    far_back = exchange(mixed)
     if by_plane:
         far_weight.append(to_partner(weight[middle:]))
-    far_parts = answer(next_asked, far_tags, 1, 0)
-    far_back, far_parts, next_back, weight, *far_weight = pinned(
-        far_back, far_parts, next_back, weight, *far_weight
-    )
-
-    far_merged = merge_far(far_back, far_index, far_use, blocks)
+    far_parts = answer(next_asked, far_tags, 1, 1, wide, 0, 1)
+    far_back, far_parts, weight, *far_weight = pinned(far_back, far_parts, weight, *far_weight)
+    near_back, next_back = next_asked, far_back
+
+    far_merged = merge_far(far_back, 0, wide, far_index, far_use, blocks)
     far_home = to_partner(far_merged)
     far_back = exchange(far_parts)
     far_home, far_back, weight = pinned(far_home, far_back, weight)
@@ -576,16 +598,18 @@
     def plane_rows(moved):
         return [moved] + [swap(moved, by) for by in range(1, PLANE)] if by_plane else [moved]
 
-    far_merged = merge_far(far_back, far_index, far_use, blocks)
+    far_merged = merge_far(far_back, 0, wide, far_index, far_use, blocks)
     far_home, near_back, weight, _ = pinned(far_home, near_back, weight, far_merged)
     next_home = to_partner(far_merged)
-    sources = plane_rows(merge_all(near_back, near_index, near_use, blocks, far_home))
+    sources = plane_rows(
+        merge_all(near_back, 0, wide, near_index, near_use, blocks, far_home)
+    )
     near_swap = [swap(weight, PLANE)] if by_plane else []
     count = len(sources)
     next_home, next_back = pinned(next_home, next_back)
     next_home, next_back, *held = pinned(next_home, next_back, *sources, *near_swap)
     sources, near_swap = held[:count], held[count:]
-    moved = merge_all(next_back, near_index, near_use, blocks, next_home)
+    moved = merge_all(next_back, 1, wide, near_index, near_use, blocks, next_home)
     if by_plane:
         place = lax.rem(here, PLANE).reshape(1)
         stay = lax.axis_index("tensor").astype(jnp.int32).reshape(1)

time: 324 us -> 320 us (0.988)
  blocking collectives: 19.7 us -> 0 us
  waiting for transfers between devices: 162 us -> 167 us
  starting transfers between devices: 62.1 us -> 66.4 us
  local copies, waits for them, and re-layouts: 15.8 us -> 19.1 us
    all_to_all x1 -> x0, blocking collectives: 19.7 us -> none  [exchange(): lax.all_to_all(x, 'dp', split_axis=0, concat_axis=0, tiled=True, axis_ind...]
    ppermute x7, waiting for transfers between devices: 106 us -> 123 us  [to_partner(): return lax.ppermute(x, 'dp', across)]
    all_to_all x6 -> x5, waiting for transfers between devices: 17.4 us -> 6.31 us  [exchange(): lax.all_to_all(x, 'dp', split_axis=0, concat_axis=0, tiled=True, axis_ind...]
    pallas_call x4, Pallas kernels: 28.5 us -> 33.6 us  [attend(): pl.pallas_call(attend_kernel, grid_spec=pltpu.PrefetchScalarGridSpec(num_...]
    ppermute x7, starting transfers between devices: 12 us -> 16.6 us  [to_partner(): return lax.ppermute(x, 'dp', across)]
    unnamed x46 -> x52, local copies, waits for them, and re-layouts: 12.9 us -> 17.3 us
    all_to_all x6 -> x5, starting transfers between devices: 26.2 us -> 22.6 us  [exchange(): lax.all_to_all(x, 'dp', split_axis=0, concat_axis=0, tiled=True, axis_ind...]
    ppermute x11, starting transfers between devices: 12.2 us -> 15.6 us  [swap(): return lax.ppermute(x, 'dp', [(i, i ^ by) for i in range(peer_count)])]
  transfers between devices with their start and end apart: 31 -> 30, of which waited for: 14 -> 14; matrix products, arithmetic and copies ran while one was open for 3% -> 3% of each run, Pallas kernels for 11% -> 13%
where the time goes in v2:
time: 320 us; the launch traced here: 318 us
  waiting for transfers between devices  167 us (52%)
  starting transfers between devices  66.4 us (21%)
  Pallas kernels  59.8 us (19%)
  local copies, waits for them, and re-layouts  19.1 us (6%)
  other arithmetic  5.41 us (2%)
    ppermute x7, waiting for transfers between devices, to_partner(): return lax.ppermute(x, 'dp', across)  123 us
    pallas_call x4, Pallas kernels, attend(): pl.pallas_call(attend_kernel, grid_spec=pltpu.PrefetchScalarGridSpec(num_...  33.6 us
    all_to_all x5, starting transfers between devices, exchange(): lax.all_to_all(x, 'dp', split_axis=0, concat_axis=0, tiled=True, axis_ind...  22.6 us
    ppermute x4, waiting for transfers between devices, local(): lax.ppermute(first_row, 'dp', [(i + PLANE, i + at) for i in range(0, peer...  20.2 us
    unnamed x52, local copies, waits for them, and re-layouts  17.3 us
    ppermute x7, starting transfers between devices, to_partner(): return lax.ppermute(x, 'dp', across)  16.6 us
    ppermute x11, starting transfers between devices, swap(): return lax.ppermute(x, 'dp', [(i, i ^ by) for i in range(peer_count)])  15.6 us
    ppermute x11, waiting for transfers between devices, swap(): return lax.ppermute(x, 'dp', [(i, i ^ by) for i in range(peer_count)])  10.6 us
  transfers between devices with their start and end apart: 30, of which 14 were waited for; matrix products, arithmetic and copies ran while one was open for 3% of the time, Pallas kernels for 13%

profile of v2, /device:TPU:0, one launch (start us, length us, event | category | flops | bytes accessed | tf_op | source)
XLA Modules:
  0.0 318.4 jit_solution(9395730265743111575)
XLA Ops:
  1.4 4.8 %collective-permute-start.3 = (bf16[1,2048]{1,0:T(2,128)(2,1)S(1)}, bf16[1,2048]{1,0:T(2,128)(2,1)S(1)}, u32[]{:S(2)}, u32[]{:S(2)}) collective-permute-start(bf16[1,2048]{1,0:T(2,128)(2,1)S(1)} %slice.35), channel_id=1, source_target_pairs={{0,2},{2,4},{4,6},{6,8},{8,10},{10,12},{12,14},{14,16},{16,18},{18... | collective-permute-start | bytes 12296 | tf_op jit(solution)/shard_map/ppermute | solution.py:23
  8.2 1.2 copy-done.4
  9.4 2.3 spread_queries.3
  11.7 5.1 %all-to-all-start.1 = ((bf16[8,64,2176]{2,1,0:T(8,128)(2,1)}), bf16[8,64,2176]{2,1,0:T(8,128)(2,1)S(1)}, u32[]{:S(2)}, u32[]{:S(2)}) async-start(bf16[8,64,2176]{2,1,0:T(8,128)(2,1)} %spread_queries.3), calls=%async_computation.1 | async-start | bytes 4456448 | tf_op jit(solution)/shard_map/all_to_all | solution.py:512
  16.9 3.3 %collective-permute-start = (bf16[256,1024]{1,0:T(8,128)(2,1)S(1)}, bf16[256,1024]{1,0:T(8,128)(2,1)S(1)}, u32[]{:S(2)}, u32[]{:S(2)}) collective-permute-start(bf16[256,1024]{1,0:T(8,128)(2,1)S(1)} %slice.34), channel_id=1, source_target_pairs={{0,16},{2,18},{4,20},{6,22},{8,24},{10,26},{12,28},{14,30},{16,0},... | collective-permute-start | bytes 1572872 | tf_op jit(solution)/shard_map/ppermute | solution.py:520
  20.2 3.3 %collective-permute-start.1 = (bf16[1,2048]{1,0:T(2,128)(2,1)S(1)}, bf16[1,2048]{1,0:T(2,128)(2,1)S(1)}, u32[]{:S(2)}, u32[]{:S(2)}) collective-permute-start(bf16[1,2048]{1,0:T(2,128)(2,1)S(1)} %slice.35), channel_id=1, source_target_pairs={{0,18},{2,20},{4,22},{6,24},{8,26},{10,28},{12,30},{14,0},{16,2},{... | collective-permute-start | bytes 12296 | tf_op jit(solution)/shard_map/ppermute | solution.py:534
  23.6 2.9 collective-permute-start.2
  26.5 25.5 %collective-permute-done.2 = s32[1,128]{1,0:T(1,128)S(1)} collective-permute-done((s32[1,128]{1,0:T(1,128)S(1)}, s32[1,128]{1,0:T(1,128)S(1)}, u32[]{:S(2)}, u32[]{:S(2)}) %collective-permute-start.2) | collective-permute-done | bytes 544 | tf_op jit(solution)/shard_map/ppermute | solution.py:520
  52.0 4.0 %collective-permute-done.1.carried_ref = bf16[1,2048]{1,0:T(2,128)(2,1)S(1)} collective-permute-done((bf16[1,2048]{1,0:T(2,128)(2,1)S(1)}, bf16[1,2048]{1,0:T(2,128)(2,1)S(1)}, u32[]{:S(2)}, u32[]{:S(2)}) %collective-permute-start.1) | collective-permute-done | bytes 4128 | tf_op jit(solution)/shard_map/ppermute | solution.py:534
  56.2 1.9 spread_queries.4
  58.1 5.2 %all-to-all-start = ((bf16[8,64,1152]{2,1,0:T(8,128)(2,1)}), bf16[8,64,1152]{2,1,0:T(8,128)(2,1)}, u32[]{:S(2)}, u32[]{:S(2)}) async-start(bf16[8,64,1152]{2,1,0:T(8,128)(2,1)} %spread_queries.4), calls=%async_computation | async-start | bytes 2359296 | tf_op jit(solution)/shard_map/all_to_all | solution.py:512
  63.4 0.9 collective-permute-start.4
  64.3 0.9 maximum_reduce_fusion.1
  65.2 9.7 %attend_blocks.5.refs_0_ = bf16[8,64,2304]{2,1,0:T(8,128)(2,1)} custom-call(s32[8]{0:T(128)} %get-tuple-element.91.valid_ref, s32[8]{0:T(128)} %get-tuple-element.90.slot_ref, bf16[8,64,2176]{2,1,0:T(8,128)(2,1)} %copy-done.24, bf16[8,128,2048]{2,1,0:T(8,128)(2,1)} %key_ref.7, bf16[8,128,2048]{2,1,0:T(8,128)(2,1)} %value_ref.7), custom_call_target="tpu_custom_call" | custom-call | flops 268435456 | bytes 6291456 | tf_op jit(solution)/shard_map/attend_blocks/pallas_call | solution.py:165
  74.9 9.7 %attend_blocks.4.refs_1_ = bf16[8,64,2304]{2,1,0:T(8,128)(2,1)} custom-call(s32[8]{0:T(128)} %get-tuple-element.91.valid_ref, s32[8]{0:T(128)} %get-tuple-element.90.slot_ref, bf16[8,64,2176]{2,1,0:T(8,128)(2,1)} %copy-done.24, bf16[8,128,2048]{2,1,0:T(8,128)(2,1)} %key_ref.7, bf16[8,128,2048]{2,1,0:T(8,128)(2,1)} %value_ref.7), custom_call_target="tpu_custom_call" | custom-call | flops 268435456 | bytes 6291456 | tf_op jit(solution)/shard_map/attend_blocks/pallas_call | solution.py:165
  84.5 0.9 collective-permute-done.4.refs_0_
  85.4 2.1 all-to-all-done.query_ref
  87.5 1.7 copy-done.2
  89.2 1.1 spread_queries.5
  90.3 1.4 copy-done.3
  91.7 4.7 %all-to-all-start.2 = ((bf16[8,64,2304]{2,1,0:T(8,128)(2,1)}), bf16[8,64,2304]{2,1,0:T(8,128)(2,1)S(1)}, u32[]{:S(2)}, u32[]{:S(2)}) async-start(bf16[8,64,2304]{2,1,0:T(8,128)(2,1)} %copy-done.3), calls=%async_computation.2 | async-start | bytes 4718592 | tf_op jit(solution)/shard_map/all_to_all | solution.py:512
  96.5 1.2 collective-permute-start.5
  97.6 1.6 maximum_reduce_fusion
  99.2 7.1 %attend_blocks.6 = bf16[8,64,2304]{2,1,0:T(8,128)(2,1)} custom-call(s32[8]{0:T(128)} %get-tuple-element.93.valid_ref, s32[8]{0:T(128)} %get-tuple-element.92.slot_ref, bf16[8,64,1152]{2,1,0:T(8,128)(2,1)} %all-to-all-done.query_ref, bf16[8,128,2048]{2,1,0:T(8,128)(2,1)} %key_ref.7, bf16[8,128,2048]{2,1,0:T(8,128)(2,1)} %value_ref.7, ...), custom_call_target="tpu_custom_call", output_to_operand_aliasing={{}: (5, {})} | custom-call | flops 268435456 | bytes 6291456 | tf_op jit(solution)/shard_map/attend_blocks/pallas_call | solution.py:165
  106.4 25.4 %collective-permute-done.5 = bf16[1024,256]{1,0:T(8,128)(2,1)} collective-permute-done((bf16[1024,256]{1,0:T(8,128)(2,1)S(1)}, bf16[1024,256]{1,0:T(8,128)(2,1)}, u32[]{:S(2)}, u32[]{:S(2)}) %collective-permute-start.5) | collective-permute-done | bytes 524320 | tf_op jit(solution)/shard_map/ppermute | solution.py:520
  131.7 2.1 all-to-all-done.2.query_ref.refs_0_.refs_1_
  133.8 1.4 copy-done
  135.3 3.9 %all-to-all-start.3 = ((bf16[8,64,2304]{2,1,0:T(8,128)(2,1)}), bf16[8,64,2304]{2,1,0:T(8,128)(2,1)S(1)}, u32[]{:S(2)}, u32[]{:S(2)}) async-start(bf16[8,64,2304]{2,1,0:T(8,128)(2,1)} %attend_blocks.6), calls=%async_computation.3 | async-start | bytes 4718592 | tf_op jit(solution)/shard_map/all_to_all | solution.py:512
  139.2 1.7 collective-permute-start.6
  140.9 7.1 %attend_blocks.7 = bf16[8,64,1152]{2,1,0:T(8,128)(2,1)} custom-call(s32[8]{0:T(128)} %get-tuple-element.93.valid_ref, s32[8]{0:T(128)} %get-tuple-element.92.slot_ref, bf16[8,64,2304]{2,1,0:T(8,128)(2,1)} %copy-done, bf16[8,128,2048]{2,1,0:T(8,128)(2,1)} %key_ref.7, bf16[8,128,2048]{2,1,0:T(8,128)(2,1)} %value_ref.7), custom_call_target="tpu_custom_call" | custom-call | flops 268435456 | bytes 6291456 | tf_op jit(solution)/shard_map/attend_blocks/pallas_call | solution.py:165
  148.0 27.1 %collective-permute-done.6 = bf16[1024,256]{1,0:T(8,128)(2,1)} collective-permute-done((bf16[1024,256]{1,0:T(8,128)(2,1)S(1)}, bf16[1024,256]{1,0:T(8,128)(2,1)}, u32[]{:S(2)}, u32[]{:S(2)}) %collective-permute-start.6) | collective-permute-done | bytes 524320 | tf_op jit(solution)/shard_map/ppermute | solution.py:520
  175.1 2.1 all-to-all-done.3.refs_0_.refs_1_
  177.2 3.7 %all-to-all-start.4 = ((bf16[8,64,1152]{2,1,0:T(8,128)(2,1)}), bf16[8,64,1152]{2,1,0:T(8,128)(2,1)S(1)}, u32[]{:S(2)}, u32[]{:S(2)}) async-start(bf16[8,64,1152]{2,1,0:T(8,128)(2,1)} %attend_blocks.7), calls=%async_computation.4 | async-start | bytes 2359296 | tf_op jit(solution)/shard_map/all_to_all | solution.py:512
  181.0 2.1 merge_far.2
  183.1 3.2 %collective-permute-start.7 = (bf16[4,64,1152]{2,1,0:T(8,128)(2,1)S(1)}, bf16[4,64,1152]{2,1,0:T(8,128)(2,1)S(1)}, u32[]{:S(2)}, u32[]{:S(2)}) collective-permute-start(bf16[4,64,1152]{2,1,0:T(8,128)(2,1)S(1)} %merge_far.2), channel_id=1, source_target_pairs={{0,16},{2,18},{4,20},{6,22},{8,24},{10,26},{12,28},{14,30},{16,0},... | collective-permute-start | bytes 1769480 | tf_op jit(solution)/shard_map/ppermute | solution.py:520
  186.3 24.6 %collective-permute-done.7.refs_2_ = bf16[4,64,1152]{2,1,0:T(8,128)(2,1)S(1)} collective-permute-done((bf16[4,64,1152]{2,1,0:T(8,128)(2,1)S(1)}, bf16[4,64,1152]{2,1,0:T(8,128)(2,1)S(1)}, u32[]{:S(2)}, u32[]{:S(2)}) %collective-permute-start.7) | collective-permute-done | bytes 589856 | tf_op jit(solution)/shard_map/ppermute | solution.py:520
  210.9 0.8 copy-done.14
  211.7 1.9 merge_far.3
  213.8 3.4 %collective-permute-start.8 = (bf16[4,64,1152]{2,1,0:T(8,128)(2,1)S(1)}, bf16[4,64,1152]{2,1,0:T(8,128)(2,1)S(1)}, u32[]{:S(2)}, u32[]{:S(2)}) collective-permute-start(bf16[4,64,1152]{2,1,0:T(8,128)(2,1)S(1)} %merge_far.3), channel_id=1, source_target_pairs={{0,16},{2,18},{4,20},{6,22},{8,24},{10,26},{12,28},{14,30},{16,0},... | collective-permute-start | bytes 1769480 | tf_op jit(solution)/shard_map/ppermute | solution.py:520
  217.2 2.4 merge_all.2.refs_0_
  219.7 2.5 collective-permute-start.11
  223.2 2.2 pad_maximum_fusion.refs_11_
  225.5 19.4 %collective-permute-done.8.refs_2_ = bf16[4,64,1152]{2,1,0:T(8,128)(2,1)S(1)} collective-permute-done((bf16[4,64,1152]{2,1,0:T(8,128)(2,1)S(1)}, bf16[4,64,1152]{2,1,0:T(8,128)(2,1)S(1)}, u32[]{:S(2)}, u32[]{:S(2)}) %collective-permute-start.8) | collective-permute-done | bytes 589856 | tf_op jit(solution)/shard_map/ppermute | solution.py:520
  244.9 0.8 copy-done.16
  245.7 0.8 copy-done.18
  246.5 0.8 copy-done.20
  247.3 3.2 %merge_all.3.refs_4_ = bf16[272,1024]{1,0:T(8,128)(2,1)} custom-call(s32[8]{0:T(128)S(1)} %subtract_select_fusion.index_ref, s32[8]{0:T(128)S(1)} %fusion.6.use_ref, bf16[8,64,2304]{2,1,0:T(8,128)(2,1)S(1)} %all-to-all-done.3.refs_0_.refs_1_, bf16[8,64,2304]{2,1,0:T(8,128)(2,1)S(1)} %all-to-all-done.3.refs_0_.refs_1_, ...), custom_call_target="tpu_custom_call" | custom-call | tf_op jit(solution)/shard_map/merge_all/pallas_call | solution.py:294
  250.5 4.9 %collective-permute-start.20 = (bf16[2048,256]{1,0:T(8,128)(2,1)}, bf16[2048,256]{1,0:T(8,128)(2,1)S(1)}, u32[]{:S(2)}, u32[]{:S(2)}) collective-permute-start(bf16[2048,256]{1,0:T(8,128)(2,1)} %pad_maximum_fusion.refs_11_), channel_id=1, source_target_pairs={{0,8},{2,10},{4,12},{6,14},{8,0},{10,2},{12,4},{14,6},{16,24},{18,... | collective-permute-start | bytes 3145736 | tf_op jit(solution)/shard_map/ppermute | solution.py:596
  257.3 2.3 collective-permute-start.13
  261.7 1.5 collective-permute-start.16
  263.2 20.2 %collective-permute-done.16 = bf16[1,2048]{1,0:T(2,128)(2,1)S(1)} collective-permute-done((bf16[1,2048]{1,0:T(2,128)(2,1)S(1)}, bf16[1,2048]{1,0:T(2,128)(2,1)S(1)}, u32[]{:S(2)}, u32[]{:S(2)}) %collective-permute-start.16) | collective-permute-done | bytes 4128 | tf_op jit(solution)/shard_map/ppermute | solution.py:628
  283.5 1.0 copy-done.9
  284.6 1.2 copy-done.13
  285.8 1.1 copy-done.17
  286.9 1.1 copy-done.19
  287.9 1.1 copy-done.21
  289.0 6.8 %project_rows.1 = (bf16[512,1024]{1,0:T(8,128)(2,1)S(1)}, bf16[512,1024]{1,0:T(8,128)(2,1)S(1)}) custom-call(s32[1]{0:T(128)} %bitcast.place_ref, s32[1]{0:T(128)} %bitcast.5.stay_ref, bf16[272,1024]{1,0:T(8,128)(2,1)S(1)} %copy-done.9, bf16[272,1024]{1,0:T(8,128)(2,1)S(1)} %copy-done.21, bf16[272,1024]{1,0:T(8,128)(2,1)S(1)} %copy-done.19, ...), custom_call_target="tpu_custom_call" | custom-call | tf_op jit(solution)/shard_map/project_rows/pallas_call | solution.py:376
  295.9 2.6 collective-permute-done.21
  298.5 1.2 add_cores.1
  299.7 3.5 %collective-permute-start.24 = (bf16[128,1024]{1,0:T(8,128)(2,1)S(1)}, bf16[128,1024]{1,0:T(8,128)(2,1)S(1)}, u32[]{:S(2)}, u32[]{:S(2)}) collective-permute-start(bf16[128,1024]{1,0:T(8,128)(2,1)S(1)} %get-tuple-element.89), channel_id=1, source_target_pairs={{0,6},{2,4},{4,2},{6,0},{8,14},{10,12},{12,10},{14,8},{16,22},{18,... | collective-permute-start | bytes 786440 | tf_op jit(solution)/shard_map/ppermute | solution.py:596
  303.2 5.8 %collective-permute-done.22.refs_1_ = bf16[128,1024]{1,0:T(8,128)(2,1)S(1)} collective-permute-done((bf16[128,1024]{1,0:T(8,128)(2,1)}, bf16[128,1024]{1,0:T(8,128)(2,1)S(1)}, u32[]{:S(2)}, u32[]{:S(2)}) %collective-permute-start.22) | collective-permute-done | bytes 262176 | tf_op jit(solution)/shard_map/ppermute | solution.py:596
  309.0 4.8 %collective-permute-done.23.refs_2_ = bf16[128,1024]{1,0:T(8,128)(2,1)S(1)} collective-permute-done((bf16[128,1024]{1,0:T(8,128)(2,1)}, bf16[128,1024]{1,0:T(8,128)(2,1)S(1)}, u32[]{:S(2)}, u32[]{:S(2)}) %collective-permute-start.23) | collective-permute-done | bytes 262176 | tf_op jit(solution)/shard_map/ppermute | solution.py:596
  313.9 1.2 copy-done.11
  315.1 3.3 %add_norm.1 = (bf16[128,4096]{1,0:T(8,128)(2,1)}, bf16[128,4096]{1,0:T(8,128)(2,1)}) custom-call(s32[1]{0:T(128)} %bitcast.place_ref, s32[4]{0:T(128)S(1)} %pad_add_fusion.line_ref, bf16[128,1024]{1,0:T(8,128)(2,1)S(1)} %get-tuple-element.86.refs_0_, bf16[128,1024]{1,0:T(8,128)(2,1)S(1)} %collective-permute-done.22.refs_1_, ...), custom_call_target="tpu_custom_call" | custom-call | tf_op jit(solution)/shard_map/add_norm/pallas_call | solution.py:455
  (88 shorter events, 8.5 us)
Async XLA Ops:
  1.4 6.8 %collective-permute-start.3 = (bf16[1,2048]{1,0:T(2,128)(2,1)S(1)}, bf16[1,2048]{1,0:T(2,128)(2,1)S(1)}, u32[]{:S(2)}, u32[]{:S(2)}) collective-permute-start(bf16[1,2048]{1,0:T(2,128)(2,1)S(1)} %slice.35), channel_id=1, source_target_pairs={{0,2},{2,4},{4,6},{6,8},{8,10},{10,12},{12,14},{14,16},{16,18},{18... | collective-permute-start | bytes 12296 | tf_op jit(solution)/shard_map/ppermute | solution.py:23
  8.2 1.2 copy-start.4
  11.7 5.1 %copy-start.5 = (bf16[256,2048]{1,0:T(8,128)(2,1)S(1)}, bf16[256,2048]{1,0:T(8,128)(2,1)}, u32[]{:S(2)}) copy-start(bf16[256,2048]{1,0:T(8,128)(2,1)} %refs_0_.1) | copy-start | bytes 3145732
  11.7 46.4 %all-to-all-start.1 = ((bf16[8,64,2176]{2,1,0:T(8,128)(2,1)}), bf16[8,64,2176]{2,1,0:T(8,128)(2,1)S(1)}, u32[]{:S(2)}, u32[]{:S(2)}) async-start(bf16[8,64,2176]{2,1,0:T(8,128)(2,1)} %spread_queries.3), calls=%async_computation.1 | async-start | bytes 4456448 | tf_op jit(solution)/shard_map/all_to_all | solution.py:512
  16.9 39.1 %collective-permute-start = (bf16[256,1024]{1,0:T(8,128)(2,1)S(1)}, bf16[256,1024]{1,0:T(8,128)(2,1)S(1)}, u32[]{:S(2)}, u32[]{:S(2)}) collective-permute-start(bf16[256,1024]{1,0:T(8,128)(2,1)S(1)} %slice.34), channel_id=1, source_target_pairs={{0,16},{2,18},{4,20},{6,22},{8,24},{10,26},{12,28},{14,30},{16,0},... | collective-permute-start | bytes 1572872 | tf_op jit(solution)/shard_map/ppermute | solution.py:520
  20.2 35.7 %collective-permute-start.1 = (bf16[1,2048]{1,0:T(2,128)(2,1)S(1)}, bf16[1,2048]{1,0:T(2,128)(2,1)S(1)}, u32[]{:S(2)}, u32[]{:S(2)}) collective-permute-start(bf16[1,2048]{1,0:T(2,128)(2,1)S(1)} %slice.35), channel_id=1, source_target_pairs={{0,18},{2,20},{4,22},{6,24},{8,26},{10,28},{12,30},{14,0},{16,2},{... | collective-permute-start | bytes 12296 | tf_op jit(solution)/shard_map/ppermute | solution.py:534
  23.6 28.4 %collective-permute-start.2 = (s32[1,128]{1,0:T(1,128)S(1)}, s32[1,128]{1,0:T(1,128)S(1)}, u32[]{:S(2)}, u32[]{:S(2)}) collective-permute-start(s32[1,128]{1,0:T(1,128)S(1)} %pad_bitcast_fusion), channel_id=1, source_target_pairs={{0,16},{2,18},{4,20},{6,22},{8,24},{10,26},{12,28},{14,30},{16,0},... | collective-permute-start | bytes 1544 | tf_op jit(solution)/shard_map/ppermute | solution.py:520
  58.1 7.0 %copy-start.24 = (bf16[8,64,2176]{2,1,0:T(8,128)(2,1)}, bf16[8,64,2176]{2,1,0:T(8,128)(2,1)S(1)}, u32[]{:S(2)}) copy-start(bf16[8,64,2176]{2,1,0:T(8,128)(2,1)S(1)} %all-to-all-done.1.query_ref) | copy-start | bytes 6684676
  58.1 29.4 %all-to-all-start = ((bf16[8,64,1152]{2,1,0:T(8,128)(2,1)}), bf16[8,64,1152]{2,1,0:T(8,128)(2,1)}, u32[]{:S(2)}, u32[]{:S(2)}) async-start(bf16[8,64,1152]{2,1,0:T(8,128)(2,1)} %spread_queries.4), calls=%async_computation | async-start | bytes 2359296 | tf_op jit(solution)/shard_map/all_to_all | solution.py:512
  63.4 22.0 %collective-permute-start.4 = (bf16[256,1024]{1,0:T(8,128)(2,1)S(1)}, bf16[256,1024]{1,0:T(8,128)(2,1)S(1)}, u32[]{:S(2)}, u32[]{:S(2)}) collective-permute-start(bf16[256,1024]{1,0:T(8,128)(2,1)S(1)} %slice.38), channel_id=1, source_target_pairs={{0,16},{2,18},{4,20},{6,22},{8,24},{10,26},{12,28},{14,30},{16,0},... | collective-permute-start | bytes 1572872 | tf_op jit(solution)/shard_map/ppermute | solution.py:520
  87.5 1.7 copy-start.2
  90.3 1.4 copy-start.3
  91.7 4.7 %copy-start.6 = (bf16[2048,256]{1,0:T(8,128)(2,1)S(1)}, bf16[2048,256]{1,0:T(8,128)(2,1)}, u32[]{:S(2)}) copy-start(bf16[2048,256]{1,0:T(8,128)(2,1)} %refs_9_) | copy-start | bytes 3145732
  91.7 42.1 %all-to-all-start.2 = ((bf16[8,64,2304]{2,1,0:T(8,128)(2,1)}), bf16[8,64,2304]{2,1,0:T(8,128)(2,1)S(1)}, u32[]{:S(2)}, u32[]{:S(2)}) async-start(bf16[8,64,2304]{2,1,0:T(8,128)(2,1)} %copy-done.3), calls=%async_computation.2 | async-start | bytes 4718592 | tf_op jit(solution)/shard_map/all_to_all | solution.py:512
  96.5 35.3 %collective-permute-start.5 = (bf16[1024,256]{1,0:T(8,128)(2,1)S(1)}, bf16[1024,256]{1,0:T(8,128)(2,1)}, u32[]{:S(2)}, u32[]{:S(2)}) collective-permute-start(bf16[1024,256]{1,0:T(8,128)(2,1)S(1)} %slice.41), channel_id=1, source_target_pairs={{0,16},{2,18},{4,20},{6,22},{8,24},{10,26},{12,28},{14,30},{16,0},... | collective-permute-start | bytes 1572872 | tf_op jit(solution)/shard_map/ppermute | solution.py:520
  133.8 1.4 copy-start
  135.3 42.0 %all-to-all-start.3 = ((bf16[8,64,2304]{2,1,0:T(8,128)(2,1)}), bf16[8,64,2304]{2,1,0:T(8,128)(2,1)S(1)}, u32[]{:S(2)}, u32[]{:S(2)}) async-start(bf16[8,64,2304]{2,1,0:T(8,128)(2,1)} %attend_blocks.6), calls=%async_computation.3 | async-start | bytes 4718592 | tf_op jit(solution)/shard_map/all_to_all | solution.py:512
  139.2 36.0 %collective-permute-start.6 = (bf16[1024,256]{1,0:T(8,128)(2,1)S(1)}, bf16[1024,256]{1,0:T(8,128)(2,1)}, u32[]{:S(2)}, u32[]{:S(2)}) collective-permute-start(bf16[1024,256]{1,0:T(8,128)(2,1)S(1)} %slice.42), channel_id=1, source_target_pairs={{0,16},{2,18},{4,20},{6,22},{8,24},{10,26},{12,28},{14,30},{16,0},... | collective-permute-start | bytes 1572872 | tf_op jit(solution)/shard_map/ppermute | solution.py:520
  177.2 34.5 %all-to-all-start.4 = ((bf16[8,64,1152]{2,1,0:T(8,128)(2,1)}), bf16[8,64,1152]{2,1,0:T(8,128)(2,1)S(1)}, u32[]{:S(2)}, u32[]{:S(2)}) async-start(bf16[8,64,1152]{2,1,0:T(8,128)(2,1)} %attend_blocks.7), calls=%async_computation.4 | async-start | bytes 2359296 | tf_op jit(solution)/shard_map/all_to_all | solution.py:512
  183.1 27.8 %collective-permute-start.7 = (bf16[4,64,1152]{2,1,0:T(8,128)(2,1)S(1)}, bf16[4,64,1152]{2,1,0:T(8,128)(2,1)S(1)}, u32[]{:S(2)}, u32[]{:S(2)}) collective-permute-start(bf16[4,64,1152]{2,1,0:T(8,128)(2,1)S(1)} %merge_far.2), channel_id=1, source_target_pairs={{0,16},{2,18},{4,20},{6,22},{8,24},{10,26},{12,28},{14,30},{16,0},... | collective-permute-start | bytes 1769480 | tf_op jit(solution)/shard_map/ppermute | solution.py:520
  210.9 0.8 copy-start.14
  211.7 5.5 %copy-start.1 = (bf16[8,64,2304]{2,1,0:T(8,128)(2,1)S(1)}, bf16[8,64,2304]{2,1,0:T(8,128)(2,1)}, u32[]{:S(2)}) copy-start(bf16[8,64,2304]{2,1,0:T(8,128)(2,1)} %copy-done) | copy-start | bytes 7077892
  211.7 5.5 %copy-start.15 = (bf16[4,64,1152]{2,1,0:T(8,128)(2,1)S(1)}, bf16[4,64,1152]{2,1,0:T(8,128)(2,1)}, u32[]{:S(2)}) copy-start(bf16[4,64,1152]{2,1,0:T(8,128)(2,1)} %copy-done.14) | copy-start | bytes 1769476
  213.7 33.7 %collective-permute-start.12 = (bf16[2048,256]{1,0:T(8,128)(2,1)}, bf16[2048,256]{1,0:T(8,128)(2,1)S(1)}, u32[]{:S(2)}, u32[]{:S(2)}) collective-permute-start(bf16[2048,256]{1,0:T(8,128)(2,1)} %refs_9_), channel_id=1, source_target_pairs={{0,8},{2,10},{4,12},{6,14},{8,0},{10,2},{12,4},{14,6},{16,24},{18,... | collective-permute-start | bytes 3145736 | tf_op jit(solution)/shard_map/ppermute | solution.py:596
  213.8 31.0 %collective-permute-start.8 = (bf16[4,64,1152]{2,1,0:T(8,128)(2,1)S(1)}, bf16[4,64,1152]{2,1,0:T(8,128)(2,1)S(1)}, u32[]{:S(2)}, u32[]{:S(2)}) collective-permute-start(bf16[4,64,1152]{2,1,0:T(8,128)(2,1)S(1)} %merge_far.3), channel_id=1, source_target_pairs={{0,16},{2,18},{4,20},{6,22},{8,24},{10,26},{12,28},{14,30},{16,0},... | collective-permute-start | bytes 1769480 | tf_op jit(solution)/shard_map/ppermute | solution.py:520
  219.7 40.0 %copy-start.8 = (bf16[272,1024]{1,0:T(8,128)(2,1)}, bf16[272,1024]{1,0:T(8,128)(2,1)S(1)}, u32[]{:S(2)}) copy-start(bf16[272,1024]{1,0:T(8,128)(2,1)S(1)} %merge_all.2.refs_0_) | copy-start | bytes 1671172
  219.7 25.2 %collective-permute-start.11 = (bf16[272,1024]{1,0:T(8,128)(2,1)S(1)}, bf16[272,1024]{1,0:T(8,128)(2,1)S(1)}, u32[]{:S(2)}, u32[]{:S(2)}) collective-permute-start(bf16[272,1024]{1,0:T(8,128)(2,1)S(1)} %merge_all.2.refs_0_), channel_id=1, source_target_pairs={{0,6},{2,4},{4,2},{6,0},{8,14},{10,12},{12,10},{14,8},{16,22},{18,... | collective-permute-start | bytes 1671176 | tf_op jit(solution)/shard_map/ppermute | solution.py:596
  222.2 23.4 %collective-permute-start.10 = (bf16[272,1024]{1,0:T(8,128)(2,1)S(1)}, bf16[272,1024]{1,0:T(8,128)(2,1)S(1)}, u32[]{:S(2)}, u32[]{:S(2)}) collective-permute-start(bf16[272,1024]{1,0:T(8,128)(2,1)S(1)} %merge_all.2.refs_0_), channel_id=1, source_target_pairs={{0,4},{2,6},{4,0},{6,2},{8,12},{10,14},{12,8},{14,10},{16,20},{18,... | collective-permute-start | bytes 1671176 | tf_op jit(solution)/shard_map/ppermute | solution.py:596
  222.8 23.7 %collective-permute-start.9 = (bf16[272,1024]{1,0:T(8,128)(2,1)S(1)}, bf16[272,1024]{1,0:T(8,128)(2,1)S(1)}, u32[]{:S(2)}, u32[]{:S(2)}) collective-permute-start(bf16[272,1024]{1,0:T(8,128)(2,1)S(1)} %merge_all.2.refs_0_), channel_id=1, source_target_pairs={{0,2},{2,0},{4,6},{6,4},{8,10},{10,8},{12,14},{14,12},{16,18},{18,... | collective-permute-start | bytes 1671176 | tf_op jit(solution)/shard_map/ppermute | solution.py:596
  225.5 58.1 %copy-start.7 = (bf16[2048,256]{1,0:T(8,128)(2,1)S(1)}, bf16[2048,256]{1,0:T(8,128)(2,1)}, u32[]{:S(2)}) copy-start(bf16[2048,256]{1,0:T(8,128)(2,1)} %refs_9_) | copy-start | bytes 3145732
  244.8 0.8 copy-start.16
  245.7 0.8 copy-start.18
  246.5 0.8 copy-start.20
  247.3 3.2 %copy-start.12 = (bf16[2048,256]{1,0:T(8,128)(2,1)}, bf16[2048,256]{1,0:T(8,128)(2,1)S(1)}, u32[]{:S(2)}) copy-start(bf16[2048,256]{1,0:T(8,128)(2,1)S(1)} %collective-permute-done.12.refs_10_) | copy-start | bytes 3145732
  250.5 33.0 %collective-permute-start.20 = (bf16[2048,256]{1,0:T(8,128)(2,1)}, bf16[2048,256]{1,0:T(8,128)(2,1)S(1)}, u32[]{:S(2)}, u32[]{:S(2)}) collective-permute-start(bf16[2048,256]{1,0:T(8,128)(2,1)} %pad_maximum_fusion.refs_11_), channel_id=1, source_target_pairs={{0,8},{2,10},{4,12},{6,14},{8,0},{10,2},{12,4},{14,6},{16,24},{18,... | collective-permute-start | bytes 3145736 | tf_op jit(solution)/shard_map/ppermute | solution.py:596
  256.2 27.3 %collective-permute-start.15 = (bf16[272,1024]{1,0:T(8,128)(2,1)}, bf16[272,1024]{1,0:T(8,128)(2,1)S(1)}, u32[]{:S(2)}, u32[]{:S(2)}) collective-permute-start(bf16[272,1024]{1,0:T(8,128)(2,1)} %merge_all.3.refs_4_), channel_id=1, source_target_pairs={{0,6},{2,4},{4,2},{6,0},{8,14},{10,12},{12,10},{14,8},{16,22},{18,... | collective-permute-start | bytes 1671176 | tf_op jit(solution)/shard_map/ppermute | solution.py:596
  256.8 26.7 %collective-permute-start.14 = (bf16[272,1024]{1,0:T(8,128)(2,1)}, bf16[272,1024]{1,0:T(8,128)(2,1)S(1)}, u32[]{:S(2)}, u32[]{:S(2)}) collective-permute-start(bf16[272,1024]{1,0:T(8,128)(2,1)} %merge_all.3.refs_4_), channel_id=1, source_target_pairs={{0,4},{2,6},{4,0},{6,2},{8,12},{10,14},{12,8},{14,10},{16,20},{18,... | collective-permute-start | bytes 1671176 | tf_op jit(solution)/shard_map/ppermute | solution.py:596
  257.3 26.2 %collective-permute-start.13 = (bf16[272,1024]{1,0:T(8,128)(2,1)}, bf16[272,1024]{1,0:T(8,128)(2,1)}, u32[]{:S(2)}, u32[]{:S(2)}) collective-permute-start(bf16[272,1024]{1,0:T(8,128)(2,1)} %merge_all.3.refs_4_), channel_id=1, source_target_pairs={{0,2},{2,0},{4,6},{6,4},{8,10},{10,8},{12,14},{14,12},{16,18},{18,... | collective-permute-start | bytes 1671176 | tf_op jit(solution)/shard_map/ppermute | solution.py:596
  259.7 0.7 collective-permute-start.19
  260.4 0.7 collective-permute-start.18
  261.1 0.7 collective-permute-start.17
  261.7 21.7 %collective-permute-start.16 = (bf16[1,2048]{1,0:T(2,128)(2,1)S(1)}, bf16[1,2048]{1,0:T(2,128)(2,1)S(1)}, u32[]{:S(2)}, u32[]{:S(2)}) collective-permute-start(bf16[1,2048]{1,0:T(2,128)(2,1)S(1)} %pad_maximum_fusion.1), channel_id=1, source_target_pairs={{8,0},{16,8},{24,16},{9,1},{17,9},{25,17}} | collective-permute-start | bytes 12296 | tf_op jit(solution)/shard_map/ppermute | solution.py:628
  283.5 1.1 copy-start.9
  284.6 1.2 copy-start.13
  285.8 1.1 copy-start.17
  286.9 1.1 copy-start.19
  287.9 1.1 copy-start.21
  295.7 18.1 %copy-start.10 = (s32[128,4096]{1,0:T(8,128)S(1)}, s32[128,4096]{1,0:T(8,128)}, u32[]{:S(2)}) copy-start(s32[128,4096]{1,0:T(8,128)} %refs_5_.1) | copy-start | bytes 6291460
  295.8 18.1 %copy-start.22 = (f32[4096]{0:T(1024)S(1)}, f32[4096]{0:T(1024)}, u32[]{:S(2)}) copy-start(f32[4096]{0:T(1024)} %param.16) | copy-start | bytes 49156
  295.8 18.1 %copy-start.23 = (f32[4096]{0:T(1024)S(1)}, f32[4096]{0:T(1024)}, u32[]{:S(2)}) copy-start(f32[4096]{0:T(1024)} %param.17) | copy-start | bytes 49156
  295.8 2.7 collective-permute-start.21
  299.7 9.4 %collective-permute-start.22 = (bf16[128,1024]{1,0:T(8,128)(2,1)}, bf16[128,1024]{1,0:T(8,128)(2,1)S(1)}, u32[]{:S(2)}, u32[]{:S(2)}) collective-permute-start(bf16[128,1024]{1,0:T(8,128)(2,1)} %get-tuple-element.87), channel_id=1, source_target_pairs={{0,2},{2,0},{4,6},{6,4},{8,10},{10,8},{12,14},{14,12},{16,18},{18,... | collective-permute-start | bytes 786440 | tf_op jit(solution)/shard_map/ppermute | solution.py:596
  299.7 14.2 %collective-permute-start.23 = (bf16[128,1024]{1,0:T(8,128)(2,1)}, bf16[128,1024]{1,0:T(8,128)(2,1)S(1)}, u32[]{:S(2)}, u32[]{:S(2)}) collective-permute-start(bf16[128,1024]{1,0:T(8,128)(2,1)} %get-tuple-element.88), channel_id=1, source_target_pairs={{0,4},{2,6},{4,0},{6,2},{8,12},{10,14},{12,8},{14,10},{16,20},{18,... | collective-permute-start | bytes 786440 | tf_op jit(solution)/shard_map/ppermute | solution.py:596
  299.7 14.2 %collective-permute-start.24 = (bf16[128,1024]{1,0:T(8,128)(2,1)S(1)}, bf16[128,1024]{1,0:T(8,128)(2,1)S(1)}, u32[]{:S(2)}, u32[]{:S(2)}) collective-permute-start(bf16[128,1024]{1,0:T(8,128)(2,1)S(1)} %get-tuple-element.89), channel_id=1, source_target_pairs={{0,6},{2,4},{4,2},{6,0},{8,14},{10,12},{12,10},{14,8},{16,22},{18,... | collective-permute-start | bytes 786440 | tf_op jit(solution)/shard_map/ppermute | solution.py:596
  313.9 1.2 copy-start.11

commit v3 on v2

--- a/solution.py
+++ b/solution.py
@@ -87,7 +87,7 @@
         ),
         out_shape=jax.ShapeDtypeStruct((peers, span_len, whole), carried.dtype),
         input_output_aliases={3 + len(pieces): 0} if extra else {},
-        compiler_params=pltpu.CompilerParams(vmem_limit_bytes=32 * MIB),
+        compiler_params=pltpu.CompilerParams(vmem_limit_bytes=10 * MIB),
         name="spread_queries",
     )(block_of_peer, slot_of_peer, carried, *pieces, *extra)
 
@@ -110,17 +110,43 @@
     )
 
 
-def attend_kernel(valid_ref, slot_ref, query_ref, key_ref, value_ref, *refs):
-    out_ref = refs[-1]
-    row_width = key_ref.shape[2]
+def attend_kernel(chunk, valid_ref, slot_ref, query_ref, key_ref, value_ref, *refs):
+    out_ref, key_held, value_held, sems = refs[-4:]
     span_len = query_ref.shape[1]
-    length = key_ref.shape[1]
+    _, length, row_width = key_held.shape
     heads = row_width // HEAD
     group = min(heads, 4)
     peer = pl.program_id(0)
+    peers = pl.num_programs(0)
+
+    def copies(at):
+        buffer = lax.rem(at, 2)
+        for kind, (ref, held) in enumerate(((key_ref, key_held), (value_ref, value_held))):
+            yield pltpu.make_async_copy(
+                ref.at[slot_ref[at], :, pl.ds(chunk * row_width, row_width)],
+                held.at[buffer],
+                sems.at[kind, buffer],
+            )
+
+    def fetch(at):
+        for copy in copies(at):
+            copy.start()
+
+    following = jnp.minimum(peer + 1, peers - 1)
+
+    @pl.when((peer == 0) & (valid_ref[0] > 0))
+    def _():
+        fetch(0)
+
+    @pl.when((peer + 1 < peers) & (valid_ref[following] > 0))
+    def _():
+        fetch(following)
 
     @pl.when(valid_ref[peer] > 0)
     def _():
+        for copy in copies(peer):
+            copy.wait()
+        buffer = lax.rem(peer, 2)
         lane = lax.broadcasted_iota(jnp.int32, (span_len, LANES), 1)
         stats = jnp.zeros((span_len, LANES), jnp.float32)
         ones = jnp.ones((length, HEAD), jnp.bfloat16)
@@ -130,7 +156,7 @@
             scores = [
                 lax.dot_general(
                     query_ref[0, :, cut],
-                    key_ref[0, :, cut],
+                    key_held[buffer, :, cut],
                     (((1,), (1,)), ((), ())),
                     preferred_element_type=jnp.float32,
                 )
@@ -144,7 +170,7 @@
             sums = [
                 jnp.dot(
                     weight,
-                    jnp.concatenate([value_ref[0, :, cut], ones], axis=1),
+                    jnp.concatenate([value_held[buffer, :, cut], ones], axis=1),
                     preferred_element_type=jnp.float32,
                 )
                 for weight, cut in zip(raised, cuts)
@@ -163,21 +189,26 @@
     wide = width + LANES
     extra = [] if shared is None else [shared]
     return pl.pallas_call(
-        attend_kernel,
+        functools.partial(attend_kernel, chunk),
         grid_spec=pltpu.PrefetchScalarGridSpec(
             num_scalar_prefetch=2,
             grid=(peers,),
             in_specs=[
                 pl.BlockSpec((1, span_len, size), lambda i, v, s: (i, 0, part)),
-                pl.BlockSpec((1, length, width), lambda i, v, s: (s[i], 0, chunk)),
-                pl.BlockSpec((1, length, width), lambda i, v, s: (s[i], 0, chunk)),
+                pl.BlockSpec(memory_space=pltpu.HBM),
+                pl.BlockSpec(memory_space=pltpu.HBM),
             ]
             + [pl.BlockSpec(memory_space=pl.ANY)] * len(extra),
             out_specs=pl.BlockSpec((1, span_len, wide), lambda i, v, s: (i, 0, place)),
+            scratch_shapes=[
+                pltpu.VMEM((2, length, width), keys.dtype),
+                pltpu.VMEM((2, length, width), keys.dtype),
+                pltpu.SemaphoreType.DMA((2, 2)),
+            ],
         ),
         out_shape=jax.ShapeDtypeStruct((peers, span_len, places * wide), asked.dtype),
         input_output_aliases={5: 0} if extra else {},
-        compiler_params=pltpu.CompilerParams(vmem_limit_bytes=56 * MIB),
+        compiler_params=pltpu.CompilerParams(vmem_limit_bytes=12 * MIB),
         cost_estimate=pl.CostEstimate(
             flops=4 * peers * heads * span_len * length * HEAD,
             bytes_accessed=2 * peers * width * (2 * span_len + 2 * length),
@@ -271,7 +302,7 @@
             out_specs=pl.BlockSpec((1, span_len, wide), lambda i, *_: (i, 0, 0)),
         ),
         out_shape=jax.ShapeDtypeStruct((blocks, span_len, wide), parts.dtype),
-        compiler_params=pltpu.CompilerParams(vmem_limit_bytes=32 * MIB),
+        compiler_params=pltpu.CompilerParams(vmem_limit_bytes=10 * MIB),
         name="merge_far",
     )(index, use, *([parts] * picked))
 
@@ -301,12 +332,12 @@
             scratch_shapes=[pltpu.VMEM((8, row_width), jnp.float32)],
         ),
         out_shape=jax.ShapeDtypeStruct((rows + ROW_TILE, row_width), parts.dtype),
-        compiler_params=pltpu.CompilerParams(vmem_limit_bytes=32 * MIB),
+        compiler_params=pltpu.CompilerParams(vmem_limit_bytes=10 * MIB),
         name="merge_all",
     )(index, use, *([parts] * picked), far)
 
 
-def project_kernel(count, place_ref, stay_ref, *refs):
+def project_kernel(count, shard_of, place_ref, stay_ref, *refs):
     sources, below_ref, weights = refs[:count], refs[count], refs[count + 1 : -7]
     keep_ref, send_ref, rows_ref, first_ref, held_ref, row_sems, weight_sems = refs[-7:]
     half = keep_ref.shape[0]
@@ -332,13 +363,22 @@
                 row_sems.at[at, 2],
             )
 
-    def weight_copy(shard):
-        return pltpu.make_async_copy(weights[shard], held_ref.at[shard], weight_sems.at[shard])
+    def weight_copies(shard):
+        at = 0
+        for piece, (ref, of) in enumerate(zip(weights, shard_of)):
+            if of == shard:
+                size = ref.shape[0]
+                yield pltpu.make_async_copy(
+                    ref, held_ref.at[shard, pl.ds(at, size)], weight_sems.at[piece]
+                )
+                at += size
 
     for copy in source_copies():
         copy.start()
-    for shard in range(len(weights)):
-        weight_copy(shard).start()
+    shards = held_ref.shape[0]
+    for shard in range(shards):
+        for copy in weight_copies(shard):
+            copy.start()
     for copy in source_copies():
         copy.wait()
     shape = (ROW_TILE, rows_ref.shape[1])
@@ -354,8 +394,9 @@
         rows_ref[end - ROW_TILE : end] = jnp.where(last, below, held).astype(rows_ref.dtype)
     stay = pl.multiple_of(stay_ref[0] * half, half)
     go = pl.multiple_of((1 - stay_ref[0]) * half, half)
-    for shard in range(len(weights)):
-        weight_copy(shard).wait()
+    for shard in range(shards):
+        for copy in weight_copies(shard):
+            copy.wait()
         for start, ref in ((go, send_ref), (stay, keep_ref)):
             ref[:, shard * tile : (shard + 1) * tile] = jnp.dot(
                 rows_ref[pl.ds(start, half)],
@@ -369,31 +410,33 @@
     row_width = below.shape[1]
     rows = PLANE * (height - ROW_TILE)
     shards = len(weights)
-    tile = weights[0].shape[1]
+    tile = weights[0][0].shape[1]
+    shard_of = [shard for shard, pieces in enumerate(weights) for _ in pieces]
+    pieces = [piece for pieces in weights for piece in pieces]
     columns = shards * tile
     half = rows // 2
     kind = sources[0].dtype
     return pl.pallas_call(
-        functools.partial(project_kernel, len(sources)),
+        functools.partial(project_kernel, len(sources), shard_of),
         grid_spec=pltpu.PrefetchScalarGridSpec(
             num_scalar_prefetch=2,
             grid=(1,),
-            in_specs=[pl.BlockSpec(memory_space=pl.ANY)] * len(sources)
+            in_specs=[pl.BlockSpec(memory_space=pltpu.HBM)] * len(sources)
             + [pl.BlockSpec((1, row_width), lambda i, *_: (0, 0))]
-            + [pl.BlockSpec(memory_space=pl.ANY)] * shards,
+            + [pl.BlockSpec(memory_space=pltpu.HBM)] * len(pieces),
             out_specs=[pl.BlockSpec((half, columns), lambda i, *_: (0, 0))] * 2,
             scratch_shapes=[
                 pltpu.VMEM((rows, row_width), kind),
                 pltpu.VMEM((PLANE * ROW_TILE, row_width), kind),
                 pltpu.VMEM((shards, row_width, tile), kind),
                 pltpu.SemaphoreType.DMA((len(sources), 3)),
-                pltpu.SemaphoreType.DMA((shards,)),
+                pltpu.SemaphoreType.DMA((len(pieces),)),
             ],
         ),
         out_shape=[jax.ShapeDtypeStruct((half, columns), kind)] * 2,
-        compiler_params=pltpu.CompilerParams(vmem_limit_bytes=30 * MIB),
+        compiler_params=pltpu.CompilerParams(vmem_limit_bytes=20 * MIB),
         name="project_rows",
-    )(place, stay, *sources, below, *weights)
+    )(place, stay, *sources, below, *pieces)
 
 
 def add_kernel(place_ref, keep_ref, other_ref, *outs):
@@ -418,7 +461,7 @@
             out_specs=[pl.BlockSpec((part, tile), lambda i, *_: (0, i))] * PLANE,
         ),
         out_shape=[jax.ShapeDtypeStruct((part, columns), keep.dtype)] * PLANE,
-        compiler_params=pltpu.CompilerParams(vmem_limit_bytes=32 * MIB),
+        compiler_params=pltpu.CompilerParams(vmem_limit_bytes=10 * MIB),
         name="add_cores",
     )(place, keep.reshape(folded), other.reshape(folded))
 
@@ -462,7 +505,7 @@
             scratch_shapes=[pltpu.VMEM((tile, columns), jnp.float32)],
         ),
         out_shape=[jax.ShapeDtypeStruct((rows, columns), residual.dtype)] * 2,
-        compiler_params=pltpu.CompilerParams(vmem_limit_bytes=32 * MIB),
+        compiler_params=pltpu.CompilerParams(vmem_limit_bytes=20 * MIB),
         name="add_norm",
     )(place, line, *branches, residual, drop_mask, gain[None], bias[None])
 
@@ -513,6 +556,9 @@
             x, "dp", split_axis=0, concat_axis=0, tiled=True, axis_index_groups=halves
         )
 
+    def swap(x, by):
+        return lax.ppermute(x, "dp", [(i, i ^ by) for i in range(peer_count)])
+
     def pinned(*values):
         return lax.optimization_barrier(values)
 
@@ -538,8 +584,9 @@
     far_table = to_partner(
         jnp.pad(jnp.concatenate([owners, slot_rows]), (0, LANES - 2 * requests))[None, :]
     )
-    far_first, far_carried, far_table, held_queries, _ = pinned(
-        far_first, far_carried, far_table, queries, near_out
+    (far_first,) = pinned(far_first)
+    far_first, far_carried, far_table, held_queries, weight, _ = pinned(
+        far_first, far_carried, far_table, queries, out_weight, near_out
     )
     far_owners = far_table[0, :requests]
     far_picked = pick_requests(
@@ -567,11 +614,12 @@
     near_tags = slots_of(near_asked)
     near_first = answer(near_asked, near_tags, 0, 0, width, 0, 2)
     near_second = answer(near_asked, near_tags, 1, 1, width, 1, 2)
-    far_asked, far_second, weight, near_first, near_second = pinned(
-        far_asked, far_second, out_weight, near_first, near_second
-    )
-
     middle = row_width // 2
+    near_swap = [swap(weight[:middle], PLANE)] if by_plane else []
+    far_asked, far_second, weight, near_first, near_second, *near_swap = pinned(
+        far_asked, far_second, weight, near_first, near_second, *near_swap
+    )
+
     mixed = spread([far_second], far_carried, *far_picked, span_len, 1, near_first)
     next_asked = exchange(mixed)
     far_asked, near_second, _ = pinned(far_asked, near_second, mixed)
@@ -590,32 +638,29 @@
     far_merged = merge_far(far_back, 0, wide, far_index, far_use, blocks)
     far_home = to_partner(far_merged)
     far_back = exchange(far_parts)
-    far_home, far_back, weight = pinned(far_home, far_back, weight)
-
-    def swap(x, by):
-        return lax.ppermute(x, "dp", [(i, i ^ by) for i in range(peer_count)])
+    if by_plane:
+        near_swap.append(swap(weight[middle:], PLANE))
+    far_home, far_back, *near_swap = pinned(far_home, far_back, *near_swap)
 
     def plane_rows(moved):
         return [moved] + [swap(moved, by) for by in range(1, PLANE)] if by_plane else [moved]
 
     far_merged = merge_far(far_back, 0, wide, far_index, far_use, blocks)
-    far_home, near_back, weight, _ = pinned(far_home, near_back, weight, far_merged)
+    far_home, near_back, _ = pinned(far_home, near_back, far_merged)
     next_home = to_partner(far_merged)
     sources = plane_rows(
         merge_all(near_back, 0, wide, near_index, near_use, blocks, far_home)
     )
-    near_swap = [swap(weight, PLANE)] if by_plane else []
+    far_swap = [swap(piece, PLANE) for piece in far_weight]
     count = len(sources)
-    next_home, next_back = pinned(next_home, next_back)
-    next_home, next_back, *held = pinned(next_home, next_back, *sources, *near_swap)
-    sources, near_swap = held[:count], held[count:]
+    (next_home,) = pinned(next_home)
+    next_home, next_back, *held = pinned(next_home, next_back, *sources, *far_swap)
+    sources, far_swap = held[:count], held[count:]
     moved = merge_all(next_back, 1, wide, near_index, near_use, blocks, next_home)
     if by_plane:
         place = lax.rem(here, PLANE).reshape(1)
         stay = lax.axis_index("tensor").astype(jnp.int32).reshape(1)
-        far_weight = jnp.concatenate(far_weight, axis=0)
-        far_weight, moved = pinned(far_weight, moved)
-        shards = [weight, *near_swap, far_weight, swap(far_weight, PLANE)]
+        shards = [[weight], near_swap, far_weight, far_swap]
         line = jnp.stack(
             [here // PLANE, (here ^ PLANE) // PLANE, partner // PLANE, (partner ^ PLANE) // PLANE]
         )

time: 320 us -> 348 us (1.087)
  local copies, waits for them, and re-layouts: 19.1 us -> 50.5 us
  waiting for transfers between devices: 167 us -> 193 us
  Pallas kernels: 59.8 us -> 37 us
  starting transfers between devices: 66.4 us -> 62.3 us
    ppermute x11 -> x13, waiting for transfers between devices: 10.6 us -> 78.9 us  [swap(): return lax.ppermute(x, 'dp', [(i, i ^ by) for i in range(peer_count)])]
    unnamed x52 -> x98, local copies, waits for them, and re-layouts: 17.3 us -> 47.6 us
    ppermute x7, waiting for transfers between devices: 123 us -> 95.7 us  [to_partner(): return lax.ppermute(x, 'dp', across)]
    pallas_call x5, Pallas kernels: 40.4 us -> 19.6 us  [the longest x4 13 us: attend(): pl.pallas_call(functools.partial(attend_kernel, chunk), grid_spec=pltpu.P...]
    ppermute x4, waiting for transfers between devices: 20.2 us -> 7.11 us  [local(): lax.ppermute(first_row, 'dp', [(i + PLANE, i + at) for i in range(0, peer...]
    ppermute x7, starting transfers between devices: 16.6 us -> 11.2 us  [to_partner(): return lax.ppermute(x, 'dp', across)]
    ppermute x11 -> x13, starting transfers between devices: 15.6 us -> 15.9 us  [swap(): return lax.ppermute(x, 'dp', [(i, i ^ by) for i in range(peer_count)])]
  transfers between devices with their start and end apart: 30 -> 32, of which waited for: 14 -> 20; matrix products, arithmetic and copies ran while one was open for 3% -> 2% of each run, Pallas kernels for 13% -> 5%
where the time goes in v3:
time: 348 us; the launch traced here: 346 us
  waiting for transfers between devices  193 us (55%)
  starting transfers between devices  62.3 us (18%)
  local copies, waits for them, and re-layouts  50.5 us (15%)
  Pallas kernels  37 us (11%)
    ppermute x7, waiting for transfers between devices, to_partner(): return lax.ppermute(x, 'dp', across)  95.7 us
    ppermute x13, waiting for transfers between devices, swap(): return lax.ppermute(x, 'dp', [(i, i ^ by) for i in range(peer_count)])  78.9 us
    unnamed x98, local copies, waits for them, and re-layouts  47.6 us
    all_to_all x5, starting transfers between devices, exchange(): lax.all_to_all(x, 'dp', split_axis=0, concat_axis=0, tiled=True, axis_ind...  23.6 us
    ppermute x13, starting transfers between devices, swap(): return lax.ppermute(x, 'dp', [(i, i ^ by) for i in range(peer_count)])  15.9 us
    pallas_call x4, Pallas kernels, attend(): pl.pallas_call(functools.partial(attend_kernel, chunk), grid_spec=pltpu.P...  13 us
    ppermute x7, starting transfers between devices, to_partner(): return lax.ppermute(x, 'dp', across)  11.2 us
    ppermute x4, waiting for transfers between devices, local(): lax.ppermute(first_row, 'dp', [(i + PLANE, i + at) for i in range(0, peer...  7.11 us
  transfers between devices with their start and end apart: 32, of which 20 were waited for; matrix products, arithmetic and copies ran while one was open for 2% of the time, Pallas kernels for 5%

profile of v3, /device:TPU:0, one launch (start us, length us, event | category | flops | bytes accessed | tf_op | source)
XLA Modules:
  0.0 345.7 jit_solution(16741041335747223952)
XLA Ops:
  1.4 4.8 %collective-permute-start.3 = (bf16[1,2048]{1,0:T(2,128)(2,1)S(1)}, bf16[1,2048]{1,0:T(2,128)(2,1)S(1)}, u32[]{:S(2)}, u32[]{:S(2)}) collective-permute-start(bf16[1,2048]{1,0:T(2,128)(2,1)S(1)} %slice.41), channel_id=1, source_target_pairs={{0,2},{2,4},{4,6},{6,8},{8,10},{10,12},{12,14},{14,16},{16,18},{18... | collective-permute-start | bytes 12296 | tf_op jit(solution)/shard_map/ppermute | solution.py:23
  8.2 1.2 copy-done.22
  9.4 1.2 spread_queries.3
  10.6 1.4 copy-done.19
  11.9 5.1 %all-to-all-start.1 = ((bf16[8,64,2176]{2,1,0:T(8,128)(2,1)}), bf16[8,64,2176]{2,1,0:T(8,128)(2,1)S(1)}, u32[]{:S(2)}, u32[]{:S(2)}) async-start(bf16[8,64,2176]{2,1,0:T(8,128)(2,1)} %copy-done.19), calls=%async_computation.1 | async-start | bytes 4456448 | tf_op jit(solution)/shard_map/all_to_all | solution.py:555
  17.1 3.3 collective-permute-start
  20.4 3.3 collective-permute-start.1
  23.8 2.9 collective-permute-start.2
  26.7 25.4 %collective-permute-done.refs_0_ = bf16[256,1024]{1,0:T(8,128)(2,1)S(1)} collective-permute-done((bf16[256,1024]{1,0:T(8,128)(2,1)S(1)}, bf16[256,1024]{1,0:T(8,128)(2,1)S(1)}, u32[]{:S(2)}, u32[]{:S(2)}) %collective-permute-start) | collective-permute-done | bytes 524320 | tf_op jit(solution)/shard_map/ppermute | solution.py:566
  52.2 4.0 %collective-permute-done.1.carried_ref = bf16[1,2048]{1,0:T(2,128)(2,1)S(1)} collective-permute-done((bf16[1,2048]{1,0:T(2,128)(2,1)S(1)}, bf16[1,2048]{1,0:T(2,128)(2,1)S(1)}, u32[]{:S(2)}, u32[]{:S(2)}) %collective-permute-start.1) | collective-permute-done | bytes 4128 | tf_op jit(solution)/shard_map/ppermute | solution.py:580
  58.5 5.2 %all-to-all-start = ((bf16[8,64,1152]{2,1,0:T(8,128)(2,1)}), bf16[8,64,1152]{2,1,0:T(8,128)(2,1)}, u32[]{:S(2)}, u32[]{:S(2)}) async-start(bf16[8,64,1152]{2,1,0:T(8,128)(2,1)} %copy-done.21), calls=%async_computation | async-start | bytes 2359296 | tf_op jit(solution)/shard_map/all_to_all | solution.py:555
  65.7 3.0 collective-permute-start.5
  69.1 2.2 copy-done
  71.3 2.2 copy-done.3
  73.5 1.6 copy-done.14
  77.8 1.4 copy-done.9
  79.3 9.8 %collective-permute-done.4.refs_0_ = bf16[256,1024]{1,0:T(8,128)(2,1)S(1)} collective-permute-done((bf16[256,1024]{1,0:T(8,128)(2,1)S(1)}, bf16[256,1024]{1,0:T(8,128)(2,1)S(1)}, u32[]{:S(2)}, u32[]{:S(2)}) %collective-permute-start.4) | collective-permute-done | bytes 524320 | tf_op jit(solution)/shard_map/ppermute | solution.py:566
  89.9 9.2 %collective-permute-done.5.refs_10_ = bf16[1024,256]{1,0:T(8,128)(2,1)S(1)} collective-permute-done((bf16[1024,256]{1,0:T(8,128)(2,1)S(1)}, bf16[1024,256]{1,0:T(8,128)(2,1)S(1)}, u32[]{:S(2)}, u32[]{:S(2)}) %collective-permute-start.5) | collective-permute-done | bytes 524320 | tf_op jit(solution)/shard_map/ppermute | solution.py:560
  102.1 1.4 copy-done.12
  103.5 4.2 %all-to-all-start.2 = ((bf16[8,64,2304]{2,1,0:T(8,128)(2,1)}), bf16[8,64,2304]{2,1,0:T(8,128)(2,1)S(1)}, u32[]{:S(2)}, u32[]{:S(2)}) async-start(bf16[8,64,2304]{2,1,0:T(8,128)(2,1)} %copy-done.12), calls=%async_computation.2 | async-start | bytes 4718592 | tf_op jit(solution)/shard_map/all_to_all | solution.py:555
  107.7 2.1 collective-permute-start.6
  111.0 2.2 copy-done.1
  113.1 2.2 copy-done.4
  115.3 1.7 copy-done.10
  117.0 6.7 %attend_blocks.6 = bf16[8,64,2304]{2,1,0:T(8,128)(2,1)S(1)} custom-call(s32[8]{0:T(128)S(1)} %get-tuple-element.91.valid_ref, s32[8]{0:T(128)S(1)} %get-tuple-element.90.slot_ref, bf16[8,64,1152]{2,1,0:T(8,128)(2,1)} %all-to-all-done.query_ref, bf16[8,128,2048]{2,1,0:T(8,128)(2,1)S(1)} %copy-done.1, ...), custom_call_target="tpu_custom_call", output_to_operand_aliasing={{}: (5, {})} | custom-call | flops 268435456 | bytes 6291456 | tf_op jit(solution)/shard_map/attend_blocks/pallas_call | solution.py:191
  123.7 1.4 copy-done.11
  125.1 17.2 %collective-permute-done.6.refs_12_ = bf16[1024,256]{1,0:T(8,128)(2,1)} collective-permute-done((bf16[1024,256]{1,0:T(8,128)(2,1)S(1)}, bf16[1024,256]{1,0:T(8,128)(2,1)}, u32[]{:S(2)}, u32[]{:S(2)}) %collective-permute-start.6) | collective-permute-done | bytes 524320 | tf_op jit(solution)/shard_map/ppermute | solution.py:566
  142.3 2.1 all-to-all-done.2.query_ref.refs_0_.refs_1_
  144.5 1.4 copy-done.6
  145.9 5.1 %all-to-all-start.3 = ((bf16[8,64,2304]{2,1,0:T(8,128)(2,1)}), bf16[8,64,2304]{2,1,0:T(8,128)(2,1)S(1)}, u32[]{:S(2)}, u32[]{:S(2)}) async-start(bf16[8,64,2304]{2,1,0:T(8,128)(2,1)} %copy-done.11), calls=%async_computation.3 | async-start | bytes 4718592 | tf_op jit(solution)/shard_map/all_to_all | solution.py:555
  151.6 2.2 copy-done.2
  153.8 2.2 copy-done.5
  156.0 1.7 copy-done.7
  157.6 4.1 %attend_blocks.7 = bf16[8,64,1152]{2,1,0:T(8,128)(2,1)S(1)} custom-call(s32[8]{0:T(128)S(1)} %get-tuple-element.91.valid_ref, s32[8]{0:T(128)S(1)} %get-tuple-element.90.slot_ref, bf16[8,64,2304]{2,1,0:T(8,128)(2,1)S(1)} %copy-done.7, bf16[8,128,2048]{2,1,0:T(8,128)(2,1)S(1)} %copy-done.2, bf16[8,128,2048]{2,1,0:T(8,128)(2,1)S(1)} %copy-done.5), custom_call_target="tpu_custom_call" | custom-call | flops 268435456 | bytes 6291456 | tf_op jit(solution)/shard_map/attend_blocks/pallas_call | solution.py:191
  162.8 22.9 %collective-permute-done.7.refs_13_ = bf16[1024,256]{1,0:T(8,128)(2,1)} collective-permute-done((bf16[1024,256]{1,0:T(8,128)(2,1)S(1)}, bf16[1024,256]{1,0:T(8,128)(2,1)}, u32[]{:S(2)}, u32[]{:S(2)}) %collective-permute-start.7) | collective-permute-done | bytes 524320 | tf_op jit(solution)/shard_map/ppermute | solution.py:566
  185.7 2.1 all-to-all-done.3.refs_0_.refs_1_
  187.8 3.9 %all-to-all-start.4 = ((bf16[8,64,1152]{2,1,0:T(8,128)(2,1)}), bf16[8,64,1152]{2,1,0:T(8,128)(2,1)S(1)}, u32[]{:S(2)}, u32[]{:S(2)}) async-start(bf16[8,64,1152]{2,1,0:T(8,128)(2,1)} %copy-done.20), calls=%async_computation.4 | async-start | bytes 2359296 | tf_op jit(solution)/shard_map/all_to_all | solution.py:555
  191.8 2.1 merge_far.2
  193.9 1.4 collective-permute-start.8
  195.3 2.1 collective-permute-start.9
  197.3 32.4 %collective-permute-done.9.refs_11_ = bf16[1024,256]{1,0:T(8,128)(2,1)S(1)} collective-permute-done((bf16[1024,256]{1,0:T(8,128)(2,1)S(1)}, bf16[1024,256]{1,0:T(8,128)(2,1)S(1)}, u32[]{:S(2)}, u32[]{:S(2)}) %collective-permute-start.9) | collective-permute-done | bytes 524320 | tf_op jit(solution)/shard_map/ppermute | solution.py:560
  231.4 1.9 merge_far.3
  233.5 2.4 merge_all.2.refs_0_
  235.9 1.6 collective-permute-start.11
  237.5 1.7 collective-permute-start.12
  239.7 20.3 %collective-permute-done.10.refs_2_ = bf16[4,64,1152]{2,1,0:T(8,128)(2,1)S(1)} collective-permute-done((bf16[4,64,1152]{2,1,0:T(8,128)(2,1)S(1)}, bf16[4,64,1152]{2,1,0:T(8,128)(2,1)S(1)}, u32[]{:S(2)}, u32[]{:S(2)}) %collective-permute-start.10) | collective-permute-done | bytes 589856 | tf_op jit(solution)/shard_map/ppermute | solution.py:566
  260.0 3.0 collective-permute-done.14.refs_14_
  263.8 10.4 %collective-permute-done.15.refs_15_ = bf16[1024,256]{1,0:T(8,128)(2,1)S(1)} collective-permute-done((bf16[1024,256]{1,0:T(8,128)(2,1)}, bf16[1024,256]{1,0:T(8,128)(2,1)S(1)}, u32[]{:S(2)}, u32[]{:S(2)}) %collective-permute-start.15) | collective-permute-done | bytes 524320 | tf_op jit(solution)/shard_map/ppermute | solution.py:560
  276.6 3.2 merge_all.3.refs_4_
  279.8 1.4 collective-permute-start.16
  281.2 1.5 collective-permute-start.17
  285.4 1.3 collective-permute-start.19
  287.6 7.1 %collective-permute-done.19 = bf16[1,2048]{1,0:T(2,128)(2,1)S(1)} collective-permute-done((bf16[1,2048]{1,0:T(2,128)(2,1)S(1)}, bf16[1,2048]{1,0:T(2,128)(2,1)S(1)}, u32[]{:S(2)}, u32[]{:S(2)}) %collective-permute-start.19) | collective-permute-done | bytes 4128 | tf_op jit(solution)/shard_map/ppermute | solution.py:673
  295.6 11.4 %collective-permute-done.17.refs_6_ = bf16[272,1024]{1,0:T(8,128)(2,1)S(1)} collective-permute-done((bf16[272,1024]{1,0:T(8,128)(2,1)}, bf16[272,1024]{1,0:T(8,128)(2,1)S(1)}, u32[]{:S(2)}, u32[]{:S(2)}) %collective-permute-start.17) | collective-permute-done | bytes 557088 | tf_op jit(solution)/shard_map/ppermute | solution.py:560
  315.3 6.6 %project_rows.1 = (bf16[512,1024]{1,0:T(8,128)(2,1)S(1)}, bf16[512,1024]{1,0:T(8,128)(2,1)S(1)}) custom-call(s32[1]{0:T(128)} %bitcast.place_ref, s32[1]{0:T(128)} %bitcast.5.stay_ref, bf16[272,1024]{1,0:T(8,128)(2,1)S(1)} %copy-done.25, bf16[272,1024]{1,0:T(8,128)(2,1)S(1)} %copy-done.31, bf16[272,1024]{1,0:T(8,128)(2,1)S(1)} %copy-done.33, ...), custom_call_target="tpu_custom_call" | custom-call | tf_op jit(solution)/shard_map/project_rows/pallas_call | solution.py:419
  322.1 2.6 collective-permute-done.23
  324.7 1.2 add_cores.1
  325.9 1.2 collective-permute-start.24
  328.0 1.4 collective-permute-start.26
  329.4 5.8 %collective-permute-done.24.refs_1_ = bf16[128,1024]{1,0:T(8,128)(2,1)S(1)} collective-permute-done((bf16[128,1024]{1,0:T(8,128)(2,1)}, bf16[128,1024]{1,0:T(8,128)(2,1)S(1)}, u32[]{:S(2)}, u32[]{:S(2)}) %collective-permute-start.24) | collective-permute-done | bytes 262176 | tf_op jit(solution)/shard_map/ppermute | solution.py:560
  335.2 4.3 %collective-permute-done.25.refs_2_ = bf16[128,1024]{1,0:T(8,128)(2,1)S(1)} collective-permute-done((bf16[128,1024]{1,0:T(8,128)(2,1)}, bf16[128,1024]{1,0:T(8,128)(2,1)S(1)}, u32[]{:S(2)}, u32[]{:S(2)}) %collective-permute-start.25) | collective-permute-done | bytes 262176 | tf_op jit(solution)/shard_map/ppermute | solution.py:560
  339.5 1.6 collective-permute-done.26.refs_3_
  341.2 1.2 copy-done.27
  342.4 3.3 add_norm.1
  (139 shorter events, 36.3 us)
Async XLA Ops:
  1.4 6.8 %collective-permute-start.3 = (bf16[1,2048]{1,0:T(2,128)(2,1)S(1)}, bf16[1,2048]{1,0:T(2,128)(2,1)S(1)}, u32[]{:S(2)}, u32[]{:S(2)}) collective-permute-start(bf16[1,2048]{1,0:T(2,128)(2,1)S(1)} %slice.41), channel_id=1, source_target_pairs={{0,2},{2,4},{4,6},{6,8},{8,10},{10,12},{12,14},{14,16},{16,18},{18... | collective-permute-start | bytes 12296 | tf_op jit(solution)/shard_map/ppermute | solution.py:23
  8.2 1.2 copy-start.22
  10.6 1.4 copy-start.19
  11.9 5.1 %copy-start.23 = (bf16[256,2048]{1,0:T(8,128)(2,1)S(1)}, bf16[256,2048]{1,0:T(8,128)(2,1)}, u32[]{:S(2)}) copy-start(bf16[256,2048]{1,0:T(8,128)(2,1)} %refs_0_.1) | copy-start | bytes 3145732
  11.9 46.6 %all-to-all-start.1 = ((bf16[8,64,2176]{2,1,0:T(8,128)(2,1)}), bf16[8,64,2176]{2,1,0:T(8,128)(2,1)S(1)}, u32[]{:S(2)}, u32[]{:S(2)}) async-start(bf16[8,64,2176]{2,1,0:T(8,128)(2,1)} %copy-done.19), calls=%async_computation.1 | async-start | bytes 4456448 | tf_op jit(solution)/shard_map/all_to_all | solution.py:555
  17.1 35.0 %collective-permute-start = (bf16[256,1024]{1,0:T(8,128)(2,1)S(1)}, bf16[256,1024]{1,0:T(8,128)(2,1)S(1)}, u32[]{:S(2)}, u32[]{:S(2)}) collective-permute-start(bf16[256,1024]{1,0:T(8,128)(2,1)S(1)} %slice.40), channel_id=1, source_target_pairs={{0,16},{2,18},{4,20},{6,22},{8,24},{10,26},{12,28},{14,30},{16,0},... | collective-permute-start | bytes 1572872 | tf_op jit(solution)/shard_map/ppermute | solution.py:566
  20.4 35.7 %collective-permute-start.1 = (bf16[1,2048]{1,0:T(2,128)(2,1)S(1)}, bf16[1,2048]{1,0:T(2,128)(2,1)S(1)}, u32[]{:S(2)}, u32[]{:S(2)}) collective-permute-start(bf16[1,2048]{1,0:T(2,128)(2,1)S(1)} %slice.41), channel_id=1, source_target_pairs={{0,18},{2,20},{4,22},{6,24},{8,26},{10,28},{12,30},{14,0},{16,2},{... | collective-permute-start | bytes 12296 | tf_op jit(solution)/shard_map/ppermute | solution.py:580
  23.8 28.4 %collective-permute-start.2 = (s32[1,128]{1,0:T(1,128)S(1)}, s32[1,128]{1,0:T(1,128)S(1)}, u32[]{:S(2)}, u32[]{:S(2)}) collective-permute-start(s32[1,128]{1,0:T(1,128)S(1)} %pad_bitcast_fusion), channel_id=1, source_target_pairs={{0,16},{2,18},{4,20},{6,22},{8,24},{10,26},{12,28},{14,30},{16,0},... | collective-permute-start | bytes 1544 | tf_op jit(solution)/shard_map/ppermute | solution.py:566
  56.4 9.2 %copy-start.16 = (bf16[2048,256]{1,0:T(8,128)(2,1)S(1)}, bf16[2048,256]{1,0:T(8,128)(2,1)}, u32[]{:S(2)}) copy-start(bf16[2048,256]{1,0:T(8,128)(2,1)} %refs_9_) | copy-start | bytes 3145732
  58.5 10.2 %copy-start.13 = (bf16[8,64,2176]{2,1,0:T(8,128)(2,1)}, bf16[8,64,2176]{2,1,0:T(8,128)(2,1)S(1)}, u32[]{:S(2)}) copy-start(bf16[8,64,2176]{2,1,0:T(8,128)(2,1)S(1)} %all-to-all-done.1.query_ref) | copy-start | bytes 6684676
  58.5 41.4 %all-to-all-start = ((bf16[8,64,1152]{2,1,0:T(8,128)(2,1)}), bf16[8,64,1152]{2,1,0:T(8,128)(2,1)}, u32[]{:S(2)}, u32[]{:S(2)}) async-start(bf16[8,64,1152]{2,1,0:T(8,128)(2,1)} %copy-done.21), calls=%async_computation | async-start | bytes 2359296 | tf_op jit(solution)/shard_map/all_to_all | solution.py:555
  64.8 24.2 %collective-permute-start.4 = (bf16[256,1024]{1,0:T(8,128)(2,1)S(1)}, bf16[256,1024]{1,0:T(8,128)(2,1)S(1)}, u32[]{:S(2)}, u32[]{:S(2)}) collective-permute-start(bf16[256,1024]{1,0:T(8,128)(2,1)S(1)} %slice.44), channel_id=1, source_target_pairs={{0,16},{2,18},{4,20},{6,22},{8,24},{10,26},{12,28},{14,30},{16,0},... | collective-permute-start | bytes 1572872 | tf_op jit(solution)/shard_map/ppermute | solution.py:566
  65.7 33.4 %collective-permute-start.5 = (bf16[1024,256]{1,0:T(8,128)(2,1)S(1)}, bf16[1024,256]{1,0:T(8,128)(2,1)S(1)}, u32[]{:S(2)}, u32[]{:S(2)}) collective-permute-start(bf16[1024,256]{1,0:T(8,128)(2,1)S(1)} %slice.46), channel_id=1, source_target_pairs={{0,8},{2,10},{4,12},{6,14},{8,0},{10,2},{12,4},{14,6},{16,24},{18,... | collective-permute-start | bytes 1572872 | tf_op jit(solution)/shard_map/ppermute | solution.py:560
  69.1 2.2 copy-start
  71.3 2.2 copy-start.3
  73.5 1.6 copy-start.14
  75.1 1.6 copy-start.15
  77.8 1.4 copy-start.9
  102.1 1.4 copy-start.12
  103.5 41.0 %all-to-all-start.2 = ((bf16[8,64,2304]{2,1,0:T(8,128)(2,1)}), bf16[8,64,2304]{2,1,0:T(8,128)(2,1)S(1)}, u32[]{:S(2)}, u32[]{:S(2)}) async-start(bf16[8,64,2304]{2,1,0:T(8,128)(2,1)} %copy-done.12), calls=%async_computation.2 | async-start | bytes 4718592 | tf_op jit(solution)/shard_map/all_to_all | solution.py:555
  107.7 34.6 %collective-permute-start.6 = (bf16[1024,256]{1,0:T(8,128)(2,1)S(1)}, bf16[1024,256]{1,0:T(8,128)(2,1)}, u32[]{:S(2)}, u32[]{:S(2)}) collective-permute-start(bf16[1024,256]{1,0:T(8,128)(2,1)S(1)} %slice.48), channel_id=1, source_target_pairs={{0,16},{2,18},{4,20},{6,22},{8,24},{10,26},{12,28},{14,30},{16,0},... | collective-permute-start | bytes 1572872 | tf_op jit(solution)/shard_map/ppermute | solution.py:566
  110.9 2.2 copy-start.1
  113.1 2.2 copy-start.4
  115.3 1.7 copy-start.10
  123.7 1.4 copy-start.11
  144.5 1.4 copy-start.6
  145.9 42.0 %all-to-all-start.3 = ((bf16[8,64,2304]{2,1,0:T(8,128)(2,1)}), bf16[8,64,2304]{2,1,0:T(8,128)(2,1)S(1)}, u32[]{:S(2)}, u32[]{:S(2)}) async-start(bf16[8,64,2304]{2,1,0:T(8,128)(2,1)} %copy-done.11), calls=%async_computation.3 | async-start | bytes 4718592 | tf_op jit(solution)/shard_map/all_to_all | solution.py:555
  151.0 34.7 %collective-permute-start.7 = (bf16[1024,256]{1,0:T(8,128)(2,1)S(1)}, bf16[1024,256]{1,0:T(8,128)(2,1)}, u32[]{:S(2)}, u32[]{:S(2)}) collective-permute-start(bf16[1024,256]{1,0:T(8,128)(2,1)S(1)} %slice.49), channel_id=1, source_target_pairs={{0,16},{2,18},{4,20},{6,22},{8,24},{10,26},{12,28},{14,30},{16,0},... | collective-permute-start | bytes 1572872 | tf_op jit(solution)/shard_map/ppermute | solution.py:566
  151.6 2.2 copy-start.2
  153.8 2.2 copy-start.5
  156.0 1.7 copy-start.7
  187.8 43.5 %all-to-all-start.4 = ((bf16[8,64,1152]{2,1,0:T(8,128)(2,1)}), bf16[8,64,1152]{2,1,0:T(8,128)(2,1)S(1)}, u32[]{:S(2)}, u32[]{:S(2)}) async-start(bf16[8,64,1152]{2,1,0:T(8,128)(2,1)} %copy-done.20), calls=%async_computation.4 | async-start | bytes 2359296 | tf_op jit(solution)/shard_map/all_to_all | solution.py:555
  191.8 3.5 %copy-start.17 = (bf16[2048,256]{1,0:T(8,128)(2,1)S(1)}, bf16[2048,256]{1,0:T(8,128)(2,1)}, u32[]{:S(2)}) copy-start(bf16[2048,256]{1,0:T(8,128)(2,1)} %refs_9_) | copy-start | bytes 3145732
  193.9 36.7 %collective-permute-start.8 = (bf16[4,64,1152]{2,1,0:T(8,128)(2,1)S(1)}, bf16[4,64,1152]{2,1,0:T(8,128)(2,1)S(1)}, u32[]{:S(2)}, u32[]{:S(2)}) collective-permute-start(bf16[4,64,1152]{2,1,0:T(8,128)(2,1)S(1)} %merge_far.2), channel_id=1, source_target_pairs={{0,16},{2,18},{4,20},{6,22},{8,24},{10,26},{12,28},{14,30},{16,0},... | collective-permute-start | bytes 1769480 | tf_op jit(solution)/shard_map/ppermute | solution.py:566
  195.3 34.5 %collective-permute-start.9 = (bf16[1024,256]{1,0:T(8,128)(2,1)S(1)}, bf16[1024,256]{1,0:T(8,128)(2,1)S(1)}, u32[]{:S(2)}, u32[]{:S(2)}) collective-permute-start(bf16[1024,256]{1,0:T(8,128)(2,1)S(1)} %slice.50), channel_id=1, source_target_pairs={{0,8},{2,10},{4,12},{6,14},{8,0},{10,2},{12,4},{14,6},{16,24},{18,... | collective-permute-start | bytes 1572872 | tf_op jit(solution)/shard_map/ppermute | solution.py:560
  231.4 2.1 copy-start.8
  231.4 2.1 copy-start.29
  233.3 26.7 %collective-permute-start.10 = (bf16[4,64,1152]{2,1,0:T(8,128)(2,1)S(1)}, bf16[4,64,1152]{2,1,0:T(8,128)(2,1)S(1)}, u32[]{:S(2)}, u32[]{:S(2)}) collective-permute-start(bf16[4,64,1152]{2,1,0:T(8,128)(2,1)S(1)} %merge_far.3), channel_id=1, source_target_pairs={{0,16},{2,18},{4,20},{6,22},{8,24},{10,26},{12,28},{14,30},{16,0},... | collective-permute-start | bytes 1769480 | tf_op jit(solution)/shard_map/ppermute | solution.py:566
  235.8 48.2 %copy-start.24 = (bf16[272,1024]{1,0:T(8,128)(2,1)}, bf16[272,1024]{1,0:T(8,128)(2,1)S(1)}, u32[]{:S(2)}) copy-start(bf16[272,1024]{1,0:T(8,128)(2,1)S(1)} %merge_all.2.refs_0_) | copy-start | bytes 1671172
  235.9 71.1 %copy-start.18 = (bf16[2048,256]{1,0:T(8,128)(2,1)S(1)}, bf16[2048,256]{1,0:T(8,128)(2,1)}, u32[]{:S(2)}) copy-start(bf16[2048,256]{1,0:T(8,128)(2,1)} %refs_9_) | copy-start | bytes 3145732
  235.9 39.1 %collective-permute-start.11 = (bf16[272,1024]{1,0:T(8,128)(2,1)S(1)}, bf16[272,1024]{1,0:T(8,128)(2,1)S(1)}, u32[]{:S(2)}, u32[]{:S(2)}) collective-permute-start(bf16[272,1024]{1,0:T(8,128)(2,1)S(1)} %merge_all.2.refs_0_), channel_id=1, source_target_pairs={{0,2},{2,0},{4,6},{6,4},{8,10},{10,8},{12,14},{14,12},{16,18},{18,... | collective-permute-start | bytes 1671176 | tf_op jit(solution)/shard_map/ppermute | solution.py:560
  237.5 37.5 %collective-permute-start.12 = (bf16[272,1024]{1,0:T(8,128)(2,1)S(1)}, bf16[272,1024]{1,0:T(8,128)(2,1)S(1)}, u32[]{:S(2)}, u32[]{:S(2)}) collective-permute-start(bf16[272,1024]{1,0:T(8,128)(2,1)S(1)} %merge_all.2.refs_0_), channel_id=1, source_target_pairs={{0,4},{2,6},{4,0},{6,2},{8,12},{10,14},{12,8},{14,10},{16,20},{18,... | collective-permute-start | bytes 1671176 | tf_op jit(solution)/shard_map/ppermute | solution.py:560
  239.2 36.6 %collective-permute-start.13 = (bf16[272,1024]{1,0:T(8,128)(2,1)S(1)}, bf16[272,1024]{1,0:T(8,128)(2,1)S(1)}, u32[]{:S(2)}, u32[]{:S(2)}) collective-permute-start(bf16[272,1024]{1,0:T(8,128)(2,1)S(1)} %merge_all.2.refs_0_), channel_id=1, source_target_pairs={{0,6},{2,4},{4,2},{6,0},{8,14},{10,12},{12,10},{14,8},{16,22},{18,... | collective-permute-start | bytes 1671176 | tf_op jit(solution)/shard_map/ppermute | solution.py:560
  239.4 23.6 %collective-permute-start.14 = (bf16[1024,256]{1,0:T(8,128)(2,1)}, bf16[1024,256]{1,0:T(8,128)(2,1)S(1)}, u32[]{:S(2)}, u32[]{:S(2)}) collective-permute-start(bf16[1024,256]{1,0:T(8,128)(2,1)} %collective-permute-done.6.refs_12_), channel_id=1, source_target_pairs={{0,8},{2,10},{4,12},{6,14},{8,0},{10,2},{12,4},{14,6},{16,24},{18,... | collective-permute-start | bytes 1572872 | tf_op jit(solution)/shard_map/ppermute | solution.py:560
  260.0 14.1 %collective-permute-start.15 = (bf16[1024,256]{1,0:T(8,128)(2,1)}, bf16[1024,256]{1,0:T(8,128)(2,1)S(1)}, u32[]{:S(2)}, u32[]{:S(2)}) collective-permute-start(bf16[1024,256]{1,0:T(8,128)(2,1)} %collective-permute-done.7.refs_13_), channel_id=1, source_target_pairs={{0,8},{2,10},{4,12},{6,14},{8,0},{10,2},{12,4},{14,6},{16,24},{18,... | collective-permute-start | bytes 1572872 | tf_op jit(solution)/shard_map/ppermute | solution.py:560
  275.0 4.8 %copy-start.30 = (bf16[272,1024]{1,0:T(8,128)(2,1)}, bf16[272,1024]{1,0:T(8,128)(2,1)S(1)}, u32[]{:S(2)}) copy-start(bf16[272,1024]{1,0:T(8,128)(2,1)S(1)} %collective-permute-done.11.refs_1_) | copy-start | bytes 1671172
  279.8 15.8 %collective-permute-start.16 = (bf16[272,1024]{1,0:T(8,128)(2,1)}, bf16[272,1024]{1,0:T(8,128)(2,1)S(1)}, u32[]{:S(2)}, u32[]{:S(2)}) collective-permute-start(bf16[272,1024]{1,0:T(8,128)(2,1)} %merge_all.3.refs_4_), channel_id=1, source_target_pairs={{0,2},{2,0},{4,6},{6,4},{8,10},{10,8},{12,14},{14,12},{16,18},{18,... | collective-permute-start | bytes 1671176 | tf_op jit(solution)/shard_map/ppermute | solution.py:560
  281.2 25.7 %collective-permute-start.17 = (bf16[272,1024]{1,0:T(8,128)(2,1)}, bf16[272,1024]{1,0:T(8,128)(2,1)S(1)}, u32[]{:S(2)}, u32[]{:S(2)}) collective-permute-start(bf16[272,1024]{1,0:T(8,128)(2,1)} %merge_all.3.refs_4_), channel_id=1, source_target_pairs={{0,4},{2,6},{4,0},{6,2},{8,12},{10,14},{12,8},{14,10},{16,20},{18,... | collective-permute-start | bytes 1671176 | tf_op jit(solution)/shard_map/ppermute | solution.py:560
  282.7 24.2 %collective-permute-start.18 = (bf16[272,1024]{1,0:T(8,128)(2,1)}, bf16[272,1024]{1,0:T(8,128)(2,1)S(1)}, u32[]{:S(2)}, u32[]{:S(2)}) collective-permute-start(bf16[272,1024]{1,0:T(8,128)(2,1)} %merge_all.3.refs_4_), channel_id=1, source_target_pairs={{0,6},{2,4},{4,2},{6,0},{8,14},{10,12},{12,10},{14,8},{16,22},{18,... | collective-permute-start | bytes 1671176 | tf_op jit(solution)/shard_map/ppermute | solution.py:560
  284.1 1.3 collective-permute-start.22
  284.7 2.0 collective-permute-start.21
  285.4 9.3 %collective-permute-start.19 = (bf16[1,2048]{1,0:T(2,128)(2,1)S(1)}, bf16[1,2048]{1,0:T(2,128)(2,1)S(1)}, u32[]{:S(2)}, u32[]{:S(2)}) collective-permute-start(bf16[1,2048]{1,0:T(2,128)(2,1)S(1)} %pad_maximum_fusion), channel_id=1, source_target_pairs={{8,0},{16,8},{24,16},{9,1},{17,9},{25,17}} | collective-permute-start | bytes 12296 | tf_op jit(solution)/shard_map/ppermute | solution.py:673
  286.7 8.0 %collective-permute-start.20 = (bf16[1,2048]{1,0:T(2,128)(2,1)S(1)}, bf16[1,2048]{1,0:T(2,128)(2,1)S(1)}, u32[]{:S(2)}, u32[]{:S(2)}) collective-permute-start(bf16[1,2048]{1,0:T(2,128)(2,1)S(1)} %pad_maximum_fusion), channel_id=1, source_target_pairs={{8,2},{16,10},{24,18},{9,3},{17,11},{25,19}} | collective-permute-start | bytes 12296 | tf_op jit(solution)/shard_map/ppermute | solution.py:673
  306.9 1.1 copy-start.25
  308.0 1.1 copy-start.31
  309.0 1.1 copy-start.33
  322.0 19.2 %copy-start.26 = (s32[128,4096]{1,0:T(8,128)S(1)}, s32[128,4096]{1,0:T(8,128)}, u32[]{:S(2)}) copy-start(s32[128,4096]{1,0:T(8,128)} %refs_5_.1) | copy-start | bytes 6291460
  322.0 19.2 %copy-start.46 = (f32[4096]{0:T(1024)S(1)}, f32[4096]{0:T(1024)}, u32[]{:S(2)}) copy-start(f32[4096]{0:T(1024)} %param.16) | copy-start | bytes 49156
  322.0 19.2 %copy-start.47 = (f32[4096]{0:T(1024)S(1)}, f32[4096]{0:T(1024)}, u32[]{:S(2)}) copy-start(f32[4096]{0:T(1024)} %param.17) | copy-start | bytes 49156
  322.0 2.7 collective-permute-start.23
  325.9 9.4 %collective-permute-start.24 = (bf16[128,1024]{1,0:T(8,128)(2,1)}, bf16[128,1024]{1,0:T(8,128)(2,1)S(1)}, u32[]{:S(2)}, u32[]{:S(2)}) collective-permute-start(bf16[128,1024]{1,0:T(8,128)(2,1)} %get-tuple-element.85), channel_id=1, source_target_pairs={{0,2},{2,0},{4,6},{6,4},{8,10},{10,8},{12,14},{14,12},{16,18},{18,... | collective-permute-start | bytes 786440 | tf_op jit(solution)/shard_map/ppermute | solution.py:560
  327.1 12.4 %collective-permute-start.25 = (bf16[128,1024]{1,0:T(8,128)(2,1)}, bf16[128,1024]{1,0:T(8,128)(2,1)S(1)}, u32[]{:S(2)}, u32[]{:S(2)}) collective-permute-start(bf16[128,1024]{1,0:T(8,128)(2,1)} %get-tuple-element.86), channel_id=1, source_target_pairs={{0,4},{2,6},{4,0},{6,2},{8,12},{10,14},{12,8},{14,10},{16,20},{18,... | collective-permute-start | bytes 786440 | tf_op jit(solution)/shard_map/ppermute | solution.py:560
  328.0 13.2 %collective-permute-start.26 = (bf16[128,1024]{1,0:T(8,128)(2,1)S(1)}, bf16[128,1024]{1,0:T(8,128)(2,1)S(1)}, u32[]{:S(2)}, u32[]{:S(2)}) collective-permute-start(bf16[128,1024]{1,0:T(8,128)(2,1)S(1)} %get-tuple-element.87), channel_id=1, source_target_pairs={{0,6},{2,4},{4,2},{6,0},{8,14},{10,12},{12,10},{14,8},{16,22},{18,... | collective-permute-start | bytes 786440 | tf_op jit(solution)/shard_map/ppermute | solution.py:560
  341.2 1.2 copy-start.27
  (16 other events, 14.8 us)

commit v4 on v3

--- a/solution.py
+++ b/solution.py
@@ -87,7 +87,7 @@
         ),
         out_shape=jax.ShapeDtypeStruct((peers, span_len, whole), carried.dtype),
         input_output_aliases={3 + len(pieces): 0} if extra else {},
-        compiler_params=pltpu.CompilerParams(vmem_limit_bytes=10 * MIB),
+        compiler_params=pltpu.CompilerParams(vmem_limit_bytes=60 * MIB),
         name="spread_queries",
     )(block_of_peer, slot_of_peer, carried, *pieces, *extra)
 
@@ -110,7 +110,7 @@
     )
 
 
-def attend_kernel(chunk, valid_ref, slot_ref, query_ref, key_ref, value_ref, *refs):
+def attend_kernel(chunk, tag_ref, query_ref, key_ref, value_ref, *refs):
     out_ref, key_held, value_held, sems = refs[-4:]
     span_len = query_ref.shape[1]
     _, length, row_width = key_held.shape
@@ -119,11 +119,15 @@
     peer = pl.program_id(0)
     peers = pl.num_programs(0)
 
+    def tag_of(at):
+        return tag_ref[at, 0:1, 0:1].astype(jnp.float32)[0, 0].astype(jnp.int32)
+
     def copies(at):
         buffer = lax.rem(at, 2)
+        slot = jnp.maximum(tag_of(at) - 1, 0)
         for kind, (ref, held) in enumerate(((key_ref, key_held), (value_ref, value_held))):
             yield pltpu.make_async_copy(
-                ref.at[slot_ref[at], :, pl.ds(chunk * row_width, row_width)],
+                ref.at[slot, :, pl.ds(chunk * row_width, row_width)],
                 held.at[buffer],
                 sems.at[kind, buffer],
             )
@@ -134,15 +138,15 @@
 
     following = jnp.minimum(peer + 1, peers - 1)
 
-    @pl.when((peer == 0) & (valid_ref[0] > 0))
+    @pl.when((peer == 0) & (tag_of(0) > 0))
     def _():
         fetch(0)
 
-    @pl.when((peer + 1 < peers) & (valid_ref[following] > 0))
+    @pl.when((peer + 1 < peers) & (tag_of(following) > 0))
     def _():
         fetch(following)
 
-    @pl.when(valid_ref[peer] > 0)
+    @pl.when(tag_of(peer) > 0)
     def _():
         for copy in copies(peer):
             copy.wait()
@@ -182,40 +186,39 @@
         out_ref[0, :, row_width:] = pack_levels(stats, heads).astype(out_ref.dtype)
 
 
-def attend(asked, keys, values, valid, slots, width, chunk, part, size, place, places, shared):
+def attend(asked, tags, keys, values, width, chunk, part, size, place, places, shared, weigh):
     peers, span_len, _ = asked.shape
     length = keys.shape[1]
     heads = width // HEAD
     wide = width + LANES
+    tag_at = tags.shape[2] // LANES - 1
     extra = [] if shared is None else [shared]
     return pl.pallas_call(
         functools.partial(attend_kernel, chunk),
-        grid_spec=pltpu.PrefetchScalarGridSpec(
-            num_scalar_prefetch=2,
-            grid=(peers,),
-            in_specs=[
-                pl.BlockSpec((1, span_len, size), lambda i, v, s: (i, 0, part)),
-                pl.BlockSpec(memory_space=pltpu.HBM),
-                pl.BlockSpec(memory_space=pltpu.HBM),
-            ]
-            + [pl.BlockSpec(memory_space=pl.ANY)] * len(extra),
-            out_specs=pl.BlockSpec((1, span_len, wide), lambda i, v, s: (i, 0, place)),
-            scratch_shapes=[
-                pltpu.VMEM((2, length, width), keys.dtype),
-                pltpu.VMEM((2, length, width), keys.dtype),
-                pltpu.SemaphoreType.DMA((2, 2)),
-            ],
-        ),
+        grid=(peers,),
+        in_specs=[
+            pl.BlockSpec((peers, ROW_TILE, LANES), lambda i: (0, 0, tag_at)),
+            pl.BlockSpec((1, span_len, size), lambda i: (i, 0, part)),
+            pl.BlockSpec(memory_space=pl.ANY),
+            pl.BlockSpec(memory_space=pl.ANY),
+        ]
+        + [pl.BlockSpec(memory_space=pl.ANY)] * len(extra),
+        out_specs=pl.BlockSpec((1, span_len, wide), lambda i: (i, 0, place)),
+        scratch_shapes=[
+            pltpu.VMEM((2, length, width), keys.dtype),
+            pltpu.VMEM((2, length, width), keys.dtype),
+            pltpu.SemaphoreType.DMA((2, 2)),
+        ],
         out_shape=jax.ShapeDtypeStruct((peers, span_len, places * wide), asked.dtype),
-        input_output_aliases={5: 0} if extra else {},
-        compiler_params=pltpu.CompilerParams(vmem_limit_bytes=12 * MIB),
+        input_output_aliases={4: 0} if extra else {},
+        compiler_params=pltpu.CompilerParams(vmem_limit_bytes=58 * MIB),
         cost_estimate=pl.CostEstimate(
-            flops=4 * peers * heads * span_len * length * HEAD,
-            bytes_accessed=2 * peers * width * (2 * span_len + 2 * length),
+            flops=4 * weigh * peers * heads * span_len * length * HEAD,
+            bytes_accessed=2 * weigh * peers * width * (2 * span_len + 2 * length),
             transcendentals=peers * heads * span_len * length,
         ),
         name="attend_blocks",
-    )(valid, slots, asked, keys, values, *extra)
+    )(tags, asked, keys, values, *extra)
 
 
 def merge_block(uses, parts):
@@ -259,8 +262,8 @@
 
 
 def merge_all_kernel(picked, index_ref, use_ref, *refs):
-    out_ref, kept = refs[-2:]
-    parts = refs[:-2]
+    parts = refs[: picked + 1]
+    out_ref, first_ref, kept = refs[-3:]
     span_len = parts[0].shape[1]
     rows, row_width = out_ref.shape
     rows -= ROW_TILE
@@ -280,7 +283,9 @@
             moved = jnp.where(last, kept[0:1, cut], moved)
             out_ref[pl.ds(start, span_len), cut] = moved.astype(out_ref.dtype)
             kept[:, cut] = merged[:8]
-            out_ref[rows:, cut] = merged[:ROW_TILE].astype(out_ref.dtype)
+            first = merged[:ROW_TILE].astype(out_ref.dtype)
+            out_ref[rows:, cut] = first
+            first_ref[:, cut] = first
 
 
 def merge_far(parts, column, wide, index, use, blocks):
@@ -328,115 +333,121 @@
             num_scalar_prefetch=2,
             grid=(blocks,),
             in_specs=specs,
-            out_specs=pl.BlockSpec((rows + ROW_TILE, row_width), lambda i, *_: (0, 0)),
+            out_specs=[
+                pl.BlockSpec((rows + ROW_TILE, row_width), lambda i, *_: (0, 0)),
+                pl.BlockSpec((ROW_TILE, row_width), lambda i, *_: (0, 0)),
+            ],
             scratch_shapes=[pltpu.VMEM((8, row_width), jnp.float32)],
         ),
-        out_shape=jax.ShapeDtypeStruct((rows + ROW_TILE, row_width), parts.dtype),
+        out_shape=[
+            jax.ShapeDtypeStruct((rows + ROW_TILE, row_width), parts.dtype),
+            jax.ShapeDtypeStruct((ROW_TILE, row_width), parts.dtype),
+        ],
         compiler_params=pltpu.CompilerParams(vmem_limit_bytes=10 * MIB),
         name="merge_all",
     )(index, use, *([parts] * picked), far)
 
 
-def project_kernel(count, shard_of, place_ref, stay_ref, *refs):
-    sources, below_ref, weights = refs[:count], refs[count], refs[count + 1 : -7]
+def project_kernel(starts, place_ref, stay_ref, *refs):
+    sources, belows = refs[:PLANE], refs[PLANE : 2 * PLANE]
+    shards = len(starts)
+    weights, before = refs[2 * PLANE : 2 * PLANE + shards], refs[2 * PLANE + shards : -7]
     keep_ref, send_ref, rows_ref, first_ref, held_ref, row_sems, weight_sems = refs[-7:]
     half = keep_ref.shape[0]
     part = half // PLANE
-    tile = held_ref.shape[2]
+    _, width, tile = held_ref.shape
 
     def source_copies():
         for at, ref in enumerate(sources):
-            member = place_ref[0] ^ (at % PLANE)
-            width = ref.shape[1]
-            cut = pl.ds(at // PLANE * width, width)
+            member = place_ref[0] ^ at
             for side in range(2):
                 to = pl.multiple_of(side * half + member * part, part)
                 yield pltpu.make_async_copy(
                     ref.at[pl.ds(side * part, part)],
-                    rows_ref.at[pl.ds(to, part), cut],
+                    rows_ref.at[pl.ds(to, part)],
                     row_sems.at[at, side],
                 )
             to = pl.multiple_of(member * ROW_TILE, ROW_TILE)
             yield pltpu.make_async_copy(
                 ref.at[pl.ds(2 * part, ROW_TILE)],
-                first_ref.at[pl.ds(to, ROW_TILE), cut],
+                first_ref.at[pl.ds(to, ROW_TILE)],
                 row_sems.at[at, 2],
             )
 
-    def weight_copies(shard):
-        at = 0
-        for piece, (ref, of) in enumerate(zip(weights, shard_of)):
-            if of == shard:
-                size = ref.shape[0]
-                yield pltpu.make_async_copy(
-                    ref, held_ref.at[shard, pl.ds(at, size)], weight_sems.at[piece]
-                )
-                at += size
+    def weight_copy(shard):
+        return pltpu.make_async_copy(
+            weights[shard].at[pl.ds(starts[shard], width)],
+            held_ref.at[shard],
+            weight_sems.at[shard],
+        )
 
     for copy in source_copies():
         copy.start()
-    shards = held_ref.shape[0]
     for shard in range(shards):
-        for copy in weight_copies(shard):
-            copy.start()
+        weight_copy(shard).start()
     for copy in source_copies():
         copy.wait()
-    shape = (ROW_TILE, rows_ref.shape[1])
-    last = lax.broadcasted_iota(jnp.int32, shape, 0) == ROW_TILE - 1
+    last = lax.broadcasted_iota(jnp.int32, (ROW_TILE, width), 0) == ROW_TILE - 1
     for member in range(PLANE):
         if member < PLANE - 1:
             at = (member + 1) * ROW_TILE
-            below = first_ref[at : at + ROW_TILE].astype(jnp.float32)[0:1]
+            below = first_ref[at : at + ROW_TILE].astype(jnp.float32)
         else:
-            below = below_ref[...].astype(jnp.float32)[0:1]
+            below = functools.reduce(jnp.add, [ref[...].astype(jnp.float32) for ref in belows])
         end = half + (member + 1) * part
         held = rows_ref[end - ROW_TILE : end].astype(jnp.float32)
-        rows_ref[end - ROW_TILE : end] = jnp.where(last, below, held).astype(rows_ref.dtype)
+        rows_ref[end - ROW_TILE : end] = jnp.where(last, below[0:1], held).astype(rows_ref.dtype)
     stay = pl.multiple_of(stay_ref[0] * half, half)
     go = pl.multiple_of((1 - stay_ref[0]) * half, half)
     for shard in range(shards):
-        for copy in weight_copies(shard):
-            copy.wait()
-        for start, ref in ((go, send_ref), (stay, keep_ref)):
-            ref[:, shard * tile : (shard + 1) * tile] = jnp.dot(
-                rows_ref[pl.ds(start, half)],
-                held_ref[shard],
-                preferred_element_type=jnp.float32,
-            ).astype(ref.dtype)
-
-
-def project(sources, below, weights, place, stay):
-    height = sources[0].shape[0]
-    row_width = below.shape[1]
+        weight_copy(shard).wait()
+        cut = slice(shard * tile, (shard + 1) * tile)
+        for at, (start, ref) in enumerate(((stay, keep_ref), (go, send_ref))):
+            result = jnp.dot(
+                rows_ref[pl.ds(start, half)], held_ref[shard], preferred_element_type=jnp.float32
+            )
+            if before:
+                result = result + before[at][:, cut]
+            ref[:, cut] = result.astype(ref.dtype)
+
+
+def project(sources, belows, weights, place, stay, before, kind):
+    height, width = sources[0].shape
     rows = PLANE * (height - ROW_TILE)
     shards = len(weights)
+    starts = [start for _, start in weights]
     tile = weights[0][0].shape[1]
-    shard_of = [shard for shard, pieces in enumerate(weights) for _ in pieces]
-    pieces = [piece for pieces in weights for piece in pieces]
     columns = shards * tile
     half = rows // 2
-    kind = sources[0].dtype
+    row_spec = pl.BlockSpec((ROW_TILE, width), lambda i, *_: (0, 0))
+    half_spec = pl.BlockSpec((half, columns), lambda i, *_: (0, 0))
     return pl.pallas_call(
-        functools.partial(project_kernel, len(sources), shard_of),
+        functools.partial(project_kernel, starts),
         grid_spec=pltpu.PrefetchScalarGridSpec(
             num_scalar_prefetch=2,
             grid=(1,),
-            in_specs=[pl.BlockSpec(memory_space=pltpu.HBM)] * len(sources)
-            + [pl.BlockSpec((1, row_width), lambda i, *_: (0, 0))]
-            + [pl.BlockSpec(memory_space=pltpu.HBM)] * len(pieces),
-            out_specs=[pl.BlockSpec((half, columns), lambda i, *_: (0, 0))] * 2,
+            in_specs=[pl.BlockSpec(memory_space=pl.ANY)] * PLANE
+            + [row_spec] * PLANE
+            + [pl.BlockSpec(memory_space=pl.ANY)] * shards
+            + [half_spec] * len(before),
+            out_specs=[half_spec] * 2,
             scratch_shapes=[
-                pltpu.VMEM((rows, row_width), kind),
-                pltpu.VMEM((PLANE * ROW_TILE, row_width), kind),
-                pltpu.VMEM((shards, row_width, tile), kind),
-                pltpu.SemaphoreType.DMA((len(sources), 3)),
-                pltpu.SemaphoreType.DMA((len(pieces),)),
+                pltpu.VMEM((rows, width), sources[0].dtype),
+                pltpu.VMEM((PLANE * ROW_TILE, width), sources[0].dtype),
+                pltpu.VMEM((shards, width, tile), sources[0].dtype),
+                pltpu.SemaphoreType.DMA((PLANE, 3)),
+                pltpu.SemaphoreType.DMA((shards,)),
             ],
         ),
         out_shape=[jax.ShapeDtypeStruct((half, columns), kind)] * 2,
-        compiler_params=pltpu.CompilerParams(vmem_limit_bytes=20 * MIB),
+        compiler_params=pltpu.CompilerParams(vmem_limit_bytes=28 * MIB),
+        cost_estimate=pl.CostEstimate(
+            flops=2 * rows * width * columns,
+            bytes_accessed=2 * width * (rows + columns) + 8 * rows * columns,
+            transcendentals=0,
+        ),
         name="project_rows",
-    )(place, stay, *sources, below, *pieces)
+    )(place, stay, *sources, *belows, *[weight for weight, _ in weights], *before)
 
 
 def add_kernel(place_ref, keep_ref, other_ref, *outs):
@@ -568,6 +579,7 @@
     chunks = 2
     width = row_width // chunks
     far_first = to_partner(queries[:, :width])
+    middle = row_width // 2
     carried = shifted(queries[-1:], "dp", 1)
     owners = neighbour_owner.reshape(-1)
     slot_rows = neighbour_slot.reshape(-1)
@@ -584,107 +596,108 @@
     far_table = to_partner(
         jnp.pad(jnp.concatenate([owners, slot_rows]), (0, LANES - 2 * requests))[None, :]
     )
-    (far_first,) = pinned(far_first)
-    far_first, far_carried, far_table, held_queries, weight, _ = pinned(
-        far_first, far_carried, far_table, queries, out_weight, near_out
+    far_first, far_carried, far_table, second, weight, _ = pinned(
+        far_first, far_carried, far_table, queries[:, width:], out_weight, near_out
     )
     far_owners = far_table[0, :requests]
     far_picked = pick_requests(
         far_owners, far_table[0, requests : 2 * requests], near_peers, per_block
     )
 
-    def slots_of(asked):
-        return asked[:, 0, -LANES].astype(jnp.int32)
-
-    def answer(asked, tags, chunk, part, size, place, places, shared=None):
-        valid = (tags > 0).astype(jnp.int32)
-        slots = jnp.maximum(tags - 1, 0)
+    def answer(asked, tags, chunk, part, size, place, places, shared=None, weigh=1):
         return attend(
-            asked, neighbour_keys, neighbour_values, valid, slots, width, chunk, part, size,
-            place, places, shared,
+            asked, tags, neighbour_keys, neighbour_values, width, chunk, part, size,
+            place, places, shared, weigh,
         )
 
     wide = width + LANES
-    far_second = to_partner(held_queries[:, width:])
+    far_second = to_partner(second)
     near_index, near_use = within(owners, base, half)
     far_index, far_use = within(far_owners, base, half)
     far_out = spread([far_first], far_carried, *far_picked, span_len, 0)
     far_asked = exchange(far_out)
     near_asked, _ = pinned(near_asked, far_out)
-    near_tags = slots_of(near_asked)
-    near_first = answer(near_asked, near_tags, 0, 0, width, 0, 2)
-    near_second = answer(near_asked, near_tags, 1, 1, width, 1, 2)
-    middle = row_width // 2
-    near_swap = [swap(weight[:middle], PLANE)] if by_plane else []
-    far_asked, far_second, weight, near_first, near_second, *near_swap = pinned(
-        far_asked, far_second, weight, near_first, near_second, *near_swap
+    near_first = answer(near_asked, near_asked, 0, 0, width, 0, 2)
+    near_second = answer(near_asked, near_asked, 1, 1, width, 1, 2)
+    (
+        far_asked, far_second, near_first, near_second, near_index, near_use, far_index,
+        far_use, weight, *weight_halves,
+    ) = pinned(
+        far_asked, far_second, near_first, near_second, near_index, near_use, far_index,
+        far_use, weight, weight[:middle], weight[middle:],
     )
 
     mixed = spread([far_second], far_carried, *far_picked, span_len, 1, near_first)
     next_asked = exchange(mixed)
-    far_asked, near_second, _ = pinned(far_asked, near_second, mixed)
-    far_weight = [to_partner(weight[:middle])] if by_plane else []
-    far_tags = slots_of(far_asked)
-    mixed = answer(far_asked, far_tags, 0, 0, wide, 0, 2, near_second)
-    mixed, next_asked, weight, *far_weight = pinned(mixed, next_asked, weight, *far_weight)
+    far_weight = [to_partner(weight_halves[0])] if by_plane else []
+    tags, near_second, _, *far_weight = pinned(far_asked, near_second, mixed, *far_weight)
+    mixed = answer(tags, tags, 0, 0, wide, 0, 2, near_second, weigh=16)
+    mixed, next_asked, weight_half = pinned(mixed, next_asked, weight_halves[1])
 
     far_back = exchange(mixed)
     if by_plane:
-        far_weight.append(to_partner(weight[middle:]))
-    far_parts = answer(next_asked, far_tags, 1, 1, wide, 0, 1)
-    far_back, far_parts, weight, *far_weight = pinned(far_back, far_parts, weight, *far_weight)
+        far_weight.append(to_partner(weight_half))
+    next_asked, *far_weight = pinned(next_asked, *far_weight)
+    far_parts = answer(next_asked, tags, 1, 1, wide, 0, 1, weigh=16)
+    far_back, far_parts = pinned(far_back, far_parts)
     near_back, next_back = next_asked, far_back
 
     far_merged = merge_far(far_back, 0, wide, far_index, far_use, blocks)
     far_home = to_partner(far_merged)
     far_back = exchange(far_parts)
-    if by_plane:
-        near_swap.append(swap(weight[middle:], PLANE))
-    far_home, far_back, *near_swap = pinned(far_home, far_back, *near_swap)
-
-    def plane_rows(moved):
-        return [moved] + [swap(moved, by) for by in range(1, PLANE)] if by_plane else [moved]
+    far_home, far_back, *far_weight = pinned(far_home, far_back, *far_weight)
+
+    def to_plane(moved, first):
+        if not by_plane:
+            return [moved, first]
+        down = [
+            lax.ppermute(
+                first, "dp", [(i + PLANE, i + at) for i in range(0, peer_count - PLANE, PLANE)]
+            )
+            for at in range(PLANE)
+        ]
+        return [moved] + [swap(moved, by) for by in range(1, PLANE)] + down
 
     far_merged = merge_far(far_back, 0, wide, far_index, far_use, blocks)
-    far_home, near_back, _ = pinned(far_home, near_back, far_merged)
+    far_home, near_back, far_merged, near_half, *far_weight = pinned(
+        far_home, near_back, far_merged, weight_halves[0], *far_weight
+    )
     next_home = to_partner(far_merged)
-    sources = plane_rows(
-        merge_all(near_back, 0, wide, near_index, near_use, blocks, far_home)
-    )
-    far_swap = [swap(piece, PLANE) for piece in far_weight]
+    sources = to_plane(*merge_all(near_back, 0, wide, near_index, near_use, blocks, far_home))
+    swaps = [swap(far_weight[0], PLANE), swap(near_half, PLANE)] if by_plane else []
     count = len(sources)
     (next_home,) = pinned(next_home)
-    next_home, next_back, *held = pinned(next_home, next_back, *sources, *far_swap)
-    sources, far_swap = held[:count], held[count:]
-    moved = merge_all(next_back, 1, wide, near_index, near_use, blocks, next_home)
+    next_home, next_back, weight_half, *held = pinned(
+        next_home, next_back, weight_halves[1], *sources, *swaps, *far_weight
+    )
+    sources, held = held[:count], held[count:]
+    moved, first = merge_all(next_back, 1, wide, near_index, near_use, blocks, next_home)
     if by_plane:
         place = lax.rem(here, PLANE).reshape(1)
         stay = lax.axis_index("tensor").astype(jnp.int32).reshape(1)
-        shards = [[weight], near_swap, far_weight, far_swap]
+        far_swap, near_swap, *far_weight = held
+        moved, first, weight_half, far_half = pinned(moved, first, weight_half, far_weight[1])
+        next_sources = to_plane(moved, first)
+        near_next, far_next = swap(weight_half, PLANE), swap(far_half, PLANE)
+        done = project(
+            sources[:PLANE], sources[PLANE:],
+            [(weight, 0), (near_swap, 0), (far_weight[0], 0), (far_swap, 0)],
+            place, stay, [], jnp.float32,
+        )
+        keep, send = project(
+            next_sources[:PLANE], next_sources[PLANE:],
+            [(weight, middle), (near_next, 0), (far_half, 0), (far_next, 0)],
+            place, stay, done, moved.dtype,
+        )
         line = jnp.stack(
             [here // PLANE, (here ^ PLANE) // PLANE, partner // PLANE, (partner ^ PLANE) // PLANE]
         )
-        first_rows = [moved_part[rows : rows + 1] for moved_part in (sources[0], moved)]
-        sources += plane_rows(moved)
-        first_row = jnp.concatenate(first_rows, axis=1)
-        below = functools.reduce(
-            jnp.add,
-            [
-                lax.ppermute(
-                    first_row,
-                    "dp",
-                    [(i + PLANE, i + at) for i in range(0, peer_count - PLANE, PLANE)],
-                )
-                for at in range(PLANE)
-            ],
-        )
-        keep, send = project(sources, below, shards, place, stay)
         summed = add_cores(keep, lax.ppermute(send, "tensor", [(0, 1), (1, 0)]), place)
         branches = [summed[0]] + [swap(summed[by], by) for by in range(1, PLANE)]
     else:
         whole_weight = lax.all_gather(out_weight, "dp", axis=1, tiled=True)
         moved = jnp.concatenate([sources[0], moved], axis=1)
-        below = shifted(moved[rows : rows + 1], "dp", -1)
+        below = shifted(jnp.concatenate([sources[1], first], axis=1)[:1], "dp", -1)
         cross_rows = jnp.concatenate([moved[: rows - 1], below], axis=0)
         branch = jnp.dot(cross_rows, whole_weight, preferred_element_type=jnp.float32)
         branches = [

time: 348 us -> 333 us (0.957)
  local copies, waits for them, and re-layouts: 50.5 us -> 17.5 us
  waiting for transfers between devices: 193 us -> 166 us
  starting transfers between devices: 62.3 us -> 85.9 us
  Pallas kernels: 37 us -> 58.7 us
    ppermute x13, waiting for transfers between devices: 78.9 us -> 29.6 us  [swap(): return lax.ppermute(x, 'dp', [(i, i ^ by) for i in range(peer_count)])]
    unnamed x98 -> x66, local copies, waits for them, and re-layouts: 47.6 us -> 14.7 us
    ppermute x7, waiting for transfers between devices: 95.7 us -> 128 us  [to_partner(): return lax.ppermute(x, 'dp', across)]
    pallas_call x5 -> x6, Pallas kernels: 19.6 us -> 34.8 us  [the longest x4 27.2 us: attend(): pl.pallas_call(functools.partial(attend_kernel, chunk), grid=(peers,), in...]
    all_to_all x5, starting transfers between devices: 23.6 us -> 36.1 us  [exchange(): lax.all_to_all(x, 'dp', split_axis=0, concat_axis=0, tiled=True, axis_ind...]
    ppermute x13, starting transfers between devices: 15.9 us -> 25.2 us  [swap(): return lax.ppermute(x, 'dp', [(i, i ^ by) for i in range(peer_count)])]
    ppermute x4 -> x8, waiting for transfers between devices: 7.11 us -> 0.02 us  [to_plane(): lax.ppermute(first, 'dp', [(i + PLANE, i + at) for i in range(0, peer_cou...]
    pallas_call x3, Pallas kernels: 3.34 us -> 9.77 us  [spread(): pl.pallas_call(functools.partial(spread_kernel, len(pieces), whole - wide...]
  transfers between devices with their start and end apart: 32 -> 36, of which waited for: 20 -> 13; matrix products, arithmetic and copies ran while one was open for 2% -> 2% of each run, Pallas kernels for 5% -> 12%
where the time goes in v4:
time: 333 us; the launch traced here: 331 us
  waiting for transfers between devices  166 us (50%)
  starting transfers between devices  85.9 us (26%)
  Pallas kernels  58.7 us (18%)
  local copies, waits for them, and re-layouts  17.5 us (5%)
    ppermute x7, waiting for transfers between devices, to_partner(): return lax.ppermute(x, 'dp', across)  128 us
    all_to_all x5, starting transfers between devices, exchange(): lax.all_to_all(x, 'dp', split_axis=0, concat_axis=0, tiled=True, axis_ind...  36.1 us
    ppermute x13, waiting for transfers between devices, swap(): return lax.ppermute(x, 'dp', [(i, i ^ by) for i in range(peer_count)])  29.6 us
    pallas_call x4, Pallas kernels, attend(): pl.pallas_call(functools.partial(attend_kernel, chunk), grid=(peers,), in...  27.2 us
    ppermute x13, starting transfers between devices, swap(): return lax.ppermute(x, 'dp', [(i, i ^ by) for i in range(peer_count)])  25.2 us
    unnamed x66, local copies, waits for them, and re-layouts  14.7 us
    pallas_call x3, Pallas kernels, spread(): pl.pallas_call(functools.partial(spread_kernel, len(pieces), whole - wide...  9.77 us
    ppermute x7, starting transfers between devices, to_partner(): return lax.ppermute(x, 'dp', across)  9.39 us
  transfers between devices with their start and end apart: 36, of which 13 were waited for; matrix products, arithmetic and copies ran while one was open for 2% of the time, Pallas kernels for 12%

profile of v4, /device:TPU:0, one launch (start us, length us, event | category | flops | bytes accessed | tf_op | source)
XLA Modules:
  0.0 331.4 jit_solution(10405790513872013833)
XLA Ops:
  0.6 0.8 slice.23
  1.4 4.8 %collective-permute-start.3 = (bf16[1,2048]{1,0:T(2,128)(2,1)S(1)}, bf16[1,2048]{1,0:T(2,128)(2,1)S(1)}, u32[]{:S(2)}, u32[]{:S(2)}) collective-permute-start(bf16[1,2048]{1,0:T(2,128)(2,1)S(1)} %slice.23), channel_id=1, source_target_pairs={{0,2},{2,4},{4,6},{6,8},{8,10},{10,12},{12,14},{14,16},{16,18},{18... | collective-permute-start | bytes 12296 | tf_op jit(solution)/shard_map/ppermute | solution.py:23
  6.3 0.8 copy.18
  8.0 0.8 fusion.1
  9.4 3.7 %spread_queries.3 = bf16[8,64,2176]{2,1,0:T(8,128)(2,1)} custom-call(s32[8]{0:T(128)} %get-tuple-element.143.block_ref, s32[8]{0:T(128)} %get-tuple-element.142.slot_ref, bf16[1,2048]{1,0:T(2,128)(2,1)} %copy-done.31, bf16[256,2048]{1,0:T(8,128)(2,1)} %refs_0_.1), custom_call_target="tpu_custom_call" | custom-call | tf_op jit(solution)/shard_map/spread_queries/pallas_call | solution.py:73
  13.1 4.9 %all-to-all-start.1 = ((bf16[8,64,2176]{2,1,0:T(8,128)(2,1)}), bf16[8,64,2176]{2,1,0:T(8,128)(2,1)S(1)}, u32[]{:S(2)}, u32[]{:S(2)}) async-start(bf16[8,64,2176]{2,1,0:T(8,128)(2,1)} %spread_queries.3), calls=%async_computation.1 | async-start | bytes 4456448 | tf_op jit(solution)/shard_map/all_to_all | solution.py:566
  18.0 0.9 fusion.7
  18.8 2.9 collective-permute-start
  21.7 3.5 %collective-permute-start.1 = (bf16[1,2048]{1,0:T(2,128)(2,1)S(1)}, bf16[1,2048]{1,0:T(2,128)(2,1)S(1)}, u32[]{:S(2)}, u32[]{:S(2)}) collective-permute-start(bf16[1,2048]{1,0:T(2,128)(2,1)S(1)} %slice.23), channel_id=1, source_target_pairs={{0,18},{2,20},{4,22},{6,24},{8,26},{10,28},{12,30},{14,0},{16,2},{... | collective-permute-start | bytes 12296 | tf_op jit(solution)/shard_map/ppermute | solution.py:592
  25.3 2.7 collective-permute-start.2
  28.0 25.3 %collective-permute-done.2 = s32[1,128]{1,0:T(1,128)S(1)} collective-permute-done((s32[1,128]{1,0:T(1,128)S(1)}, s32[1,128]{1,0:T(1,128)S(1)}, u32[]{:S(2)}, u32[]{:S(2)}) %collective-permute-start.2) | collective-permute-done | bytes 544 | tf_op jit(solution)/shard_map/ppermute | solution.py:577
  53.3 4.0 %collective-permute-done.1.carried_ref = bf16[1,2048]{1,0:T(2,128)(2,1)S(1)} collective-permute-done((bf16[1,2048]{1,0:T(2,128)(2,1)S(1)}, bf16[1,2048]{1,0:T(2,128)(2,1)S(1)}, u32[]{:S(2)}, u32[]{:S(2)}) %collective-permute-start.1) | collective-permute-done | bytes 4128 | tf_op jit(solution)/shard_map/ppermute | solution.py:592
  57.4 0.8 fusion.3
  58.2 3.0 spread_queries.4
  61.2 4.6 %all-to-all-start = ((bf16[8,64,1152]{2,1,0:T(8,128)(2,1)}), bf16[8,64,1152]{2,1,0:T(8,128)(2,1)}, u32[]{:S(2)}, u32[]{:S(2)}) async-start(bf16[8,64,1152]{2,1,0:T(8,128)(2,1)} %spread_queries.4), calls=%async_computation | async-start | bytes 2359296 | tf_op jit(solution)/shard_map/all_to_all | solution.py:566
  65.8 1.8 collective-permute-start.4
  67.7 1.0 fusion.6
  68.7 7.8 %attend_blocks.5.refs_0_ = bf16[8,64,2304]{2,1,0:T(8,128)(2,1)} custom-call(bf16[8,64,2176]{2,1,0:T(8,128)(2,1)} %copy-done.25, bf16[8,64,2176]{2,1,0:T(8,128)(2,1)} %copy-done.25, bf16[8,128,2048]{2,1,0:T(8,128)(2,1)} %key_ref.7, bf16[8,128,2048]{2,1,0:T(8,128)(2,1)} %value_ref.7), custom_call_target="tpu_custom_call" | custom-call | flops 268435456 | bytes 6291456 | tf_op jit(solution)/shard_map/attend_blocks/pallas_call | solution.py:196
  76.5 7.8 %attend_blocks.4.refs_1_ = bf16[8,64,2304]{2,1,0:T(8,128)(2,1)} custom-call(bf16[8,64,2176]{2,1,0:T(8,128)(2,1)} %copy-done.25, bf16[8,64,2176]{2,1,0:T(8,128)(2,1)} %copy-done.25, bf16[8,128,2048]{2,1,0:T(8,128)(2,1)} %key_ref.7, bf16[8,128,2048]{2,1,0:T(8,128)(2,1)} %value_ref.7), custom_call_target="tpu_custom_call" | custom-call | flops 268435456 | bytes 6291456 | tf_op jit(solution)/shard_map/attend_blocks/pallas_call | solution.py:196
  84.3 4.1 %collective-permute-done.4.refs_0_ = bf16[256,1024]{1,0:T(8,128)(2,1)} collective-permute-done((bf16[256,1024]{1,0:T(8,128)(2,1)}, bf16[256,1024]{1,0:T(8,128)(2,1)}, u32[]{:S(2)}, u32[]{:S(2)}) %collective-permute-start.4) | collective-permute-done | bytes 524320 | tf_op jit(solution)/shard_map/ppermute | solution.py:577
  88.3 2.0 all-to-all-done.tag_ref.query_ref
  90.3 3.1 spread_queries.5
  93.4 5.5 %all-to-all-start.2 = ((bf16[8,64,2304]{2,1,0:T(8,128)(2,1)}), bf16[8,64,2304]{2,1,0:T(8,128)(2,1)S(1)}, u32[]{:S(2)}, u32[]{:S(2)}) async-start(bf16[8,64,2304]{2,1,0:T(8,128)(2,1)} %spread_queries.5), calls=%async_computation.2 | async-start | bytes 4718592 | tf_op jit(solution)/shard_map/all_to_all | solution.py:566
  99.6 33.6 %collective-permute-done.5.refs_10_ = bf16[1024,256]{1,0:T(8,128)(2,1)S(1)} collective-permute-done((bf16[1024,256]{1,0:T(8,128)(2,1)S(1)}, bf16[1024,256]{1,0:T(8,128)(2,1)S(1)}, u32[]{:S(2)}, u32[]{:S(2)}) %collective-permute-start.5) | collective-permute-done | bytes 524320 | tf_op jit(solution)/shard_map/ppermute | solution.py:577
  133.2 5.9 %attend_blocks.6 = bf16[8,64,2304]{2,1,0:T(8,128)(2,1)} custom-call(bf16[8,64,1152]{2,1,0:T(8,128)(2,1)} %all-to-all-done.tag_ref.query_ref, bf16[8,64,1152]{2,1,0:T(8,128)(2,1)} %all-to-all-done.tag_ref.query_ref, bf16[8,128,2048]{2,1,0:T(8,128)(2,1)} %key_ref.7, bf16[8,128,2048]{2,1,0:T(8,128)(2,1)} %value_ref.7, ...), custom_call_target="tpu_custom_call", output_to_operand_aliasing={{}: (4, {})} | custom-call | flops 4294967296 | bytes 100663296 | tf_op jit(solution)/shard_map/attend_blocks/pallas_call | solution.py:196
  139.1 1.4 copy-done
  140.5 10.4 %all-to-all-start.3 = ((bf16[8,64,2304]{2,1,0:T(8,128)(2,1)}), bf16[8,64,2304]{2,1,0:T(8,128)(2,1)S(1)}, u32[]{:S(2)}, u32[]{:S(2)}) async-start(bf16[8,64,2304]{2,1,0:T(8,128)(2,1)} %attend_blocks.6), calls=%async_computation.3 | async-start | bytes 4718592 | tf_op jit(solution)/shard_map/all_to_all | solution.py:566
  151.5 32.8 %collective-permute-done.6.refs_10_ = bf16[1024,256]{1,0:T(8,128)(2,1)} collective-permute-done((bf16[1024,256]{1,0:T(8,128)(2,1)}, bf16[1024,256]{1,0:T(8,128)(2,1)}, u32[]{:S(2)}, u32[]{:S(2)}) %collective-permute-start.6) | collective-permute-done | bytes 524320 | tf_op jit(solution)/shard_map/ppermute | solution.py:577
  184.4 5.7 %attend_blocks.7 = bf16[8,64,1152]{2,1,0:T(8,128)(2,1)} custom-call(bf16[8,64,1152]{2,1,0:T(8,128)(2,1)} %all-to-all-done.tag_ref.query_ref, bf16[8,64,2304]{2,1,0:T(8,128)(2,1)} %copy-done, bf16[8,128,2048]{2,1,0:T(8,128)(2,1)} %key_ref.7, bf16[8,128,2048]{2,1,0:T(8,128)(2,1)} %value_ref.7), custom_call_target="tpu_custom_call" | custom-call | flops 4294967296 | bytes 100663296 | tf_op jit(solution)/shard_map/attend_blocks/pallas_call | solution.py:196
  190.1 10.7 %all-to-all-start.4 = ((bf16[8,64,1152]{2,1,0:T(8,128)(2,1)}), bf16[8,64,1152]{2,1,0:T(8,128)(2,1)S(1)}, u32[]{:S(2)}, u32[]{:S(2)}) async-start(bf16[8,64,1152]{2,1,0:T(8,128)(2,1)} %attend_blocks.7), calls=%async_computation.4 | async-start | bytes 2359296 | tf_op jit(solution)/shard_map/all_to_all | solution.py:566
  200.9 2.1 merge_far.2
  203.7 32.2 %collective-permute-done.7.refs_2_ = bf16[4,64,1152]{2,1,0:T(8,128)(2,1)S(1)} collective-permute-done((bf16[4,64,1152]{2,1,0:T(8,128)(2,1)S(1)}, bf16[4,64,1152]{2,1,0:T(8,128)(2,1)S(1)}, u32[]{:S(2)}, u32[]{:S(2)}) %collective-permute-start.7) | collective-permute-done | bytes 589856 | tf_op jit(solution)/shard_map/ppermute | solution.py:577
  235.9 0.8 copy-done.6
  236.8 1.9 merge_far.3
  238.8 2.4 merge_all.2
  243.2 1.3 collective-permute-start.12
  244.6 7.7 %collective-permute-start.11 = (bf16[272,1024]{1,0:T(8,128)(2,1)S(1)}, bf16[272,1024]{1,0:T(8,128)(2,1)S(1)}, u32[]{:S(2)}, u32[]{:S(2)}) collective-permute-start(bf16[272,1024]{1,0:T(8,128)(2,1)S(1)} %get-tuple-element.121.refs_0_), channel_id=1, source_target_pairs={{0,6},{2,4},{4,2},{6,0},{8,14},{10,12},{12,10},{14,8},{16,22},{18,... | collective-permute-start | bytes 1671176 | tf_op jit(solution)/shard_map/ppermute | solution.py:571
  252.8 4.0 %collective-permute-start.9 = (bf16[272,1024]{1,0:T(8,128)(2,1)S(1)}, bf16[272,1024]{1,0:T(8,128)(2,1)S(1)}, u32[]{:S(2)}, u32[]{:S(2)}) collective-permute-start(bf16[272,1024]{1,0:T(8,128)(2,1)S(1)} %get-tuple-element.121.refs_0_), channel_id=1, source_target_pairs={{0,2},{2,0},{4,6},{6,4},{8,10},{10,8},{12,14},{14,12},{16,18},{18,... | collective-permute-start | bytes 1671176 | tf_op jit(solution)/shard_map/ppermute | solution.py:571
  256.7 0.8 copy-done.10
  257.5 2.1 collective-permute-start.17
  259.7 10.3 %collective-permute-done.17.refs_9_ = bf16[1024,256]{1,0:T(8,128)(2,1)S(1)} collective-permute-done((bf16[1024,256]{1,0:T(8,128)(2,1)S(1)}, bf16[1024,256]{1,0:T(8,128)(2,1)S(1)}, u32[]{:S(2)}, u32[]{:S(2)}) %collective-permute-start.17) | collective-permute-done | bytes 524320 | tf_op jit(solution)/shard_map/ppermute | solution.py:571
  270.0 0.9 copy-done.21
  270.9 5.8 %collective-permute-done.16.refs_11_ = bf16[1024,256]{1,0:T(8,128)(2,1)S(1)} collective-permute-done((bf16[1024,256]{1,0:T(8,128)(2,1)S(1)}, bf16[1024,256]{1,0:T(8,128)(2,1)S(1)}, u32[]{:S(2)}, u32[]{:S(2)}) %collective-permute-start.16) | collective-permute-done | bytes 524320 | tf_op jit(solution)/shard_map/ppermute | solution.py:571
  276.7 3.2 merge_all.3
  282.0 1.5 collective-permute-start.21
  283.6 4.1 %collective-permute-start.18 = (bf16[272,1024]{1,0:T(8,128)(2,1)}, bf16[272,1024]{1,0:T(8,128)(2,1)S(1)}, u32[]{:S(2)}, u32[]{:S(2)}) collective-permute-start(bf16[272,1024]{1,0:T(8,128)(2,1)} %get-tuple-element.116.refs_0_), channel_id=1, source_target_pairs={{0,2},{2,0},{4,6},{6,4},{8,10},{10,8},{12,14},{14,12},{16,18},{18,... | collective-permute-start | bytes 1671176 | tf_op jit(solution)/shard_map/ppermute | solution.py:571
  287.7 3.1 collective-permute-start.25
  290.9 1.1 copy-done.11
  292.0 1.1 copy-done.13
  293.0 1.1 copy-done.15
  294.1 1.1 copy-done.17
  295.1 1.0 copy-done.20
  296.2 1.0 copy-done.22
  297.2 1.0 copy-done.24
  298.2 3.5 %project_rows.2 = (f32[512,1024]{1,0:T(8,128)S(1)}, f32[512,1024]{1,0:T(8,128)S(1)}) custom-call(s32[1]{0:T(128)} %bitcast.place_ref, s32[1]{0:T(128)} %bitcast.5.stay_ref, bf16[272,1024]{1,0:T(8,128)(2,1)S(1)} %copy-done.11, bf16[272,1024]{1,0:T(8,128)(2,1)S(1)} %copy-done.17, bf16[272,1024]{1,0:T(8,128)(2,1)S(1)} %copy-done.15, ...), custom_call_target="tpu_custom_call" | custom-call | flops 2147483648 | bytes 12582912 | tf_op jit(solution)/shard_map/project_rows/pallas_call | solution.py:424
  301.8 2.8 collective-permute-done.26.refs_11_
  304.6 4.1 %project_rows.3 = (bf16[512,1024]{1,0:T(8,128)(2,1)S(1)}, bf16[512,1024]{1,0:T(8,128)(2,1)S(1)}) custom-call(s32[1]{0:T(128)} %bitcast.place_ref, s32[1]{0:T(128)} %bitcast.5.stay_ref, bf16[272,1024]{1,0:T(8,128)(2,1)} %get-tuple-element.116.refs_0_, bf16[272,1024]{1,0:T(8,128)(2,1)S(1)} %collective-permute-done.18.refs_1_, ...), custom_call_target="tpu_custom_call" | custom-call | flops 2147483648 | bytes 12582912 | tf_op jit(solution)/shard_map/project_rows/pallas_call | solution.py:424
  308.8 2.6 collective-permute-done.27
  311.4 1.2 add_cores.1
  312.8 3.3 collective-permute-start.30
  316.2 5.8 %collective-permute-done.28.refs_1_ = bf16[128,1024]{1,0:T(8,128)(2,1)S(1)} collective-permute-done((bf16[128,1024]{1,0:T(8,128)(2,1)}, bf16[128,1024]{1,0:T(8,128)(2,1)S(1)}, u32[]{:S(2)}, u32[]{:S(2)}) %collective-permute-start.28) | collective-permute-done | bytes 262176 | tf_op jit(solution)/shard_map/ppermute | solution.py:571
  322.0 4.8 %collective-permute-done.29.refs_2_ = bf16[128,1024]{1,0:T(8,128)(2,1)S(1)} collective-permute-done((bf16[128,1024]{1,0:T(8,128)(2,1)}, bf16[128,1024]{1,0:T(8,128)(2,1)S(1)}, u32[]{:S(2)}, u32[]{:S(2)}) %collective-permute-start.29) | collective-permute-done | bytes 262176 | tf_op jit(solution)/shard_map/ppermute | solution.py:571
  326.8 1.2 copy-done.5
  328.0 3.4 %add_norm.1 = (bf16[128,4096]{1,0:T(8,128)(2,1)}, bf16[128,4096]{1,0:T(8,128)(2,1)}) custom-call(s32[1]{0:T(128)} %bitcast.place_ref, s32[4]{0:T(128)S(1)} %pad_add_fusion.line_ref, bf16[128,1024]{1,0:T(8,128)(2,1)S(1)} %get-tuple-element.136.refs_0_, bf16[128,1024]{1,0:T(8,128)(2,1)S(1)} %collective-permute-done.28.refs_1_, ...), custom_call_target="tpu_custom_call" | custom-call | tf_op jit(solution)/shard_map/add_norm/pallas_call | solution.py:509
  (106 shorter events, 9.1 us)
Async XLA Ops:
  1.4 7.4 %collective-permute-start.3 = (bf16[1,2048]{1,0:T(2,128)(2,1)S(1)}, bf16[1,2048]{1,0:T(2,128)(2,1)S(1)}, u32[]{:S(2)}, u32[]{:S(2)}) collective-permute-start(bf16[1,2048]{1,0:T(2,128)(2,1)S(1)} %slice.23), channel_id=1, source_target_pairs={{0,2},{2,4},{4,6},{6,8},{8,10},{10,12},{12,14},{14,16},{16,18},{18... | collective-permute-start | bytes 12296 | tf_op jit(solution)/shard_map/ppermute | solution.py:23
  13.1 4.9 %copy-start.26 = (bf16[256,2048]{1,0:T(8,128)(2,1)S(1)}, bf16[256,2048]{1,0:T(8,128)(2,1)}, u32[]{:S(2)}) copy-start(bf16[256,2048]{1,0:T(8,128)(2,1)} %refs_0_.1) | copy-start | bytes 3145732
  13.1 48.1 %all-to-all-start.1 = ((bf16[8,64,2176]{2,1,0:T(8,128)(2,1)}), bf16[8,64,2176]{2,1,0:T(8,128)(2,1)S(1)}, u32[]{:S(2)}, u32[]{:S(2)}) async-start(bf16[8,64,2176]{2,1,0:T(8,128)(2,1)} %spread_queries.3), calls=%async_computation.1 | async-start | bytes 4456448 | tf_op jit(solution)/shard_map/all_to_all | solution.py:566
  18.8 48.8 %copy-start.2 = (bf16[2048,256]{1,0:T(8,128)(2,1)S(1)}, bf16[2048,256]{1,0:T(8,128)(2,1)}, u32[]{:S(2)}) copy-start(bf16[2048,256]{1,0:T(8,128)(2,1)} %refs_8_.1) | copy-start | bytes 3145732
  18.8 38.5 %collective-permute-start = (bf16[256,1024]{1,0:T(8,128)(2,1)S(1)}, bf16[256,1024]{1,0:T(8,128)(2,1)S(1)}, u32[]{:S(2)}, u32[]{:S(2)}) collective-permute-start(bf16[256,1024]{1,0:T(8,128)(2,1)S(1)} %get-tuple-element.147), channel_id=1, source_target_pairs={{0,16},{2,18},{4,20},{6,22},{8,24},{10,26},{12,28},{14,30},{16,0},... | collective-permute-start | bytes 1572872 | tf_op jit(solution)/shard_map/ppermute | solution.py:577
  21.7 35.6 %collective-permute-start.1 = (bf16[1,2048]{1,0:T(2,128)(2,1)S(1)}, bf16[1,2048]{1,0:T(2,128)(2,1)S(1)}, u32[]{:S(2)}, u32[]{:S(2)}) collective-permute-start(bf16[1,2048]{1,0:T(2,128)(2,1)S(1)} %slice.23), channel_id=1, source_target_pairs={{0,18},{2,20},{4,22},{6,24},{8,26},{10,28},{12,30},{14,0},{16,2},{... | collective-permute-start | bytes 12296 | tf_op jit(solution)/shard_map/ppermute | solution.py:592
  25.3 28.0 %collective-permute-start.2 = (s32[1,128]{1,0:T(1,128)S(1)}, s32[1,128]{1,0:T(1,128)S(1)}, u32[]{:S(2)}, u32[]{:S(2)}) collective-permute-start(s32[1,128]{1,0:T(1,128)S(1)} %pad_bitcast_fusion), channel_id=1, source_target_pairs={{0,16},{2,18},{4,20},{6,22},{8,24},{10,26},{12,28},{14,30},{16,0},... | collective-permute-start | bytes 1544 | tf_op jit(solution)/shard_map/ppermute | solution.py:577
  57.3 0.9 copy-start.30
  57.3 0.9 copy-start.27
  61.2 7.5 %copy-start.25 = (bf16[8,64,2176]{2,1,0:T(8,128)(2,1)}, bf16[8,64,2176]{2,1,0:T(8,128)(2,1)S(1)}, u32[]{:S(2)}) copy-start(bf16[8,64,2176]{2,1,0:T(8,128)(2,1)S(1)} %all-to-all-done.1.tag_ref.query_ref) | copy-start | bytes 6684676
  61.2 29.1 %all-to-all-start = ((bf16[8,64,1152]{2,1,0:T(8,128)(2,1)}), bf16[8,64,1152]{2,1,0:T(8,128)(2,1)}, u32[]{:S(2)}, u32[]{:S(2)}) async-start(bf16[8,64,1152]{2,1,0:T(8,128)(2,1)} %spread_queries.4), calls=%async_computation | async-start | bytes 2359296 | tf_op jit(solution)/shard_map/all_to_all | solution.py:566
  65.8 22.5 %collective-permute-start.4 = (bf16[256,1024]{1,0:T(8,128)(2,1)}, bf16[256,1024]{1,0:T(8,128)(2,1)}, u32[]{:S(2)}, u32[]{:S(2)}) collective-permute-start(bf16[256,1024]{1,0:T(8,128)(2,1)} %get-tuple-element.74), channel_id=1, source_target_pairs={{0,16},{2,18},{4,20},{6,22},{8,24},{10,26},{12,28},{14,30},{16,0},... | collective-permute-start | bytes 1572872 | tf_op jit(solution)/shard_map/ppermute | solution.py:577
  93.4 5.5 %copy-start.28 = (bf16[1024,256]{1,0:T(8,128)(2,1)S(1)}, bf16[1024,256]{1,0:T(8,128)(2,1)}, u32[]{:S(2)}) copy-start(bf16[1024,256]{1,0:T(8,128)(2,1)} %get-tuple-element.108) | copy-start | bytes 1572868
  93.4 45.7 %all-to-all-start.2 = ((bf16[8,64,2304]{2,1,0:T(8,128)(2,1)}), bf16[8,64,2304]{2,1,0:T(8,128)(2,1)S(1)}, u32[]{:S(2)}, u32[]{:S(2)}) async-start(bf16[8,64,2304]{2,1,0:T(8,128)(2,1)} %spread_queries.5), calls=%async_computation.2 | async-start | bytes 4718592 | tf_op jit(solution)/shard_map/all_to_all | solution.py:566
  98.9 34.3 %collective-permute-start.5 = (bf16[1024,256]{1,0:T(8,128)(2,1)S(1)}, bf16[1024,256]{1,0:T(8,128)(2,1)S(1)}, u32[]{:S(2)}, u32[]{:S(2)}) collective-permute-start(bf16[1024,256]{1,0:T(8,128)(2,1)S(1)} %copy-done.28), channel_id=1, source_target_pairs={{0,16},{2,18},{4,20},{6,22},{8,24},{10,26},{12,28},{14,30},{16,0},... | collective-permute-start | bytes 1572872 | tf_op jit(solution)/shard_map/ppermute | solution.py:577
  133.2 5.9 %copy-start.18 = (bf16[1024,256]{1,0:T(8,128)(2,1)}, bf16[1024,256]{1,0:T(8,128)(2,1)S(1)}, u32[]{:S(2)}) copy-start(bf16[1024,256]{1,0:T(8,128)(2,1)S(1)} %collective-permute-done.5.refs_10_) | copy-start | bytes 1572868
  139.1 1.4 copy-start
  140.5 49.6 %all-to-all-start.3 = ((bf16[8,64,2304]{2,1,0:T(8,128)(2,1)}), bf16[8,64,2304]{2,1,0:T(8,128)(2,1)S(1)}, u32[]{:S(2)}, u32[]{:S(2)}) async-start(bf16[8,64,2304]{2,1,0:T(8,128)(2,1)} %attend_blocks.6), calls=%async_computation.3 | async-start | bytes 4718592 | tf_op jit(solution)/shard_map/all_to_all | solution.py:566
  151.0 33.4 %collective-permute-start.6 = (bf16[1024,256]{1,0:T(8,128)(2,1)}, bf16[1024,256]{1,0:T(8,128)(2,1)}, u32[]{:S(2)}, u32[]{:S(2)}) collective-permute-start(bf16[1024,256]{1,0:T(8,128)(2,1)} %get-tuple-element.119), channel_id=1, source_target_pairs={{0,16},{2,18},{4,20},{6,22},{8,24},{10,26},{12,28},{14,30},{16,0},... | collective-permute-start | bytes 1572872 | tf_op jit(solution)/shard_map/ppermute | solution.py:577
  190.1 46.6 %all-to-all-start.4 = ((bf16[8,64,1152]{2,1,0:T(8,128)(2,1)}), bf16[8,64,1152]{2,1,0:T(8,128)(2,1)S(1)}, u32[]{:S(2)}, u32[]{:S(2)}) async-start(bf16[8,64,1152]{2,1,0:T(8,128)(2,1)} %attend_blocks.7), calls=%async_computation.4 | async-start | bytes 2359296 | tf_op jit(solution)/shard_map/all_to_all | solution.py:566
  202.9 33.0 %collective-permute-start.7 = (bf16[4,64,1152]{2,1,0:T(8,128)(2,1)S(1)}, bf16[4,64,1152]{2,1,0:T(8,128)(2,1)S(1)}, u32[]{:S(2)}, u32[]{:S(2)}) collective-permute-start(bf16[4,64,1152]{2,1,0:T(8,128)(2,1)S(1)} %merge_far.2), channel_id=1, source_target_pairs={{0,16},{2,18},{4,20},{6,22},{8,24},{10,26},{12,28},{14,30},{16,0},... | collective-permute-start | bytes 1769480 | tf_op jit(solution)/shard_map/ppermute | solution.py:577
  236.8 2.1 copy-start.1
  236.8 2.1 copy-start.7
  238.7 18.8 %copy-start.29 = (bf16[1024,256]{1,0:T(8,128)(2,1)S(1)}, bf16[1024,256]{1,0:T(8,128)(2,1)}, u32[]{:S(2)}) copy-start(bf16[1024,256]{1,0:T(8,128)(2,1)} %get-tuple-element.108) | copy-start | bytes 1572868
  238.7 20.9 %copy-start.19 = (bf16[1024,256]{1,0:T(8,128)(2,1)S(1)}, bf16[1024,256]{1,0:T(8,128)(2,1)}, u32[]{:S(2)}) copy-start(bf16[1024,256]{1,0:T(8,128)(2,1)} %copy-done.18) | copy-start | bytes 1572868
  238.7 20.9 %collective-permute-start.8 = (bf16[4,64,1152]{2,1,0:T(8,128)(2,1)S(1)}, bf16[4,64,1152]{2,1,0:T(8,128)(2,1)S(1)}, u32[]{:S(2)}, u32[]{:S(2)}) collective-permute-start(bf16[4,64,1152]{2,1,0:T(8,128)(2,1)S(1)} %merge_far.3), channel_id=1, source_target_pairs={{0,16},{2,18},{4,20},{6,22},{8,24},{10,26},{12,28},{14,30},{16,0},... | collective-permute-start | bytes 1769480 | tf_op jit(solution)/shard_map/ppermute | solution.py:577
  241.2 3.3 %collective-permute-start.15 = (bf16[16,1024]{1,0:T(8,128)(2,1)S(1)}, bf16[16,1024]{1,0:T(8,128)(2,1)S(1)}, u32[]{:S(2)}, u32[]{:S(2)}) collective-permute-start(bf16[16,1024]{1,0:T(8,128)(2,1)S(1)} %get-tuple-element.106), channel_id=1, source_target_pairs={{8,6},{16,14},{24,22},{9,7},{17,15},{25,23}} | collective-permute-start | bytes 98312 | tf_op jit(solution)/shard_map/ppermute | solution.py:654
  241.9 10.4 %collective-permute-start.14 = (bf16[16,1024]{1,0:T(8,128)(2,1)S(1)}, bf16[16,1024]{1,0:T(8,128)(2,1)S(1)}, u32[]{:S(2)}, u32[]{:S(2)}) collective-permute-start(bf16[16,1024]{1,0:T(8,128)(2,1)S(1)} %get-tuple-element.106), channel_id=1, source_target_pairs={{8,4},{16,12},{24,20},{9,5},{17,13},{25,21}} | collective-permute-start | bytes 98312 | tf_op jit(solution)/shard_map/ppermute | solution.py:654
  242.6 10.2 %collective-permute-start.13 = (bf16[16,1024]{1,0:T(8,128)(2,1)S(1)}, bf16[16,1024]{1,0:T(8,128)(2,1)S(1)}, u32[]{:S(2)}, u32[]{:S(2)}) collective-permute-start(bf16[16,1024]{1,0:T(8,128)(2,1)S(1)} %get-tuple-element.106), channel_id=1, source_target_pairs={{8,2},{16,10},{24,18},{9,3},{17,11},{25,19}} | collective-permute-start | bytes 98312 | tf_op jit(solution)/shard_map/ppermute | solution.py:654
  243.2 14.3 %collective-permute-start.12 = (bf16[16,1024]{1,0:T(8,128)(2,1)S(1)}, bf16[16,1024]{1,0:T(8,128)(2,1)S(1)}, u32[]{:S(2)}, u32[]{:S(2)}) collective-permute-start(bf16[16,1024]{1,0:T(8,128)(2,1)S(1)} %get-tuple-element.106), channel_id=1, source_target_pairs={{8,0},{16,8},{24,16},{9,1},{17,9},{25,17}} | collective-permute-start | bytes 98312 | tf_op jit(solution)/shard_map/ppermute | solution.py:654
  244.6 46.3 %copy-start.3 = (bf16[2048,256]{1,0:T(8,128)(2,1)S(1)}, bf16[2048,256]{1,0:T(8,128)(2,1)}, u32[]{:S(2)}) copy-start(bf16[2048,256]{1,0:T(8,128)(2,1)} %refs_8_.1) | copy-start | bytes 3145732
  244.6 32.1 %collective-permute-start.11 = (bf16[272,1024]{1,0:T(8,128)(2,1)S(1)}, bf16[272,1024]{1,0:T(8,128)(2,1)S(1)}, u32[]{:S(2)}, u32[]{:S(2)}) collective-permute-start(bf16[272,1024]{1,0:T(8,128)(2,1)S(1)} %get-tuple-element.121.refs_0_), channel_id=1, source_target_pairs={{0,6},{2,4},{4,2},{6,0},{8,14},{10,12},{12,10},{14,8},{16,22},{18,... | collective-permute-start | bytes 1671176 | tf_op jit(solution)/shard_map/ppermute | solution.py:571
  252.3 24.4 %collective-permute-start.10 = (bf16[272,1024]{1,0:T(8,128)(2,1)S(1)}, bf16[272,1024]{1,0:T(8,128)(2,1)S(1)}, u32[]{:S(2)}, u32[]{:S(2)}) collective-permute-start(bf16[272,1024]{1,0:T(8,128)(2,1)S(1)} %get-tuple-element.121.refs_0_), channel_id=1, source_target_pairs={{0,4},{2,6},{4,0},{6,2},{8,12},{10,14},{12,8},{14,10},{16,20},{18,... | collective-permute-start | bytes 1671176 | tf_op jit(solution)/shard_map/ppermute | solution.py:571
  252.8 24.0 %collective-permute-start.9 = (bf16[272,1024]{1,0:T(8,128)(2,1)S(1)}, bf16[272,1024]{1,0:T(8,128)(2,1)S(1)}, u32[]{:S(2)}, u32[]{:S(2)}) collective-permute-start(bf16[272,1024]{1,0:T(8,128)(2,1)S(1)} %get-tuple-element.121.refs_0_), channel_id=1, source_target_pairs={{0,2},{2,0},{4,6},{6,4},{8,10},{10,8},{12,14},{14,12},{16,18},{18,... | collective-permute-start | bytes 1671176 | tf_op jit(solution)/shard_map/ppermute | solution.py:571
  257.5 12.5 %collective-permute-start.17 = (bf16[1024,256]{1,0:T(8,128)(2,1)S(1)}, bf16[1024,256]{1,0:T(8,128)(2,1)S(1)}, u32[]{:S(2)}, u32[]{:S(2)}) collective-permute-start(bf16[1024,256]{1,0:T(8,128)(2,1)S(1)} %copy-done.29), channel_id=1, source_target_pairs={{0,8},{2,10},{4,12},{6,14},{8,0},{10,2},{12,4},{14,6},{16,24},{18,... | collective-permute-start | bytes 1572872 | tf_op jit(solution)/shard_map/ppermute | solution.py:571
  259.6 17.1 %collective-permute-start.16 = (bf16[1024,256]{1,0:T(8,128)(2,1)S(1)}, bf16[1024,256]{1,0:T(8,128)(2,1)S(1)}, u32[]{:S(2)}, u32[]{:S(2)}) collective-permute-start(bf16[1024,256]{1,0:T(8,128)(2,1)S(1)} %copy-done.19), channel_id=1, source_target_pairs={{0,8},{2,10},{4,12},{6,14},{8,0},{10,2},{12,4},{14,6},{16,24},{18,... | collective-permute-start | bytes 1572872 | tf_op jit(solution)/shard_map/ppermute | solution.py:571
  276.7 3.2 copy-start.23
  276.7 3.2 copy-start.12
  276.7 3.2 copy-start.14
  276.7 3.2 copy-start.16
  279.9 3.6 %collective-permute-start.24 = (bf16[16,1024]{1,0:T(8,128)(2,1)S(1)}, bf16[16,1024]{1,0:T(8,128)(2,1)S(1)}, u32[]{:S(2)}, u32[]{:S(2)}) collective-permute-start(bf16[16,1024]{1,0:T(8,128)(2,1)S(1)} %get-tuple-element.117), channel_id=1, source_target_pairs={{8,6},{16,14},{24,22},{9,7},{17,15},{25,23}} | collective-permute-start | bytes 98312 | tf_op jit(solution)/shard_map/ppermute | solution.py:654
  280.6 3.0 collective-permute-start.23
  281.3 6.4 %collective-permute-start.22 = (bf16[16,1024]{1,0:T(8,128)(2,1)S(1)}, bf16[16,1024]{1,0:T(8,128)(2,1)S(1)}, u32[]{:S(2)}, u32[]{:S(2)}) collective-permute-start(bf16[16,1024]{1,0:T(8,128)(2,1)S(1)} %get-tuple-element.117), channel_id=1, source_target_pairs={{8,2},{16,10},{24,18},{9,3},{17,11},{25,19}} | collective-permute-start | bytes 98312 | tf_op jit(solution)/shard_map/ppermute | solution.py:654
  282.0 8.8 %collective-permute-start.21 = (bf16[16,1024]{1,0:T(8,128)(2,1)S(1)}, bf16[16,1024]{1,0:T(8,128)(2,1)S(1)}, u32[]{:S(2)}, u32[]{:S(2)}) collective-permute-start(bf16[16,1024]{1,0:T(8,128)(2,1)S(1)} %get-tuple-element.117), channel_id=1, source_target_pairs={{8,0},{16,8},{24,16},{9,1},{17,9},{25,17}} | collective-permute-start | bytes 98312 | tf_op jit(solution)/shard_map/ppermute | solution.py:654
  283.4 21.1 %collective-permute-start.20 = (bf16[272,1024]{1,0:T(8,128)(2,1)}, bf16[272,1024]{1,0:T(8,128)(2,1)S(1)}, u32[]{:S(2)}, u32[]{:S(2)}) collective-permute-start(bf16[272,1024]{1,0:T(8,128)(2,1)} %get-tuple-element.116.refs_0_), channel_id=1, source_target_pairs={{0,6},{2,4},{4,2},{6,0},{8,14},{10,12},{12,10},{14,8},{16,22},{18,... | collective-permute-start | bytes 1671176 | tf_op jit(solution)/shard_map/ppermute | solution.py:571
  283.5 21.1 %collective-permute-start.19 = (bf16[272,1024]{1,0:T(8,128)(2,1)}, bf16[272,1024]{1,0:T(8,128)(2,1)S(1)}, u32[]{:S(2)}, u32[]{:S(2)}) collective-permute-start(bf16[272,1024]{1,0:T(8,128)(2,1)} %get-tuple-element.116.refs_0_), channel_id=1, source_target_pairs={{0,4},{2,6},{4,0},{6,2},{8,12},{10,14},{12,8},{14,10},{16,20},{18,... | collective-permute-start | bytes 1671176 | tf_op jit(solution)/shard_map/ppermute | solution.py:571
  283.6 21.0 %collective-permute-start.18 = (bf16[272,1024]{1,0:T(8,128)(2,1)}, bf16[272,1024]{1,0:T(8,128)(2,1)S(1)}, u32[]{:S(2)}, u32[]{:S(2)}) collective-permute-start(bf16[272,1024]{1,0:T(8,128)(2,1)} %get-tuple-element.116.refs_0_), channel_id=1, source_target_pairs={{0,2},{2,0},{4,6},{6,4},{8,10},{10,8},{12,14},{14,12},{16,18},{18,... | collective-permute-start | bytes 1671176 | tf_op jit(solution)/shard_map/ppermute | solution.py:571
  287.7 14.1 %collective-permute-start.25 = (bf16[1024,256]{1,0:T(8,128)(2,1)}, bf16[1024,256]{1,0:T(8,128)(2,1)S(1)}, u32[]{:S(2)}, u32[]{:S(2)}) collective-permute-start(bf16[1024,256]{1,0:T(8,128)(2,1)} %get-tuple-element.119), channel_id=1, source_target_pairs={{0,8},{2,10},{4,12},{6,14},{8,0},{10,2},{12,4},{14,6},{16,24},{18,... | collective-permute-start | bytes 1572872 | tf_op jit(solution)/shard_map/ppermute | solution.py:571
  290.8 13.8 %collective-permute-start.26 = (bf16[1024,256]{1,0:T(8,128)(2,1)}, bf16[1024,256]{1,0:T(8,128)(2,1)}, u32[]{:S(2)}, u32[]{:S(2)}) collective-permute-start(bf16[1024,256]{1,0:T(8,128)(2,1)} %collective-permute-done.6.refs_10_), channel_id=1, source_target_pairs={{0,8},{2,10},{4,12},{6,14},{8,0},{10,2},{12,4},{14,6},{16,24},{18,... | collective-permute-start | bytes 1572872 | tf_op jit(solution)/shard_map/ppermute | solution.py:571
  290.9 1.1 copy-start.11
  291.9 1.1 copy-start.13
  293.0 1.1 copy-start.15
  294.1 1.1 copy-start.17
  295.1 1.0 copy-start.20
  296.2 1.0 copy-start.22
  297.2 1.0 copy-start.24
  308.7 18.1 %copy-start.4 = (s32[128,4096]{1,0:T(8,128)S(1)}, s32[128,4096]{1,0:T(8,128)}, u32[]{:S(2)}) copy-start(s32[128,4096]{1,0:T(8,128)} %refs_5_.1) | copy-start | bytes 6291460
  308.7 18.1 %copy-start.8 = (f32[4096]{0:T(1024)S(1)}, f32[4096]{0:T(1024)}, u32[]{:S(2)}) copy-start(f32[4096]{0:T(1024)} %param.16) | copy-start | bytes 49156
  308.7 18.1 %copy-start.9 = (f32[4096]{0:T(1024)S(1)}, f32[4096]{0:T(1024)}, u32[]{:S(2)}) copy-start(f32[4096]{0:T(1024)} %param.17) | copy-start | bytes 49156
  308.7 2.7 collective-permute-start.27
  312.6 9.4 %collective-permute-start.28 = (bf16[128,1024]{1,0:T(8,128)(2,1)}, bf16[128,1024]{1,0:T(8,128)(2,1)S(1)}, u32[]{:S(2)}, u32[]{:S(2)}) collective-permute-start(bf16[128,1024]{1,0:T(8,128)(2,1)} %get-tuple-element.137), channel_id=1, source_target_pairs={{0,2},{2,0},{4,6},{6,4},{8,10},{10,8},{12,14},{14,12},{16,18},{18,... | collective-permute-start | bytes 786440 | tf_op jit(solution)/shard_map/ppermute | solution.py:571
  312.6 14.2 %collective-permute-start.29 = (bf16[128,1024]{1,0:T(8,128)(2,1)}, bf16[128,1024]{1,0:T(8,128)(2,1)S(1)}, u32[]{:S(2)}, u32[]{:S(2)}) collective-permute-start(bf16[128,1024]{1,0:T(8,128)(2,1)} %get-tuple-element.138), channel_id=1, source_target_pairs={{0,4},{2,6},{4,0},{6,2},{8,12},{10,14},{12,8},{14,10},{16,20},{18,... | collective-permute-start | bytes 786440 | tf_op jit(solution)/shard_map/ppermute | solution.py:571
  312.8 14.0 %collective-permute-start.30 = (bf16[128,1024]{1,0:T(8,128)(2,1)S(1)}, bf16[128,1024]{1,0:T(8,128)(2,1)S(1)}, u32[]{:S(2)}, u32[]{:S(2)}) collective-permute-start(bf16[128,1024]{1,0:T(8,128)(2,1)S(1)} %get-tuple-element.139), channel_id=1, source_target_pairs={{0,6},{2,4},{4,2},{6,0},{8,14},{10,12},{12,10},{14,8},{16,22},{18,... | collective-permute-start | bytes 786440 | tf_op jit(solution)/shard_map/ppermute | solution.py:571
  326.8 1.2 copy-start.5
  (4 other events, 3.1 us)

commit v5 on v4

--- a/solution.py
+++ b/solution.py
@@ -87,7 +87,7 @@
         ),
         out_shape=jax.ShapeDtypeStruct((peers, span_len, whole), carried.dtype),
         input_output_aliases={3 + len(pieces): 0} if extra else {},
-        compiler_params=pltpu.CompilerParams(vmem_limit_bytes=60 * MIB),
+        compiler_params=pltpu.CompilerParams(vmem_limit_bytes=(60 if extra else 10) * MIB),
         name="spread_queries",
     )(block_of_peer, slot_of_peer, carried, *pieces, *extra)
 
@@ -186,7 +186,7 @@
         out_ref[0, :, row_width:] = pack_levels(stats, heads).astype(out_ref.dtype)
 
 
-def attend(asked, tags, keys, values, width, chunk, part, size, place, places, shared, weigh):
+def attend(asked, tags, keys, values, width, chunk, part, size, place, places, shared):
     peers, span_len, _ = asked.shape
     length = keys.shape[1]
     heads = width // HEAD
@@ -213,8 +213,8 @@
         input_output_aliases={4: 0} if extra else {},
         compiler_params=pltpu.CompilerParams(vmem_limit_bytes=58 * MIB),
         cost_estimate=pl.CostEstimate(
-            flops=4 * weigh * peers * heads * span_len * length * HEAD,
-            bytes_accessed=2 * weigh * peers * width * (2 * span_len + 2 * length),
+            flops=4 * peers * heads * span_len * length * HEAD,
+            bytes_accessed=2 * peers * width * (2 * span_len + 2 * length),
             transcendentals=peers * heads * span_len * length,
         ),
         name="attend_blocks",
@@ -261,7 +261,7 @@
         out_ref[0, :, cut] = merged.astype(out_ref.dtype)
 
 
-def merge_all_kernel(picked, index_ref, use_ref, *refs):
+def merge_all_kernel(picked, earlier, index_ref, use_ref, *refs):
     parts = refs[: picked + 1]
     out_ref, first_ref, kept = refs[-3:]
     span_len = parts[0].shape[1]
@@ -272,10 +272,13 @@
     uses = [use_ref[block * picked + r] > 0 for r in range(picked)] + [None]
     start = pl.multiple_of(block * span_len, span_len)
     last = lax.broadcasted_iota(jnp.int32, (span_len, HEAD), 0) == span_len - 1
+    at = first_ref.shape[1] - row_width
 
     @pl.when(step == 0)
     def _():
         kept[...] = jnp.zeros_like(kept)
+        if earlier:
+            first_ref[:, :at] = refs[picked + 1][...]
 
     for cut, merged in merge_block(uses, parts):
         if cut.start < row_width:
@@ -285,7 +288,7 @@
             kept[:, cut] = merged[:8]
             first = merged[:ROW_TILE].astype(out_ref.dtype)
             out_ref[rows:, cut] = first
-            first_ref[:, cut] = first
+            first_ref[:, at + cut.start : at + cut.stop] = first
 
 
 def merge_far(parts, column, wide, index, use, blocks):
@@ -312,7 +315,7 @@
     )(index, use, *([parts] * picked))
 
 
-def merge_all(parts, column, wide, index, use, blocks, far):
+def merge_all(parts, column, wide, index, use, blocks, far, earlier=None):
     span_len = parts.shape[1]
     row_width = wide - LANES
     picked = index.shape[0] // blocks
@@ -327,31 +330,35 @@
         for r in range(picked)
     ]
     specs.append(pl.BlockSpec((1, span_len, wide), lambda i, *_: (blocks - 1 - i, 0, 0)))
+    extra = [] if earlier is None else [earlier]
+    first_width = row_width * (1 + len(extra))
+    specs += [pl.BlockSpec((ROW_TILE, row_width), lambda i, *_: (0, 0))] * len(extra)
     return pl.pallas_call(
-        functools.partial(merge_all_kernel, picked),
+        functools.partial(merge_all_kernel, picked, len(extra)),
         grid_spec=pltpu.PrefetchScalarGridSpec(
             num_scalar_prefetch=2,
             grid=(blocks,),
             in_specs=specs,
             out_specs=[
                 pl.BlockSpec((rows + ROW_TILE, row_width), lambda i, *_: (0, 0)),
-                pl.BlockSpec((ROW_TILE, row_width), lambda i, *_: (0, 0)),
+                pl.BlockSpec((ROW_TILE, first_width), lambda i, *_: (0, 0)),
             ],
             scratch_shapes=[pltpu.VMEM((8, row_width), jnp.float32)],
         ),
         out_shape=[
             jax.ShapeDtypeStruct((rows + ROW_TILE, row_width), parts.dtype),
-            jax.ShapeDtypeStruct((ROW_TILE, row_width), parts.dtype),
+            jax.ShapeDtypeStruct((ROW_TILE, first_width), parts.dtype),
         ],
         compiler_params=pltpu.CompilerParams(vmem_limit_bytes=10 * MIB),
         name="merge_all",
-    )(index, use, *([parts] * picked), far)
+    )(index, use, *([parts] * picked), far, *extra)
 
 
 def project_kernel(starts, place_ref, stay_ref, *refs):
-    sources, belows = refs[:PLANE], refs[PLANE : 2 * PLANE]
-    shards = len(starts)
-    weights, before = refs[2 * PLANE : 2 * PLANE + shards], refs[2 * PLANE + shards : -7]
+    sources, refs = refs[:PLANE], refs[PLANE:]
+    last_part = len(starts) > PLANE
+    belows, refs = (refs[:PLANE], refs[PLANE:]) if last_part else ([], refs)
+    weights, before = refs[: len(starts)], refs[len(starts) : -7]
     keep_ref, send_ref, rows_ref, first_ref, held_ref, row_sems, weight_sems = refs[-7:]
     half = keep_ref.shape[0]
     part = half // PLANE
@@ -374,52 +381,71 @@
                 row_sems.at[at, 2],
             )
 
-    def weight_copy(shard):
+    def weight_copy(at):
         return pltpu.make_async_copy(
-            weights[shard].at[pl.ds(starts[shard], width)],
-            held_ref.at[shard],
-            weight_sems.at[shard],
+            weights[at].at[pl.ds(starts[at], width)], held_ref.at[at], weight_sems.at[at]
         )
 
     for copy in source_copies():
         copy.start()
-    for shard in range(shards):
-        weight_copy(shard).start()
+    for at in range(len(starts)):
+        weight_copy(at).start()
     for copy in source_copies():
         copy.wait()
     last = lax.broadcasted_iota(jnp.int32, (ROW_TILE, width), 0) == ROW_TILE - 1
     for member in range(PLANE):
-        if member < PLANE - 1:
-            at = (member + 1) * ROW_TILE
-            below = first_ref[at : at + ROW_TILE].astype(jnp.float32)
-        else:
-            below = functools.reduce(jnp.add, [ref[...].astype(jnp.float32) for ref in belows])
+        at = (member + 1) % PLANE * ROW_TILE
+        below = first_ref[at : at + ROW_TILE].astype(jnp.float32)[0:1]
+        if member == PLANE - 1:
+            below = jnp.zeros_like(below)
         end = half + (member + 1) * part
         held = rows_ref[end - ROW_TILE : end].astype(jnp.float32)
-        rows_ref[end - ROW_TILE : end] = jnp.where(last, below[0:1], held).astype(rows_ref.dtype)
+        rows_ref[end - ROW_TILE : end] = jnp.where(last, below, held).astype(rows_ref.dtype)
+    if last_part:
+        below = functools.reduce(jnp.add, [ref[...].astype(jnp.float32) for ref in belows])
+        below = below.astype(rows_ref.dtype)
     stay = pl.multiple_of(stay_ref[0] * half, half)
     go = pl.multiple_of((1 - stay_ref[0]) * half, half)
-    for shard in range(shards):
+    for shard in range(PLANE):
         weight_copy(shard).wait()
+        if last_part:
+            weight_copy(PLANE + shard).wait()
         cut = slice(shard * tile, (shard + 1) * tile)
         for at, (start, ref) in enumerate(((stay, keep_ref), (go, send_ref))):
             result = jnp.dot(
                 rows_ref[pl.ds(start, half)], held_ref[shard], preferred_element_type=jnp.float32
             )
-            if before:
+            if last_part:
                 result = result + before[at][:, cut]
             ref[:, cut] = result.astype(ref.dtype)
+        if last_part:
+            row = functools.reduce(
+                jnp.add,
+                [
+                    jnp.dot(
+                        below[:, side * width : (side + 1) * width],
+                        held_ref[at],
+                        preferred_element_type=jnp.float32,
+                    )
+                    for side, at in ((0, PLANE + shard), (1, shard))
+                ],
+            )[0:1]
+            at_end = lax.broadcasted_iota(jnp.int32, (ROW_TILE, tile), 0) == ROW_TILE - 1
+            for upper, ref in ((stay_ref[0] > 0, keep_ref), (stay_ref[0] == 0, send_ref)):
+
+                @pl.when(upper)
+                def _():
+                    held = ref[half - ROW_TILE :, cut].astype(jnp.float32)
+                    ref[half - ROW_TILE :, cut] = jnp.where(at_end, row, held).astype(ref.dtype)
 
 
 def project(sources, belows, weights, place, stay, before, kind):
     height, width = sources[0].shape
     rows = PLANE * (height - ROW_TILE)
-    shards = len(weights)
     starts = [start for _, start in weights]
     tile = weights[0][0].shape[1]
-    columns = shards * tile
+    columns = PLANE * tile
     half = rows // 2
-    row_spec = pl.BlockSpec((ROW_TILE, width), lambda i, *_: (0, 0))
     half_spec = pl.BlockSpec((half, columns), lambda i, *_: (0, 0))
     return pl.pallas_call(
         functools.partial(project_kernel, starts),
@@ -427,20 +453,20 @@
             num_scalar_prefetch=2,
             grid=(1,),
             in_specs=[pl.BlockSpec(memory_space=pl.ANY)] * PLANE
-            + [row_spec] * PLANE
-            + [pl.BlockSpec(memory_space=pl.ANY)] * shards
+            + [pl.BlockSpec(row.shape, lambda i, *_: (0, 0)) for row in belows]
+            + [pl.BlockSpec(memory_space=pl.ANY)] * len(starts)
             + [half_spec] * len(before),
             out_specs=[half_spec] * 2,
             scratch_shapes=[
                 pltpu.VMEM((rows, width), sources[0].dtype),
                 pltpu.VMEM((PLANE * ROW_TILE, width), sources[0].dtype),
-                pltpu.VMEM((shards, width, tile), sources[0].dtype),
+                pltpu.VMEM((len(starts), width, tile), sources[0].dtype),
                 pltpu.SemaphoreType.DMA((PLANE, 3)),
-                pltpu.SemaphoreType.DMA((shards,)),
+                pltpu.SemaphoreType.DMA((len(starts),)),
             ],
         ),
         out_shape=[jax.ShapeDtypeStruct((half, columns), kind)] * 2,
-        compiler_params=pltpu.CompilerParams(vmem_limit_bytes=28 * MIB),
+        compiler_params=pltpu.CompilerParams(vmem_limit_bytes=30 * MIB),
         cost_estimate=pl.CostEstimate(
             flops=2 * rows * width * columns,
             bytes_accessed=2 * width * (rows + columns) + 8 * rows * columns,
@@ -584,18 +610,19 @@
     owners = neighbour_owner.reshape(-1)
     slot_rows = neighbour_slot.reshape(-1)
     near_peers = base + jnp.arange(half, dtype=jnp.int32)
+    far_carried = lax.ppermute(
+        queries[-1:], "dp", [(i - 1, (i + half) % peer_count) for i in range(1, peer_count)]
+    )
+    requests = owners.shape[0]
+    far_table = to_partner(
+        jnp.pad(jnp.concatenate([owners, slot_rows]), (0, LANES - 2 * requests))[None, :]
+    )
+    carried, far_carried, far_table = pinned(carried, far_carried, far_table)
     near_out = spread(
         [queries], carried, *pick_requests(owners, slot_rows, near_peers, per_block),
         span_len, 0,
     )
     near_asked = exchange(near_out)
-    far_carried = lax.ppermute(
-        queries[-1:], "dp", [(i - 1, (i + half) % peer_count) for i in range(1, peer_count)]
-    )
-    requests = owners.shape[0]
-    far_table = to_partner(
-        jnp.pad(jnp.concatenate([owners, slot_rows]), (0, LANES - 2 * requests))[None, :]
-    )
     far_first, far_carried, far_table, second, weight, _ = pinned(
         far_first, far_carried, far_table, queries[:, width:], out_weight, near_out
     )
@@ -604,10 +631,10 @@
         far_owners, far_table[0, requests : 2 * requests], near_peers, per_block
     )
 
-    def answer(asked, tags, chunk, part, size, place, places, shared=None, weigh=1):
+    def answer(asked, tags, chunk, part, size, place, places, shared=None):
         return attend(
             asked, tags, neighbour_keys, neighbour_values, width, chunk, part, size,
-            place, places, shared, weigh,
+            place, places, shared,
         )
 
     wide = width + LANES
@@ -630,64 +657,62 @@
     mixed = spread([far_second], far_carried, *far_picked, span_len, 1, near_first)
     next_asked = exchange(mixed)
     far_weight = [to_partner(weight_halves[0])] if by_plane else []
-    tags, near_second, _, *far_weight = pinned(far_asked, near_second, mixed, *far_weight)
-    mixed = answer(tags, tags, 0, 0, wide, 0, 2, near_second, weigh=16)
-    mixed, next_asked, weight_half = pinned(mixed, next_asked, weight_halves[1])
+    tags, near_second, _ = pinned(far_asked, near_second, mixed)
+    mixed = answer(tags, tags, 0, 0, wide, 0, 2, near_second)
+    mixed, next_asked, weight_half, *far_weight = pinned(
+        mixed, next_asked, weight_halves[1], *far_weight
+    )
 
     far_back = exchange(mixed)
     if by_plane:
         far_weight.append(to_partner(weight_half))
-    next_asked, *far_weight = pinned(next_asked, *far_weight)
-    far_parts = answer(next_asked, tags, 1, 1, wide, 0, 1, weigh=16)
-    far_back, far_parts = pinned(far_back, far_parts)
+    far_parts = answer(next_asked, tags, 1, 1, wide, 0, 1)
+    far_back, far_parts, *far_weight = pinned(far_back, far_parts, *far_weight)
     near_back, next_back = next_asked, far_back
 
     far_merged = merge_far(far_back, 0, wide, far_index, far_use, blocks)
     far_home = to_partner(far_merged)
     far_back = exchange(far_parts)
-    far_home, far_back, *far_weight = pinned(far_home, far_back, *far_weight)
-
-    def to_plane(moved, first):
-        if not by_plane:
-            return [moved, first]
-        down = [
+    far_home, far_back, weight, *far_weight = pinned(far_home, far_back, weight, *far_weight)
+
+    def to_plane(moved):
+        return [moved] + [swap(moved, by) for by in range(1, PLANE)] if by_plane else [moved]
+
+    far_merged = merge_far(far_back, 0, wide, far_index, far_use, blocks)
+    far_home, near_back, far_merged, weight, *far_weight = pinned(
+        far_home, near_back, far_merged, weight, *far_weight
+    )
+    next_home = to_partner(far_merged)
+    moved, first = merge_all(near_back, 0, wide, near_index, near_use, blocks, far_home)
+    sources = to_plane(moved)
+    swaps = [swap(weight, PLANE)] if by_plane else []
+    count = len(sources)
+    (next_home,) = pinned(next_home)
+    next_home, next_back, *held = pinned(next_home, next_back, *sources, *swaps, *far_weight)
+    sources, held = held[:count], held[count:]
+    moved, first = merge_all(
+        next_back, 1, wide, near_index, near_use, blocks, next_home, first
+    )
+    if by_plane:
+        place = lax.rem(here, PLANE).reshape(1)
+        stay = lax.axis_index("tensor").astype(jnp.int32).reshape(1)
+        near_swap, *far_weight = held
+        moved, first, *far_weight = pinned(moved, first, *far_weight)
+        next_sources = to_plane(moved)
+        far_swap = [swap(piece, PLANE) for piece in far_weight]
+        belows = [
             lax.ppermute(
                 first, "dp", [(i + PLANE, i + at) for i in range(0, peer_count - PLANE, PLANE)]
             )
             for at in range(PLANE)
         ]
-        return [moved] + [swap(moved, by) for by in range(1, PLANE)] + down
-
-    far_merged = merge_far(far_back, 0, wide, far_index, far_use, blocks)
-    far_home, near_back, far_merged, near_half, *far_weight = pinned(
-        far_home, near_back, far_merged, weight_halves[0], *far_weight
-    )
-    next_home = to_partner(far_merged)
-    sources = to_plane(*merge_all(near_back, 0, wide, near_index, near_use, blocks, far_home))
-    swaps = [swap(far_weight[0], PLANE), swap(near_half, PLANE)] if by_plane else []
-    count = len(sources)
-    (next_home,) = pinned(next_home)
-    next_home, next_back, weight_half, *held = pinned(
-        next_home, next_back, weight_halves[1], *sources, *swaps, *far_weight
-    )
-    sources, held = held[:count], held[count:]
-    moved, first = merge_all(next_back, 1, wide, near_index, near_use, blocks, next_home)
-    if by_plane:
-        place = lax.rem(here, PLANE).reshape(1)
-        stay = lax.axis_index("tensor").astype(jnp.int32).reshape(1)
-        far_swap, near_swap, *far_weight = held
-        moved, first, weight_half, far_half = pinned(moved, first, weight_half, far_weight[1])
-        next_sources = to_plane(moved, first)
-        near_next, far_next = swap(weight_half, PLANE), swap(far_half, PLANE)
-        done = project(
-            sources[:PLANE], sources[PLANE:],
-            [(weight, 0), (near_swap, 0), (far_weight[0], 0), (far_swap, 0)],
-            place, stay, [], jnp.float32,
-        )
+        first_weights = [(weight, 0), (near_swap, 0), (far_weight[0], 0), (far_swap[0], 0)]
+        next_weights = [
+            (weight, middle), (near_swap, middle), (far_weight[1], 0), (far_swap[1], 0)
+        ]
+        done = project(sources, [], first_weights, place, stay, [], jnp.float32)
         keep, send = project(
-            next_sources[:PLANE], next_sources[PLANE:],
-            [(weight, middle), (near_next, 0), (far_half, 0), (far_next, 0)],
-            place, stay, done, moved.dtype,
+            next_sources, belows, next_weights + first_weights, place, stay, done, moved.dtype
         )
         line = jnp.stack(
             [here // PLANE, (here ^ PLANE) // PLANE, partner // PLANE, (partner ^ PLANE) // PLANE]
@@ -697,7 +722,7 @@
     else:
         whole_weight = lax.all_gather(out_weight, "dp", axis=1, tiled=True)
         moved = jnp.concatenate([sources[0], moved], axis=1)
-        below = shifted(jnp.concatenate([sources[1], first], axis=1)[:1], "dp", -1)
+        below = shifted(first[:1], "dp", -1)
         cross_rows = jnp.concatenate([moved[: rows - 1], below], axis=0)
         branch = jnp.dot(cross_rows, whole_weight, preferred_element_type=jnp.float32)
         branches = [

time: 333 us -> 321 us (0.964)
  starting transfers between devices: 85.9 us -> 63.9 us
  Pallas kernels: 58.7 us -> 65.9 us
  waiting for transfers between devices: 166 us -> 171 us
    all_to_all x5, starting transfers between devices: 36.1 us -> 23.1 us  [exchange(): lax.all_to_all(x, 'dp', split_axis=0, concat_axis=0, tiled=True, axis_ind...]
    ppermute x13 -> x12, waiting for transfers between devices: 29.6 us -> 17.6 us  [swap(): return lax.ppermute(x, 'dp', [(i, i ^ by) for i in range(peer_count)])]
    ppermute x8 -> x4, waiting for transfers between devices: 0.02 us -> 9.51 us  [local(): lax.ppermute(first, 'dp', [(i + PLANE, i + at) for i in range(0, peer_cou...]
    ppermute x13 -> x12, starting transfers between devices: 25.2 us -> 16 us  [swap(): return lax.ppermute(x, 'dp', [(i, i ^ by) for i in range(peer_count)])]
    pallas_call x4, Pallas kernels: 27.2 us -> 36.1 us  [attend(): pl.pallas_call(functools.partial(attend_kernel, chunk), grid=(peers,), in...]
    ppermute x7, waiting for transfers between devices: 128 us -> 134 us  [to_partner(): return lax.ppermute(x, 'dp', across)]
    all_to_all x5, waiting for transfers between devices: 1.97 us -> 6.34 us  [exchange(): lax.all_to_all(x, 'dp', split_axis=0, concat_axis=0, tiled=True, axis_ind...]
    ppermute x1, waiting for transfers between devices: 4.03 us -> 0.01 us  [local(): lax.ppermute(queries[-1:], 'dp', [(i - 1, (i + half) % peer_count) for i...]
  transfers between devices with their start and end apart: 36 -> 31, of which waited for: 13 -> 15; matrix products, arithmetic and copies ran while one was open for 2% -> 1% of each run, Pallas kernels for 12% -> 14%
where the time goes in v5:
time: 321 us; the launch traced here: 319 us
  waiting for transfers between devices  171 us (53%)
  Pallas kernels  65.9 us (21%)
  starting transfers between devices  63.9 us (20%)
  local copies, waits for them, and re-layouts  17.1 us (5%)
    ppermute x7, waiting for transfers between devices, to_partner(): return lax.ppermute(x, 'dp', across)  134 us
    pallas_call x4, Pallas kernels, attend(): pl.pallas_call(functools.partial(attend_kernel, chunk), grid=(peers,), in...  36.1 us
    all_to_all x5, starting transfers between devices, exchange(): lax.all_to_all(x, 'dp', split_axis=0, concat_axis=0, tiled=True, axis_ind...  23.1 us
    ppermute x12, waiting for transfers between devices, swap(): return lax.ppermute(x, 'dp', [(i, i ^ by) for i in range(peer_count)])  17.6 us
    ppermute x12, starting transfers between devices, swap(): return lax.ppermute(x, 'dp', [(i, i ^ by) for i in range(peer_count)])  16 us
    unnamed x58, local copies, waits for them, and re-layouts  14.2 us
    ppermute x7, starting transfers between devices, to_partner(): return lax.ppermute(x, 'dp', across)  11.3 us
    ppermute x4, waiting for transfers between devices, local(): lax.ppermute(first, 'dp', [(i + PLANE, i + at) for i in range(0, peer_cou...  9.51 us
  transfers between devices with their start and end apart: 31, of which 15 were waited for; matrix products, arithmetic and copies ran while one was open for 1% of the time, Pallas kernels for 14%

profile of v5, /device:TPU:0, one launch (start us, length us, event | category | flops | bytes accessed | tf_op | source)
XLA Modules:
  0.0 319.1 jit_solution(9167053558085765009)
XLA Ops:
  0.6 0.8 slice.23
  1.4 4.8 %collective-permute-start.1 = (bf16[1,2048]{1,0:T(2,128)(2,1)S(1)}, bf16[1,2048]{1,0:T(2,128)(2,1)S(1)}, u32[]{:S(2)}, u32[]{:S(2)}) collective-permute-start(bf16[1,2048]{1,0:T(2,128)(2,1)S(1)} %slice.23), channel_id=1, source_target_pairs={{0,2},{2,4},{4,6},{6,8},{8,10},{10,12},{12,14},{14,16},{16,18},{18... | collective-permute-start | bytes 12296 | tf_op jit(solution)/shard_map/ppermute | solution.py:23
  6.3 5.4 %collective-permute-start.2 = (bf16[1,2048]{1,0:T(2,128)(2,1)S(1)}, bf16[1,2048]{1,0:T(2,128)(2,1)S(1)}, u32[]{:S(2)}, u32[]{:S(2)}) collective-permute-start(bf16[1,2048]{1,0:T(2,128)(2,1)S(1)} %slice.23), channel_id=1, source_target_pairs={{0,18},{2,20},{4,22},{6,24},{8,26},{10,28},{12,30},{14,0},{16,2},{... | collective-permute-start | bytes 12296 | tf_op jit(solution)/shard_map/ppermute | solution.py:613
  14.0 3.9 %collective-permute-done.3 = s32[1,128]{1,0:T(1,128)S(1)} collective-permute-done((s32[1,128]{1,0:T(1,128)S(1)}, s32[1,128]{1,0:T(1,128)S(1)}, u32[]{:S(2)}, u32[]{:S(2)}) %collective-permute-start.3) | collective-permute-done | bytes 544 | tf_op jit(solution)/shard_map/ppermute | solution.py:603
  17.9 1.2 copy-done.4
  19.2 2.3 spread_queries.3
  21.5 3.9 %all-to-all-start.1 = ((bf16[8,64,2176]{2,1,0:T(8,128)(2,1)}), bf16[8,64,2176]{2,1,0:T(8,128)(2,1)S(1)}, u32[]{:S(2)}, u32[]{:S(2)}) async-start(bf16[8,64,2176]{2,1,0:T(8,128)(2,1)} %spread_queries.3), calls=%async_computation.1 | async-start | bytes 4456448 | tf_op jit(solution)/shard_map/all_to_all | solution.py:592
  25.4 0.9 fusion.7
  26.7 32.5 %collective-permute-done.refs_0_ = bf16[256,1024]{1,0:T(8,128)(2,1)S(1)} collective-permute-done((bf16[256,1024]{1,0:T(8,128)(2,1)S(1)}, bf16[256,1024]{1,0:T(8,128)(2,1)S(1)}, u32[]{:S(2)}, u32[]{:S(2)}) %collective-permute-start) | collective-permute-done | bytes 524320 | tf_op jit(solution)/shard_map/ppermute | solution.py:603
  59.4 1.8 spread_queries.4
  61.3 6.0 %all-to-all-start = ((bf16[8,64,1152]{2,1,0:T(8,128)(2,1)}), bf16[8,64,1152]{2,1,0:T(8,128)(2,1)}, u32[]{:S(2)}, u32[]{:S(2)}) async-start(bf16[8,64,1152]{2,1,0:T(8,128)(2,1)} %spread_queries.4), calls=%async_computation | async-start | bytes 2359296 | tf_op jit(solution)/shard_map/all_to_all | solution.py:592
  67.3 1.7 collective-permute-start.4
  69.0 1.1 fusion.6
  70.1 7.8 %attend_blocks.4.refs_1_ = bf16[8,64,2304]{2,1,0:T(8,128)(2,1)} custom-call(bf16[8,64,2176]{2,1,0:T(8,128)(2,1)} %copy-done.25, bf16[8,64,2176]{2,1,0:T(8,128)(2,1)} %copy-done.25, bf16[8,128,2048]{2,1,0:T(8,128)(2,1)} %key_ref.7, bf16[8,128,2048]{2,1,0:T(8,128)(2,1)} %value_ref.7), custom_call_target="tpu_custom_call" | custom-call | flops 268435456 | bytes 6291456 | tf_op jit(solution)/shard_map/attend_blocks/pallas_call | solution.py:196
  77.9 7.8 %attend_blocks.5.refs_0_ = bf16[8,64,2304]{2,1,0:T(8,128)(2,1)} custom-call(bf16[8,64,2176]{2,1,0:T(8,128)(2,1)} %copy-done.25, bf16[8,64,2176]{2,1,0:T(8,128)(2,1)} %copy-done.25, bf16[8,128,2048]{2,1,0:T(8,128)(2,1)} %key_ref.7, bf16[8,128,2048]{2,1,0:T(8,128)(2,1)} %value_ref.7), custom_call_target="tpu_custom_call" | custom-call | flops 268435456 | bytes 6291456 | tf_op jit(solution)/shard_map/attend_blocks/pallas_call | solution.py:196
  85.7 3.3 %collective-permute-done.4.refs_0_ = bf16[256,1024]{1,0:T(8,128)(2,1)} collective-permute-done((bf16[256,1024]{1,0:T(8,128)(2,1)}, bf16[256,1024]{1,0:T(8,128)(2,1)}, u32[]{:S(2)}, u32[]{:S(2)}) %collective-permute-start.4) | collective-permute-done | bytes 524320 | tf_op jit(solution)/shard_map/ppermute | solution.py:603
  89.0 2.1 all-to-all-done.tag_ref.query_ref
  91.1 3.1 spread_queries.5
  94.3 5.7 %all-to-all-start.2 = ((bf16[8,64,2304]{2,1,0:T(8,128)(2,1)}), bf16[8,64,2304]{2,1,0:T(8,128)(2,1)S(1)}, u32[]{:S(2)}, u32[]{:S(2)}) async-start(bf16[8,64,2304]{2,1,0:T(8,128)(2,1)} %spread_queries.5), calls=%async_computation.2 | async-start | bytes 4718592 | tf_op jit(solution)/shard_map/all_to_all | solution.py:592
  100.2 10.3 %attend_blocks.6 = bf16[8,64,2304]{2,1,0:T(8,128)(2,1)} custom-call(bf16[8,64,1152]{2,1,0:T(8,128)(2,1)} %all-to-all-done.tag_ref.query_ref, bf16[8,64,1152]{2,1,0:T(8,128)(2,1)} %all-to-all-done.tag_ref.query_ref, bf16[8,128,2048]{2,1,0:T(8,128)(2,1)} %key_ref.7, bf16[8,128,2048]{2,1,0:T(8,128)(2,1)} %value_ref.7, ...), custom_call_target="tpu_custom_call", output_to_operand_aliasing={{}: (4, {})} | custom-call | flops 268435456 | bytes 6291456 | tf_op jit(solution)/shard_map/attend_blocks/pallas_call | solution.py:196
  110.5 23.7 %collective-permute-done.5.refs_6_.refs_14_ = bf16[1024,256]{1,0:T(8,128)(2,1)} collective-permute-done((bf16[1024,256]{1,0:T(8,128)(2,1)S(1)}, bf16[1024,256]{1,0:T(8,128)(2,1)}, u32[]{:S(2)}, u32[]{:S(2)}) %collective-permute-start.5) | collective-permute-done | bytes 524320 | tf_op jit(solution)/shard_map/ppermute | solution.py:603
  134.2 2.1 all-to-all-done.2.query_ref.refs_0_.refs_1_
  136.3 1.5 copy-done
  137.7 3.7 %all-to-all-start.3 = ((bf16[8,64,2304]{2,1,0:T(8,128)(2,1)}), bf16[8,64,2304]{2,1,0:T(8,128)(2,1)S(1)}, u32[]{:S(2)}, u32[]{:S(2)}) async-start(bf16[8,64,2304]{2,1,0:T(8,128)(2,1)} %attend_blocks.6), calls=%async_computation.3 | async-start | bytes 4718592 | tf_op jit(solution)/shard_map/all_to_all | solution.py:592
  141.4 1.7 collective-permute-start.6
  143.1 10.2 %attend_blocks.7 = bf16[8,64,1152]{2,1,0:T(8,128)(2,1)} custom-call(bf16[8,64,1152]{2,1,0:T(8,128)(2,1)} %all-to-all-done.tag_ref.query_ref, bf16[8,64,2304]{2,1,0:T(8,128)(2,1)} %copy-done, bf16[8,128,2048]{2,1,0:T(8,128)(2,1)} %key_ref.7, bf16[8,128,2048]{2,1,0:T(8,128)(2,1)} %value_ref.7), custom_call_target="tpu_custom_call" | custom-call | flops 268435456 | bytes 6291456 | tf_op jit(solution)/shard_map/attend_blocks/pallas_call | solution.py:196
  153.3 24.3 %collective-permute-done.6.refs_10_ = bf16[1024,256]{1,0:T(8,128)(2,1)} collective-permute-done((bf16[1024,256]{1,0:T(8,128)(2,1)S(1)}, bf16[1024,256]{1,0:T(8,128)(2,1)}, u32[]{:S(2)}, u32[]{:S(2)}) %collective-permute-start.6) | collective-permute-done | bytes 524320 | tf_op jit(solution)/shard_map/ppermute | solution.py:603
  177.6 2.1 all-to-all-done.3.refs_0_.refs_1_
  179.7 3.7 %all-to-all-start.4 = ((bf16[8,64,1152]{2,1,0:T(8,128)(2,1)}), bf16[8,64,1152]{2,1,0:T(8,128)(2,1)S(1)}, u32[]{:S(2)}, u32[]{:S(2)}) async-start(bf16[8,64,1152]{2,1,0:T(8,128)(2,1)} %attend_blocks.7), calls=%async_computation.4 | async-start | bytes 2359296 | tf_op jit(solution)/shard_map/all_to_all | solution.py:592
  183.4 2.1 merge_far.2
  185.5 3.6 %collective-permute-start.7 = (bf16[4,64,1152]{2,1,0:T(8,128)(2,1)S(1)}, bf16[4,64,1152]{2,1,0:T(8,128)(2,1)S(1)}, u32[]{:S(2)}, u32[]{:S(2)}) collective-permute-start(bf16[4,64,1152]{2,1,0:T(8,128)(2,1)S(1)} %merge_far.2), channel_id=1, source_target_pairs={{0,16},{2,18},{4,20},{6,22},{8,24},{10,26},{12,28},{14,30},{16,0},... | collective-permute-start | bytes 1769480 | tf_op jit(solution)/shard_map/ppermute | solution.py:603
  189.1 24.3 %collective-permute-done.7.refs_2_ = bf16[4,64,1152]{2,1,0:T(8,128)(2,1)S(1)} collective-permute-done((bf16[4,64,1152]{2,1,0:T(8,128)(2,1)S(1)}, bf16[4,64,1152]{2,1,0:T(8,128)(2,1)S(1)}, u32[]{:S(2)}, u32[]{:S(2)}) %collective-permute-start.7) | collective-permute-done | bytes 589856 | tf_op jit(solution)/shard_map/ppermute | solution.py:603
  213.4 0.8 copy-done.10
  214.2 1.9 merge_far.3
  216.9 3.4 %collective-permute-start.8 = (bf16[4,64,1152]{2,1,0:T(8,128)(2,1)S(1)}, bf16[4,64,1152]{2,1,0:T(8,128)(2,1)S(1)}, u32[]{:S(2)}, u32[]{:S(2)}) collective-permute-start(bf16[4,64,1152]{2,1,0:T(8,128)(2,1)S(1)} %merge_far.3), channel_id=1, source_target_pairs={{0,16},{2,18},{4,20},{6,22},{8,24},{10,26},{12,28},{14,30},{16,0},... | collective-permute-start | bytes 1769480 | tf_op jit(solution)/shard_map/ppermute | solution.py:603
  220.3 2.4 merge_all.2
  222.7 1.5 collective-permute-start.10
  224.2 1.4 collective-permute-start.11
  226.2 22.6 %collective-permute-done.8.refs_2_ = bf16[4,64,1152]{2,1,0:T(8,128)(2,1)S(1)} collective-permute-done((bf16[4,64,1152]{2,1,0:T(8,128)(2,1)S(1)}, bf16[4,64,1152]{2,1,0:T(8,128)(2,1)S(1)}, u32[]{:S(2)}, u32[]{:S(2)}) %collective-permute-start.8) | collective-permute-done | bytes 589856 | tf_op jit(solution)/shard_map/ppermute | solution.py:603
  248.8 0.8 copy-done.19
  249.6 0.8 copy-done.21
  250.4 0.8 copy-done.23
  251.2 3.2 merge_all.3
  254.4 4.3 %collective-permute-start.21 = (bf16[1024,256]{1,0:T(8,128)(2,1)}, bf16[1024,256]{1,0:T(8,128)(2,1)S(1)}, u32[]{:S(2)}, u32[]{:S(2)}) collective-permute-start(bf16[1024,256]{1,0:T(8,128)(2,1)} %collective-permute-done.5.refs_6_.refs_14_), channel_id=1, source_target_pairs={{0,8},{2,10},{4,12},{6,14},{8,0},{10,2},{12,4},{14,6},{16,24},{18,... | collective-permute-start | bytes 1572872 | tf_op jit(solution)/shard_map/ppermute | solution.py:597
  258.7 1.3 collective-permute-start.16
  261.3 1.5 collective-permute-start.13
  262.9 9.5 %collective-permute-done.16.refs_4_ = bf16[16,2048]{1,0:T(8,128)(2,1)S(1)} collective-permute-done((bf16[16,2048]{1,0:T(8,128)(2,1)S(1)}, bf16[16,2048]{1,0:T(8,128)(2,1)S(1)}, u32[]{:S(2)}, u32[]{:S(2)}) %collective-permute-start.16) | collective-permute-done | bytes 65568 | tf_op jit(solution)/shard_map/ppermute | solution.py:704
  272.4 2.3 collective-permute-start.20
  275.4 1.2 copy-done.7
  276.6 1.1 copy-done.18
  277.7 1.1 copy-done.20
  278.7 1.1 copy-done.22
  279.8 1.1 copy-done.24
  280.9 3.5 %project_rows.2 = (f32[512,1024]{1,0:T(8,128)S(1)}, f32[512,1024]{1,0:T(8,128)S(1)}) custom-call(s32[1]{0:T(128)} %bitcast.place_ref, s32[1]{0:T(128)} %bitcast.5.stay_ref, bf16[272,1024]{1,0:T(8,128)(2,1)S(1)} %copy-done.18, bf16[272,1024]{1,0:T(8,128)(2,1)S(1)} %copy-done.24, bf16[272,1024]{1,0:T(8,128)(2,1)S(1)} %copy-done.20, ...), custom_call_target="tpu_custom_call" | custom-call | flops 2147483648 | bytes 12582912 | tf_op jit(solution)/shard_map/project_rows/pallas_call | solution.py:450
  284.4 6.0 %collective-permute-done.14.refs_2_ = bf16[272,1024]{1,0:T(8,128)(2,1)S(1)} collective-permute-done((bf16[272,1024]{1,0:T(8,128)(2,1)}, bf16[272,1024]{1,0:T(8,128)(2,1)S(1)}, u32[]{:S(2)}, u32[]{:S(2)}) %collective-permute-start.14) | collective-permute-done | bytes 557088 | tf_op jit(solution)/shard_map/ppermute | solution.py:597
  290.4 5.1 %project_rows.3 = (bf16[512,1024]{1,0:T(8,128)(2,1)S(1)}, bf16[512,1024]{1,0:T(8,128)(2,1)S(1)}) custom-call(s32[1]{0:T(128)} %bitcast.place_ref, s32[1]{0:T(128)} %bitcast.5.stay_ref, bf16[272,1024]{1,0:T(8,128)(2,1)} %get-tuple-element.117.refs_0_, bf16[272,1024]{1,0:T(8,128)(2,1)S(1)} %collective-permute-done.13.refs_1_, ...), custom_call_target="tpu_custom_call" | custom-call | flops 2147483648 | bytes 12582912 | tf_op jit(solution)/shard_map/project_rows/pallas_call | solution.py:450
  295.6 2.6 collective-permute-done.22
  298.2 1.2 add_cores.1
  299.4 1.5 collective-permute-start.24
  300.9 2.0 collective-permute-start.25
  303.0 5.8 %collective-permute-done.23.refs_1_ = bf16[128,1024]{1,0:T(8,128)(2,1)S(1)} collective-permute-done((bf16[128,1024]{1,0:T(8,128)(2,1)}, bf16[128,1024]{1,0:T(8,128)(2,1)S(1)}, u32[]{:S(2)}, u32[]{:S(2)}) %collective-permute-start.23) | collective-permute-done | bytes 262176 | tf_op jit(solution)/shard_map/ppermute | solution.py:597
  308.8 5.8 %collective-permute-done.25.refs_3_ = bf16[128,1024]{1,0:T(8,128)(2,1)S(1)} collective-permute-done((bf16[128,1024]{1,0:T(8,128)(2,1)S(1)}, bf16[128,1024]{1,0:T(8,128)(2,1)S(1)}, u32[]{:S(2)}, u32[]{:S(2)}) %collective-permute-start.25) | collective-permute-done | bytes 262176 | tf_op jit(solution)/shard_map/ppermute | solution.py:597
  314.6 1.2 copy-done.9
  315.8 3.3 %add_norm.1 = (bf16[128,4096]{1,0:T(8,128)(2,1)}, bf16[128,4096]{1,0:T(8,128)(2,1)}) custom-call(s32[1]{0:T(128)} %bitcast.place_ref, s32[4]{0:T(128)S(1)} %pad_add_fusion.line_ref, bf16[128,1024]{1,0:T(8,128)(2,1)S(1)} %get-tuple-element.130.refs_0_, bf16[128,1024]{1,0:T(8,128)(2,1)S(1)} %collective-permute-done.23.refs_1_, ...), custom_call_target="tpu_custom_call" | custom-call | tf_op jit(solution)/shard_map/add_norm/pallas_call | solution.py:535
  (88 shorter events, 6.9 us)
Async XLA Ops:
  1.4 16.5 %collective-permute-start.1 = (bf16[1,2048]{1,0:T(2,128)(2,1)S(1)}, bf16[1,2048]{1,0:T(2,128)(2,1)S(1)}, u32[]{:S(2)}, u32[]{:S(2)}) collective-permute-start(bf16[1,2048]{1,0:T(2,128)(2,1)S(1)} %slice.23), channel_id=1, source_target_pairs={{0,2},{2,4},{4,6},{6,8},{8,10},{10,12},{12,14},{14,16},{16,18},{18... | collective-permute-start | bytes 12296 | tf_op jit(solution)/shard_map/ppermute | solution.py:23
  6.3 11.7 %collective-permute-start.2 = (bf16[1,2048]{1,0:T(2,128)(2,1)S(1)}, bf16[1,2048]{1,0:T(2,128)(2,1)S(1)}, u32[]{:S(2)}, u32[]{:S(2)}) collective-permute-start(bf16[1,2048]{1,0:T(2,128)(2,1)S(1)} %slice.23), channel_id=1, source_target_pairs={{0,18},{2,20},{4,22},{6,24},{8,26},{10,28},{12,30},{14,0},{16,2},{... | collective-permute-start | bytes 12296 | tf_op jit(solution)/shard_map/ppermute | solution.py:613
  13.5 4.4 %collective-permute-start.3 = (s32[1,128]{1,0:T(1,128)S(1)}, s32[1,128]{1,0:T(1,128)S(1)}, u32[]{:S(2)}, u32[]{:S(2)}) collective-permute-start(s32[1,128]{1,0:T(1,128)S(1)} %pad_bitcast_fusion), channel_id=1, source_target_pairs={{0,16},{2,18},{4,20},{6,22},{8,24},{10,26},{12,28},{14,30},{16,0},... | collective-permute-start | bytes 1544 | tf_op jit(solution)/shard_map/ppermute | solution.py:603
  17.9 41.5 %copy-start.12 = (bf16[1,2048]{1,0:T(2,128)(2,1)}, bf16[1,2048]{1,0:T(2,128)(2,1)S(1)}, u32[]{:S(2)}) copy-start(bf16[1,2048]{1,0:T(2,128)(2,1)S(1)} %collective-permute-done.2.carried_ref) | copy-start | bytes 12292
  17.9 1.2 copy-start.4
  21.5 3.9 %copy-start.5 = (bf16[256,2048]{1,0:T(8,128)(2,1)S(1)}, bf16[256,2048]{1,0:T(8,128)(2,1)}, u32[]{:S(2)}) copy-start(bf16[256,2048]{1,0:T(8,128)(2,1)} %refs_0_.1) | copy-start | bytes 3145732
  21.5 39.8 %all-to-all-start.1 = ((bf16[8,64,2176]{2,1,0:T(8,128)(2,1)}), bf16[8,64,2176]{2,1,0:T(8,128)(2,1)S(1)}, u32[]{:S(2)}, u32[]{:S(2)}) async-start(bf16[8,64,2176]{2,1,0:T(8,128)(2,1)} %spread_queries.3), calls=%async_computation.1 | async-start | bytes 4456448 | tf_op jit(solution)/shard_map/all_to_all | solution.py:592
  26.3 42.7 %copy-start.2 = (bf16[2048,256]{1,0:T(8,128)(2,1)S(1)}, bf16[2048,256]{1,0:T(8,128)(2,1)}, u32[]{:S(2)}) copy-start(bf16[2048,256]{1,0:T(8,128)(2,1)} %refs_12_) | copy-start | bytes 3145732
  26.3 32.8 %collective-permute-start = (bf16[256,1024]{1,0:T(8,128)(2,1)S(1)}, bf16[256,1024]{1,0:T(8,128)(2,1)S(1)}, u32[]{:S(2)}, u32[]{:S(2)}) collective-permute-start(bf16[256,1024]{1,0:T(8,128)(2,1)S(1)} %get-tuple-element.141), channel_id=1, source_target_pairs={{0,16},{2,18},{4,20},{6,22},{8,24},{10,26},{12,28},{14,30},{16,0},... | collective-permute-start | bytes 1572872 | tf_op jit(solution)/shard_map/ppermute | solution.py:603
  59.4 10.7 %copy-start.15 = (s32[8]{0:T(128)}, s32[8]{0:T(128)S(1)}, u32[]{:S(2)}) copy-start(s32[8]{0:T(128)S(1)} %get-tuple-element.134.slot_ref) | copy-start | bytes 100
  59.4 10.7 %copy-start.16 = (s32[8]{0:T(128)}, s32[8]{0:T(128)S(1)}, u32[]{:S(2)}) copy-start(s32[8]{0:T(128)S(1)} %get-tuple-element.135.block_ref) | copy-start | bytes 100
  61.3 8.8 %copy-start.25 = (bf16[8,64,2176]{2,1,0:T(8,128)(2,1)}, bf16[8,64,2176]{2,1,0:T(8,128)(2,1)S(1)}, u32[]{:S(2)}) copy-start(bf16[8,64,2176]{2,1,0:T(8,128)(2,1)S(1)} %all-to-all-done.1.tag_ref.query_ref) | copy-start | bytes 6684676
  61.3 29.8 %all-to-all-start = ((bf16[8,64,1152]{2,1,0:T(8,128)(2,1)}), bf16[8,64,1152]{2,1,0:T(8,128)(2,1)}, u32[]{:S(2)}, u32[]{:S(2)}) async-start(bf16[8,64,1152]{2,1,0:T(8,128)(2,1)} %spread_queries.4), calls=%async_computation | async-start | bytes 2359296 | tf_op jit(solution)/shard_map/all_to_all | solution.py:592
  67.3 21.7 %collective-permute-start.4 = (bf16[256,1024]{1,0:T(8,128)(2,1)}, bf16[256,1024]{1,0:T(8,128)(2,1)}, u32[]{:S(2)}, u32[]{:S(2)}) collective-permute-start(bf16[256,1024]{1,0:T(8,128)(2,1)} %get-tuple-element.74), channel_id=1, source_target_pairs={{0,16},{2,18},{4,20},{6,22},{8,24},{10,26},{12,28},{14,30},{16,0},... | collective-permute-start | bytes 1572872 | tf_op jit(solution)/shard_map/ppermute | solution.py:603
  94.3 5.7 %copy-start.27 = (bf16[1024,256]{1,0:T(8,128)(2,1)S(1)}, bf16[1024,256]{1,0:T(8,128)(2,1)}, u32[]{:S(2)}) copy-start(bf16[1024,256]{1,0:T(8,128)(2,1)} %get-tuple-element.88) | copy-start | bytes 1572868
  94.3 42.0 %all-to-all-start.2 = ((bf16[8,64,2304]{2,1,0:T(8,128)(2,1)}), bf16[8,64,2304]{2,1,0:T(8,128)(2,1)S(1)}, u32[]{:S(2)}, u32[]{:S(2)}) async-start(bf16[8,64,2304]{2,1,0:T(8,128)(2,1)} %spread_queries.5), calls=%async_computation.2 | async-start | bytes 4718592 | tf_op jit(solution)/shard_map/all_to_all | solution.py:592
  100.0 34.2 %collective-permute-start.5 = (bf16[1024,256]{1,0:T(8,128)(2,1)S(1)}, bf16[1024,256]{1,0:T(8,128)(2,1)}, u32[]{:S(2)}, u32[]{:S(2)}) collective-permute-start(bf16[1024,256]{1,0:T(8,128)(2,1)S(1)} %copy-done.27), channel_id=1, source_target_pairs={{0,16},{2,18},{4,20},{6,22},{8,24},{10,26},{12,28},{14,30},{16,0},... | collective-permute-start | bytes 1572872 | tf_op jit(solution)/shard_map/ppermute | solution.py:603
  110.5 30.9 %copy-start.26 = (bf16[1024,256]{1,0:T(8,128)(2,1)S(1)}, bf16[1024,256]{1,0:T(8,128)(2,1)}, u32[]{:S(2)}) copy-start(bf16[1024,256]{1,0:T(8,128)(2,1)} %get-tuple-element.92) | copy-start | bytes 1572868
  136.3 1.5 copy-start
  137.7 42.0 %all-to-all-start.3 = ((bf16[8,64,2304]{2,1,0:T(8,128)(2,1)}), bf16[8,64,2304]{2,1,0:T(8,128)(2,1)S(1)}, u32[]{:S(2)}, u32[]{:S(2)}) async-start(bf16[8,64,2304]{2,1,0:T(8,128)(2,1)} %attend_blocks.6), calls=%async_computation.3 | async-start | bytes 4718592 | tf_op jit(solution)/shard_map/all_to_all | solution.py:592
  141.4 36.2 %collective-permute-start.6 = (bf16[1024,256]{1,0:T(8,128)(2,1)S(1)}, bf16[1024,256]{1,0:T(8,128)(2,1)}, u32[]{:S(2)}, u32[]{:S(2)}) collective-permute-start(bf16[1024,256]{1,0:T(8,128)(2,1)S(1)} %copy-done.26), channel_id=1, source_target_pairs={{0,16},{2,18},{4,20},{6,22},{8,24},{10,26},{12,28},{14,30},{16,0},... | collective-permute-start | bytes 1572872 | tf_op jit(solution)/shard_map/ppermute | solution.py:603
  179.7 34.5 %all-to-all-start.4 = ((bf16[8,64,1152]{2,1,0:T(8,128)(2,1)}), bf16[8,64,1152]{2,1,0:T(8,128)(2,1)S(1)}, u32[]{:S(2)}, u32[]{:S(2)}) async-start(bf16[8,64,1152]{2,1,0:T(8,128)(2,1)} %attend_blocks.7), calls=%async_computation.4 | async-start | bytes 2359296 | tf_op jit(solution)/shard_map/all_to_all | solution.py:592
  185.5 27.8 %collective-permute-start.7 = (bf16[4,64,1152]{2,1,0:T(8,128)(2,1)S(1)}, bf16[4,64,1152]{2,1,0:T(8,128)(2,1)S(1)}, u32[]{:S(2)}, u32[]{:S(2)}) collective-permute-start(bf16[4,64,1152]{2,1,0:T(8,128)(2,1)S(1)} %merge_far.2), channel_id=1, source_target_pairs={{0,16},{2,18},{4,20},{6,22},{8,24},{10,26},{12,28},{14,30},{16,0},... | collective-permute-start | bytes 1769480 | tf_op jit(solution)/shard_map/ppermute | solution.py:603
  213.4 0.8 copy-start.10
  214.2 6.1 %copy-start.1 = (bf16[8,64,2304]{2,1,0:T(8,128)(2,1)S(1)}, bf16[8,64,2304]{2,1,0:T(8,128)(2,1)}, u32[]{:S(2)}) copy-start(bf16[8,64,2304]{2,1,0:T(8,128)(2,1)} %copy-done) | copy-start | bytes 7077892
  214.2 6.1 %copy-start.11 = (bf16[4,64,1152]{2,1,0:T(8,128)(2,1)S(1)}, bf16[4,64,1152]{2,1,0:T(8,128)(2,1)}, u32[]{:S(2)}) copy-start(bf16[4,64,1152]{2,1,0:T(8,128)(2,1)} %copy-done.10) | copy-start | bytes 1769476
  216.1 35.1 %collective-permute-start.12 = (bf16[2048,256]{1,0:T(8,128)(2,1)}, bf16[2048,256]{1,0:T(8,128)(2,1)S(1)}, u32[]{:S(2)}, u32[]{:S(2)}) collective-permute-start(bf16[2048,256]{1,0:T(8,128)(2,1)} %refs_12_), channel_id=1, source_target_pairs={{0,8},{2,10},{4,12},{6,14},{8,0},{10,2},{12,4},{14,6},{16,24},{18,... | collective-permute-start | bytes 3145736 | tf_op jit(solution)/shard_map/ppermute | solution.py:597
  216.9 31.9 %collective-permute-start.8 = (bf16[4,64,1152]{2,1,0:T(8,128)(2,1)S(1)}, bf16[4,64,1152]{2,1,0:T(8,128)(2,1)S(1)}, u32[]{:S(2)}, u32[]{:S(2)}) collective-permute-start(bf16[4,64,1152]{2,1,0:T(8,128)(2,1)S(1)} %merge_far.3), channel_id=1, source_target_pairs={{0,16},{2,18},{4,20},{6,22},{8,24},{10,26},{12,28},{14,30},{16,0},... | collective-permute-start | bytes 1769480 | tf_op jit(solution)/shard_map/ppermute | solution.py:603
  222.7 31.7 %copy-start.17 = (bf16[272,1024]{1,0:T(8,128)(2,1)}, bf16[272,1024]{1,0:T(8,128)(2,1)S(1)}, u32[]{:S(2)}) copy-start(bf16[272,1024]{1,0:T(8,128)(2,1)S(1)} %get-tuple-element.122.refs_0_) | copy-start | bytes 1671172
  222.7 26.1 %collective-permute-start.10 = (bf16[272,1024]{1,0:T(8,128)(2,1)S(1)}, bf16[272,1024]{1,0:T(8,128)(2,1)S(1)}, u32[]{:S(2)}, u32[]{:S(2)}) collective-permute-start(bf16[272,1024]{1,0:T(8,128)(2,1)S(1)} %get-tuple-element.122.refs_0_), channel_id=1, source_target_pairs={{0,4},{2,6},{4,0},{6,2},{8,12},{10,14},{12,8},{14,10},{16,20},{18,... | collective-permute-start | bytes 1671176 | tf_op jit(solution)/shard_map/ppermute | solution.py:597
  224.2 25.4 %collective-permute-start.11 = (bf16[272,1024]{1,0:T(8,128)(2,1)S(1)}, bf16[272,1024]{1,0:T(8,128)(2,1)S(1)}, u32[]{:S(2)}, u32[]{:S(2)}) collective-permute-start(bf16[272,1024]{1,0:T(8,128)(2,1)S(1)} %get-tuple-element.122.refs_0_), channel_id=1, source_target_pairs={{0,6},{2,4},{4,2},{6,0},{8,14},{10,12},{12,10},{14,8},{16,22},{18,... | collective-permute-start | bytes 1671176 | tf_op jit(solution)/shard_map/ppermute | solution.py:597
  225.7 24.8 %collective-permute-start.9 = (bf16[272,1024]{1,0:T(8,128)(2,1)S(1)}, bf16[272,1024]{1,0:T(8,128)(2,1)S(1)}, u32[]{:S(2)}, u32[]{:S(2)}) collective-permute-start(bf16[272,1024]{1,0:T(8,128)(2,1)S(1)} %get-tuple-element.122.refs_0_), channel_id=1, source_target_pairs={{0,2},{2,0},{4,6},{6,4},{8,10},{10,8},{12,14},{14,12},{16,18},{18,... | collective-permute-start | bytes 1671176 | tf_op jit(solution)/shard_map/ppermute | solution.py:597
  248.8 0.8 copy-start.19
  249.6 0.8 copy-start.21
  250.4 0.8 copy-start.23
  251.2 3.2 copy-start.6
  251.2 24.2 %copy-start.3 = (bf16[2048,256]{1,0:T(8,128)(2,1)S(1)}, bf16[2048,256]{1,0:T(8,128)(2,1)}, u32[]{:S(2)}) copy-start(bf16[2048,256]{1,0:T(8,128)(2,1)} %refs_12_) | copy-start | bytes 3145732
  254.4 20.3 %collective-permute-start.21 = (bf16[1024,256]{1,0:T(8,128)(2,1)}, bf16[1024,256]{1,0:T(8,128)(2,1)S(1)}, u32[]{:S(2)}, u32[]{:S(2)}) collective-permute-start(bf16[1024,256]{1,0:T(8,128)(2,1)} %collective-permute-done.5.refs_6_.refs_14_), channel_id=1, source_target_pairs={{0,8},{2,10},{4,12},{6,14},{8,0},{10,2},{12,4},{14,6},{16,24},{18,... | collective-permute-start | bytes 1572872 | tf_op jit(solution)/shard_map/ppermute | solution.py:597
  258.7 13.7 %collective-permute-start.16 = (bf16[16,2048]{1,0:T(8,128)(2,1)S(1)}, bf16[16,2048]{1,0:T(8,128)(2,1)S(1)}, u32[]{:S(2)}, u32[]{:S(2)}) collective-permute-start(bf16[16,2048]{1,0:T(8,128)(2,1)S(1)} %get-tuple-element.118), channel_id=1, source_target_pairs={{8,0},{16,8},{24,16},{9,1},{17,9},{25,17}} | collective-permute-start | bytes 196616 | tf_op jit(solution)/shard_map/ppermute | solution.py:704
  260.0 12.4 %collective-permute-start.17 = (bf16[16,2048]{1,0:T(8,128)(2,1)S(1)}, bf16[16,2048]{1,0:T(8,128)(2,1)S(1)}, u32[]{:S(2)}, u32[]{:S(2)}) collective-permute-start(bf16[16,2048]{1,0:T(8,128)(2,1)S(1)} %get-tuple-element.118), channel_id=1, source_target_pairs={{8,2},{16,10},{24,18},{9,3},{17,11},{25,19}} | collective-permute-start | bytes 196616 | tf_op jit(solution)/shard_map/ppermute | solution.py:704
  260.7 11.7 %collective-permute-start.18 = (bf16[16,2048]{1,0:T(8,128)(2,1)S(1)}, bf16[16,2048]{1,0:T(8,128)(2,1)S(1)}, u32[]{:S(2)}, u32[]{:S(2)}) collective-permute-start(bf16[16,2048]{1,0:T(8,128)(2,1)S(1)} %get-tuple-element.118), channel_id=1, source_target_pairs={{8,4},{16,12},{24,20},{9,5},{17,13},{25,21}} | collective-permute-start | bytes 196616 | tf_op jit(solution)/shard_map/ppermute | solution.py:704
  261.3 23.0 %collective-permute-start.13 = (bf16[272,1024]{1,0:T(8,128)(2,1)}, bf16[272,1024]{1,0:T(8,128)(2,1)S(1)}, u32[]{:S(2)}, u32[]{:S(2)}) collective-permute-start(bf16[272,1024]{1,0:T(8,128)(2,1)} %get-tuple-element.117.refs_0_), channel_id=1, source_target_pairs={{0,2},{2,0},{4,6},{6,4},{8,10},{10,8},{12,14},{14,12},{16,18},{18,... | collective-permute-start | bytes 1671176 | tf_op jit(solution)/shard_map/ppermute | solution.py:597
  272.4 18.0 %collective-permute-start.14 = (bf16[272,1024]{1,0:T(8,128)(2,1)}, bf16[272,1024]{1,0:T(8,128)(2,1)S(1)}, u32[]{:S(2)}, u32[]{:S(2)}) collective-permute-start(bf16[272,1024]{1,0:T(8,128)(2,1)} %get-tuple-element.117.refs_0_), channel_id=1, source_target_pairs={{0,4},{2,6},{4,0},{6,2},{8,12},{10,14},{12,8},{14,10},{16,20},{18,... | collective-permute-start | bytes 1671176 | tf_op jit(solution)/shard_map/ppermute | solution.py:597
  272.4 18.0 %collective-permute-start.15 = (bf16[272,1024]{1,0:T(8,128)(2,1)}, bf16[272,1024]{1,0:T(8,128)(2,1)S(1)}, u32[]{:S(2)}, u32[]{:S(2)}) collective-permute-start(bf16[272,1024]{1,0:T(8,128)(2,1)} %get-tuple-element.117.refs_0_), channel_id=1, source_target_pairs={{0,6},{2,4},{4,2},{6,0},{8,14},{10,12},{12,10},{14,8},{16,22},{18,... | collective-permute-start | bytes 1671176 | tf_op jit(solution)/shard_map/ppermute | solution.py:597
  272.4 11.9 %collective-permute-start.20 = (bf16[1024,256]{1,0:T(8,128)(2,1)}, bf16[1024,256]{1,0:T(8,128)(2,1)}, u32[]{:S(2)}, u32[]{:S(2)}) collective-permute-start(bf16[1024,256]{1,0:T(8,128)(2,1)} %collective-permute-done.6.refs_10_), channel_id=1, source_target_pairs={{0,8},{2,10},{4,12},{6,14},{8,0},{10,2},{12,4},{14,6},{16,24},{18,... | collective-permute-start | bytes 1572872 | tf_op jit(solution)/shard_map/ppermute | solution.py:597
  274.7 9.6 %collective-permute-start.19 = (bf16[16,2048]{1,0:T(8,128)(2,1)S(1)}, bf16[16,2048]{1,0:T(8,128)(2,1)S(1)}, u32[]{:S(2)}, u32[]{:S(2)}) collective-permute-start(bf16[16,2048]{1,0:T(8,128)(2,1)S(1)} %get-tuple-element.118), channel_id=1, source_target_pairs={{8,6},{16,14},{24,22},{9,7},{17,15},{25,23}} | collective-permute-start | bytes 196616 | tf_op jit(solution)/shard_map/ppermute | solution.py:704
  275.4 1.2 copy-start.7
  276.6 1.1 copy-start.18
  277.7 1.1 copy-start.20
  278.7 1.1 copy-start.22
  279.8 1.1 copy-start.24
  295.5 19.1 %copy-start.8 = (s32[128,4096]{1,0:T(8,128)S(1)}, s32[128,4096]{1,0:T(8,128)}, u32[]{:S(2)}) copy-start(s32[128,4096]{1,0:T(8,128)} %refs_5_.1) | copy-start | bytes 6291460
  295.5 19.0 %copy-start.13 = (f32[4096]{0:T(1024)S(1)}, f32[4096]{0:T(1024)}, u32[]{:S(2)}) copy-start(f32[4096]{0:T(1024)} %param.16) | copy-start | bytes 49156
  295.5 19.0 %copy-start.14 = (f32[4096]{0:T(1024)S(1)}, f32[4096]{0:T(1024)}, u32[]{:S(2)}) copy-start(f32[4096]{0:T(1024)} %param.17) | copy-start | bytes 49156
  295.5 2.7 collective-permute-start.22
  299.4 9.4 %collective-permute-start.23 = (bf16[128,1024]{1,0:T(8,128)(2,1)}, bf16[128,1024]{1,0:T(8,128)(2,1)S(1)}, u32[]{:S(2)}, u32[]{:S(2)}) collective-permute-start(bf16[128,1024]{1,0:T(8,128)(2,1)} %get-tuple-element.131), channel_id=1, source_target_pairs={{0,2},{2,0},{4,6},{6,4},{8,10},{10,8},{12,14},{14,12},{16,18},{18,... | collective-permute-start | bytes 786440 | tf_op jit(solution)/shard_map/ppermute | solution.py:597
  299.4 9.4 %collective-permute-start.24 = (bf16[128,1024]{1,0:T(8,128)(2,1)}, bf16[128,1024]{1,0:T(8,128)(2,1)S(1)}, u32[]{:S(2)}, u32[]{:S(2)}) collective-permute-start(bf16[128,1024]{1,0:T(8,128)(2,1)} %get-tuple-element.132), channel_id=1, source_target_pairs={{0,4},{2,6},{4,0},{6,2},{8,12},{10,14},{12,8},{14,10},{16,20},{18,... | collective-permute-start | bytes 786440 | tf_op jit(solution)/shard_map/ppermute | solution.py:597
  300.9 13.6 %collective-permute-start.25 = (bf16[128,1024]{1,0:T(8,128)(2,1)S(1)}, bf16[128,1024]{1,0:T(8,128)(2,1)S(1)}, u32[]{:S(2)}, u32[]{:S(2)}) collective-permute-start(bf16[128,1024]{1,0:T(8,128)(2,1)S(1)} %get-tuple-element.133), channel_id=1, source_target_pairs={{0,6},{2,4},{4,2},{6,0},{8,14},{10,12},{12,10},{14,8},{16,22},{18,... | collective-permute-start | bytes 786440 | tf_op jit(solution)/shard_map/ppermute | solution.py:597
  314.5 1.2 copy-start.9

commit v6 on v5

--- a/solution.py
+++ b/solution.py
@@ -617,7 +617,6 @@
     far_table = to_partner(
         jnp.pad(jnp.concatenate([owners, slot_rows]), (0, LANES - 2 * requests))[None, :]
     )
-    carried, far_carried, far_table = pinned(carried, far_carried, far_table)
     near_out = spread(
         [queries], carried, *pick_requests(owners, slot_rows, near_peers, per_block),
         span_len, 0,
@@ -700,17 +699,18 @@
         moved, first, *far_weight = pinned(moved, first, *far_weight)
         next_sources = to_plane(moved)
         far_swap = [swap(piece, PLANE) for piece in far_weight]
+        first_weights = [(weight, 0), (near_swap, 0), (far_weight[0], 0), (far_swap[0], 0)]
+        next_weights = [
+            (weight, middle), (near_swap, middle), (far_weight[1], 0), (far_swap[1], 0)
+        ]
+        done = project(sources, [], first_weights, place, stay, [], jnp.float32)
+        first, *done = pinned(first, *done)
         belows = [
             lax.ppermute(
                 first, "dp", [(i + PLANE, i + at) for i in range(0, peer_count - PLANE, PLANE)]
             )
             for at in range(PLANE)
         ]
-        first_weights = [(weight, 0), (near_swap, 0), (far_weight[0], 0), (far_swap[0], 0)]
-        next_weights = [
-            (weight, middle), (near_swap, middle), (far_weight[1], 0), (far_swap[1], 0)
-        ]
-        done = project(sources, [], first_weights, place, stay, [], jnp.float32)
         keep, send = project(
             next_sources, belows, next_weights + first_weights, place, stay, done, moved.dtype
         )

time: 321 us -> 319 us (level)
    ppermute x7, waiting for transfers between devices: 134 us -> 127 us  [to_partner(): return lax.ppermute(x, 'dp', across)]
    ppermute x7, starting transfers between devices: 11.3 us -> 16.4 us  [to_partner(): return lax.ppermute(x, 'dp', across)]
    ppermute x1, waiting for transfers between devices: 0.01 us -> 4 us  [local(): lax.ppermute(queries[-1:], 'dp', [(i - 1, (i + half) % peer_count) for i...]
    pallas_call x4, Pallas kernels: 36.1 us -> 32.8 us  [attend(): pl.pallas_call(functools.partial(attend_kernel, chunk), grid=(peers,), in...]
  transfers between devices with their start and end apart: 31 -> 31, of which waited for: 15 -> 15; matrix products, arithmetic and copies ran while one was open for 1% -> 1% of each run, Pallas kernels for 14% -> 13%
where the time goes in v6:
time: 319 us; the launch traced here: 317 us
  waiting for transfers between devices  170 us (53%)
  starting transfers between devices  65.8 us (21%)
  Pallas kernels  62.8 us (20%)
  local copies, waits for them, and re-layouts  17.1 us (5%)
    ppermute x7, waiting for transfers between devices, to_partner(): return lax.ppermute(x, 'dp', across)  127 us
    pallas_call x4, Pallas kernels, attend(): pl.pallas_call(functools.partial(attend_kernel, chunk), grid=(peers,), in...  32.8 us
    all_to_all x5, starting transfers between devices, exchange(): lax.all_to_all(x, 'dp', split_axis=0, concat_axis=0, tiled=True, axis_ind...  22.5 us
    ppermute x12, waiting for transfers between devices, swap(): return lax.ppermute(x, 'dp', [(i, i ^ by) for i in range(peer_count)])  20.1 us
    ppermute x7, starting transfers between devices, to_partner(): return lax.ppermute(x, 'dp', across)  16.4 us
    ppermute x12, starting transfers between devices, swap(): return lax.ppermute(x, 'dp', [(i, i ^ by) for i in range(peer_count)])  15.3 us
    unnamed x58, local copies, waits for them, and re-layouts  14.2 us
    ppermute x4, waiting for transfers between devices, local(): lax.ppermute(first, 'dp', [(i + PLANE, i + at) for i in range(0, peer_cou...  9.13 us
  transfers between devices with their start and end apart: 31, of which 15 were waited for; matrix products, arithmetic and copies ran while one was open for 1% of the time, Pallas kernels for 13%

profile of v6, /device:TPU:0, one launch (start us, length us, event | category | flops | bytes accessed | tf_op | source)
XLA Modules:
  0.0 317.0 jit_solution(9741694809516061987)
XLA Ops:
  0.6 0.8 slice.23
  1.4 4.8 %collective-permute-start.3 = (bf16[1,2048]{1,0:T(2,128)(2,1)S(1)}, bf16[1,2048]{1,0:T(2,128)(2,1)S(1)}, u32[]{:S(2)}, u32[]{:S(2)}) collective-permute-start(bf16[1,2048]{1,0:T(2,128)(2,1)S(1)} %slice.23), channel_id=1, source_target_pairs={{0,2},{2,4},{4,6},{6,8},{8,10},{10,12},{12,14},{14,16},{16,18},{18... | collective-permute-start | bytes 12296 | tf_op jit(solution)/shard_map/ppermute | solution.py:23
  8.2 1.2 copy-done.4
  9.4 2.3 spread_queries.3
  11.7 5.1 %all-to-all-start.1 = ((bf16[8,64,2176]{2,1,0:T(8,128)(2,1)}), bf16[8,64,2176]{2,1,0:T(8,128)(2,1)S(1)}, u32[]{:S(2)}, u32[]{:S(2)}) async-start(bf16[8,64,2176]{2,1,0:T(8,128)(2,1)} %spread_queries.3), calls=%async_computation.1 | async-start | bytes 4456448 | tf_op jit(solution)/shard_map/all_to_all | solution.py:592
  16.8 0.9 fusion.7
  17.7 3.3 %collective-permute-start = (bf16[256,1024]{1,0:T(8,128)(2,1)S(1)}, bf16[256,1024]{1,0:T(8,128)(2,1)S(1)}, u32[]{:S(2)}, u32[]{:S(2)}) collective-permute-start(bf16[256,1024]{1,0:T(8,128)(2,1)S(1)} %get-tuple-element.141), channel_id=1, source_target_pairs={{0,16},{2,18},{4,20},{6,22},{8,24},{10,26},{12,28},{14,30},{16,0},... | collective-permute-start | bytes 1572872 | tf_op jit(solution)/shard_map/ppermute | solution.py:603
  21.0 3.4 %collective-permute-start.1 = (bf16[1,2048]{1,0:T(2,128)(2,1)S(1)}, bf16[1,2048]{1,0:T(2,128)(2,1)S(1)}, u32[]{:S(2)}, u32[]{:S(2)}) collective-permute-start(bf16[1,2048]{1,0:T(2,128)(2,1)S(1)} %slice.23), channel_id=1, source_target_pairs={{0,18},{2,20},{4,22},{6,24},{8,26},{10,28},{12,30},{14,0},{16,2},{... | collective-permute-start | bytes 12296 | tf_op jit(solution)/shard_map/ppermute | solution.py:613
  24.4 2.8 collective-permute-start.2
  27.2 24.7 %collective-permute-done.2 = s32[1,128]{1,0:T(1,128)S(1)} collective-permute-done((s32[1,128]{1,0:T(1,128)S(1)}, s32[1,128]{1,0:T(1,128)S(1)}, u32[]{:S(2)}, u32[]{:S(2)}) %collective-permute-start.2) | collective-permute-done | bytes 544 | tf_op jit(solution)/shard_map/ppermute | solution.py:603
  52.0 4.0 %collective-permute-done.1.carried_ref = bf16[1,2048]{1,0:T(2,128)(2,1)S(1)} collective-permute-done((bf16[1,2048]{1,0:T(2,128)(2,1)S(1)}, bf16[1,2048]{1,0:T(2,128)(2,1)S(1)}, u32[]{:S(2)}, u32[]{:S(2)}) %collective-permute-start.1) | collective-permute-done | bytes 4128 | tf_op jit(solution)/shard_map/ppermute | solution.py:613
  56.3 1.8 spread_queries.4
  58.1 5.2 %all-to-all-start = ((bf16[8,64,1152]{2,1,0:T(8,128)(2,1)}), bf16[8,64,1152]{2,1,0:T(8,128)(2,1)}, u32[]{:S(2)}, u32[]{:S(2)}) async-start(bf16[8,64,1152]{2,1,0:T(8,128)(2,1)} %spread_queries.4), calls=%async_computation | async-start | bytes 2359296 | tf_op jit(solution)/shard_map/all_to_all | solution.py:592
  63.3 0.9 collective-permute-start.4
  64.2 1.1 fusion.6
  65.3 8.2 %attend_blocks.5.refs_0_ = bf16[8,64,2304]{2,1,0:T(8,128)(2,1)} custom-call(bf16[8,64,2176]{2,1,0:T(8,128)(2,1)} %copy-done.25, bf16[8,64,2176]{2,1,0:T(8,128)(2,1)} %copy-done.25, bf16[8,128,2048]{2,1,0:T(8,128)(2,1)} %key_ref.7, bf16[8,128,2048]{2,1,0:T(8,128)(2,1)} %value_ref.7), custom_call_target="tpu_custom_call" | custom-call | flops 268435456 | bytes 6291456 | tf_op jit(solution)/shard_map/attend_blocks/pallas_call | solution.py:196
  73.5 8.2 %attend_blocks.4.refs_1_ = bf16[8,64,2304]{2,1,0:T(8,128)(2,1)} custom-call(bf16[8,64,2176]{2,1,0:T(8,128)(2,1)} %copy-done.25, bf16[8,64,2176]{2,1,0:T(8,128)(2,1)} %copy-done.25, bf16[8,128,2048]{2,1,0:T(8,128)(2,1)} %key_ref.7, bf16[8,128,2048]{2,1,0:T(8,128)(2,1)} %value_ref.7), custom_call_target="tpu_custom_call" | custom-call | flops 268435456 | bytes 6291456 | tf_op jit(solution)/shard_map/attend_blocks/pallas_call | solution.py:196
  81.7 3.7 %collective-permute-done.4.refs_0_ = bf16[256,1024]{1,0:T(8,128)(2,1)} collective-permute-done((bf16[256,1024]{1,0:T(8,128)(2,1)}, bf16[256,1024]{1,0:T(8,128)(2,1)}, u32[]{:S(2)}, u32[]{:S(2)}) %collective-permute-start.4) | collective-permute-done | bytes 524320 | tf_op jit(solution)/shard_map/ppermute | solution.py:603
  85.4 2.1 all-to-all-done.tag_ref.query_ref
  87.5 3.1 spread_queries.5
  90.6 4.7 %all-to-all-start.2 = ((bf16[8,64,2304]{2,1,0:T(8,128)(2,1)}), bf16[8,64,2304]{2,1,0:T(8,128)(2,1)S(1)}, u32[]{:S(2)}, u32[]{:S(2)}) async-start(bf16[8,64,2304]{2,1,0:T(8,128)(2,1)} %spread_queries.5), calls=%async_computation.2 | async-start | bytes 4718592 | tf_op jit(solution)/shard_map/all_to_all | solution.py:592
  95.4 1.2 collective-permute-start.5
  96.6 8.2 %attend_blocks.6 = bf16[8,64,2304]{2,1,0:T(8,128)(2,1)} custom-call(bf16[8,64,1152]{2,1,0:T(8,128)(2,1)} %all-to-all-done.tag_ref.query_ref, bf16[8,64,1152]{2,1,0:T(8,128)(2,1)} %all-to-all-done.tag_ref.query_ref, bf16[8,128,2048]{2,1,0:T(8,128)(2,1)} %key_ref.7, bf16[8,128,2048]{2,1,0:T(8,128)(2,1)} %value_ref.7, ...), custom_call_target="tpu_custom_call", output_to_operand_aliasing={{}: (4, {})} | custom-call | flops 268435456 | bytes 6291456 | tf_op jit(solution)/shard_map/attend_blocks/pallas_call | solution.py:196
  104.8 25.7 %collective-permute-done.5.refs_6_.refs_14_ = bf16[1024,256]{1,0:T(8,128)(2,1)} collective-permute-done((bf16[1024,256]{1,0:T(8,128)(2,1)S(1)}, bf16[1024,256]{1,0:T(8,128)(2,1)}, u32[]{:S(2)}, u32[]{:S(2)}) %collective-permute-start.5) | collective-permute-done | bytes 524320 | tf_op jit(solution)/shard_map/ppermute | solution.py:603
  130.5 2.1 all-to-all-done.2.query_ref.refs_0_.refs_1_
  132.6 1.5 copy-done
  134.1 3.8 %all-to-all-start.3 = ((bf16[8,64,2304]{2,1,0:T(8,128)(2,1)}), bf16[8,64,2304]{2,1,0:T(8,128)(2,1)S(1)}, u32[]{:S(2)}, u32[]{:S(2)}) async-start(bf16[8,64,2304]{2,1,0:T(8,128)(2,1)} %attend_blocks.6), calls=%async_computation.3 | async-start | bytes 4718592 | tf_op jit(solution)/shard_map/all_to_all | solution.py:592
  137.9 1.5 collective-permute-start.6
  139.4 8.2 %attend_blocks.7 = bf16[8,64,1152]{2,1,0:T(8,128)(2,1)} custom-call(bf16[8,64,1152]{2,1,0:T(8,128)(2,1)} %all-to-all-done.tag_ref.query_ref, bf16[8,64,2304]{2,1,0:T(8,128)(2,1)} %copy-done, bf16[8,128,2048]{2,1,0:T(8,128)(2,1)} %key_ref.7, bf16[8,128,2048]{2,1,0:T(8,128)(2,1)} %value_ref.7), custom_call_target="tpu_custom_call" | custom-call | flops 268435456 | bytes 6291456 | tf_op jit(solution)/shard_map/attend_blocks/pallas_call | solution.py:196
  147.6 26.4 %collective-permute-done.6.refs_10_ = bf16[1024,256]{1,0:T(8,128)(2,1)} collective-permute-done((bf16[1024,256]{1,0:T(8,128)(2,1)S(1)}, bf16[1024,256]{1,0:T(8,128)(2,1)}, u32[]{:S(2)}, u32[]{:S(2)}) %collective-permute-start.6) | collective-permute-done | bytes 524320 | tf_op jit(solution)/shard_map/ppermute | solution.py:603
  174.0 2.0 all-to-all-done.3.refs_0_.refs_1_
  176.1 3.7 %all-to-all-start.4 = ((bf16[8,64,1152]{2,1,0:T(8,128)(2,1)}), bf16[8,64,1152]{2,1,0:T(8,128)(2,1)S(1)}, u32[]{:S(2)}, u32[]{:S(2)}) async-start(bf16[8,64,1152]{2,1,0:T(8,128)(2,1)} %attend_blocks.7), calls=%async_computation.4 | async-start | bytes 2359296 | tf_op jit(solution)/shard_map/all_to_all | solution.py:592
  179.8 2.1 merge_far.2
  181.9 3.4 %collective-permute-start.7 = (bf16[4,64,1152]{2,1,0:T(8,128)(2,1)S(1)}, bf16[4,64,1152]{2,1,0:T(8,128)(2,1)S(1)}, u32[]{:S(2)}, u32[]{:S(2)}) collective-permute-start(bf16[4,64,1152]{2,1,0:T(8,128)(2,1)S(1)} %merge_far.2), channel_id=1, source_target_pairs={{0,16},{2,18},{4,20},{6,22},{8,24},{10,26},{12,28},{14,30},{16,0},... | collective-permute-start | bytes 1769480 | tf_op jit(solution)/shard_map/ppermute | solution.py:603
  185.3 24.5 %collective-permute-done.7.refs_2_ = bf16[4,64,1152]{2,1,0:T(8,128)(2,1)S(1)} collective-permute-done((bf16[4,64,1152]{2,1,0:T(8,128)(2,1)S(1)}, bf16[4,64,1152]{2,1,0:T(8,128)(2,1)S(1)}, u32[]{:S(2)}, u32[]{:S(2)}) %collective-permute-start.7) | collective-permute-done | bytes 589856 | tf_op jit(solution)/shard_map/ppermute | solution.py:603
  209.8 0.8 copy-done.10
  210.6 1.9 merge_far.3
  213.0 3.4 %collective-permute-start.8 = (bf16[4,64,1152]{2,1,0:T(8,128)(2,1)S(1)}, bf16[4,64,1152]{2,1,0:T(8,128)(2,1)S(1)}, u32[]{:S(2)}, u32[]{:S(2)}) collective-permute-start(bf16[4,64,1152]{2,1,0:T(8,128)(2,1)S(1)} %merge_far.3), channel_id=1, source_target_pairs={{0,16},{2,18},{4,20},{6,22},{8,24},{10,26},{12,28},{14,30},{16,0},... | collective-permute-start | bytes 1769480 | tf_op jit(solution)/shard_map/ppermute | solution.py:603
  216.4 2.4 merge_all.2
  218.8 2.4 collective-permute-start.11
  222.4 22.4 %collective-permute-done.8.refs_2_ = bf16[4,64,1152]{2,1,0:T(8,128)(2,1)S(1)} collective-permute-done((bf16[4,64,1152]{2,1,0:T(8,128)(2,1)S(1)}, bf16[4,64,1152]{2,1,0:T(8,128)(2,1)S(1)}, u32[]{:S(2)}, u32[]{:S(2)}) %collective-permute-start.8) | collective-permute-done | bytes 589856 | tf_op jit(solution)/shard_map/ppermute | solution.py:603
  244.8 0.8 copy-done.19
  245.6 0.8 copy-done.21
  246.4 0.8 copy-done.23
  247.2 3.2 %merge_all.3 = (bf16[272,1024]{1,0:T(8,128)(2,1)}, bf16[16,2048]{1,0:T(8,128)(2,1)S(1)}) custom-call(s32[8]{0:T(128)S(1)} %subtract_select_fusion.1.index_ref, s32[8]{0:T(128)S(1)} %fusion.4.use_ref, bf16[8,64,2304]{2,1,0:T(8,128)(2,1)S(1)} %all-to-all-done.3.refs_0_.refs_1_, bf16[8,64,2304]{2,1,0:T(8,128)(2,1)S(1)} %all-to-all-done.3.refs_0_.refs_1_, ...), custom_call_target="tpu_custom_call" | custom-call | tf_op jit(solution)/shard_map/merge_all/pallas_call | solution.py:336
  250.5 4.3 %collective-permute-start.16 = (bf16[1024,256]{1,0:T(8,128)(2,1)}, bf16[1024,256]{1,0:T(8,128)(2,1)S(1)}, u32[]{:S(2)}, u32[]{:S(2)}) collective-permute-start(bf16[1024,256]{1,0:T(8,128)(2,1)} %collective-permute-done.5.refs_6_.refs_14_), channel_id=1, source_target_pairs={{0,8},{2,10},{4,12},{6,14},{8,0},{10,2},{12,4},{14,6},{16,24},{18,... | collective-permute-start | bytes 1572872 | tf_op jit(solution)/shard_map/ppermute | solution.py:597
  254.7 2.4 collective-permute-start.15
  258.3 9.5 %collective-permute-done.16.refs_7_.refs_15_ = bf16[1024,256]{1,0:T(8,128)(2,1)S(1)} collective-permute-done((bf16[1024,256]{1,0:T(8,128)(2,1)}, bf16[1024,256]{1,0:T(8,128)(2,1)S(1)}, u32[]{:S(2)}, u32[]{:S(2)}) %collective-permute-start.16) | collective-permute-done | bytes 524320 | tf_op jit(solution)/shard_map/ppermute | solution.py:597
  267.8 1.2 copy-done.7
  269.0 1.1 copy-done.18
  270.0 1.1 copy-done.20
  271.1 1.1 copy-done.22
  272.2 1.1 copy-done.24
  273.2 3.5 %project_rows.2 = (f32[512,1024]{1,0:T(8,128)S(1)}, f32[512,1024]{1,0:T(8,128)S(1)}) custom-call(s32[1]{0:T(128)} %bitcast.place_ref, s32[1]{0:T(128)} %bitcast.5.stay_ref, bf16[272,1024]{1,0:T(8,128)(2,1)S(1)} %copy-done.18, bf16[272,1024]{1,0:T(8,128)(2,1)S(1)} %copy-done.24, bf16[272,1024]{1,0:T(8,128)(2,1)S(1)} %copy-done.22, ...), custom_call_target="tpu_custom_call" | custom-call | flops 2147483648 | bytes 12582912 | tf_op jit(solution)/shard_map/project_rows/pallas_call | solution.py:450
  278.7 1.3 collective-permute-start.17
  280.1 9.1 %collective-permute-done.17.refs_4_ = bf16[16,2048]{1,0:T(8,128)(2,1)S(1)} collective-permute-done((bf16[16,2048]{1,0:T(8,128)(2,1)S(1)}, bf16[16,2048]{1,0:T(8,128)(2,1)S(1)}, u32[]{:S(2)}, u32[]{:S(2)}) %collective-permute-start.17) | collective-permute-done | bytes 65568 | tf_op jit(solution)/shard_map/ppermute | solution.py:709
  289.2 5.1 %project_rows.3 = (bf16[512,1024]{1,0:T(8,128)(2,1)S(1)}, bf16[512,1024]{1,0:T(8,128)(2,1)S(1)}) custom-call(s32[1]{0:T(128)} %bitcast.place_ref, s32[1]{0:T(128)} %bitcast.5.stay_ref, bf16[272,1024]{1,0:T(8,128)(2,1)} %get-tuple-element.114.refs_0_, bf16[272,1024]{1,0:T(8,128)(2,1)S(1)} %collective-permute-done.13.refs_1_, ...), custom_call_target="tpu_custom_call" | custom-call | flops 2147483648 | bytes 12582912 | tf_op jit(solution)/shard_map/project_rows/pallas_call | solution.py:450
  294.4 2.6 collective-permute-done.22
  297.1 1.2 add_cores.1
  298.2 3.5 %collective-permute-start.25 = (bf16[128,1024]{1,0:T(8,128)(2,1)S(1)}, bf16[128,1024]{1,0:T(8,128)(2,1)S(1)}, u32[]{:S(2)}, u32[]{:S(2)}) collective-permute-start(bf16[128,1024]{1,0:T(8,128)(2,1)S(1)} %get-tuple-element.133), channel_id=1, source_target_pairs={{0,6},{2,4},{4,2},{6,0},{8,14},{10,12},{12,10},{14,8},{16,22},{18,... | collective-permute-start | bytes 786440 | tf_op jit(solution)/shard_map/ppermute | solution.py:597
  301.8 5.8 %collective-permute-done.23.refs_1_ = bf16[128,1024]{1,0:T(8,128)(2,1)S(1)} collective-permute-done((bf16[128,1024]{1,0:T(8,128)(2,1)}, bf16[128,1024]{1,0:T(8,128)(2,1)S(1)}, u32[]{:S(2)}, u32[]{:S(2)}) %collective-permute-start.23) | collective-permute-done | bytes 262176 | tf_op jit(solution)/shard_map/ppermute | solution.py:597
  307.6 4.8 %collective-permute-done.24.refs_2_ = bf16[128,1024]{1,0:T(8,128)(2,1)S(1)} collective-permute-done((bf16[128,1024]{1,0:T(8,128)(2,1)}, bf16[128,1024]{1,0:T(8,128)(2,1)S(1)}, u32[]{:S(2)}, u32[]{:S(2)}) %collective-permute-start.24) | collective-permute-done | bytes 262176 | tf_op jit(solution)/shard_map/ppermute | solution.py:597
  312.4 1.2 copy-done.9
  313.7 3.3 %add_norm.1 = (bf16[128,4096]{1,0:T(8,128)(2,1)}, bf16[128,4096]{1,0:T(8,128)(2,1)}) custom-call(s32[1]{0:T(128)} %bitcast.place_ref, s32[4]{0:T(128)S(1)} %pad_add_fusion.line_ref, bf16[128,1024]{1,0:T(8,128)(2,1)S(1)} %get-tuple-element.130.refs_0_, bf16[128,1024]{1,0:T(8,128)(2,1)S(1)} %collective-permute-done.23.refs_1_, ...), custom_call_target="tpu_custom_call" | custom-call | tf_op jit(solution)/shard_map/add_norm/pallas_call | solution.py:535
  (88 shorter events, 7.4 us)
Async XLA Ops:
  1.4 6.8 %collective-permute-start.3 = (bf16[1,2048]{1,0:T(2,128)(2,1)S(1)}, bf16[1,2048]{1,0:T(2,128)(2,1)S(1)}, u32[]{:S(2)}, u32[]{:S(2)}) collective-permute-start(bf16[1,2048]{1,0:T(2,128)(2,1)S(1)} %slice.23), channel_id=1, source_target_pairs={{0,2},{2,4},{4,6},{6,8},{8,10},{10,12},{12,14},{14,16},{16,18},{18... | collective-permute-start | bytes 12296 | tf_op jit(solution)/shard_map/ppermute | solution.py:23
  8.2 1.2 copy-start.4
  11.7 5.1 %copy-start.5 = (bf16[256,2048]{1,0:T(8,128)(2,1)S(1)}, bf16[256,2048]{1,0:T(8,128)(2,1)}, u32[]{:S(2)}) copy-start(bf16[256,2048]{1,0:T(8,128)(2,1)} %refs_0_.1) | copy-start | bytes 3145732
  11.7 46.4 %all-to-all-start.1 = ((bf16[8,64,2176]{2,1,0:T(8,128)(2,1)}), bf16[8,64,2176]{2,1,0:T(8,128)(2,1)S(1)}, u32[]{:S(2)}, u32[]{:S(2)}) async-start(bf16[8,64,2176]{2,1,0:T(8,128)(2,1)} %spread_queries.3), calls=%async_computation.1 | async-start | bytes 4456448 | tf_op jit(solution)/shard_map/all_to_all | solution.py:592
  17.7 46.5 %copy-start.2 = (bf16[2048,256]{1,0:T(8,128)(2,1)S(1)}, bf16[2048,256]{1,0:T(8,128)(2,1)}, u32[]{:S(2)}) copy-start(bf16[2048,256]{1,0:T(8,128)(2,1)} %refs_12_) | copy-start | bytes 3145732
  17.7 38.3 %collective-permute-start = (bf16[256,1024]{1,0:T(8,128)(2,1)S(1)}, bf16[256,1024]{1,0:T(8,128)(2,1)S(1)}, u32[]{:S(2)}, u32[]{:S(2)}) collective-permute-start(bf16[256,1024]{1,0:T(8,128)(2,1)S(1)} %get-tuple-element.141), channel_id=1, source_target_pairs={{0,16},{2,18},{4,20},{6,22},{8,24},{10,26},{12,28},{14,30},{16,0},... | collective-permute-start | bytes 1572872 | tf_op jit(solution)/shard_map/ppermute | solution.py:603
  21.0 35.0 %collective-permute-start.1 = (bf16[1,2048]{1,0:T(2,128)(2,1)S(1)}, bf16[1,2048]{1,0:T(2,128)(2,1)S(1)}, u32[]{:S(2)}, u32[]{:S(2)}) collective-permute-start(bf16[1,2048]{1,0:T(2,128)(2,1)S(1)} %slice.23), channel_id=1, source_target_pairs={{0,18},{2,20},{4,22},{6,24},{8,26},{10,28},{12,30},{14,0},{16,2},{... | collective-permute-start | bytes 12296 | tf_op jit(solution)/shard_map/ppermute | solution.py:613
  24.4 27.5 %collective-permute-start.2 = (s32[1,128]{1,0:T(1,128)S(1)}, s32[1,128]{1,0:T(1,128)S(1)}, u32[]{:S(2)}, u32[]{:S(2)}) collective-permute-start(s32[1,128]{1,0:T(1,128)S(1)} %pad_bitcast_fusion), channel_id=1, source_target_pairs={{0,16},{2,18},{4,20},{6,22},{8,24},{10,26},{12,28},{14,30},{16,0},... | collective-permute-start | bytes 1544 | tf_op jit(solution)/shard_map/ppermute | solution.py:603
  56.0 9.3 %copy-start.12 = (bf16[1,2048]{1,0:T(2,128)(2,1)}, bf16[1,2048]{1,0:T(2,128)(2,1)S(1)}, u32[]{:S(2)}) copy-start(bf16[1,2048]{1,0:T(2,128)(2,1)S(1)} %collective-permute-done.1.carried_ref) | copy-start | bytes 12292
  56.3 9.0 %copy-start.15 = (s32[8]{0:T(128)}, s32[8]{0:T(128)S(1)}, u32[]{:S(2)}) copy-start(s32[8]{0:T(128)S(1)} %get-tuple-element.134.slot_ref) | copy-start | bytes 100
  56.3 9.0 %copy-start.16 = (s32[8]{0:T(128)}, s32[8]{0:T(128)S(1)}, u32[]{:S(2)}) copy-start(s32[8]{0:T(128)S(1)} %get-tuple-element.135.block_ref) | copy-start | bytes 100
  58.1 7.2 %copy-start.25 = (bf16[8,64,2176]{2,1,0:T(8,128)(2,1)}, bf16[8,64,2176]{2,1,0:T(8,128)(2,1)S(1)}, u32[]{:S(2)}) copy-start(bf16[8,64,2176]{2,1,0:T(8,128)(2,1)S(1)} %all-to-all-done.1.tag_ref.query_ref) | copy-start | bytes 6684676
  58.1 29.4 %all-to-all-start = ((bf16[8,64,1152]{2,1,0:T(8,128)(2,1)}), bf16[8,64,1152]{2,1,0:T(8,128)(2,1)}, u32[]{:S(2)}, u32[]{:S(2)}) async-start(bf16[8,64,1152]{2,1,0:T(8,128)(2,1)} %spread_queries.4), calls=%async_computation | async-start | bytes 2359296 | tf_op jit(solution)/shard_map/all_to_all | solution.py:592
  63.3 22.1 %collective-permute-start.4 = (bf16[256,1024]{1,0:T(8,128)(2,1)}, bf16[256,1024]{1,0:T(8,128)(2,1)}, u32[]{:S(2)}, u32[]{:S(2)}) collective-permute-start(bf16[256,1024]{1,0:T(8,128)(2,1)} %get-tuple-element.71), channel_id=1, source_target_pairs={{0,16},{2,18},{4,20},{6,22},{8,24},{10,26},{12,28},{14,30},{16,0},... | collective-permute-start | bytes 1572872 | tf_op jit(solution)/shard_map/ppermute | solution.py:603
  90.6 4.8 %copy-start.27 = (bf16[1024,256]{1,0:T(8,128)(2,1)S(1)}, bf16[1024,256]{1,0:T(8,128)(2,1)}, u32[]{:S(2)}) copy-start(bf16[1024,256]{1,0:T(8,128)(2,1)} %get-tuple-element.85) | copy-start | bytes 1572868
  90.6 42.0 %all-to-all-start.2 = ((bf16[8,64,2304]{2,1,0:T(8,128)(2,1)}), bf16[8,64,2304]{2,1,0:T(8,128)(2,1)S(1)}, u32[]{:S(2)}, u32[]{:S(2)}) async-start(bf16[8,64,2304]{2,1,0:T(8,128)(2,1)} %spread_queries.5), calls=%async_computation.2 | async-start | bytes 4718592 | tf_op jit(solution)/shard_map/all_to_all | solution.py:592
  95.4 35.1 %collective-permute-start.5 = (bf16[1024,256]{1,0:T(8,128)(2,1)S(1)}, bf16[1024,256]{1,0:T(8,128)(2,1)}, u32[]{:S(2)}, u32[]{:S(2)}) collective-permute-start(bf16[1024,256]{1,0:T(8,128)(2,1)S(1)} %copy-done.27), channel_id=1, source_target_pairs={{0,16},{2,18},{4,20},{6,22},{8,24},{10,26},{12,28},{14,30},{16,0},... | collective-permute-start | bytes 1572872 | tf_op jit(solution)/shard_map/ppermute | solution.py:603
  104.8 33.1 %copy-start.26 = (bf16[1024,256]{1,0:T(8,128)(2,1)S(1)}, bf16[1024,256]{1,0:T(8,128)(2,1)}, u32[]{:S(2)}) copy-start(bf16[1024,256]{1,0:T(8,128)(2,1)} %get-tuple-element.89) | copy-start | bytes 1572868
  132.6 1.5 copy-start
  134.1 42.0 %all-to-all-start.3 = ((bf16[8,64,2304]{2,1,0:T(8,128)(2,1)}), bf16[8,64,2304]{2,1,0:T(8,128)(2,1)S(1)}, u32[]{:S(2)}, u32[]{:S(2)}) async-start(bf16[8,64,2304]{2,1,0:T(8,128)(2,1)} %attend_blocks.6), calls=%async_computation.3 | async-start | bytes 4718592 | tf_op jit(solution)/shard_map/all_to_all | solution.py:592
  137.9 36.2 %collective-permute-start.6 = (bf16[1024,256]{1,0:T(8,128)(2,1)S(1)}, bf16[1024,256]{1,0:T(8,128)(2,1)}, u32[]{:S(2)}, u32[]{:S(2)}) collective-permute-start(bf16[1024,256]{1,0:T(8,128)(2,1)S(1)} %copy-done.26), channel_id=1, source_target_pairs={{0,16},{2,18},{4,20},{6,22},{8,24},{10,26},{12,28},{14,30},{16,0},... | collective-permute-start | bytes 1572872 | tf_op jit(solution)/shard_map/ppermute | solution.py:603
  176.1 34.5 %all-to-all-start.4 = ((bf16[8,64,1152]{2,1,0:T(8,128)(2,1)}), bf16[8,64,1152]{2,1,0:T(8,128)(2,1)S(1)}, u32[]{:S(2)}, u32[]{:S(2)}) async-start(bf16[8,64,1152]{2,1,0:T(8,128)(2,1)} %attend_blocks.7), calls=%async_computation.4 | async-start | bytes 2359296 | tf_op jit(solution)/shard_map/all_to_all | solution.py:592
  181.9 27.9 %collective-permute-start.7 = (bf16[4,64,1152]{2,1,0:T(8,128)(2,1)S(1)}, bf16[4,64,1152]{2,1,0:T(8,128)(2,1)S(1)}, u32[]{:S(2)}, u32[]{:S(2)}) collective-permute-start(bf16[4,64,1152]{2,1,0:T(8,128)(2,1)S(1)} %merge_far.2), channel_id=1, source_target_pairs={{0,16},{2,18},{4,20},{6,22},{8,24},{10,26},{12,28},{14,30},{16,0},... | collective-permute-start | bytes 1769480 | tf_op jit(solution)/shard_map/ppermute | solution.py:603
  209.8 0.8 copy-start.10
  210.6 5.8 %copy-start.1 = (bf16[8,64,2304]{2,1,0:T(8,128)(2,1)S(1)}, bf16[8,64,2304]{2,1,0:T(8,128)(2,1)}, u32[]{:S(2)}) copy-start(bf16[8,64,2304]{2,1,0:T(8,128)(2,1)} %copy-done) | copy-start | bytes 7077892
  210.6 5.8 %copy-start.11 = (bf16[4,64,1152]{2,1,0:T(8,128)(2,1)S(1)}, bf16[4,64,1152]{2,1,0:T(8,128)(2,1)}, u32[]{:S(2)}) copy-start(bf16[4,64,1152]{2,1,0:T(8,128)(2,1)} %copy-done.10) | copy-start | bytes 1769476
  212.5 34.7 %collective-permute-start.12 = (bf16[2048,256]{1,0:T(8,128)(2,1)}, bf16[2048,256]{1,0:T(8,128)(2,1)S(1)}, u32[]{:S(2)}, u32[]{:S(2)}) collective-permute-start(bf16[2048,256]{1,0:T(8,128)(2,1)} %refs_12_), channel_id=1, source_target_pairs={{0,8},{2,10},{4,12},{6,14},{8,0},{10,2},{12,4},{14,6},{16,24},{18,... | collective-permute-start | bytes 3145736 | tf_op jit(solution)/shard_map/ppermute | solution.py:597
  213.0 31.8 %collective-permute-start.8 = (bf16[4,64,1152]{2,1,0:T(8,128)(2,1)S(1)}, bf16[4,64,1152]{2,1,0:T(8,128)(2,1)S(1)}, u32[]{:S(2)}, u32[]{:S(2)}) collective-permute-start(bf16[4,64,1152]{2,1,0:T(8,128)(2,1)S(1)} %merge_far.3), channel_id=1, source_target_pairs={{0,16},{2,18},{4,20},{6,22},{8,24},{10,26},{12,28},{14,30},{16,0},... | collective-permute-start | bytes 1769480 | tf_op jit(solution)/shard_map/ppermute | solution.py:603
  218.8 31.7 %copy-start.17 = (bf16[272,1024]{1,0:T(8,128)(2,1)}, bf16[272,1024]{1,0:T(8,128)(2,1)S(1)}, u32[]{:S(2)}) copy-start(bf16[272,1024]{1,0:T(8,128)(2,1)S(1)} %get-tuple-element.116.refs_0_) | copy-start | bytes 1671172
  218.8 26.0 %collective-permute-start.11 = (bf16[272,1024]{1,0:T(8,128)(2,1)S(1)}, bf16[272,1024]{1,0:T(8,128)(2,1)S(1)}, u32[]{:S(2)}, u32[]{:S(2)}) collective-permute-start(bf16[272,1024]{1,0:T(8,128)(2,1)S(1)} %get-tuple-element.116.refs_0_), channel_id=1, source_target_pairs={{0,6},{2,4},{4,2},{6,0},{8,14},{10,12},{12,10},{14,8},{16,22},{18,... | collective-permute-start | bytes 1671176 | tf_op jit(solution)/shard_map/ppermute | solution.py:597
  221.2 24.4 %collective-permute-start.10 = (bf16[272,1024]{1,0:T(8,128)(2,1)S(1)}, bf16[272,1024]{1,0:T(8,128)(2,1)S(1)}, u32[]{:S(2)}, u32[]{:S(2)}) collective-permute-start(bf16[272,1024]{1,0:T(8,128)(2,1)S(1)} %get-tuple-element.116.refs_0_), channel_id=1, source_target_pairs={{0,4},{2,6},{4,0},{6,2},{8,12},{10,14},{12,8},{14,10},{16,20},{18,... | collective-permute-start | bytes 1671176 | tf_op jit(solution)/shard_map/ppermute | solution.py:597
  221.8 24.6 %collective-permute-start.9 = (bf16[272,1024]{1,0:T(8,128)(2,1)S(1)}, bf16[272,1024]{1,0:T(8,128)(2,1)S(1)}, u32[]{:S(2)}, u32[]{:S(2)}) collective-permute-start(bf16[272,1024]{1,0:T(8,128)(2,1)S(1)} %get-tuple-element.116.refs_0_), channel_id=1, source_target_pairs={{0,2},{2,0},{4,6},{6,4},{8,10},{10,8},{12,14},{14,12},{16,18},{18,... | collective-permute-start | bytes 1671176 | tf_op jit(solution)/shard_map/ppermute | solution.py:597
  244.8 0.8 copy-start.19
  245.6 0.8 copy-start.21
  246.4 0.8 copy-start.23
  247.2 3.2 %copy-start.6 = (bf16[2048,256]{1,0:T(8,128)(2,1)}, bf16[2048,256]{1,0:T(8,128)(2,1)S(1)}, u32[]{:S(2)}) copy-start(bf16[2048,256]{1,0:T(8,128)(2,1)S(1)} %collective-permute-done.12.refs_5_.refs_9_.refs_13_) | copy-start | bytes 3145732
  247.2 20.5 %copy-start.3 = (bf16[2048,256]{1,0:T(8,128)(2,1)S(1)}, bf16[2048,256]{1,0:T(8,128)(2,1)}, u32[]{:S(2)}) copy-start(bf16[2048,256]{1,0:T(8,128)(2,1)} %refs_12_) | copy-start | bytes 3145732
  250.5 17.3 %collective-permute-start.16 = (bf16[1024,256]{1,0:T(8,128)(2,1)}, bf16[1024,256]{1,0:T(8,128)(2,1)S(1)}, u32[]{:S(2)}, u32[]{:S(2)}) collective-permute-start(bf16[1024,256]{1,0:T(8,128)(2,1)} %collective-permute-done.5.refs_6_.refs_14_), channel_id=1, source_target_pairs={{0,8},{2,10},{4,12},{6,14},{8,0},{10,2},{12,4},{14,6},{16,24},{18,... | collective-permute-start | bytes 1572872 | tf_op jit(solution)/shard_map/ppermute | solution.py:597
  254.7 23.3 %collective-permute-start.15 = (bf16[272,1024]{1,0:T(8,128)(2,1)}, bf16[272,1024]{1,0:T(8,128)(2,1)S(1)}, u32[]{:S(2)}, u32[]{:S(2)}) collective-permute-start(bf16[272,1024]{1,0:T(8,128)(2,1)} %get-tuple-element.114.refs_0_), channel_id=1, source_target_pairs={{0,6},{2,4},{4,2},{6,0},{8,14},{10,12},{12,10},{14,8},{16,22},{18,... | collective-permute-start | bytes 1671176 | tf_op jit(solution)/shard_map/ppermute | solution.py:597
  257.1 21.7 %collective-permute-start.14 = (bf16[272,1024]{1,0:T(8,128)(2,1)}, bf16[272,1024]{1,0:T(8,128)(2,1)S(1)}, u32[]{:S(2)}, u32[]{:S(2)}) collective-permute-start(bf16[272,1024]{1,0:T(8,128)(2,1)} %get-tuple-element.114.refs_0_), channel_id=1, source_target_pairs={{0,4},{2,6},{4,0},{6,2},{8,12},{10,14},{12,8},{14,10},{16,20},{18,... | collective-permute-start | bytes 1671176 | tf_op jit(solution)/shard_map/ppermute | solution.py:597
  257.6 19.7 %collective-permute-start.21 = (bf16[1024,256]{1,0:T(8,128)(2,1)}, bf16[1024,256]{1,0:T(8,128)(2,1)}, u32[]{:S(2)}, u32[]{:S(2)}) collective-permute-start(bf16[1024,256]{1,0:T(8,128)(2,1)} %collective-permute-done.6.refs_10_), channel_id=1, source_target_pairs={{0,8},{2,10},{4,12},{6,14},{8,0},{10,2},{12,4},{14,6},{16,24},{18,... | collective-permute-start | bytes 1572872 | tf_op jit(solution)/shard_map/ppermute | solution.py:597
  257.7 22.3 %collective-permute-start.13 = (bf16[272,1024]{1,0:T(8,128)(2,1)}, bf16[272,1024]{1,0:T(8,128)(2,1)S(1)}, u32[]{:S(2)}, u32[]{:S(2)}) collective-permute-start(bf16[272,1024]{1,0:T(8,128)(2,1)} %get-tuple-element.114.refs_0_), channel_id=1, source_target_pairs={{0,2},{2,0},{4,6},{6,4},{8,10},{10,8},{12,14},{14,12},{16,18},{18,... | collective-permute-start | bytes 1671176 | tf_op jit(solution)/shard_map/ppermute | solution.py:597
  267.8 1.2 copy-start.7
  269.0 1.1 copy-start.18
  270.0 1.1 copy-start.20
  271.1 1.1 copy-start.22
  272.2 1.1 copy-start.24
  276.7 3.4 %collective-permute-start.20 = (bf16[16,2048]{1,0:T(8,128)(2,1)S(1)}, bf16[16,2048]{1,0:T(8,128)(2,1)S(1)}, u32[]{:S(2)}, u32[]{:S(2)}) collective-permute-start(bf16[16,2048]{1,0:T(8,128)(2,1)S(1)} %get-tuple-element.124), channel_id=1, source_target_pairs={{8,6},{16,14},{24,22},{9,7},{17,15},{25,23}} | collective-permute-start | bytes 196616 | tf_op jit(solution)/shard_map/ppermute | solution.py:709
  277.4 2.7 collective-permute-start.19
  278.1 2.0 collective-permute-start.18
  278.7 10.5 %collective-permute-start.17 = (bf16[16,2048]{1,0:T(8,128)(2,1)S(1)}, bf16[16,2048]{1,0:T(8,128)(2,1)S(1)}, u32[]{:S(2)}, u32[]{:S(2)}) collective-permute-start(bf16[16,2048]{1,0:T(8,128)(2,1)S(1)} %get-tuple-element.124), channel_id=1, source_target_pairs={{8,0},{16,8},{24,16},{9,1},{17,9},{25,17}} | collective-permute-start | bytes 196616 | tf_op jit(solution)/shard_map/ppermute | solution.py:709
  294.3 18.1 %copy-start.8 = (s32[128,4096]{1,0:T(8,128)S(1)}, s32[128,4096]{1,0:T(8,128)}, u32[]{:S(2)}) copy-start(s32[128,4096]{1,0:T(8,128)} %refs_5_.1) | copy-start | bytes 6291460
  294.3 18.1 %copy-start.13 = (f32[4096]{0:T(1024)S(1)}, f32[4096]{0:T(1024)}, u32[]{:S(2)}) copy-start(f32[4096]{0:T(1024)} %param.16) | copy-start | bytes 49156
  294.3 18.1 %copy-start.14 = (f32[4096]{0:T(1024)S(1)}, f32[4096]{0:T(1024)}, u32[]{:S(2)}) copy-start(f32[4096]{0:T(1024)} %param.17) | copy-start | bytes 49156
  294.3 2.7 collective-permute-start.22
  298.2 9.4 %collective-permute-start.23 = (bf16[128,1024]{1,0:T(8,128)(2,1)}, bf16[128,1024]{1,0:T(8,128)(2,1)S(1)}, u32[]{:S(2)}, u32[]{:S(2)}) collective-permute-start(bf16[128,1024]{1,0:T(8,128)(2,1)} %get-tuple-element.131), channel_id=1, source_target_pairs={{0,2},{2,0},{4,6},{6,4},{8,10},{10,8},{12,14},{14,12},{16,18},{18,... | collective-permute-start | bytes 786440 | tf_op jit(solution)/shard_map/ppermute | solution.py:597
  298.2 14.2 %collective-permute-start.24 = (bf16[128,1024]{1,0:T(8,128)(2,1)}, bf16[128,1024]{1,0:T(8,128)(2,1)S(1)}, u32[]{:S(2)}, u32[]{:S(2)}) collective-permute-start(bf16[128,1024]{1,0:T(8,128)(2,1)} %get-tuple-element.132), channel_id=1, source_target_pairs={{0,4},{2,6},{4,0},{6,2},{8,12},{10,14},{12,8},{14,10},{16,20},{18,... | collective-permute-start | bytes 786440 | tf_op jit(solution)/shard_map/ppermute | solution.py:597
  298.2 14.2 %collective-permute-start.25 = (bf16[128,1024]{1,0:T(8,128)(2,1)S(1)}, bf16[128,1024]{1,0:T(8,128)(2,1)S(1)}, u32[]{:S(2)}, u32[]{:S(2)}) collective-permute-start(bf16[128,1024]{1,0:T(8,128)(2,1)S(1)} %get-tuple-element.133), channel_id=1, source_target_pairs={{0,6},{2,4},{4,2},{6,0},{8,14},{10,12},{12,10},{14,8},{16,22},{18,... | collective-permute-start | bytes 786440 | tf_op jit(solution)/shard_map/ppermute | solution.py:597
  312.4 1.2 copy-start.9

commit v7 on v5

--- a/solution.py
+++ b/solution.py
@@ -398,12 +398,14 @@
         below = first_ref[at : at + ROW_TILE].astype(jnp.float32)[0:1]
         if member == PLANE - 1:
             below = jnp.zeros_like(below)
+            if last_part:
+                under = functools.reduce(jnp.add, [ref[...].astype(jnp.float32) for ref in belows])
+                below = under[0:1, width:]
         end = half + (member + 1) * part
         held = rows_ref[end - ROW_TILE : end].astype(jnp.float32)
         rows_ref[end - ROW_TILE : end] = jnp.where(last, below, held).astype(rows_ref.dtype)
     if last_part:
-        below = functools.reduce(jnp.add, [ref[...].astype(jnp.float32) for ref in belows])
-        below = below.astype(rows_ref.dtype)
+        under = under[:, :width].astype(rows_ref.dtype)
     stay = pl.multiple_of(stay_ref[0] * half, half)
     go = pl.multiple_of((1 - stay_ref[0]) * half, half)
     for shard in range(PLANE):
@@ -419,24 +421,14 @@
                 result = result + before[at][:, cut]
             ref[:, cut] = result.astype(ref.dtype)
         if last_part:
-            row = functools.reduce(
-                jnp.add,
-                [
-                    jnp.dot(
-                        below[:, side * width : (side + 1) * width],
-                        held_ref[at],
-                        preferred_element_type=jnp.float32,
-                    )
-                    for side, at in ((0, PLANE + shard), (1, shard))
-                ],
-            )[0:1]
+            row = jnp.dot(under, held_ref[PLANE + shard], preferred_element_type=jnp.float32)[0:1]
             at_end = lax.broadcasted_iota(jnp.int32, (ROW_TILE, tile), 0) == ROW_TILE - 1
             for upper, ref in ((stay_ref[0] > 0, keep_ref), (stay_ref[0] == 0, send_ref)):
 
                 @pl.when(upper)
                 def _():
                     held = ref[half - ROW_TILE :, cut].astype(jnp.float32)
-                    ref[half - ROW_TILE :, cut] = jnp.where(at_end, row, held).astype(ref.dtype)
+                    ref[half - ROW_TILE :, cut] = jnp.where(at_end, held + row, held).astype(ref.dtype)
 
 
 def project(sources, belows, weights, place, stay, before, kind):
@@ -542,7 +534,7 @@
             scratch_shapes=[pltpu.VMEM((tile, columns), jnp.float32)],
         ),
         out_shape=[jax.ShapeDtypeStruct((rows, columns), residual.dtype)] * 2,
-        compiler_params=pltpu.CompilerParams(vmem_limit_bytes=20 * MIB),
+        compiler_params=pltpu.CompilerParams(vmem_limit_bytes=60 * MIB),
         name="add_norm",
     )(place, line, *branches, residual, drop_mask, gain[None], bias[None])
 
@@ -610,6 +602,11 @@
     owners = neighbour_owner.reshape(-1)
     slot_rows = neighbour_slot.reshape(-1)
     near_peers = base + jnp.arange(half, dtype=jnp.int32)
+    near_out = spread(
+        [queries], carried, *pick_requests(owners, slot_rows, near_peers, per_block),
+        span_len, 0,
+    )
+    near_asked = exchange(near_out)
     far_carried = lax.ppermute(
         queries[-1:], "dp", [(i - 1, (i + half) % peer_count) for i in range(1, peer_count)]
     )
@@ -617,12 +614,6 @@
     far_table = to_partner(
         jnp.pad(jnp.concatenate([owners, slot_rows]), (0, LANES - 2 * requests))[None, :]
     )
-    carried, far_carried, far_table = pinned(carried, far_carried, far_table)
-    near_out = spread(
-        [queries], carried, *pick_requests(owners, slot_rows, near_peers, per_block),
-        span_len, 0,
-    )
-    near_asked = exchange(near_out)
     far_first, far_carried, far_table, second, weight, _ = pinned(
         far_first, far_carried, far_table, queries[:, width:], out_weight, near_out
     )
@@ -673,22 +664,25 @@
     far_merged = merge_far(far_back, 0, wide, far_index, far_use, blocks)
     far_home = to_partner(far_merged)
     far_back = exchange(far_parts)
-    far_home, far_back, weight, *far_weight = pinned(far_home, far_back, weight, *far_weight)
+    joined = jnp.concatenate([weight_halves[0], *far_weight[:1]], axis=0)
+    far_home, far_back, joined, far_weight = pinned(far_home, far_back, joined, far_weight)
 
     def to_plane(moved):
         return [moved] + [swap(moved, by) for by in range(1, PLANE)] if by_plane else [moved]
 
     far_merged = merge_far(far_back, 0, wide, far_index, far_use, blocks)
-    far_home, near_back, far_merged, weight, *far_weight = pinned(
-        far_home, near_back, far_merged, weight, *far_weight
+    far_home, near_back, far_merged, joined, far_weight = pinned(
+        far_home, near_back, far_merged, joined, far_weight
     )
     next_home = to_partner(far_merged)
     moved, first = merge_all(near_back, 0, wide, near_index, near_use, blocks, far_home)
     sources = to_plane(moved)
-    swaps = [swap(weight, PLANE)] if by_plane else []
+    swaps = [swap(joined, PLANE)] if by_plane else []
     count = len(sources)
     (next_home,) = pinned(next_home)
-    next_home, next_back, *held = pinned(next_home, next_back, *sources, *swaps, *far_weight)
+    next_home, next_back, weight_half, far_weight, *held = pinned(
+        next_home, next_back, weight_halves[1], far_weight, *sources, *swaps
+    )
     sources, held = held[:count], held[count:]
     moved, first = merge_all(
         next_back, 1, wide, near_index, near_use, blocks, next_home, first
@@ -696,20 +690,17 @@
     if by_plane:
         place = lax.rem(here, PLANE).reshape(1)
         stay = lax.axis_index("tensor").astype(jnp.int32).reshape(1)
-        near_swap, *far_weight = held
-        moved, first, *far_weight = pinned(moved, first, *far_weight)
+        moved, first, weight_half, far_half = pinned(moved, first, weight_half, far_weight[1])
         next_sources = to_plane(moved)
-        far_swap = [swap(piece, PLANE) for piece in far_weight]
+        near_next, far_next = swap(weight_half, PLANE), swap(far_half, PLANE)
         belows = [
             lax.ppermute(
                 first, "dp", [(i + PLANE, i + at) for i in range(0, peer_count - PLANE, PLANE)]
             )
             for at in range(PLANE)
         ]
-        first_weights = [(weight, 0), (near_swap, 0), (far_weight[0], 0), (far_swap[0], 0)]
-        next_weights = [
-            (weight, middle), (near_swap, middle), (far_weight[1], 0), (far_swap[1], 0)
-        ]
+        first_weights = [(weight, 0), (held[0], 0), (far_weight[0], 0), (held[0], middle)]
+        next_weights = [(weight, middle), (near_next, 0), (far_half, 0), (far_next, 0)]
         done = project(sources, [], first_weights, place, stay, [], jnp.float32)
         keep, send = project(
             next_sources, belows, next_weights + first_weights, place, stay, done, moved.dtype

time: 321 us -> 314 us (0.978)
  Pallas kernels: 65.9 us -> 58 us
    pallas_call x4, Pallas kernels: 36.1 us -> 27 us  [attend(): pl.pallas_call(functools.partial(attend_kernel, chunk), grid=(peers,), in...]
    ppermute x4, waiting for transfers between devices: 9.51 us -> 3.47 us  [local(): lax.ppermute(first, 'dp', [(i + PLANE, i + at) for i in range(0, peer_cou...]
    ppermute x7, starting transfers between devices: 11.3 us -> 16.3 us  [to_partner(): return lax.ppermute(x, 'dp', across)]
    ppermute x1, waiting for transfers between devices: 0.01 us -> 4 us  [local(): lax.ppermute(queries[-1:], 'dp', [(i - 1, (i + half) % peer_count) for i...]
    ppermute x7, waiting for transfers between devices: 134 us -> 130 us  [to_partner(): return lax.ppermute(x, 'dp', across)]
    ppermute x12, waiting for transfers between devices: 17.6 us -> 21 us  [swap(): return lax.ppermute(x, 'dp', [(i, i ^ by) for i in range(peer_count)])]
    unnamed x58 -> x60, local copies, waits for them, and re-layouts: 14.2 us -> 14.5 us
  transfers between devices with their start and end apart: 31 -> 31, of which waited for: 15 -> 16; matrix products, arithmetic and copies ran while one was open for 1% -> 2% of each run, Pallas kernels for 14% -> 12%
where the time goes in v7:
time: 314 us; the launch traced here: 312 us
  waiting for transfers between devices  168 us (54%)
  starting transfers between devices  64.9 us (21%)
  Pallas kernels  58 us (18%)
  local copies, waits for them, and re-layouts  17.3 us (6%)
  other arithmetic  3.24 us (1%)
    ppermute x7, waiting for transfers between devices, to_partner(): return lax.ppermute(x, 'dp', across)  130 us
    pallas_call x4, Pallas kernels, attend(): pl.pallas_call(functools.partial(attend_kernel, chunk), grid=(peers,), in...  27 us
    all_to_all x5, starting transfers between devices, exchange(): lax.all_to_all(x, 'dp', split_axis=0, concat_axis=0, tiled=True, axis_ind...  22.5 us
    ppermute x12, waiting for transfers between devices, swap(): return lax.ppermute(x, 'dp', [(i, i ^ by) for i in range(peer_count)])  21 us
    ppermute x7, starting transfers between devices, to_partner(): return lax.ppermute(x, 'dp', across)  16.3 us
    ppermute x12, starting transfers between devices, swap(): return lax.ppermute(x, 'dp', [(i, i ^ by) for i in range(peer_count)])  14.5 us
    unnamed x60, local copies, waits for them, and re-layouts  14.5 us
    pallas_call x2, Pallas kernels, project(): pl.pallas_call(functools.partial(project_kernel, starts), grid_spec=pltpu...  8.08 us
  transfers between devices with their start and end apart: 31, of which 16 were waited for; matrix products, arithmetic and copies ran while one was open for 2% of the time, Pallas kernels for 12%

profile of v7, /device:TPU:0, one launch (start us, length us, event | category | flops | bytes accessed | tf_op | source)
XLA Modules:
  0.0 312.3 jit_solution(17244933242483265361)
XLA Ops:
  1.4 4.8 %collective-permute-start.3 = (bf16[1,2048]{1,0:T(2,128)(2,1)S(1)}, bf16[1,2048]{1,0:T(2,128)(2,1)S(1)}, u32[]{:S(2)}, u32[]{:S(2)}) collective-permute-start(bf16[1,2048]{1,0:T(2,128)(2,1)S(1)} %slice.23), channel_id=1, source_target_pairs={{0,2},{2,4},{4,6},{6,8},{8,10},{10,12},{12,14},{14,16},{16,18},{18... | collective-permute-start | bytes 12296 | tf_op jit(solution)/shard_map/ppermute | solution.py:23
  8.2 1.2 copy-done.4
  9.4 2.3 spread_queries.3
  11.7 5.1 %all-to-all-start.1 = ((bf16[8,64,2176]{2,1,0:T(8,128)(2,1)}), bf16[8,64,2176]{2,1,0:T(8,128)(2,1)S(1)}, u32[]{:S(2)}, u32[]{:S(2)}) async-start(bf16[8,64,2176]{2,1,0:T(8,128)(2,1)} %spread_queries.3), calls=%async_computation.1 | async-start | bytes 4456448 | tf_op jit(solution)/shard_map/all_to_all | solution.py:584
  16.8 0.9 fusion.7
  17.7 3.3 %collective-permute-start = (bf16[256,1024]{1,0:T(8,128)(2,1)S(1)}, bf16[256,1024]{1,0:T(8,128)(2,1)S(1)}, u32[]{:S(2)}, u32[]{:S(2)}) collective-permute-start(bf16[256,1024]{1,0:T(8,128)(2,1)S(1)} %get-tuple-element.137), channel_id=1, source_target_pairs={{0,16},{2,18},{4,20},{6,22},{8,24},{10,26},{12,28},{14,30},{16,0},... | collective-permute-start | bytes 1572872 | tf_op jit(solution)/shard_map/ppermute | solution.py:595
  21.0 3.4 %collective-permute-start.1 = (bf16[1,2048]{1,0:T(2,128)(2,1)S(1)}, bf16[1,2048]{1,0:T(2,128)(2,1)S(1)}, u32[]{:S(2)}, u32[]{:S(2)}) collective-permute-start(bf16[1,2048]{1,0:T(2,128)(2,1)S(1)} %slice.23), channel_id=1, source_target_pairs={{0,18},{2,20},{4,22},{6,24},{8,26},{10,28},{12,30},{14,0},{16,2},{... | collective-permute-start | bytes 12296 | tf_op jit(solution)/shard_map/ppermute | solution.py:610
  24.4 2.8 collective-permute-start.2
  27.2 24.7 %collective-permute-done.2 = s32[1,128]{1,0:T(1,128)S(1)} collective-permute-done((s32[1,128]{1,0:T(1,128)S(1)}, s32[1,128]{1,0:T(1,128)S(1)}, u32[]{:S(2)}, u32[]{:S(2)}) %collective-permute-start.2) | collective-permute-done | bytes 544 | tf_op jit(solution)/shard_map/ppermute | solution.py:595
  52.0 4.0 %collective-permute-done.1.carried_ref = bf16[1,2048]{1,0:T(2,128)(2,1)S(1)} collective-permute-done((bf16[1,2048]{1,0:T(2,128)(2,1)S(1)}, bf16[1,2048]{1,0:T(2,128)(2,1)S(1)}, u32[]{:S(2)}, u32[]{:S(2)}) %collective-permute-start.1) | collective-permute-done | bytes 4128 | tf_op jit(solution)/shard_map/ppermute | solution.py:610
  56.3 1.8 spread_queries.4
  58.1 5.2 %all-to-all-start = ((bf16[8,64,1152]{2,1,0:T(8,128)(2,1)}), bf16[8,64,1152]{2,1,0:T(8,128)(2,1)}, u32[]{:S(2)}, u32[]{:S(2)}) async-start(bf16[8,64,1152]{2,1,0:T(8,128)(2,1)} %spread_queries.4), calls=%async_computation | async-start | bytes 2359296 | tf_op jit(solution)/shard_map/all_to_all | solution.py:584
  63.3 0.9 collective-permute-start.4
  64.2 1.0 fusion.6
  65.2 7.8 %attend_blocks.4.refs_1_ = bf16[8,64,2304]{2,1,0:T(8,128)(2,1)} custom-call(bf16[8,64,2176]{2,1,0:T(8,128)(2,1)} %copy-done.23, bf16[8,64,2176]{2,1,0:T(8,128)(2,1)} %copy-done.23, bf16[8,128,2048]{2,1,0:T(8,128)(2,1)} %key_ref.7, bf16[8,128,2048]{2,1,0:T(8,128)(2,1)} %value_ref.7), custom_call_target="tpu_custom_call" | custom-call | flops 268435456 | bytes 6291456 | tf_op jit(solution)/shard_map/attend_blocks/pallas_call | solution.py:196
  73.0 7.8 %attend_blocks.5.refs_0_ = bf16[8,64,2304]{2,1,0:T(8,128)(2,1)} custom-call(bf16[8,64,2176]{2,1,0:T(8,128)(2,1)} %copy-done.23, bf16[8,64,2176]{2,1,0:T(8,128)(2,1)} %copy-done.23, bf16[8,128,2048]{2,1,0:T(8,128)(2,1)} %key_ref.7, bf16[8,128,2048]{2,1,0:T(8,128)(2,1)} %value_ref.7), custom_call_target="tpu_custom_call" | custom-call | flops 268435456 | bytes 6291456 | tf_op jit(solution)/shard_map/attend_blocks/pallas_call | solution.py:196
  80.8 4.6 %collective-permute-done.4.refs_0_ = bf16[256,1024]{1,0:T(8,128)(2,1)} collective-permute-done((bf16[256,1024]{1,0:T(8,128)(2,1)}, bf16[256,1024]{1,0:T(8,128)(2,1)}, u32[]{:S(2)}, u32[]{:S(2)}) %collective-permute-start.4) | collective-permute-done | bytes 524320 | tf_op jit(solution)/shard_map/ppermute | solution.py:595
  85.4 2.1 all-to-all-done.tag_ref.query_ref
  87.5 3.1 spread_queries.5
  90.6 4.7 %all-to-all-start.2 = ((bf16[8,64,2304]{2,1,0:T(8,128)(2,1)}), bf16[8,64,2304]{2,1,0:T(8,128)(2,1)S(1)}, u32[]{:S(2)}, u32[]{:S(2)}) async-start(bf16[8,64,2304]{2,1,0:T(8,128)(2,1)} %spread_queries.5), calls=%async_computation.2 | async-start | bytes 4718592 | tf_op jit(solution)/shard_map/all_to_all | solution.py:584
  95.3 1.2 collective-permute-start.5
  96.5 5.8 %attend_blocks.6 = bf16[8,64,2304]{2,1,0:T(8,128)(2,1)} custom-call(bf16[8,64,1152]{2,1,0:T(8,128)(2,1)} %all-to-all-done.tag_ref.query_ref, bf16[8,64,1152]{2,1,0:T(8,128)(2,1)} %all-to-all-done.tag_ref.query_ref, bf16[8,128,2048]{2,1,0:T(8,128)(2,1)} %key_ref.7, bf16[8,128,2048]{2,1,0:T(8,128)(2,1)} %value_ref.7, ...), custom_call_target="tpu_custom_call", output_to_operand_aliasing={{}: (4, {})} | custom-call | flops 268435456 | bytes 6291456 | tf_op jit(solution)/shard_map/attend_blocks/pallas_call | solution.py:196
  102.3 28.2 %collective-permute-done.5.refs_6_.refs_14_ = bf16[1024,256]{1,0:T(8,128)(2,1)} collective-permute-done((bf16[1024,256]{1,0:T(8,128)(2,1)S(1)}, bf16[1024,256]{1,0:T(8,128)(2,1)}, u32[]{:S(2)}, u32[]{:S(2)}) %collective-permute-start.5) | collective-permute-done | bytes 524320 | tf_op jit(solution)/shard_map/ppermute | solution.py:595
  130.4 2.1 all-to-all-done.2.query_ref.refs_0_.refs_1_
  132.6 1.5 copy-done
  134.0 3.8 %all-to-all-start.3 = ((bf16[8,64,2304]{2,1,0:T(8,128)(2,1)}), bf16[8,64,2304]{2,1,0:T(8,128)(2,1)S(1)}, u32[]{:S(2)}, u32[]{:S(2)}) async-start(bf16[8,64,2304]{2,1,0:T(8,128)(2,1)} %attend_blocks.6), calls=%async_computation.3 | async-start | bytes 4718592 | tf_op jit(solution)/shard_map/all_to_all | solution.py:584
  137.8 1.4 collective-permute-start.6
  139.3 5.7 %attend_blocks.7 = bf16[8,64,1152]{2,1,0:T(8,128)(2,1)} custom-call(bf16[8,64,1152]{2,1,0:T(8,128)(2,1)} %all-to-all-done.tag_ref.query_ref, bf16[8,64,2304]{2,1,0:T(8,128)(2,1)} %copy-done, bf16[8,128,2048]{2,1,0:T(8,128)(2,1)} %key_ref.7, bf16[8,128,2048]{2,1,0:T(8,128)(2,1)} %value_ref.7), custom_call_target="tpu_custom_call" | custom-call | flops 268435456 | bytes 6291456 | tf_op jit(solution)/shard_map/attend_blocks/pallas_call | solution.py:196
  145.0 29.1 %collective-permute-done.6.refs_10_ = bf16[1024,256]{1,0:T(8,128)(2,1)} collective-permute-done((bf16[1024,256]{1,0:T(8,128)(2,1)}, bf16[1024,256]{1,0:T(8,128)(2,1)}, u32[]{:S(2)}, u32[]{:S(2)}) %collective-permute-start.6) | collective-permute-done | bytes 524320 | tf_op jit(solution)/shard_map/ppermute | solution.py:595
  174.1 2.0 all-to-all-done.3.refs_0_.refs_1_
  176.1 3.7 %all-to-all-start.4 = ((bf16[8,64,1152]{2,1,0:T(8,128)(2,1)}), bf16[8,64,1152]{2,1,0:T(8,128)(2,1)S(1)}, u32[]{:S(2)}, u32[]{:S(2)}) async-start(bf16[8,64,1152]{2,1,0:T(8,128)(2,1)} %attend_blocks.7), calls=%async_computation.4 | async-start | bytes 2359296 | tf_op jit(solution)/shard_map/all_to_all | solution.py:584
  179.8 2.1 merge_far.2
  181.9 3.4 %collective-permute-start.7 = (bf16[4,64,1152]{2,1,0:T(8,128)(2,1)S(1)}, bf16[4,64,1152]{2,1,0:T(8,128)(2,1)S(1)}, u32[]{:S(2)}, u32[]{:S(2)}) collective-permute-start(bf16[4,64,1152]{2,1,0:T(8,128)(2,1)S(1)} %merge_far.2), channel_id=1, source_target_pairs={{0,16},{2,18},{4,20},{6,22},{8,24},{10,26},{12,28},{14,30},{16,0},... | collective-permute-start | bytes 1769480 | tf_op jit(solution)/shard_map/ppermute | solution.py:595
  185.3 2.1 pad_maximum_fusion
  187.4 22.2 %collective-permute-done.7.refs_2_ = bf16[4,64,1152]{2,1,0:T(8,128)(2,1)S(1)} collective-permute-done((bf16[4,64,1152]{2,1,0:T(8,128)(2,1)S(1)}, bf16[4,64,1152]{2,1,0:T(8,128)(2,1)S(1)}, u32[]{:S(2)}, u32[]{:S(2)}) %collective-permute-start.7) | collective-permute-done | bytes 589856 | tf_op jit(solution)/shard_map/ppermute | solution.py:595
  209.6 0.8 copy-done.9
  210.4 1.9 merge_far.3
  212.9 3.4 %collective-permute-start.8 = (bf16[4,64,1152]{2,1,0:T(8,128)(2,1)S(1)}, bf16[4,64,1152]{2,1,0:T(8,128)(2,1)S(1)}, u32[]{:S(2)}, u32[]{:S(2)}) collective-permute-start(bf16[4,64,1152]{2,1,0:T(8,128)(2,1)S(1)} %merge_far.3), channel_id=1, source_target_pairs={{0,16},{2,18},{4,20},{6,22},{8,24},{10,26},{12,28},{14,30},{16,0},... | collective-permute-start | bytes 1769480 | tf_op jit(solution)/shard_map/ppermute | solution.py:595
  216.3 2.4 merge_all.2
  218.8 1.5 collective-permute-start.10
  220.3 1.5 collective-permute-start.11
  222.3 0.8 copy-done.15
  223.1 21.6 %collective-permute-done.8.refs_2_ = bf16[4,64,1152]{2,1,0:T(8,128)(2,1)S(1)} collective-permute-done((bf16[4,64,1152]{2,1,0:T(8,128)(2,1)S(1)}, bf16[4,64,1152]{2,1,0:T(8,128)(2,1)S(1)}, u32[]{:S(2)}, u32[]{:S(2)}) %collective-permute-start.8) | collective-permute-done | bytes 589856 | tf_op jit(solution)/shard_map/ppermute | solution.py:595
  244.8 0.8 copy-done.19
  245.6 0.8 copy-done.21
  246.4 3.2 %merge_all.3 = (bf16[272,1024]{1,0:T(8,128)(2,1)}, bf16[16,2048]{1,0:T(8,128)(2,1)S(1)}) custom-call(s32[8]{0:T(128)S(1)} %subtract_select_fusion.1.index_ref, s32[8]{0:T(128)S(1)} %fusion.4.use_ref, bf16[8,64,2304]{2,1,0:T(8,128)(2,1)S(1)} %all-to-all-done.3.refs_0_.refs_1_, bf16[8,64,2304]{2,1,0:T(8,128)(2,1)S(1)} %all-to-all-done.3.refs_0_.refs_1_, ...), custom_call_target="tpu_custom_call" | custom-call | tf_op jit(solution)/shard_map/merge_all/pallas_call | solution.py:336
  249.6 1.3 collective-permute-start.16
  252.9 1.6 collective-permute-start.13
  254.5 3.5 %collective-permute-done.16.refs_4_ = bf16[16,2048]{1,0:T(8,128)(2,1)S(1)} collective-permute-done((bf16[16,2048]{1,0:T(8,128)(2,1)S(1)}, bf16[16,2048]{1,0:T(8,128)(2,1)S(1)}, u32[]{:S(2)}, u32[]{:S(2)}) %collective-permute-start.16) | collective-permute-done | bytes 65568 | tf_op jit(solution)/shard_map/ppermute | solution.py:697
  258.0 5.2 %collective-permute-start.20 = (bf16[1024,256]{1,0:T(8,128)(2,1)}, bf16[1024,256]{1,0:T(8,128)(2,1)S(1)}, u32[]{:S(2)}, u32[]{:S(2)}) collective-permute-start(bf16[1024,256]{1,0:T(8,128)(2,1)} %get-tuple-element.114), channel_id=1, source_target_pairs={{0,8},{2,10},{4,12},{6,14},{8,0},{10,2},{12,4},{14,6},{16,24},{18,... | collective-permute-start | bytes 1572872 | tf_op jit(solution)/shard_map/ppermute | solution.py:589
  263.3 1.2 copy-done.7
  264.5 1.1 copy-done.16
  265.6 1.1 copy-done.18
  266.7 1.1 copy-done.20
  267.7 1.1 copy-done.22
  268.8 3.5 %project_rows.2 = (f32[512,1024]{1,0:T(8,128)S(1)}, f32[512,1024]{1,0:T(8,128)S(1)}) custom-call(s32[1]{0:T(128)} %bitcast.place_ref, s32[1]{0:T(128)} %bitcast.5.stay_ref, bf16[272,1024]{1,0:T(8,128)(2,1)S(1)} %copy-done.16, bf16[272,1024]{1,0:T(8,128)(2,1)S(1)} %copy-done.22, bf16[272,1024]{1,0:T(8,128)(2,1)S(1)} %copy-done.18, ...), custom_call_target="tpu_custom_call" | custom-call | flops 2147483648 | bytes 12582912 | tf_op jit(solution)/shard_map/project_rows/pallas_call | solution.py:442
  272.2 4.1 %collective-permute-done.20.refs_9_ = bf16[1024,256]{1,0:T(8,128)(2,1)S(1)} collective-permute-done((bf16[1024,256]{1,0:T(8,128)(2,1)}, bf16[1024,256]{1,0:T(8,128)(2,1)S(1)}, u32[]{:S(2)}, u32[]{:S(2)}) %collective-permute-start.20) | collective-permute-done | bytes 524320 | tf_op jit(solution)/shard_map/ppermute | solution.py:589
  276.3 7.0 %collective-permute-done.21.refs_11_ = bf16[1024,256]{1,0:T(8,128)(2,1)} collective-permute-done((bf16[1024,256]{1,0:T(8,128)(2,1)}, bf16[1024,256]{1,0:T(8,128)(2,1)}, u32[]{:S(2)}, u32[]{:S(2)}) %collective-permute-start.21) | collective-permute-done | bytes 524320 | tf_op jit(solution)/shard_map/ppermute | solution.py:589
  283.3 4.6 %project_rows.3 = (bf16[512,1024]{1,0:T(8,128)(2,1)S(1)}, bf16[512,1024]{1,0:T(8,128)(2,1)S(1)}) custom-call(s32[1]{0:T(128)} %bitcast.place_ref, s32[1]{0:T(128)} %bitcast.5.stay_ref, bf16[272,1024]{1,0:T(8,128)(2,1)} %get-tuple-element.111.refs_0_, bf16[272,1024]{1,0:T(8,128)(2,1)S(1)} %collective-permute-done.13.refs_1_, ...), custom_call_target="tpu_custom_call" | custom-call | flops 2147483648 | bytes 12582912 | tf_op jit(solution)/shard_map/project_rows/pallas_call | solution.py:442
  288.0 2.6 collective-permute-done.22
  291.9 3.5 %collective-permute-start.25 = (bf16[128,1024]{1,0:T(8,128)(2,1)S(1)}, bf16[128,1024]{1,0:T(8,128)(2,1)S(1)}, u32[]{:S(2)}, u32[]{:S(2)}) collective-permute-start(bf16[128,1024]{1,0:T(8,128)(2,1)S(1)} %get-tuple-element.129), channel_id=1, source_target_pairs={{0,6},{2,4},{4,2},{6,0},{8,14},{10,12},{12,10},{14,8},{16,22},{18,... | collective-permute-start | bytes 786440 | tf_op jit(solution)/shard_map/ppermute | solution.py:589
  296.0 5.0 %collective-permute-done.23.refs_1_ = bf16[128,1024]{1,0:T(8,128)(2,1)S(1)} collective-permute-done((bf16[128,1024]{1,0:T(8,128)(2,1)S(1)}, bf16[128,1024]{1,0:T(8,128)(2,1)S(1)}, u32[]{:S(2)}, u32[]{:S(2)}) %collective-permute-start.23) | collective-permute-done | bytes 262176 | tf_op jit(solution)/shard_map/ppermute | solution.py:589
  301.1 4.8 %collective-permute-done.24.refs_2_ = bf16[128,1024]{1,0:T(8,128)(2,1)S(1)} collective-permute-done((bf16[128,1024]{1,0:T(8,128)(2,1)S(1)}, bf16[128,1024]{1,0:T(8,128)(2,1)S(1)}, u32[]{:S(2)}, u32[]{:S(2)}) %collective-permute-start.24) | collective-permute-done | bytes 262176 | tf_op jit(solution)/shard_map/ppermute | solution.py:589
  306.7 5.6 %add_norm.1 = (bf16[128,4096]{1,0:T(8,128)(2,1)}, bf16[128,4096]{1,0:T(8,128)(2,1)}) custom-call(s32[1]{0:T(128)} %bitcast.place_ref, s32[4]{0:T(128)} %pad_add_fusion.line_ref, bf16[128,1024]{1,0:T(8,128)(2,1)} %copy-done.11, bf16[128,1024]{1,0:T(8,128)(2,1)} %copy-done.26, bf16[128,1024]{1,0:T(8,128)(2,1)} %copy-done.27, bf16[128,1024]{1,0:T(8,128)(2,1)} %copy-done.28, ...), custom_call_target="tpu_custom_call" | custom-call | tf_op jit(solution)/shard_map/add_norm/pallas_call | solution.py:527
  (91 shorter events, 9.1 us)
Async XLA Ops:
  1.4 6.8 %collective-permute-start.3 = (bf16[1,2048]{1,0:T(2,128)(2,1)S(1)}, bf16[1,2048]{1,0:T(2,128)(2,1)S(1)}, u32[]{:S(2)}, u32[]{:S(2)}) collective-permute-start(bf16[1,2048]{1,0:T(2,128)(2,1)S(1)} %slice.23), channel_id=1, source_target_pairs={{0,2},{2,4},{4,6},{6,8},{8,10},{10,12},{12,14},{14,16},{16,18},{18... | collective-permute-start | bytes 12296 | tf_op jit(solution)/shard_map/ppermute | solution.py:23
  8.2 1.2 copy-start.4
  11.7 5.1 %copy-start.5 = (bf16[256,2048]{1,0:T(8,128)(2,1)S(1)}, bf16[256,2048]{1,0:T(8,128)(2,1)}, u32[]{:S(2)}) copy-start(bf16[256,2048]{1,0:T(8,128)(2,1)} %refs_0_.1) | copy-start | bytes 3145732
  11.7 46.4 %all-to-all-start.1 = ((bf16[8,64,2176]{2,1,0:T(8,128)(2,1)}), bf16[8,64,2176]{2,1,0:T(8,128)(2,1)S(1)}, u32[]{:S(2)}, u32[]{:S(2)}) async-start(bf16[8,64,2176]{2,1,0:T(8,128)(2,1)} %spread_queries.3), calls=%async_computation.1 | async-start | bytes 4456448 | tf_op jit(solution)/shard_map/all_to_all | solution.py:584
  17.7 46.5 %copy-start.2 = (bf16[2048,256]{1,0:T(8,128)(2,1)S(1)}, bf16[2048,256]{1,0:T(8,128)(2,1)}, u32[]{:S(2)}) copy-start(bf16[2048,256]{1,0:T(8,128)(2,1)} %refs_12_) | copy-start | bytes 3145732
  17.7 38.3 %collective-permute-start = (bf16[256,1024]{1,0:T(8,128)(2,1)S(1)}, bf16[256,1024]{1,0:T(8,128)(2,1)S(1)}, u32[]{:S(2)}, u32[]{:S(2)}) collective-permute-start(bf16[256,1024]{1,0:T(8,128)(2,1)S(1)} %get-tuple-element.137), channel_id=1, source_target_pairs={{0,16},{2,18},{4,20},{6,22},{8,24},{10,26},{12,28},{14,30},{16,0},... | collective-permute-start | bytes 1572872 | tf_op jit(solution)/shard_map/ppermute | solution.py:595
  21.0 35.0 %collective-permute-start.1 = (bf16[1,2048]{1,0:T(2,128)(2,1)S(1)}, bf16[1,2048]{1,0:T(2,128)(2,1)S(1)}, u32[]{:S(2)}, u32[]{:S(2)}) collective-permute-start(bf16[1,2048]{1,0:T(2,128)(2,1)S(1)} %slice.23), channel_id=1, source_target_pairs={{0,18},{2,20},{4,22},{6,24},{8,26},{10,28},{12,30},{14,0},{16,2},{... | collective-permute-start | bytes 12296 | tf_op jit(solution)/shard_map/ppermute | solution.py:610
  24.4 27.5 %collective-permute-start.2 = (s32[1,128]{1,0:T(1,128)S(1)}, s32[1,128]{1,0:T(1,128)S(1)}, u32[]{:S(2)}, u32[]{:S(2)}) collective-permute-start(s32[1,128]{1,0:T(1,128)S(1)} %pad_bitcast_fusion), channel_id=1, source_target_pairs={{0,16},{2,18},{4,20},{6,22},{8,24},{10,26},{12,28},{14,30},{16,0},... | collective-permute-start | bytes 1544 | tf_op jit(solution)/shard_map/ppermute | solution.py:595
  56.0 9.2 %copy-start.12 = (bf16[1,2048]{1,0:T(2,128)(2,1)}, bf16[1,2048]{1,0:T(2,128)(2,1)S(1)}, u32[]{:S(2)}) copy-start(bf16[1,2048]{1,0:T(2,128)(2,1)S(1)} %collective-permute-done.1.carried_ref) | copy-start | bytes 12292
  56.3 9.0 %copy-start.13 = (s32[8]{0:T(128)}, s32[8]{0:T(128)S(1)}, u32[]{:S(2)}) copy-start(s32[8]{0:T(128)S(1)} %get-tuple-element.130.slot_ref) | copy-start | bytes 100
  56.3 9.0 %copy-start.14 = (s32[8]{0:T(128)}, s32[8]{0:T(128)S(1)}, u32[]{:S(2)}) copy-start(s32[8]{0:T(128)S(1)} %get-tuple-element.131.block_ref) | copy-start | bytes 100
  58.1 7.1 %copy-start.23 = (bf16[8,64,2176]{2,1,0:T(8,128)(2,1)}, bf16[8,64,2176]{2,1,0:T(8,128)(2,1)S(1)}, u32[]{:S(2)}) copy-start(bf16[8,64,2176]{2,1,0:T(8,128)(2,1)S(1)} %all-to-all-done.1.tag_ref.query_ref) | copy-start | bytes 6684676
  58.1 29.4 %all-to-all-start = ((bf16[8,64,1152]{2,1,0:T(8,128)(2,1)}), bf16[8,64,1152]{2,1,0:T(8,128)(2,1)}, u32[]{:S(2)}, u32[]{:S(2)}) async-start(bf16[8,64,1152]{2,1,0:T(8,128)(2,1)} %spread_queries.4), calls=%async_computation | async-start | bytes 2359296 | tf_op jit(solution)/shard_map/all_to_all | solution.py:584
  63.3 22.1 %collective-permute-start.4 = (bf16[256,1024]{1,0:T(8,128)(2,1)}, bf16[256,1024]{1,0:T(8,128)(2,1)}, u32[]{:S(2)}, u32[]{:S(2)}) collective-permute-start(bf16[256,1024]{1,0:T(8,128)(2,1)} %get-tuple-element.69), channel_id=1, source_target_pairs={{0,16},{2,18},{4,20},{6,22},{8,24},{10,26},{12,28},{14,30},{16,0},... | collective-permute-start | bytes 1572872 | tf_op jit(solution)/shard_map/ppermute | solution.py:595
  90.6 4.8 %copy-start.24 = (bf16[1024,256]{1,0:T(8,128)(2,1)S(1)}, bf16[1024,256]{1,0:T(8,128)(2,1)}, u32[]{:S(2)}) copy-start(bf16[1024,256]{1,0:T(8,128)(2,1)} %get-tuple-element.83) | copy-start | bytes 1572868
  90.6 42.0 %all-to-all-start.2 = ((bf16[8,64,2304]{2,1,0:T(8,128)(2,1)}), bf16[8,64,2304]{2,1,0:T(8,128)(2,1)S(1)}, u32[]{:S(2)}, u32[]{:S(2)}) async-start(bf16[8,64,2304]{2,1,0:T(8,128)(2,1)} %spread_queries.5), calls=%async_computation.2 | async-start | bytes 4718592 | tf_op jit(solution)/shard_map/all_to_all | solution.py:584
  95.3 35.1 %collective-permute-start.5 = (bf16[1024,256]{1,0:T(8,128)(2,1)S(1)}, bf16[1024,256]{1,0:T(8,128)(2,1)}, u32[]{:S(2)}, u32[]{:S(2)}) collective-permute-start(bf16[1024,256]{1,0:T(8,128)(2,1)S(1)} %copy-done.24), channel_id=1, source_target_pairs={{0,16},{2,18},{4,20},{6,22},{8,24},{10,26},{12,28},{14,30},{16,0},... | collective-permute-start | bytes 1572872 | tf_op jit(solution)/shard_map/ppermute | solution.py:595
  132.6 1.5 copy-start
  134.0 42.0 %all-to-all-start.3 = ((bf16[8,64,2304]{2,1,0:T(8,128)(2,1)}), bf16[8,64,2304]{2,1,0:T(8,128)(2,1)S(1)}, u32[]{:S(2)}, u32[]{:S(2)}) async-start(bf16[8,64,2304]{2,1,0:T(8,128)(2,1)} %attend_blocks.6), calls=%async_computation.3 | async-start | bytes 4718592 | tf_op jit(solution)/shard_map/all_to_all | solution.py:584
  137.8 36.3 %collective-permute-start.6 = (bf16[1024,256]{1,0:T(8,128)(2,1)}, bf16[1024,256]{1,0:T(8,128)(2,1)}, u32[]{:S(2)}, u32[]{:S(2)}) collective-permute-start(bf16[1024,256]{1,0:T(8,128)(2,1)} %get-tuple-element.114), channel_id=1, source_target_pairs={{0,16},{2,18},{4,20},{6,22},{8,24},{10,26},{12,28},{14,30},{16,0},... | collective-permute-start | bytes 1572872 | tf_op jit(solution)/shard_map/ppermute | solution.py:595
  176.1 34.3 %all-to-all-start.4 = ((bf16[8,64,1152]{2,1,0:T(8,128)(2,1)}), bf16[8,64,1152]{2,1,0:T(8,128)(2,1)S(1)}, u32[]{:S(2)}, u32[]{:S(2)}) async-start(bf16[8,64,1152]{2,1,0:T(8,128)(2,1)} %attend_blocks.7), calls=%async_computation.4 | async-start | bytes 2359296 | tf_op jit(solution)/shard_map/all_to_all | solution.py:584
  179.8 5.5 %copy-start.25 = (bf16[1024,256]{1,0:T(8,128)(2,1)S(1)}, bf16[1024,256]{1,0:T(8,128)(2,1)}, u32[]{:S(2)}) copy-start(bf16[1024,256]{1,0:T(8,128)(2,1)} %get-tuple-element.83) | copy-start | bytes 1572868
  181.9 27.7 %collective-permute-start.7 = (bf16[4,64,1152]{2,1,0:T(8,128)(2,1)S(1)}, bf16[4,64,1152]{2,1,0:T(8,128)(2,1)S(1)}, u32[]{:S(2)}, u32[]{:S(2)}) collective-permute-start(bf16[4,64,1152]{2,1,0:T(8,128)(2,1)S(1)} %merge_far.2), channel_id=1, source_target_pairs={{0,16},{2,18},{4,20},{6,22},{8,24},{10,26},{12,28},{14,30},{16,0},... | collective-permute-start | bytes 1769480 | tf_op jit(solution)/shard_map/ppermute | solution.py:595
  209.6 0.8 copy-start.9
  210.4 5.9 %copy-start.1 = (bf16[8,64,2304]{2,1,0:T(8,128)(2,1)S(1)}, bf16[8,64,2304]{2,1,0:T(8,128)(2,1)}, u32[]{:S(2)}) copy-start(bf16[8,64,2304]{2,1,0:T(8,128)(2,1)} %copy-done) | copy-start | bytes 7077892
  210.4 5.9 %copy-start.10 = (bf16[4,64,1152]{2,1,0:T(8,128)(2,1)S(1)}, bf16[4,64,1152]{2,1,0:T(8,128)(2,1)}, u32[]{:S(2)}) copy-start(bf16[4,64,1152]{2,1,0:T(8,128)(2,1)} %copy-done.9) | copy-start | bytes 1769476
  212.4 34.0 %collective-permute-start.12 = (bf16[2048,256]{1,0:T(8,128)(2,1)}, bf16[2048,256]{1,0:T(8,128)(2,1)S(1)}, u32[]{:S(2)}, u32[]{:S(2)}) collective-permute-start(bf16[2048,256]{1,0:T(8,128)(2,1)} %pad_maximum_fusion), channel_id=1, source_target_pairs={{0,8},{2,10},{4,12},{6,14},{8,0},{10,2},{12,4},{14,6},{16,24},{18,... | collective-permute-start | bytes 3145736 | tf_op jit(solution)/shard_map/ppermute | solution.py:589
  212.9 31.8 %collective-permute-start.8 = (bf16[4,64,1152]{2,1,0:T(8,128)(2,1)S(1)}, bf16[4,64,1152]{2,1,0:T(8,128)(2,1)S(1)}, u32[]{:S(2)}, u32[]{:S(2)}) collective-permute-start(bf16[4,64,1152]{2,1,0:T(8,128)(2,1)S(1)} %merge_far.3), channel_id=1, source_target_pairs={{0,16},{2,18},{4,20},{6,22},{8,24},{10,26},{12,28},{14,30},{16,0},... | collective-permute-start | bytes 1769480 | tf_op jit(solution)/shard_map/ppermute | solution.py:595
  218.8 26.0 %collective-permute-start.10 = (bf16[272,1024]{1,0:T(8,128)(2,1)S(1)}, bf16[272,1024]{1,0:T(8,128)(2,1)S(1)}, u32[]{:S(2)}, u32[]{:S(2)}) collective-permute-start(bf16[272,1024]{1,0:T(8,128)(2,1)S(1)} %get-tuple-element.118.refs_0_), channel_id=1, source_target_pairs={{0,4},{2,6},{4,0},{6,2},{8,12},{10,14},{12,8},{14,10},{16,20},{18,... | collective-permute-start | bytes 1671176 | tf_op jit(solution)/shard_map/ppermute | solution.py:589
  220.3 24.5 %collective-permute-start.11 = (bf16[272,1024]{1,0:T(8,128)(2,1)S(1)}, bf16[272,1024]{1,0:T(8,128)(2,1)S(1)}, u32[]{:S(2)}, u32[]{:S(2)}) collective-permute-start(bf16[272,1024]{1,0:T(8,128)(2,1)S(1)} %get-tuple-element.118.refs_0_), channel_id=1, source_target_pairs={{0,6},{2,4},{4,2},{6,0},{8,14},{10,12},{12,10},{14,8},{16,22},{18,... | collective-permute-start | bytes 1671176 | tf_op jit(solution)/shard_map/ppermute | solution.py:589
  221.7 23.8 %collective-permute-start.9 = (bf16[272,1024]{1,0:T(8,128)(2,1)S(1)}, bf16[272,1024]{1,0:T(8,128)(2,1)S(1)}, u32[]{:S(2)}, u32[]{:S(2)}) collective-permute-start(bf16[272,1024]{1,0:T(8,128)(2,1)S(1)} %get-tuple-element.118.refs_0_), channel_id=1, source_target_pairs={{0,2},{2,0},{4,6},{6,4},{8,10},{10,8},{12,14},{14,12},{16,18},{18,... | collective-permute-start | bytes 1671176 | tf_op jit(solution)/shard_map/ppermute | solution.py:589
  222.3 0.8 copy-start.15
  244.8 4.9 %copy-start.17 = (bf16[272,1024]{1,0:T(8,128)(2,1)}, bf16[272,1024]{1,0:T(8,128)(2,1)S(1)}, u32[]{:S(2)}) copy-start(bf16[272,1024]{1,0:T(8,128)(2,1)S(1)} %collective-permute-done.10.refs_2_) | copy-start | bytes 1671172
  244.8 0.8 copy-start.19
  245.6 0.8 copy-start.21
  246.4 3.2 %copy-start.6 = (bf16[2048,256]{1,0:T(8,128)(2,1)}, bf16[2048,256]{1,0:T(8,128)(2,1)S(1)}, u32[]{:S(2)}) copy-start(bf16[2048,256]{1,0:T(8,128)(2,1)S(1)} %collective-permute-done.12.refs_5_.refs_7_.refs_13_.refs_15_) | copy-start | bytes 3145732
  246.4 16.9 %copy-start.3 = (bf16[2048,256]{1,0:T(8,128)(2,1)S(1)}, bf16[2048,256]{1,0:T(8,128)(2,1)}, u32[]{:S(2)}) copy-start(bf16[2048,256]{1,0:T(8,128)(2,1)} %refs_12_) | copy-start | bytes 3145732
  249.6 8.4 %collective-permute-start.16 = (bf16[16,2048]{1,0:T(8,128)(2,1)S(1)}, bf16[16,2048]{1,0:T(8,128)(2,1)S(1)}, u32[]{:S(2)}, u32[]{:S(2)}) collective-permute-start(bf16[16,2048]{1,0:T(8,128)(2,1)S(1)} %get-tuple-element.112), channel_id=1, source_target_pairs={{8,0},{16,8},{24,16},{9,1},{17,9},{25,17}} | collective-permute-start | bytes 196616 | tf_op jit(solution)/shard_map/ppermute | solution.py:697
  250.9 7.1 %collective-permute-start.17 = (bf16[16,2048]{1,0:T(8,128)(2,1)S(1)}, bf16[16,2048]{1,0:T(8,128)(2,1)S(1)}, u32[]{:S(2)}, u32[]{:S(2)}) collective-permute-start(bf16[16,2048]{1,0:T(8,128)(2,1)S(1)} %get-tuple-element.112), channel_id=1, source_target_pairs={{8,2},{16,10},{24,18},{9,3},{17,11},{25,19}} | collective-permute-start | bytes 196616 | tf_op jit(solution)/shard_map/ppermute | solution.py:697
  251.6 6.4 %collective-permute-start.18 = (bf16[16,2048]{1,0:T(8,128)(2,1)S(1)}, bf16[16,2048]{1,0:T(8,128)(2,1)S(1)}, u32[]{:S(2)}, u32[]{:S(2)}) collective-permute-start(bf16[16,2048]{1,0:T(8,128)(2,1)S(1)} %get-tuple-element.112), channel_id=1, source_target_pairs={{8,4},{16,12},{24,20},{9,5},{17,13},{25,21}} | collective-permute-start | bytes 196616 | tf_op jit(solution)/shard_map/ppermute | solution.py:697
  252.2 11.0 %collective-permute-start.19 = (bf16[16,2048]{1,0:T(8,128)(2,1)S(1)}, bf16[16,2048]{1,0:T(8,128)(2,1)S(1)}, u32[]{:S(2)}, u32[]{:S(2)}) collective-permute-start(bf16[16,2048]{1,0:T(8,128)(2,1)S(1)} %get-tuple-element.112), channel_id=1, source_target_pairs={{8,6},{16,14},{24,22},{9,7},{17,15},{25,23}} | collective-permute-start | bytes 196616 | tf_op jit(solution)/shard_map/ppermute | solution.py:697
  252.9 30.4 %collective-permute-start.13 = (bf16[272,1024]{1,0:T(8,128)(2,1)}, bf16[272,1024]{1,0:T(8,128)(2,1)S(1)}, u32[]{:S(2)}, u32[]{:S(2)}) collective-permute-start(bf16[272,1024]{1,0:T(8,128)(2,1)} %get-tuple-element.111.refs_0_), channel_id=1, source_target_pairs={{0,2},{2,0},{4,6},{6,4},{8,10},{10,8},{12,14},{14,12},{16,18},{18,... | collective-permute-start | bytes 1671176 | tf_op jit(solution)/shard_map/ppermute | solution.py:589
  258.0 25.3 %collective-permute-start.14 = (bf16[272,1024]{1,0:T(8,128)(2,1)}, bf16[272,1024]{1,0:T(8,128)(2,1)S(1)}, u32[]{:S(2)}, u32[]{:S(2)}) collective-permute-start(bf16[272,1024]{1,0:T(8,128)(2,1)} %get-tuple-element.111.refs_0_), channel_id=1, source_target_pairs={{0,4},{2,6},{4,0},{6,2},{8,12},{10,14},{12,8},{14,10},{16,20},{18,... | collective-permute-start | bytes 1671176 | tf_op jit(solution)/shard_map/ppermute | solution.py:589
  258.0 25.3 %collective-permute-start.15 = (bf16[272,1024]{1,0:T(8,128)(2,1)}, bf16[272,1024]{1,0:T(8,128)(2,1)S(1)}, u32[]{:S(2)}, u32[]{:S(2)}) collective-permute-start(bf16[272,1024]{1,0:T(8,128)(2,1)} %get-tuple-element.111.refs_0_), channel_id=1, source_target_pairs={{0,6},{2,4},{4,2},{6,0},{8,14},{10,12},{12,10},{14,8},{16,22},{18,... | collective-permute-start | bytes 1671176 | tf_op jit(solution)/shard_map/ppermute | solution.py:589
  258.0 18.3 %collective-permute-start.20 = (bf16[1024,256]{1,0:T(8,128)(2,1)}, bf16[1024,256]{1,0:T(8,128)(2,1)S(1)}, u32[]{:S(2)}, u32[]{:S(2)}) collective-permute-start(bf16[1024,256]{1,0:T(8,128)(2,1)} %get-tuple-element.114), channel_id=1, source_target_pairs={{0,8},{2,10},{4,12},{6,14},{8,0},{10,2},{12,4},{14,6},{16,24},{18,... | collective-permute-start | bytes 1572872 | tf_op jit(solution)/shard_map/ppermute | solution.py:589
  263.2 20.1 %collective-permute-start.21 = (bf16[1024,256]{1,0:T(8,128)(2,1)}, bf16[1024,256]{1,0:T(8,128)(2,1)}, u32[]{:S(2)}, u32[]{:S(2)}) collective-permute-start(bf16[1024,256]{1,0:T(8,128)(2,1)} %collective-permute-done.6.refs_10_), channel_id=1, source_target_pairs={{0,8},{2,10},{4,12},{6,14},{8,0},{10,2},{12,4},{14,6},{16,24},{18,... | collective-permute-start | bytes 1572872 | tf_op jit(solution)/shard_map/ppermute | solution.py:589
  263.3 1.2 copy-start.7
  264.5 1.1 copy-start.16
  265.6 1.1 copy-start.18
  266.7 1.1 copy-start.20
  267.7 1.1 copy-start.22
  268.8 14.6 %copy-start.8 = (bf16[2048,256]{1,0:T(8,128)(2,1)S(1)}, bf16[2048,256]{1,0:T(8,128)(2,1)}, u32[]{:S(2)}) copy-start(bf16[2048,256]{1,0:T(8,128)(2,1)} %copy-done.6) | copy-start | bytes 3145732
  288.0 2.7 collective-permute-start.22
  291.2 0.7 copy-start.11
  291.9 9.1 %collective-permute-start.23 = (bf16[128,1024]{1,0:T(8,128)(2,1)S(1)}, bf16[128,1024]{1,0:T(8,128)(2,1)S(1)}, u32[]{:S(2)}, u32[]{:S(2)}) collective-permute-start(bf16[128,1024]{1,0:T(8,128)(2,1)S(1)} %get-tuple-element.127), channel_id=1, source_target_pairs={{0,2},{2,0},{4,6},{6,4},{8,10},{10,8},{12,14},{14,12},{16,18},{18,... | collective-permute-start | bytes 786440 | tf_op jit(solution)/shard_map/ppermute | solution.py:589
  291.9 14.0 %collective-permute-start.24 = (bf16[128,1024]{1,0:T(8,128)(2,1)S(1)}, bf16[128,1024]{1,0:T(8,128)(2,1)S(1)}, u32[]{:S(2)}, u32[]{:S(2)}) collective-permute-start(bf16[128,1024]{1,0:T(8,128)(2,1)S(1)} %get-tuple-element.128), channel_id=1, source_target_pairs={{0,4},{2,6},{4,0},{6,2},{8,12},{10,14},{12,8},{14,10},{16,20},{18,... | collective-permute-start | bytes 786440 | tf_op jit(solution)/shard_map/ppermute | solution.py:589
  291.9 14.0 %collective-permute-start.25 = (bf16[128,1024]{1,0:T(8,128)(2,1)S(1)}, bf16[128,1024]{1,0:T(8,128)(2,1)S(1)}, u32[]{:S(2)}, u32[]{:S(2)}) collective-permute-start(bf16[128,1024]{1,0:T(8,128)(2,1)S(1)} %get-tuple-element.129), channel_id=1, source_target_pairs={{0,6},{2,4},{4,2},{6,0},{8,14},{10,12},{12,10},{14,8},{16,22},{18,... | collective-permute-start | bytes 786440 | tf_op jit(solution)/shard_map/ppermute | solution.py:589
  301.1 4.8 %copy-start.26 = (bf16[128,1024]{1,0:T(8,128)(2,1)}, bf16[128,1024]{1,0:T(8,128)(2,1)S(1)}, u32[]{:S(2)}) copy-start(bf16[128,1024]{1,0:T(8,128)(2,1)S(1)} %collective-permute-done.23.refs_1_) | copy-start | bytes 786436
  305.9 0.7 copy-start.27
  305.9 0.8 copy-start.28

commit v8 on v7

--- a/solution.py
+++ b/solution.py
@@ -211,7 +211,7 @@
         ],
         out_shape=jax.ShapeDtypeStruct((peers, span_len, places * wide), asked.dtype),
         input_output_aliases={4: 0} if extra else {},
-        compiler_params=pltpu.CompilerParams(vmem_limit_bytes=58 * MIB),
+        compiler_params=pltpu.CompilerParams(vmem_limit_bytes=54 * MIB),
         cost_estimate=pl.CostEstimate(
             flops=4 * peers * heads * span_len * length * HEAD,
             bytes_accessed=2 * peers * width * (2 * span_len + 2 * length),
@@ -398,14 +398,12 @@
         below = first_ref[at : at + ROW_TILE].astype(jnp.float32)[0:1]
         if member == PLANE - 1:
             below = jnp.zeros_like(below)
-            if last_part:
-                under = functools.reduce(jnp.add, [ref[...].astype(jnp.float32) for ref in belows])
-                below = under[0:1, width:]
         end = half + (member + 1) * part
         held = rows_ref[end - ROW_TILE : end].astype(jnp.float32)
         rows_ref[end - ROW_TILE : end] = jnp.where(last, below, held).astype(rows_ref.dtype)
     if last_part:
-        under = under[:, :width].astype(rows_ref.dtype)
+        below = functools.reduce(jnp.add, [ref[...].astype(jnp.float32) for ref in belows])
+        below = below.astype(rows_ref.dtype)
     stay = pl.multiple_of(stay_ref[0] * half, half)
     go = pl.multiple_of((1 - stay_ref[0]) * half, half)
     for shard in range(PLANE):
@@ -421,14 +419,24 @@
                 result = result + before[at][:, cut]
             ref[:, cut] = result.astype(ref.dtype)
         if last_part:
-            row = jnp.dot(under, held_ref[PLANE + shard], preferred_element_type=jnp.float32)[0:1]
+            row = functools.reduce(
+                jnp.add,
+                [
+                    jnp.dot(
+                        below[:, side * width : (side + 1) * width],
+                        held_ref[at],
+                        preferred_element_type=jnp.float32,
+                    )
+                    for side, at in ((0, PLANE + shard), (1, shard))
+                ],
+            )[0:1]
             at_end = lax.broadcasted_iota(jnp.int32, (ROW_TILE, tile), 0) == ROW_TILE - 1
             for upper, ref in ((stay_ref[0] > 0, keep_ref), (stay_ref[0] == 0, send_ref)):
 
                 @pl.when(upper)
                 def _():
                     held = ref[half - ROW_TILE :, cut].astype(jnp.float32)
-                    ref[half - ROW_TILE :, cut] = jnp.where(at_end, held + row, held).astype(ref.dtype)
+                    ref[half - ROW_TILE :, cut] = jnp.where(at_end, row, held).astype(ref.dtype)
 
 
 def project(sources, belows, weights, place, stay, before, kind):
@@ -534,7 +542,7 @@
             scratch_shapes=[pltpu.VMEM((tile, columns), jnp.float32)],
         ),
         out_shape=[jax.ShapeDtypeStruct((rows, columns), residual.dtype)] * 2,
-        compiler_params=pltpu.CompilerParams(vmem_limit_bytes=60 * MIB),
+        compiler_params=pltpu.CompilerParams(vmem_limit_bytes=20 * MIB),
         name="add_norm",
     )(place, line, *branches, residual, drop_mask, gain[None], bias[None])
 

time: 314 us -> 313 us (level)
  waiting for transfers between devices: 168 us -> 163 us
  Pallas kernels: 58 us -> 62.6 us
    pallas_call x4, Pallas kernels: 27 us -> 32.6 us  [attend(): pl.pallas_call(functools.partial(attend_kernel, chunk), grid=(peers,), in...]
    ppermute x7, waiting for transfers between devices: 130 us -> 125 us  [to_partner(): return lax.ppermute(x, 'dp', across)]
  transfers between devices with their start and end apart: 31 -> 31, of which waited for: 16 -> 16; matrix products, arithmetic and copies ran while one was open for 2% -> 2% of each run, Pallas kernels for 12% -> 14%
where the time goes in v8:
time: 313 us; the launch traced here: 311 us
  waiting for transfers between devices  163 us (52%)
  starting transfers between devices  64.9 us (21%)
  Pallas kernels  62.6 us (20%)
  local copies, waits for them, and re-layouts  17.1 us (5%)
    ppermute x7, waiting for transfers between devices, to_partner(): return lax.ppermute(x, 'dp', across)  125 us
    pallas_call x4, Pallas kernels, attend(): pl.pallas_call(functools.partial(attend_kernel, chunk), grid=(peers,), in...  32.6 us
    all_to_all x5, starting transfers between devices, exchange(): lax.all_to_all(x, 'dp', split_axis=0, concat_axis=0, tiled=True, axis_ind...  22.5 us
    ppermute x12, waiting for transfers between devices, swap(): return lax.ppermute(x, 'dp', [(i, i ^ by) for i in range(peer_count)])  21.7 us
    ppermute x7, starting transfers between devices, to_partner(): return lax.ppermute(x, 'dp', across)  16.3 us
    ppermute x12, starting transfers between devices, swap(): return lax.ppermute(x, 'dp', [(i, i ^ by) for i in range(peer_count)])  14.5 us
    unnamed x60, local copies, waits for them, and re-layouts  14.2 us
    pallas_call x2, Pallas kernels, project(): pl.pallas_call(functools.partial(project_kernel, starts), grid_spec=pltpu...  8.65 us
  transfers between devices with their start and end apart: 31, of which 16 were waited for; matrix products, arithmetic and copies ran while one was open for 2% of the time, Pallas kernels for 14%

profile of v8, /device:TPU:0, one launch (start us, length us, event | category | flops | bytes accessed | tf_op | source)
XLA Modules:
  0.0 311.2 jit_solution(14324762074905935486)
XLA Ops:
  1.4 4.8 %collective-permute-start.3 = (bf16[1,2048]{1,0:T(2,128)(2,1)S(1)}, bf16[1,2048]{1,0:T(2,128)(2,1)S(1)}, u32[]{:S(2)}, u32[]{:S(2)}) collective-permute-start(bf16[1,2048]{1,0:T(2,128)(2,1)S(1)} %slice.23), channel_id=1, source_target_pairs={{0,2},{2,4},{4,6},{6,8},{8,10},{10,12},{12,14},{14,16},{16,18},{18... | collective-permute-start | bytes 12296 | tf_op jit(solution)/shard_map/ppermute | solution.py:23
  8.2 1.2 copy-done.4
  9.4 2.3 spread_queries.3
  11.7 5.1 %all-to-all-start.1 = ((bf16[8,64,2176]{2,1,0:T(8,128)(2,1)}), bf16[8,64,2176]{2,1,0:T(8,128)(2,1)S(1)}, u32[]{:S(2)}, u32[]{:S(2)}) async-start(bf16[8,64,2176]{2,1,0:T(8,128)(2,1)} %spread_queries.3), calls=%async_computation.1 | async-start | bytes 4456448 | tf_op jit(solution)/shard_map/all_to_all | solution.py:592
  16.8 0.9 fusion.7
  17.7 3.3 %collective-permute-start = (bf16[256,1024]{1,0:T(8,128)(2,1)S(1)}, bf16[256,1024]{1,0:T(8,128)(2,1)S(1)}, u32[]{:S(2)}, u32[]{:S(2)}) collective-permute-start(bf16[256,1024]{1,0:T(8,128)(2,1)S(1)} %get-tuple-element.137), channel_id=1, source_target_pairs={{0,16},{2,18},{4,20},{6,22},{8,24},{10,26},{12,28},{14,30},{16,0},... | collective-permute-start | bytes 1572872 | tf_op jit(solution)/shard_map/ppermute | solution.py:603
  21.0 3.4 %collective-permute-start.1 = (bf16[1,2048]{1,0:T(2,128)(2,1)S(1)}, bf16[1,2048]{1,0:T(2,128)(2,1)S(1)}, u32[]{:S(2)}, u32[]{:S(2)}) collective-permute-start(bf16[1,2048]{1,0:T(2,128)(2,1)S(1)} %slice.23), channel_id=1, source_target_pairs={{0,18},{2,20},{4,22},{6,24},{8,26},{10,28},{12,30},{14,0},{16,2},{... | collective-permute-start | bytes 12296 | tf_op jit(solution)/shard_map/ppermute | solution.py:618
  24.4 2.8 collective-permute-start.2
  27.2 24.7 %collective-permute-done.2 = s32[1,128]{1,0:T(1,128)S(1)} collective-permute-done((s32[1,128]{1,0:T(1,128)S(1)}, s32[1,128]{1,0:T(1,128)S(1)}, u32[]{:S(2)}, u32[]{:S(2)}) %collective-permute-start.2) | collective-permute-done | bytes 544 | tf_op jit(solution)/shard_map/ppermute | solution.py:603
  52.0 4.0 %collective-permute-done.1.carried_ref = bf16[1,2048]{1,0:T(2,128)(2,1)S(1)} collective-permute-done((bf16[1,2048]{1,0:T(2,128)(2,1)S(1)}, bf16[1,2048]{1,0:T(2,128)(2,1)S(1)}, u32[]{:S(2)}, u32[]{:S(2)}) %collective-permute-start.1) | collective-permute-done | bytes 4128 | tf_op jit(solution)/shard_map/ppermute | solution.py:618
  56.3 1.8 spread_queries.4
  58.1 5.2 %all-to-all-start = ((bf16[8,64,1152]{2,1,0:T(8,128)(2,1)}), bf16[8,64,1152]{2,1,0:T(8,128)(2,1)}, u32[]{:S(2)}, u32[]{:S(2)}) async-start(bf16[8,64,1152]{2,1,0:T(8,128)(2,1)} %spread_queries.4), calls=%async_computation | async-start | bytes 2359296 | tf_op jit(solution)/shard_map/all_to_all | solution.py:592
  63.3 0.9 collective-permute-start.4
  64.2 1.0 fusion.6
  65.2 7.7 %attend_blocks.4.refs_1_ = bf16[8,64,2304]{2,1,0:T(8,128)(2,1)} custom-call(bf16[8,64,2176]{2,1,0:T(8,128)(2,1)} %copy-done.26, bf16[8,64,2176]{2,1,0:T(8,128)(2,1)} %copy-done.26, bf16[8,128,2048]{2,1,0:T(8,128)(2,1)} %key_ref.7, bf16[8,128,2048]{2,1,0:T(8,128)(2,1)} %value_ref.7), custom_call_target="tpu_custom_call" | custom-call | flops 268435456 | bytes 6291456 | tf_op jit(solution)/shard_map/attend_blocks/pallas_call | solution.py:196
  73.0 7.7 %attend_blocks.5.refs_0_ = bf16[8,64,2304]{2,1,0:T(8,128)(2,1)} custom-call(bf16[8,64,2176]{2,1,0:T(8,128)(2,1)} %copy-done.26, bf16[8,64,2176]{2,1,0:T(8,128)(2,1)} %copy-done.26, bf16[8,128,2048]{2,1,0:T(8,128)(2,1)} %key_ref.7, bf16[8,128,2048]{2,1,0:T(8,128)(2,1)} %value_ref.7), custom_call_target="tpu_custom_call" | custom-call | flops 268435456 | bytes 6291456 | tf_op jit(solution)/shard_map/attend_blocks/pallas_call | solution.py:196
  80.7 4.7 %collective-permute-done.4.refs_0_ = bf16[256,1024]{1,0:T(8,128)(2,1)} collective-permute-done((bf16[256,1024]{1,0:T(8,128)(2,1)}, bf16[256,1024]{1,0:T(8,128)(2,1)}, u32[]{:S(2)}, u32[]{:S(2)}) %collective-permute-start.4) | collective-permute-done | bytes 524320 | tf_op jit(solution)/shard_map/ppermute | solution.py:603
  85.4 2.1 all-to-all-done.tag_ref.query_ref
  87.5 3.1 spread_queries.5
  90.6 4.7 %all-to-all-start.2 = ((bf16[8,64,2304]{2,1,0:T(8,128)(2,1)}), bf16[8,64,2304]{2,1,0:T(8,128)(2,1)S(1)}, u32[]{:S(2)}, u32[]{:S(2)}) async-start(bf16[8,64,2304]{2,1,0:T(8,128)(2,1)} %spread_queries.5), calls=%async_computation.2 | async-start | bytes 4718592 | tf_op jit(solution)/shard_map/all_to_all | solution.py:592
  95.3 1.2 collective-permute-start.5
  96.5 8.6 %attend_blocks.6 = bf16[8,64,2304]{2,1,0:T(8,128)(2,1)} custom-call(bf16[8,64,1152]{2,1,0:T(8,128)(2,1)} %all-to-all-done.tag_ref.query_ref, bf16[8,64,1152]{2,1,0:T(8,128)(2,1)} %all-to-all-done.tag_ref.query_ref, bf16[8,128,2048]{2,1,0:T(8,128)(2,1)} %key_ref.7, bf16[8,128,2048]{2,1,0:T(8,128)(2,1)} %value_ref.7, ...), custom_call_target="tpu_custom_call", output_to_operand_aliasing={{}: (4, {})} | custom-call | flops 268435456 | bytes 6291456 | tf_op jit(solution)/shard_map/attend_blocks/pallas_call | solution.py:196
  105.1 25.4 %collective-permute-done.5.refs_6_.refs_14_ = bf16[1024,256]{1,0:T(8,128)(2,1)} collective-permute-done((bf16[1024,256]{1,0:T(8,128)(2,1)S(1)}, bf16[1024,256]{1,0:T(8,128)(2,1)}, u32[]{:S(2)}, u32[]{:S(2)}) %collective-permute-start.5) | collective-permute-done | bytes 524320 | tf_op jit(solution)/shard_map/ppermute | solution.py:603
  130.4 2.1 all-to-all-done.2.query_ref.refs_0_.refs_1_
  132.6 1.5 copy-done
  134.0 3.8 %all-to-all-start.3 = ((bf16[8,64,2304]{2,1,0:T(8,128)(2,1)}), bf16[8,64,2304]{2,1,0:T(8,128)(2,1)S(1)}, u32[]{:S(2)}, u32[]{:S(2)}) async-start(bf16[8,64,2304]{2,1,0:T(8,128)(2,1)} %attend_blocks.6), calls=%async_computation.3 | async-start | bytes 4718592 | tf_op jit(solution)/shard_map/all_to_all | solution.py:592
  137.8 1.4 collective-permute-start.6
  139.3 8.6 %attend_blocks.7 = bf16[8,64,1152]{2,1,0:T(8,128)(2,1)} custom-call(bf16[8,64,1152]{2,1,0:T(8,128)(2,1)} %all-to-all-done.tag_ref.query_ref, bf16[8,64,2304]{2,1,0:T(8,128)(2,1)} %copy-done, bf16[8,128,2048]{2,1,0:T(8,128)(2,1)} %key_ref.7, bf16[8,128,2048]{2,1,0:T(8,128)(2,1)} %value_ref.7), custom_call_target="tpu_custom_call" | custom-call | flops 268435456 | bytes 6291456 | tf_op jit(solution)/shard_map/attend_blocks/pallas_call | solution.py:196
  147.9 26.2 %collective-permute-done.6.refs_10_ = bf16[1024,256]{1,0:T(8,128)(2,1)} collective-permute-done((bf16[1024,256]{1,0:T(8,128)(2,1)}, bf16[1024,256]{1,0:T(8,128)(2,1)}, u32[]{:S(2)}, u32[]{:S(2)}) %collective-permute-start.6) | collective-permute-done | bytes 524320 | tf_op jit(solution)/shard_map/ppermute | solution.py:603
  174.1 2.0 all-to-all-done.3.refs_0_.refs_1_
  176.1 3.7 %all-to-all-start.4 = ((bf16[8,64,1152]{2,1,0:T(8,128)(2,1)}), bf16[8,64,1152]{2,1,0:T(8,128)(2,1)S(1)}, u32[]{:S(2)}, u32[]{:S(2)}) async-start(bf16[8,64,1152]{2,1,0:T(8,128)(2,1)} %attend_blocks.7), calls=%async_computation.4 | async-start | bytes 2359296 | tf_op jit(solution)/shard_map/all_to_all | solution.py:592
  179.8 2.1 merge_far.2
  181.9 3.4 %collective-permute-start.7 = (bf16[4,64,1152]{2,1,0:T(8,128)(2,1)S(1)}, bf16[4,64,1152]{2,1,0:T(8,128)(2,1)S(1)}, u32[]{:S(2)}, u32[]{:S(2)}) collective-permute-start(bf16[4,64,1152]{2,1,0:T(8,128)(2,1)S(1)} %merge_far.2), channel_id=1, source_target_pairs={{0,16},{2,18},{4,20},{6,22},{8,24},{10,26},{12,28},{14,30},{16,0},... | collective-permute-start | bytes 1769480 | tf_op jit(solution)/shard_map/ppermute | solution.py:603
  185.3 2.1 pad_maximum_fusion
  187.3 22.2 %collective-permute-done.7.refs_2_ = bf16[4,64,1152]{2,1,0:T(8,128)(2,1)S(1)} collective-permute-done((bf16[4,64,1152]{2,1,0:T(8,128)(2,1)S(1)}, bf16[4,64,1152]{2,1,0:T(8,128)(2,1)S(1)}, u32[]{:S(2)}, u32[]{:S(2)}) %collective-permute-start.7) | collective-permute-done | bytes 589856 | tf_op jit(solution)/shard_map/ppermute | solution.py:603
  209.6 0.8 copy-done.11
  210.4 1.9 merge_far.3
  213.0 3.4 %collective-permute-start.8 = (bf16[4,64,1152]{2,1,0:T(8,128)(2,1)S(1)}, bf16[4,64,1152]{2,1,0:T(8,128)(2,1)S(1)}, u32[]{:S(2)}, u32[]{:S(2)}) collective-permute-start(bf16[4,64,1152]{2,1,0:T(8,128)(2,1)S(1)} %merge_far.3), channel_id=1, source_target_pairs={{0,16},{2,18},{4,20},{6,22},{8,24},{10,26},{12,28},{14,30},{16,0},... | collective-permute-start | bytes 1769480 | tf_op jit(solution)/shard_map/ppermute | solution.py:603
  216.3 2.4 merge_all.2
  218.8 1.5 collective-permute-start.10
  220.3 1.5 collective-permute-start.11
  223.1 21.6 %collective-permute-done.8.refs_2_ = bf16[4,64,1152]{2,1,0:T(8,128)(2,1)S(1)} collective-permute-done((bf16[4,64,1152]{2,1,0:T(8,128)(2,1)S(1)}, bf16[4,64,1152]{2,1,0:T(8,128)(2,1)S(1)}, u32[]{:S(2)}, u32[]{:S(2)}) %collective-permute-start.8) | collective-permute-done | bytes 589856 | tf_op jit(solution)/shard_map/ppermute | solution.py:603
  244.8 0.8 copy-done.22
  246.4 3.2 %merge_all.3 = (bf16[272,1024]{1,0:T(8,128)(2,1)}, bf16[16,2048]{1,0:T(8,128)(2,1)S(1)}) custom-call(s32[8]{0:T(128)S(1)} %subtract_select_fusion.1.index_ref, s32[8]{0:T(128)S(1)} %fusion.4.use_ref, bf16[8,64,2304]{2,1,0:T(8,128)(2,1)S(1)} %all-to-all-done.3.refs_0_.refs_1_, bf16[8,64,2304]{2,1,0:T(8,128)(2,1)S(1)} %all-to-all-done.3.refs_0_.refs_1_, ...), custom_call_target="tpu_custom_call" | custom-call | tf_op jit(solution)/shard_map/merge_all/pallas_call | solution.py:336
  249.6 1.3 collective-permute-start.16
  252.9 1.6 collective-permute-start.13
  254.5 3.5 %collective-permute-done.16.refs_4_ = bf16[16,2048]{1,0:T(8,128)(2,1)S(1)} collective-permute-done((bf16[16,2048]{1,0:T(8,128)(2,1)S(1)}, bf16[16,2048]{1,0:T(8,128)(2,1)S(1)}, u32[]{:S(2)}, u32[]{:S(2)}) %collective-permute-start.16) | collective-permute-done | bytes 65568 | tf_op jit(solution)/shard_map/ppermute | solution.py:705
  258.0 5.2 %collective-permute-start.20 = (bf16[1024,256]{1,0:T(8,128)(2,1)}, bf16[1024,256]{1,0:T(8,128)(2,1)S(1)}, u32[]{:S(2)}, u32[]{:S(2)}) collective-permute-start(bf16[1024,256]{1,0:T(8,128)(2,1)} %get-tuple-element.114), channel_id=1, source_target_pairs={{0,8},{2,10},{4,12},{6,14},{8,0},{10,2},{12,4},{14,6},{16,24},{18,... | collective-permute-start | bytes 1572872 | tf_op jit(solution)/shard_map/ppermute | solution.py:597
  263.3 1.2 copy-done.7
  264.6 1.1 copy-done.19
  265.6 1.1 copy-done.21
  266.7 1.1 copy-done.23
  267.7 1.1 copy-done.25
  268.8 3.5 %project_rows.2 = (f32[512,1024]{1,0:T(8,128)S(1)}, f32[512,1024]{1,0:T(8,128)S(1)}) custom-call(s32[1]{0:T(128)} %bitcast.place_ref, s32[1]{0:T(128)} %bitcast.5.stay_ref, bf16[272,1024]{1,0:T(8,128)(2,1)S(1)} %copy-done.19, bf16[272,1024]{1,0:T(8,128)(2,1)S(1)} %copy-done.25, bf16[272,1024]{1,0:T(8,128)(2,1)S(1)} %copy-done.21, ...), custom_call_target="tpu_custom_call" | custom-call | flops 2147483648 | bytes 12582912 | tf_op jit(solution)/shard_map/project_rows/pallas_call | solution.py:450
  272.2 4.0 %collective-permute-done.20.refs_9_ = bf16[1024,256]{1,0:T(8,128)(2,1)S(1)} collective-permute-done((bf16[1024,256]{1,0:T(8,128)(2,1)}, bf16[1024,256]{1,0:T(8,128)(2,1)S(1)}, u32[]{:S(2)}, u32[]{:S(2)}) %collective-permute-start.20) | collective-permute-done | bytes 524320 | tf_op jit(solution)/shard_map/ppermute | solution.py:597
  276.3 7.0 %collective-permute-done.21.refs_11_ = bf16[1024,256]{1,0:T(8,128)(2,1)} collective-permute-done((bf16[1024,256]{1,0:T(8,128)(2,1)}, bf16[1024,256]{1,0:T(8,128)(2,1)}, u32[]{:S(2)}, u32[]{:S(2)}) %collective-permute-start.21) | collective-permute-done | bytes 524320 | tf_op jit(solution)/shard_map/ppermute | solution.py:597
  283.3 5.2 %project_rows.3 = (bf16[512,1024]{1,0:T(8,128)(2,1)S(1)}, bf16[512,1024]{1,0:T(8,128)(2,1)S(1)}) custom-call(s32[1]{0:T(128)} %bitcast.place_ref, s32[1]{0:T(128)} %bitcast.5.stay_ref, bf16[272,1024]{1,0:T(8,128)(2,1)} %get-tuple-element.111.refs_0_, bf16[272,1024]{1,0:T(8,128)(2,1)S(1)} %collective-permute-done.13.refs_1_, ...), custom_call_target="tpu_custom_call" | custom-call | flops 2147483648 | bytes 12582912 | tf_op jit(solution)/shard_map/project_rows/pallas_call | solution.py:450
  288.6 2.6 collective-permute-done.22
  291.3 1.2 add_cores.1
  292.5 3.5 %collective-permute-start.25 = (bf16[128,1024]{1,0:T(8,128)(2,1)S(1)}, bf16[128,1024]{1,0:T(8,128)(2,1)S(1)}, u32[]{:S(2)}, u32[]{:S(2)}) collective-permute-start(bf16[128,1024]{1,0:T(8,128)(2,1)S(1)} %get-tuple-element.129), channel_id=1, source_target_pairs={{0,6},{2,4},{4,2},{6,0},{8,14},{10,12},{12,10},{14,8},{16,22},{18,... | collective-permute-start | bytes 786440 | tf_op jit(solution)/shard_map/ppermute | solution.py:597
  296.0 5.8 %collective-permute-done.23.refs_1_ = bf16[128,1024]{1,0:T(8,128)(2,1)S(1)} collective-permute-done((bf16[128,1024]{1,0:T(8,128)(2,1)}, bf16[128,1024]{1,0:T(8,128)(2,1)S(1)}, u32[]{:S(2)}, u32[]{:S(2)}) %collective-permute-start.23) | collective-permute-done | bytes 262176 | tf_op jit(solution)/shard_map/ppermute | solution.py:597
  301.8 4.8 %collective-permute-done.24.refs_2_ = bf16[128,1024]{1,0:T(8,128)(2,1)S(1)} collective-permute-done((bf16[128,1024]{1,0:T(8,128)(2,1)}, bf16[128,1024]{1,0:T(8,128)(2,1)S(1)}, u32[]{:S(2)}, u32[]{:S(2)}) %collective-permute-start.24) | collective-permute-done | bytes 262176 | tf_op jit(solution)/shard_map/ppermute | solution.py:597
  306.7 1.2 copy-done.10
  307.9 3.4 %add_norm.1 = (bf16[128,4096]{1,0:T(8,128)(2,1)}, bf16[128,4096]{1,0:T(8,128)(2,1)}) custom-call(s32[1]{0:T(128)} %bitcast.place_ref, s32[4]{0:T(128)S(1)} %pad_add_fusion.line_ref, bf16[128,1024]{1,0:T(8,128)(2,1)S(1)} %get-tuple-element.126.refs_0_, bf16[128,1024]{1,0:T(8,128)(2,1)S(1)} %collective-permute-done.23.refs_1_, ...), custom_call_target="tpu_custom_call" | custom-call | tf_op jit(solution)/shard_map/add_norm/pallas_call | solution.py:535
  (91 shorter events, 8.2 us)
Async XLA Ops:
  1.4 6.8 %collective-permute-start.3 = (bf16[1,2048]{1,0:T(2,128)(2,1)S(1)}, bf16[1,2048]{1,0:T(2,128)(2,1)S(1)}, u32[]{:S(2)}, u32[]{:S(2)}) collective-permute-start(bf16[1,2048]{1,0:T(2,128)(2,1)S(1)} %slice.23), channel_id=1, source_target_pairs={{0,2},{2,4},{4,6},{6,8},{8,10},{10,12},{12,14},{14,16},{16,18},{18... | collective-permute-start | bytes 12296 | tf_op jit(solution)/shard_map/ppermute | solution.py:23
  8.2 1.2 copy-start.4
  11.7 5.1 %copy-start.5 = (bf16[256,2048]{1,0:T(8,128)(2,1)S(1)}, bf16[256,2048]{1,0:T(8,128)(2,1)}, u32[]{:S(2)}) copy-start(bf16[256,2048]{1,0:T(8,128)(2,1)} %refs_0_.1) | copy-start | bytes 3145732
  11.7 46.4 %all-to-all-start.1 = ((bf16[8,64,2176]{2,1,0:T(8,128)(2,1)}), bf16[8,64,2176]{2,1,0:T(8,128)(2,1)S(1)}, u32[]{:S(2)}, u32[]{:S(2)}) async-start(bf16[8,64,2176]{2,1,0:T(8,128)(2,1)} %spread_queries.3), calls=%async_computation.1 | async-start | bytes 4456448 | tf_op jit(solution)/shard_map/all_to_all | solution.py:592
  17.7 46.5 %copy-start.2 = (bf16[2048,256]{1,0:T(8,128)(2,1)S(1)}, bf16[2048,256]{1,0:T(8,128)(2,1)}, u32[]{:S(2)}) copy-start(bf16[2048,256]{1,0:T(8,128)(2,1)} %refs_12_) | copy-start | bytes 3145732
  17.7 38.3 %collective-permute-start = (bf16[256,1024]{1,0:T(8,128)(2,1)S(1)}, bf16[256,1024]{1,0:T(8,128)(2,1)S(1)}, u32[]{:S(2)}, u32[]{:S(2)}) collective-permute-start(bf16[256,1024]{1,0:T(8,128)(2,1)S(1)} %get-tuple-element.137), channel_id=1, source_target_pairs={{0,16},{2,18},{4,20},{6,22},{8,24},{10,26},{12,28},{14,30},{16,0},... | collective-permute-start | bytes 1572872 | tf_op jit(solution)/shard_map/ppermute | solution.py:603
  21.0 35.0 %collective-permute-start.1 = (bf16[1,2048]{1,0:T(2,128)(2,1)S(1)}, bf16[1,2048]{1,0:T(2,128)(2,1)S(1)}, u32[]{:S(2)}, u32[]{:S(2)}) collective-permute-start(bf16[1,2048]{1,0:T(2,128)(2,1)S(1)} %slice.23), channel_id=1, source_target_pairs={{0,18},{2,20},{4,22},{6,24},{8,26},{10,28},{12,30},{14,0},{16,2},{... | collective-permute-start | bytes 12296 | tf_op jit(solution)/shard_map/ppermute | solution.py:618
  24.4 27.5 %collective-permute-start.2 = (s32[1,128]{1,0:T(1,128)S(1)}, s32[1,128]{1,0:T(1,128)S(1)}, u32[]{:S(2)}, u32[]{:S(2)}) collective-permute-start(s32[1,128]{1,0:T(1,128)S(1)} %pad_bitcast_fusion), channel_id=1, source_target_pairs={{0,16},{2,18},{4,20},{6,22},{8,24},{10,26},{12,28},{14,30},{16,0},... | collective-permute-start | bytes 1544 | tf_op jit(solution)/shard_map/ppermute | solution.py:603
  56.0 9.2 %copy-start.13 = (bf16[1,2048]{1,0:T(2,128)(2,1)}, bf16[1,2048]{1,0:T(2,128)(2,1)S(1)}, u32[]{:S(2)}) copy-start(bf16[1,2048]{1,0:T(2,128)(2,1)S(1)} %collective-permute-done.1.carried_ref) | copy-start | bytes 12292
  56.3 9.0 %copy-start.16 = (s32[8]{0:T(128)}, s32[8]{0:T(128)S(1)}, u32[]{:S(2)}) copy-start(s32[8]{0:T(128)S(1)} %get-tuple-element.130.slot_ref) | copy-start | bytes 100
  56.3 9.0 %copy-start.17 = (s32[8]{0:T(128)}, s32[8]{0:T(128)S(1)}, u32[]{:S(2)}) copy-start(s32[8]{0:T(128)S(1)} %get-tuple-element.131.block_ref) | copy-start | bytes 100
  58.1 7.1 %copy-start.26 = (bf16[8,64,2176]{2,1,0:T(8,128)(2,1)}, bf16[8,64,2176]{2,1,0:T(8,128)(2,1)S(1)}, u32[]{:S(2)}) copy-start(bf16[8,64,2176]{2,1,0:T(8,128)(2,1)S(1)} %all-to-all-done.1.tag_ref.query_ref) | copy-start | bytes 6684676
  58.1 29.4 %all-to-all-start = ((bf16[8,64,1152]{2,1,0:T(8,128)(2,1)}), bf16[8,64,1152]{2,1,0:T(8,128)(2,1)}, u32[]{:S(2)}, u32[]{:S(2)}) async-start(bf16[8,64,1152]{2,1,0:T(8,128)(2,1)} %spread_queries.4), calls=%async_computation | async-start | bytes 2359296 | tf_op jit(solution)/shard_map/all_to_all | solution.py:592
  63.3 22.1 %collective-permute-start.4 = (bf16[256,1024]{1,0:T(8,128)(2,1)}, bf16[256,1024]{1,0:T(8,128)(2,1)}, u32[]{:S(2)}, u32[]{:S(2)}) collective-permute-start(bf16[256,1024]{1,0:T(8,128)(2,1)} %get-tuple-element.69), channel_id=1, source_target_pairs={{0,16},{2,18},{4,20},{6,22},{8,24},{10,26},{12,28},{14,30},{16,0},... | collective-permute-start | bytes 1572872 | tf_op jit(solution)/shard_map/ppermute | solution.py:603
  90.6 4.8 %copy-start.27 = (bf16[1024,256]{1,0:T(8,128)(2,1)S(1)}, bf16[1024,256]{1,0:T(8,128)(2,1)}, u32[]{:S(2)}) copy-start(bf16[1024,256]{1,0:T(8,128)(2,1)} %get-tuple-element.83) | copy-start | bytes 1572868
  90.6 42.0 %all-to-all-start.2 = ((bf16[8,64,2304]{2,1,0:T(8,128)(2,1)}), bf16[8,64,2304]{2,1,0:T(8,128)(2,1)S(1)}, u32[]{:S(2)}, u32[]{:S(2)}) async-start(bf16[8,64,2304]{2,1,0:T(8,128)(2,1)} %spread_queries.5), calls=%async_computation.2 | async-start | bytes 4718592 | tf_op jit(solution)/shard_map/all_to_all | solution.py:592
  95.3 35.1 %collective-permute-start.5 = (bf16[1024,256]{1,0:T(8,128)(2,1)S(1)}, bf16[1024,256]{1,0:T(8,128)(2,1)}, u32[]{:S(2)}, u32[]{:S(2)}) collective-permute-start(bf16[1024,256]{1,0:T(8,128)(2,1)S(1)} %copy-done.27), channel_id=1, source_target_pairs={{0,16},{2,18},{4,20},{6,22},{8,24},{10,26},{12,28},{14,30},{16,0},... | collective-permute-start | bytes 1572872 | tf_op jit(solution)/shard_map/ppermute | solution.py:603
  132.6 1.5 copy-start
  134.0 42.0 %all-to-all-start.3 = ((bf16[8,64,2304]{2,1,0:T(8,128)(2,1)}), bf16[8,64,2304]{2,1,0:T(8,128)(2,1)S(1)}, u32[]{:S(2)}, u32[]{:S(2)}) async-start(bf16[8,64,2304]{2,1,0:T(8,128)(2,1)} %attend_blocks.6), calls=%async_computation.3 | async-start | bytes 4718592 | tf_op jit(solution)/shard_map/all_to_all | solution.py:592
  137.8 36.3 %collective-permute-start.6 = (bf16[1024,256]{1,0:T(8,128)(2,1)}, bf16[1024,256]{1,0:T(8,128)(2,1)}, u32[]{:S(2)}, u32[]{:S(2)}) collective-permute-start(bf16[1024,256]{1,0:T(8,128)(2,1)} %get-tuple-element.114), channel_id=1, source_target_pairs={{0,16},{2,18},{4,20},{6,22},{8,24},{10,26},{12,28},{14,30},{16,0},... | collective-permute-start | bytes 1572872 | tf_op jit(solution)/shard_map/ppermute | solution.py:603
  176.1 34.3 %all-to-all-start.4 = ((bf16[8,64,1152]{2,1,0:T(8,128)(2,1)}), bf16[8,64,1152]{2,1,0:T(8,128)(2,1)S(1)}, u32[]{:S(2)}, u32[]{:S(2)}) async-start(bf16[8,64,1152]{2,1,0:T(8,128)(2,1)} %attend_blocks.7), calls=%async_computation.4 | async-start | bytes 2359296 | tf_op jit(solution)/shard_map/all_to_all | solution.py:592
  179.8 5.5 %copy-start.28 = (bf16[1024,256]{1,0:T(8,128)(2,1)S(1)}, bf16[1024,256]{1,0:T(8,128)(2,1)}, u32[]{:S(2)}) copy-start(bf16[1024,256]{1,0:T(8,128)(2,1)} %get-tuple-element.83) | copy-start | bytes 1572868
  181.9 27.7 %collective-permute-start.7 = (bf16[4,64,1152]{2,1,0:T(8,128)(2,1)S(1)}, bf16[4,64,1152]{2,1,0:T(8,128)(2,1)S(1)}, u32[]{:S(2)}, u32[]{:S(2)}) collective-permute-start(bf16[4,64,1152]{2,1,0:T(8,128)(2,1)S(1)} %merge_far.2), channel_id=1, source_target_pairs={{0,16},{2,18},{4,20},{6,22},{8,24},{10,26},{12,28},{14,30},{16,0},... | collective-permute-start | bytes 1769480 | tf_op jit(solution)/shard_map/ppermute | solution.py:603
  209.6 0.8 copy-start.11
  210.4 5.9 %copy-start.1 = (bf16[8,64,2304]{2,1,0:T(8,128)(2,1)S(1)}, bf16[8,64,2304]{2,1,0:T(8,128)(2,1)}, u32[]{:S(2)}) copy-start(bf16[8,64,2304]{2,1,0:T(8,128)(2,1)} %copy-done) | copy-start | bytes 7077892
  210.4 5.9 %copy-start.12 = (bf16[4,64,1152]{2,1,0:T(8,128)(2,1)S(1)}, bf16[4,64,1152]{2,1,0:T(8,128)(2,1)}, u32[]{:S(2)}) copy-start(bf16[4,64,1152]{2,1,0:T(8,128)(2,1)} %copy-done.11) | copy-start | bytes 1769476
  212.4 34.1 %collective-permute-start.12 = (bf16[2048,256]{1,0:T(8,128)(2,1)}, bf16[2048,256]{1,0:T(8,128)(2,1)S(1)}, u32[]{:S(2)}, u32[]{:S(2)}) collective-permute-start(bf16[2048,256]{1,0:T(8,128)(2,1)} %pad_maximum_fusion), channel_id=1, source_target_pairs={{0,8},{2,10},{4,12},{6,14},{8,0},{10,2},{12,4},{14,6},{16,24},{18,... | collective-permute-start | bytes 3145736 | tf_op jit(solution)/shard_map/ppermute | solution.py:597
  213.0 31.8 %collective-permute-start.8 = (bf16[4,64,1152]{2,1,0:T(8,128)(2,1)S(1)}, bf16[4,64,1152]{2,1,0:T(8,128)(2,1)S(1)}, u32[]{:S(2)}, u32[]{:S(2)}) collective-permute-start(bf16[4,64,1152]{2,1,0:T(8,128)(2,1)S(1)} %merge_far.3), channel_id=1, source_target_pairs={{0,16},{2,18},{4,20},{6,22},{8,24},{10,26},{12,28},{14,30},{16,0},... | collective-permute-start | bytes 1769480 | tf_op jit(solution)/shard_map/ppermute | solution.py:603
  218.8 26.0 %collective-permute-start.10 = (bf16[272,1024]{1,0:T(8,128)(2,1)S(1)}, bf16[272,1024]{1,0:T(8,128)(2,1)S(1)}, u32[]{:S(2)}, u32[]{:S(2)}) collective-permute-start(bf16[272,1024]{1,0:T(8,128)(2,1)S(1)} %get-tuple-element.118.refs_0_), channel_id=1, source_target_pairs={{0,4},{2,6},{4,0},{6,2},{8,12},{10,14},{12,8},{14,10},{16,20},{18,... | collective-permute-start | bytes 1671176 | tf_op jit(solution)/shard_map/ppermute | solution.py:597
  220.3 24.5 %collective-permute-start.11 = (bf16[272,1024]{1,0:T(8,128)(2,1)S(1)}, bf16[272,1024]{1,0:T(8,128)(2,1)S(1)}, u32[]{:S(2)}, u32[]{:S(2)}) collective-permute-start(bf16[272,1024]{1,0:T(8,128)(2,1)S(1)} %get-tuple-element.118.refs_0_), channel_id=1, source_target_pairs={{0,6},{2,4},{4,2},{6,0},{8,14},{10,12},{12,10},{14,8},{16,22},{18,... | collective-permute-start | bytes 1671176 | tf_op jit(solution)/shard_map/ppermute | solution.py:597
  221.8 23.9 %collective-permute-start.9 = (bf16[272,1024]{1,0:T(8,128)(2,1)S(1)}, bf16[272,1024]{1,0:T(8,128)(2,1)S(1)}, u32[]{:S(2)}, u32[]{:S(2)}) collective-permute-start(bf16[272,1024]{1,0:T(8,128)(2,1)S(1)} %get-tuple-element.118.refs_0_), channel_id=1, source_target_pairs={{0,2},{2,0},{4,6},{6,4},{8,10},{10,8},{12,14},{14,12},{16,18},{18,... | collective-permute-start | bytes 1671176 | tf_op jit(solution)/shard_map/ppermute | solution.py:597
  222.3 0.8 copy-start.18
  244.8 4.8 %copy-start.20 = (bf16[272,1024]{1,0:T(8,128)(2,1)}, bf16[272,1024]{1,0:T(8,128)(2,1)S(1)}, u32[]{:S(2)}) copy-start(bf16[272,1024]{1,0:T(8,128)(2,1)S(1)} %collective-permute-done.10.refs_2_) | copy-start | bytes 1671172
  244.8 0.8 copy-start.22
  245.6 0.8 copy-start.24
  246.4 3.2 %copy-start.6 = (bf16[2048,256]{1,0:T(8,128)(2,1)}, bf16[2048,256]{1,0:T(8,128)(2,1)S(1)}, u32[]{:S(2)}) copy-start(bf16[2048,256]{1,0:T(8,128)(2,1)S(1)} %collective-permute-done.12.refs_5_.refs_7_.refs_13_.refs_15_) | copy-start | bytes 3145732
  246.4 16.9 %copy-start.3 = (bf16[2048,256]{1,0:T(8,128)(2,1)S(1)}, bf16[2048,256]{1,0:T(8,128)(2,1)}, u32[]{:S(2)}) copy-start(bf16[2048,256]{1,0:T(8,128)(2,1)} %refs_12_) | copy-start | bytes 3145732
  249.6 8.4 %collective-permute-start.16 = (bf16[16,2048]{1,0:T(8,128)(2,1)S(1)}, bf16[16,2048]{1,0:T(8,128)(2,1)S(1)}, u32[]{:S(2)}, u32[]{:S(2)}) collective-permute-start(bf16[16,2048]{1,0:T(8,128)(2,1)S(1)} %get-tuple-element.112), channel_id=1, source_target_pairs={{8,0},{16,8},{24,16},{9,1},{17,9},{25,17}} | collective-permute-start | bytes 196616 | tf_op jit(solution)/shard_map/ppermute | solution.py:705
  250.9 7.1 %collective-permute-start.17 = (bf16[16,2048]{1,0:T(8,128)(2,1)S(1)}, bf16[16,2048]{1,0:T(8,128)(2,1)S(1)}, u32[]{:S(2)}, u32[]{:S(2)}) collective-permute-start(bf16[16,2048]{1,0:T(8,128)(2,1)S(1)} %get-tuple-element.112), channel_id=1, source_target_pairs={{8,2},{16,10},{24,18},{9,3},{17,11},{25,19}} | collective-permute-start | bytes 196616 | tf_op jit(solution)/shard_map/ppermute | solution.py:705
  251.6 6.4 %collective-permute-start.18 = (bf16[16,2048]{1,0:T(8,128)(2,1)S(1)}, bf16[16,2048]{1,0:T(8,128)(2,1)S(1)}, u32[]{:S(2)}, u32[]{:S(2)}) collective-permute-start(bf16[16,2048]{1,0:T(8,128)(2,1)S(1)} %get-tuple-element.112), channel_id=1, source_target_pairs={{8,4},{16,12},{24,20},{9,5},{17,13},{25,21}} | collective-permute-start | bytes 196616 | tf_op jit(solution)/shard_map/ppermute | solution.py:705
  252.2 11.0 %collective-permute-start.19 = (bf16[16,2048]{1,0:T(8,128)(2,1)S(1)}, bf16[16,2048]{1,0:T(8,128)(2,1)S(1)}, u32[]{:S(2)}, u32[]{:S(2)}) collective-permute-start(bf16[16,2048]{1,0:T(8,128)(2,1)S(1)} %get-tuple-element.112), channel_id=1, source_target_pairs={{8,6},{16,14},{24,22},{9,7},{17,15},{25,23}} | collective-permute-start | bytes 196616 | tf_op jit(solution)/shard_map/ppermute | solution.py:705
  252.9 30.4 %collective-permute-start.13 = (bf16[272,1024]{1,0:T(8,128)(2,1)}, bf16[272,1024]{1,0:T(8,128)(2,1)S(1)}, u32[]{:S(2)}, u32[]{:S(2)}) collective-permute-start(bf16[272,1024]{1,0:T(8,128)(2,1)} %get-tuple-element.111.refs_0_), channel_id=1, source_target_pairs={{0,2},{2,0},{4,6},{6,4},{8,10},{10,8},{12,14},{14,12},{16,18},{18,... | collective-permute-start | bytes 1671176 | tf_op jit(solution)/shard_map/ppermute | solution.py:597
  258.0 25.3 %collective-permute-start.14 = (bf16[272,1024]{1,0:T(8,128)(2,1)}, bf16[272,1024]{1,0:T(8,128)(2,1)S(1)}, u32[]{:S(2)}, u32[]{:S(2)}) collective-permute-start(bf16[272,1024]{1,0:T(8,128)(2,1)} %get-tuple-element.111.refs_0_), channel_id=1, source_target_pairs={{0,4},{2,6},{4,0},{6,2},{8,12},{10,14},{12,8},{14,10},{16,20},{18,... | collective-permute-start | bytes 1671176 | tf_op jit(solution)/shard_map/ppermute | solution.py:597
  258.0 25.3 %collective-permute-start.15 = (bf16[272,1024]{1,0:T(8,128)(2,1)}, bf16[272,1024]{1,0:T(8,128)(2,1)S(1)}, u32[]{:S(2)}, u32[]{:S(2)}) collective-permute-start(bf16[272,1024]{1,0:T(8,128)(2,1)} %get-tuple-element.111.refs_0_), channel_id=1, source_target_pairs={{0,6},{2,4},{4,2},{6,0},{8,14},{10,12},{12,10},{14,8},{16,22},{18,... | collective-permute-start | bytes 1671176 | tf_op jit(solution)/shard_map/ppermute | solution.py:597
  258.0 18.3 %collective-permute-start.20 = (bf16[1024,256]{1,0:T(8,128)(2,1)}, bf16[1024,256]{1,0:T(8,128)(2,1)S(1)}, u32[]{:S(2)}, u32[]{:S(2)}) collective-permute-start(bf16[1024,256]{1,0:T(8,128)(2,1)} %get-tuple-element.114), channel_id=1, source_target_pairs={{0,8},{2,10},{4,12},{6,14},{8,0},{10,2},{12,4},{14,6},{16,24},{18,... | collective-permute-start | bytes 1572872 | tf_op jit(solution)/shard_map/ppermute | solution.py:597
  263.3 20.1 %collective-permute-start.21 = (bf16[1024,256]{1,0:T(8,128)(2,1)}, bf16[1024,256]{1,0:T(8,128)(2,1)}, u32[]{:S(2)}, u32[]{:S(2)}) collective-permute-start(bf16[1024,256]{1,0:T(8,128)(2,1)} %collective-permute-done.6.refs_10_), channel_id=1, source_target_pairs={{0,8},{2,10},{4,12},{6,14},{8,0},{10,2},{12,4},{14,6},{16,24},{18,... | collective-permute-start | bytes 1572872 | tf_op jit(solution)/shard_map/ppermute | solution.py:597
  263.3 1.2 copy-start.7
  264.6 1.1 copy-start.19
  265.6 1.1 copy-start.21
  266.7 1.1 copy-start.23
  267.7 1.1 copy-start.25
  268.8 14.6 %copy-start.8 = (bf16[2048,256]{1,0:T(8,128)(2,1)S(1)}, bf16[2048,256]{1,0:T(8,128)(2,1)}, u32[]{:S(2)}) copy-start(bf16[2048,256]{1,0:T(8,128)(2,1)} %copy-done.6) | copy-start | bytes 3145732
  288.5 18.1 %copy-start.9 = (s32[128,4096]{1,0:T(8,128)S(1)}, s32[128,4096]{1,0:T(8,128)}, u32[]{:S(2)}) copy-start(s32[128,4096]{1,0:T(8,128)} %refs_5_.1) | copy-start | bytes 6291460
  288.5 18.1 %copy-start.14 = (f32[4096]{0:T(1024)S(1)}, f32[4096]{0:T(1024)}, u32[]{:S(2)}) copy-start(f32[4096]{0:T(1024)} %param.16) | copy-start | bytes 49156
  288.6 18.1 %copy-start.15 = (f32[4096]{0:T(1024)S(1)}, f32[4096]{0:T(1024)}, u32[]{:S(2)}) copy-start(f32[4096]{0:T(1024)} %param.17) | copy-start | bytes 49156
  288.6 2.7 collective-permute-start.22
  292.5 9.4 %collective-permute-start.23 = (bf16[128,1024]{1,0:T(8,128)(2,1)}, bf16[128,1024]{1,0:T(8,128)(2,1)S(1)}, u32[]{:S(2)}, u32[]{:S(2)}) collective-permute-start(bf16[128,1024]{1,0:T(8,128)(2,1)} %get-tuple-element.127), channel_id=1, source_target_pairs={{0,2},{2,0},{4,6},{6,4},{8,10},{10,8},{12,14},{14,12},{16,18},{18,... | collective-permute-start | bytes 786440 | tf_op jit(solution)/shard_map/ppermute | solution.py:597
  292.5 14.2 %collective-permute-start.24 = (bf16[128,1024]{1,0:T(8,128)(2,1)}, bf16[128,1024]{1,0:T(8,128)(2,1)S(1)}, u32[]{:S(2)}, u32[]{:S(2)}) collective-permute-start(bf16[128,1024]{1,0:T(8,128)(2,1)} %get-tuple-element.128), channel_id=1, source_target_pairs={{0,4},{2,6},{4,0},{6,2},{8,12},{10,14},{12,8},{14,10},{16,20},{18,... | collective-permute-start | bytes 786440 | tf_op jit(solution)/shard_map/ppermute | solution.py:597
  292.5 14.2 %collective-permute-start.25 = (bf16[128,1024]{1,0:T(8,128)(2,1)S(1)}, bf16[128,1024]{1,0:T(8,128)(2,1)S(1)}, u32[]{:S(2)}, u32[]{:S(2)}) collective-permute-start(bf16[128,1024]{1,0:T(8,128)(2,1)S(1)} %get-tuple-element.129), channel_id=1, source_target_pairs={{0,6},{2,4},{4,2},{6,0},{8,14},{10,12},{12,10},{14,8},{16,22},{18,... | collective-permute-start | bytes 786440 | tf_op jit(solution)/shard_map/ppermute | solution.py:597
  306.7 1.2 copy-start.10
